TPU v7x, 32 devices: a whole 2x2x4 slice. The times are simulated.
32 devices in a mesh: seq: 8 (over z, y), head: 2 (over x), dp: 2 (over core).
Axes of the slice: x: 2, y: 2, z: 4, core: 2. Of those that a mesh axis runs over, the one named last changes fastest.
Arguments:
- inputs: bfloat16 [2, 4096, 3584], P('dp', 'seq', 'head'), may hold values from -6 to 6
- value_weight: bfloat16 [3584, 3584], P(None, 'head'), may hold values from -0.09375 to 0.09375
- cotangent: bfloat16 [2, 4096, 3584], P('dp', 'seq', 'head'), may hold values from -6 to 6
- spikes_q: int32 [2, 4096, 3584], P('dp', 'seq', 'head'), may hold values from 0 to 3
- spikes_k: int32 [2, 4096, 3584], P('dp', 'seq', 'head'), may hold values from 0 to 3
- log_decay: float32 [2, 28, 4096], P('dp', 'head', 'seq'), may hold values from -1.0976562 to 0, as said below
Outputs:
- grad_input: bfloat16 [2, 4096, 3584], P('dp', 'seq', 'head')
- grad_weight: float32 [3584, 3584], P(('seq', 'dp'), 'head')
Inputs may be any that keep to these rules, and one draw needn't show every extreme that they name: `spikes_q`: spike count of a token in a channel. `spikes_k`: spike count of a token in a channel. `log_decay`: negative.
All inputs are finite; a program needn't handle non-finite values.
Results may differ from a plain program's by a relative error of at most 0.0051.
Values may be sent and summed in bfloat16 or wider, within the bound.
No kernel may reach another device: no remote copies, remote signals or barrier semaphores. Data moves between devices by JAX's collectives and lax.ppermute only.
A program may use at most 128 MiB of HBM per device.

v0:
```python
import math

import jax
import jax.numpy as jnp
from jax import lax
from jax.sharding import PartitionSpec as P


def carried_in(array, axis, combine, identity):
    count, mine = (lax.axis_size(axis), lax.axis_index(axis))
    everything = jax.tree.map(lambda part: lax.all_gather(part, axis), array)
    start = jax.tree.map(
        lambda part, zero: jnp.broadcast_to(jnp.asarray(zero, part.dtype), part.shape),
        array,
        identity,
    )

    def lap(k, before):
        at = count - 1 - k
        reached = at > mine
        new = combine(before, jax.tree.map(lambda part: part[at], everything))
        return jax.tree.map(lambda a, b: jnp.where(reached, a, b), new, before)

    return lax.fori_loop(0, count, lap, start)


def chain_step(earlier, later_part):
    return (later_part[0] * earlier[0], later_part[1] + later_part[0][:, None, None] * earlier[1])


def local(inputs, value_weight, cotangent, spikes_q, spikes_k, log_decay):
    token_count = inputs.shape[1]
    feature_count = value_weight.shape[1]
    heads_here = log_decay.shape[1]
    head_size = feature_count // heads_here
    block_rows = min(token_count, 512)
    block_count = token_count // block_rows
    seq_length = token_count * lax.axis_size("seq")
    grad_scale = 1.0 / (2.25 * head_size * math.sqrt(seq_length))
    shape_four = (block_count, block_rows, heads_here, head_size)
    query_bf = spikes_q.reshape(shape_four).astype(jnp.bfloat16)
    query_f32 = spikes_q.reshape(shape_four).astype(jnp.float32)
    key_bf = spikes_k.reshape(shape_four).astype(jnp.bfloat16)
    key_f32 = spikes_k.reshape(shape_four).astype(jnp.float32)
    grads_out = cotangent.reshape(shape_four)
    cumulative = jnp.cumsum(log_decay.reshape(heads_here, block_count, block_rows), axis=2)
    scores = jnp.einsum("nthd,nshd->hnts", query_bf, key_bf, preferred_element_type=jnp.float32)
    causal = jnp.arange(block_rows)[:, None] >= jnp.arange(block_rows)[None, :]
    log_gaps = jnp.where(causal, cumulative[..., :, None] - cumulative[..., None, :], -jnp.inf)
    weighted = (scores * jnp.exp(log_gaps)).astype(jnp.bfloat16)
    local_part = jnp.einsum(
        "hnts,nthe->hnse", weighted, grads_out, preferred_element_type=jnp.float32
    )
    query_decayed = query_f32 * jnp.exp(cumulative).transpose(1, 2, 0)[..., None]
    state_terms = jnp.einsum(
        "nthd,nthe->hnde",
        query_decayed,
        grads_out.astype(jnp.float32),
        precision=lax.Precision.HIGHEST,
    )
    decays = jnp.exp(cumulative[..., -1])
    total_decay = decays[:, block_count - 1]
    total_term = state_terms[:, block_count - 1]
    identity = (jnp.ones_like(total_decay), jnp.zeros_like(total_term))
    carry_in = carried_in((total_decay, total_term), "seq", chain_step, identity)[1]
    block_states = [carry_in]
    states = jnp.stack(block_states, axis=1)
    carried = jnp.exp(cumulative[..., -1:] - cumulative)[..., None] * jnp.einsum(
        "nshd,hnde->hnse", key_f32, states, precision=lax.Precision.HIGHEST
    )
    value_grad = (grad_scale * (local_part + carried)).astype(jnp.bfloat16)
    value_grad = value_grad.transpose(1, 2, 0, 3).reshape(token_count, feature_count)
    all_features = lax.all_gather(inputs, "head", axis=2, tiled=True)[0]
    weight_part = lax.psum_scatter(
        lax.dot_general(
            all_features, value_grad, (((0,), (0,)), ((), ())), preferred_element_type=jnp.float32
        ),
        ("seq", "dp"),
        scatter_dimension=0,
        tiled=True,
    )
    grad_weight = weight_part * (1.0 / math.sqrt(lax.axis_size("dp") * seq_length))
    input_term = lax.dot_general(
        value_grad, value_weight, (((1,), (1,)), ((), ())), preferred_element_type=jnp.float32
    )
    grad_input = lax.psum_scatter(input_term, "head", scatter_dimension=1, tiled=True).astype(
        jnp.bfloat16
    )
    return (grad_input.reshape(1, token_count, -1), grad_weight)


def solution(mesh):
    return jax.shard_map(
        local,
        mesh=mesh,
        in_specs=(
            P("dp", "seq", "head"),
            P(None, "head"),
            P("dp", "seq", "head"),
            P("dp", "seq", "head"),
            P("dp", "seq", "head"),
            P("dp", "head", "seq"),
        ),
        out_specs=(P("dp", "seq", "head"), P(("seq", "dp"), "head")),
        check_vma=False,
    )
```

profile of v0, /device:TPU:0, one launch (start us, length us, event | category | flops | bytes accessed | tf_op | source)
XLA Modules:
  0.0 547.4 jit_solution(17932699760438331742)
XLA Ops:
  7.2 0.0 all-gather.7.cloned.1.call-start
  7.2 0.8 copy.49
  8.0 1.1 reduce-window.6
  9.1 0.2 slice_reduce_fusion
  9.3 0.1 copy.51
  9.4 0.1 broadcast.38
  9.5 0.1 exponential_bitcast_fusion
  9.6 2.8 copy.52
  12.4 5.1 copy.45
  17.6 5.4 fusion.10
  22.9 0.0 copy-start
  22.9 2.8 fusion.4
  25.8 0.0 all-gather.7.cloned.1.call-update
  25.8 0.0 all-gather.5.cloned.1.call-start
  25.8 0.7 all-gather.5.cloned.1.call-update
  26.5 0.0 reduce-scatter.5.cloned.1.call-start
  26.6 0.1 iota_compare_fusion
  26.8 0.3 slice_reduce_fusion.1
  27.1 0.0 copy-done
  27.1 0.6 dynamic-slice
  28.2 0.2 dynamic-update-slice
  28.4 23.9 %all-reduce = f32[112]{0:T(128)S(1)} all-reduce(f32[112]{0:T(128)S(1)} %dynamic-update-slice), channel_id=3, replica_groups=mesh['seq'=8,'head'=2,'dp'=2] {'seq'}, use_global_device_ids=true, to_apply=%add | all-reduce | flops 112 | bytes 896
  52.3 0.1 reshape.212
  52.4 5.1 copy.46
  57.5 6.5 %fusion.9 = (f32[1,512,1792]{1,2,0:T(8,128)}, bf16[1,512,1792]{1,2,0:T(8,128)(2,1)}) fusion(s32[1,512,1792]{1,2,0:T(8,128)} %copy.46), kind=kLoop, calls=%fused_computation.25 | loop fusion | flops 1835008 | bytes 9175040 | tf_op jit(solution)/shard_map/convert_element_type | solution.py:44
  64.1 0.1 subtract_exponential_fusion
  64.2 8.3 %fusion.6 = f32[14,512,128]{1,2,0:T(8,128)} fusion(bf16[512,14,128]{0,2,1:T(8,128)(2,1)S(1)} %bitcast.69, bf16[512,14,128]{0,2,1:T(8,128)(2,1)} %bitcast.73, bf16[512,14,128]{0,2,1:T(8,128)(2,1)} %bitcast.74, f32[14,512]{1,0:T(8,128)S(1)} %get-tuple-element.174, pred[512,512]{1,0:T(8,128)(4,1)S(1)} %iota_compare_fusion), kind=kOutput, calls=%fused_computation.11 | convolution fusion | flops 1893728256 | bytes 9465856 | tf_op jit(solution)/shard_map/hnts,nthe->hnse/dot_general | solution.py:51
  72.5 68.4 %all-gather.7.cloned.1.call-done = f32[112,128,128]{2,1,0:T(8,128)} async-done(((f32[14,128,128]{2,1,0:T(8,128)}), f32[112,128,128]{2,1,0:T(8,128)}) %all-gather.7.cloned.1.call-update) | async-done | bytes 7340048 | tf_op jit(solution)/shard_map/all_gather | solution.py:11
  140.9 11.8 %while.16 = (s32[]{:T(128)}, f32[14,128,128]{2,1,0:T(8,128)S(1)}, s32[]{:T(128)}, f32[8,14,128,128]{3,2,1,0:T(8,128)}, f32[8,14]{1,0:T(8,128)S(1)}, /*index=5*/s32[]{:T(128)}, s32[]{:T(128)}, s32[]{:T(128)}, s32[]{:T(128)}) while((s32[]{:T(128)}, f32[14,128,128]{2,1,0:T(8,128)S(1)}, s32[]{:T(128)}, f32[8,14,128,128]{3,2,1,0:T(8,128)}, ...), condition=%wide.region_3.4_spmd.clone, body=%wide.region_2.3_spmd.clone.sunk | while | flops 917512 | bytes 2752855 | solution.py:24
  140.9 1.4 fusion.22
  142.3 1.4 fusion.22
  143.7 1.4 fusion.22
  145.1 1.4 fusion.22
  146.6 1.5 fusion.22
  148.1 1.5 fusion.22
  149.7 1.4 fusion.22
  151.2 1.5 fusion.22
  152.6 6.9 %fusion.3 = bf16[14,512,128]{1,2,0:T(8,128)(2,1)S(1)} fusion(f32[14,512,128]{1,2,0:T(8,128)} %fusion.6, f32[14,128,128]{2,1,0:T(8,128)S(1)} %get-tuple-element.134, f32[512,14,128]{0,2,1:T(8,128)} %bitcast.67, f32[14,512]{1,0:T(8,128)S(1)} %get-tuple-element.173), kind=kOutput, calls=%fused_computation.8 | convolution fusion | flops 1412956160 | bytes 10121216 | tf_op jit(solution)/shard_map/nshd,hnde->hnse/dot_general | solution.py:68
  159.5 11.7 %fusion.11 = f32[512,3584]{1,0:T(8,128)} fusion(bf16[512,1792]{0,1:T(8,128)(2,1)S(1)} %bitcast.71, bf16[3584,1792]{1,0:T(8,128)(2,1)} %param.9), kind=kOutput, calls=%fused_computation.27 | convolution fusion | flops 6576668672 | bytes 22020096 | tf_op jit(solution)/shard_map/dot_general | solution.py:83
  171.3 0.0 reduce-scatter.5.cloned.1.call-update
  171.3 0.3 reduce-scatter.7.cloned.1.call-start
  171.6 19.9 %all-gather.5.cloned.1.call-done = bf16[1,512,3584]{2,1,0:T(8,128)(2,1)} async-done(((bf16[1,512,1792]{2,1,0:T(8,128)(2,1)}), bf16[1,512,3584]{2,1,0:T(8,128)(2,1)}) %all-gather.5.cloned.1.call-update) | async-done | bytes 3670032 | tf_op jit(solution)/shard_map/all_gather | solution.py:73
  191.5 14.9 %convolution_bitcast_fusion = f32[3584,1792]{0,1:T(8,128)} fusion(bf16[512,1792]{0,1:T(8,128)(2,1)S(1)} %bitcast.72, bf16[1,512,3584]{2,1,0:T(8,128)(2,1)} %all-gather.5.cloned.1.call-done), kind=kOutput, calls=%fused_computation.3 | convolution fusion | flops 6576668672 | bytes 31195136 | tf_op jit(solution)/shard_map/dot_general | solution.py:75
  206.3 27.6 %copy.65 = f32[3584,1792]{1,0:T(8,128)} copy(f32[3584,1792]{0,1:T(8,128)} %convolution_bitcast_fusion) | data formatting | bytes 51380224
  234.0 0.0 reduce-scatter.7.cloned.1.call-update
  234.0 48.2 %reduce-scatter.5.cloned.1.call-done = f32[512,1792]{1,0:T(8,128)} async-done(((f32[512,3584]{1,0:T(8,128)}), f32[512,1792]{1,0:T(8,128)}) %reduce-scatter.5.cloned.1.call-update) | async-done | bytes 3670032 | tf_op jit(solution)/shard_map/reduce_scatter | solution.py:86
  282.2 3.4 convert_bitcast_fusion
  285.7 249.3 %reduce-scatter.7.cloned.1.call-done = f32[224,1792]{1,0:T(8,128)} async-done(((f32[3584,1792]{1,0:T(8,128)}), f32[224,1792]{1,0:T(8,128)}) %reduce-scatter.7.cloned.1.call-update) | async-done | bytes 1605648
  535.0 1.8 copy.66
  536.8 1.4 broadcast_multiply_fusion
  538.2 2.7 copy.59
  (19 shorter events, 0.2 us)
Async XLA Ops:
  7.2 133.7 %all-gather.7.cloned.1.call-start = ((), (), s32[]{:S(2)}) async-start(), calls=%async_computation.4 | async-start | bytes 8257536 | tf_op jit(solution)/shard_map/all_gather | solution.py:11
  22.9 4.1 copy-start
  25.8 165.7 %all-gather.5.cloned.1.call-start = ((), (), s32[]{:S(2)}) async-start(), calls=%async_computation.3 | async-start | bytes 5505024 | tf_op jit(solution)/shard_map/all_gather | solution.py:73
  26.5 255.7 %reduce-scatter.5.cloned.1.call-start = ((), (), s32[]{:S(2)}) async-start(), calls=%async_computation.2 | async-start | bytes 11010048 | tf_op jit(solution)/shard_map/reduce_scatter | solution.py:86
  171.3 363.7 %reduce-scatter.7.cloned.1.call-start = ((), (), s32[]{:S(2)}) async-start(), calls=%async_computation.5 | async-start | bytes 27295744
Sparse Core Ops, SparseCore 0:
  25.9 114.9 all-gather.6
  142.4 49.0 all-gather.4
  193.8 88.4 reduce-scatter.4
  286.8 248.1 reduce-scatter.6
where the time goes:
time: 549 us; the launch traced here: 547 us
  waiting for transfers between devices  387 us (70%)
  local copies, waits for them, and re-layouts  47.6 us (9%)
  matrix products  44.6 us (8%)
  other arithmetic  29.6 us (5%)
  blocking collectives  23.9 us (4%)
  between operations  14.5 us (3%)
    unnamed x5, waiting for transfers between devices  250 us
    all_gather x1, waiting for transfers between devices, carried_in(): everything = jax.tree.map(lambda part: lax.all_gather(part, axis), array)  68.4 us
    reduce_scatter x1, waiting for transfers between devices, local(): lax.psum_scatter(input_term, 'head', scatter_dimension=1, tiled=True)  48.2 us
    unnamed x16, local copies, waits for them, and re-layouts  46 us
    unnamed x1, blocking collectives  23.9 us
    all_gather x1, waiting for transfers between devices, local(): all_features = lax.all_gather(inputs, 'head', axis=2, tiled=True)[0]  19.9 us
    dot_general x1, matrix products, local(): lax.dot_general(all_features, value_grad, (((0,), (0,)), ((), ())), prefe...  14.9 us
    dot_general x1, matrix products, local(): lax.dot_general(value_grad, value_weight, (((1,), (1,)), ((), ())), prefe...  11.7 us
  transfers between devices with their start and end apart: 4, of which 4 were waited for; matrix products, arithmetic and copies ran while one was open for 18% of the time, Pallas kernels for 0%

commit v1 on v0

v1 whole, which is shorter than its diff:
```python
import functools
import math

import jax
import jax.numpy as jnp
from jax import lax
from jax.experimental import pallas as pl
from jax.experimental.pallas import tpu as pltpu
from jax.sharding import PartitionSpec as P

BF = jnp.bfloat16
F32 = jnp.float32
HD = 128
PLANE = 16
EXTRA = 3 * PLANE
PARAMS = pltpu.CompilerParams(vmem_limit_bytes=56 * 1024 * 1024)
VM = pl.BlockSpec(memory_space=pltpu.VMEM)
SM = pl.BlockSpec(memory_space=pltpu.SMEM)


def dot(a, b, contract):
    return lax.dot_general(a, b, (contract, ((), ())), preferred_element_type=F32)


def hi_lo(x):
    hi = x.astype(BF)
    return hi, (x - hi.astype(F32)).astype(BF)


def transpose_kernel(a_ref, o_ref):
    o_ref[...] = a_ref[...].T


def transposed(a):
    rows, cols = a.shape
    tile = 256 if cols % 256 == 0 else 128
    return pl.pallas_call(
        transpose_kernel,
        grid=(cols // tile,),
        in_specs=[pl.BlockSpec((rows, tile), lambda i: (0, i))],
        out_specs=pl.BlockSpec((tile, rows), lambda i: (i, 0)),
        out_shape=jax.ShapeDtypeStruct((cols, rows), a.dtype),
        compiler_params=PARAMS,
        name="transpose_inputs",
    )(a)


def state_kernel(first, heads, q_ref, c_ref, ld_ref, pay_ref, own_ref, cum_ref, cumt_ref):
    tokens = ld_ref.shape[1]
    x = ld_ref[first : first + heads, :]
    x = jnp.concatenate([x, jnp.zeros((PLANE - heads, tokens), F32)], axis=0)
    lane = lax.broadcasted_iota(jnp.int32, x.shape, 1)
    shift = 1
    while shift < tokens:
        x = x + jnp.where(lane >= shift, pltpu.roll(x, shift, 1), 0.0)
        shift *= 2
    cum_ref[...] = x
    xt = jnp.concatenate([x, jnp.zeros((HD - PLANE, tokens), F32)], axis=0).T
    cumt_ref[...] = xt
    et = jnp.exp(xt)
    d = jnp.broadcast_to(jnp.exp(x[:, tokens - 1 : tokens]), (PLANE, HD))
    d_hi, d_mid = hi_lo(d)
    d_lo = (d - d_hi.astype(F32) - d_mid.astype(F32)).astype(BF)
    at = heads * HD
    pay_ref[at : at + PLANE, :] = d_hi
    pay_ref[at + PLANE : at + 2 * PLANE, :] = d_mid
    pay_ref[at + 2 * PLANE : at + EXTRA, :] = d_lo
    own_ref[at : at + PLANE, :] = d
    own_ref[at + PLANE : at + EXTRA, :] = jnp.zeros((EXTRA - PLANE, HD), F32)
    for h in range(heads):
        s = slice(h * HD, (h + 1) * HD)
        q = q_ref[:, s].astype(F32).astype(BF)
        hi, lo = hi_lo(c_ref[:, s].astype(F32) * et[:, h : h + 1])
        both = dot(q, jnp.concatenate([hi, lo], axis=1), ((0,), (0,)))
        term = both[:, :HD] + both[:, HD:]
        own_ref[s, :] = term
        pay_ref[s, :] = term.astype(BF)


def state_terms(group, heads, q, c, ld):
    tokens = q.shape[0]
    rows = heads * HD + EXTRA
    cols = pl.BlockSpec((tokens, heads * HD), lambda i: (0, group))
    whole = lambda shape: pl.BlockSpec(shape, lambda i: (0, 0))
    return pl.pallas_call(
        functools.partial(state_kernel, group * heads, heads),
        grid=(1,),
        in_specs=[cols, cols, whole(ld.shape)],
        out_specs=[whole((rows, HD)), whole((rows, HD)), whole((PLANE, tokens)), whole((tokens, HD))],
        out_shape=[
            jax.ShapeDtypeStruct((rows, HD), BF),
            jax.ShapeDtypeStruct((rows, HD), F32),
            jax.ShapeDtypeStruct((PLANE, tokens), F32),
            jax.ShapeDtypeStruct((tokens, HD), F32),
        ],
        compiler_params=PARAMS,
        name="state_terms",
    )(q, c, ld)


def decays(ref, heads):
    p = ref[heads * HD :, :].astype(F32)
    return p[:PLANE] + p[PLANE : 2 * PLANE] + p[2 * PLANE :]


def append_kernel(heads, swap_ref, a_ref, b_ref, pay_ref, own_ref):
    swap = swap_ref[0] != 0
    da, db = decays(a_ref, heads), decays(b_ref, heads)
    one = jnp.ones_like(da)
    scale_a = jnp.where(swap, db, one)
    scale_b = jnp.where(swap, one, da)
    d = da * db
    d_hi, d_mid = hi_lo(d)
    d_lo = (d - d_hi.astype(F32) - d_mid.astype(F32)).astype(BF)
    at = heads * HD
    pay_ref[at : at + PLANE, :] = d_hi
    pay_ref[at + PLANE : at + 2 * PLANE, :] = d_mid
    pay_ref[at + 2 * PLANE : at + EXTRA, :] = d_lo
    own_ref[at : at + PLANE, :] = d
    own_ref[at + PLANE : at + EXTRA, :] = jnp.zeros((EXTRA - PLANE, HD), F32)
    for h in range(heads):
        s = slice(h * HD, (h + 1) * HD)
        term = scale_a[h : h + 1] * a_ref[s, :].astype(F32) + scale_b[h : h + 1] * b_ref[s, :].astype(F32)
        own_ref[s, :] = term
        pay_ref[s, :] = term.astype(BF)


def append(heads, swap, a, b):
    return pl.pallas_call(
        functools.partial(append_kernel, heads),
        in_specs=[SM, VM, VM],
        out_specs=[VM, VM],
        out_shape=[jax.ShapeDtypeStruct(a.shape, BF), jax.ShapeDtypeStruct(a.shape, F32)],
        compiler_params=PARAMS,
        name="join_states",
    )(swap, a, b)


def local_kernel(heads, q_ref, k_ref, c_ref, cum_ref, cumt_ref, o_ref):
    tokens = q_ref.shape[0]
    tile = 128
    for h in range(heads):
        s = slice(h * HD, (h + 1) * HD)
        q = q_ref[:, s].astype(F32).astype(BF)
        k = k_ref[:, s].astype(F32).astype(BF)
        c = c_ref[:, s]
        for at in range(0, tokens, tile):
            scores = dot(k[at : at + tile], q[at:], ((1,), (1,)))
            gap = cum_ref[h : h + 1, at:] - cumt_ref[at : at + tile, h : h + 1]
            row = lax.broadcasted_iota(jnp.int32, gap.shape, 0)
            col = lax.broadcasted_iota(jnp.int32, gap.shape, 1)
            gap = jnp.where(col >= row, gap, -jnp.inf)
            weighted = (scores * jnp.exp(gap)).astype(BF)
            o_ref[at : at + tile, s] = dot(weighted, c[at:], ((1,), (0,)))


def local_part(group, heads, q, k, c, cum, cumt):
    tokens = q.shape[0]
    cols = pl.BlockSpec((tokens, heads * HD), lambda i: (0, group))
    whole = lambda shape: pl.BlockSpec(shape, lambda i: (0, 0))
    return pl.pallas_call(
        functools.partial(local_kernel, heads),
        grid=(1,),
        in_specs=[cols, cols, cols, whole(cum.shape), whole(cumt.shape)],
        out_specs=whole((tokens, heads * HD)),
        out_shape=jax.ShapeDtypeStruct((tokens, heads * HD), F32),
        compiler_params=PARAMS,
        name="local_part",
    )(q, k, c, cum, cumt)


def value_kernel(heads, chunks, scale, first_ref, k_ref, l_ref, cumt_ref, oth_ref, e_ref, r_ref, *outs):
    tokens = k_ref.shape[0]
    first = first_ref[0] != 0
    de = decays(e_ref, heads)
    do = decays(oth_ref, heads)
    use_oth = jnp.where(first, 1.0, 0.0)
    scale_e = jnp.where(first, do, jnp.ones_like(do))
    fall = jnp.exp(cumt_ref[tokens - 1 : tokens, :] - cumt_ref[...])
    h = 0
    for out, count in zip(outs, chunks):
        for j in range(count):
            s = slice(h * HD, (h + 1) * HD)
            e = e_ref[s, :].astype(F32) + de[h : h + 1] * r_ref[s, :].astype(F32)
            carry = use_oth * oth_ref[s, :].astype(F32) + scale_e[h : h + 1] * e
            hi, lo = hi_lo(carry)
            k = k_ref[:, s].astype(F32).astype(BF)
            both = dot(k, jnp.concatenate([hi, lo], axis=1), ((1,), (0,)))
            carried = fall[:, h : h + 1] * (both[:, :HD] + both[:, HD:])
            out[:, j * HD : (j + 1) * HD] = (scale * (l_ref[:, s] + carried)).astype(BF)
            h += 1


def value_grads(group, heads, chunks, scale, first, k, local, cumt, oth, e, r):
    tokens = k.shape[0]
    cols = pl.BlockSpec((tokens, heads * HD), lambda i: (0, group))
    whole = lambda shape: pl.BlockSpec(shape, lambda i: (0, 0))
    return pl.pallas_call(
        functools.partial(value_kernel, heads, chunks, scale),
        grid=(1,),
        in_specs=[SM, cols] + [whole(a.shape) for a in (local, cumt, oth, e, r)],
        out_specs=[whole((tokens, n * HD)) for n in chunks],
        out_shape=[jax.ShapeDtypeStruct((tokens, n * HD), BF) for n in chunks],
        compiler_params=PARAMS,
        name="value_grad",
    )(first, k, local, cumt, oth, e, r)


def input_kernel(at_ref, *refs):
    vs, w_ref, o_ref = refs[:-2], refs[-2], refs[-1]
    start, total = 0, None
    for v in vs:
        width = v.shape[1]
        part = dot(v[...], w_ref[:, start : start + width], ((1,), (1,)))
        total = part if total is None else total + part
        start += width
    o_ref[...] = total.astype(o_ref.dtype)


def input_part(at, vs, w, rows_here, dtype):
    tokens = vs[0].shape[0]
    tile = 256 if rows_here % 256 == 0 else 128
    tiles = rows_here // tile
    spec = pltpu.PrefetchScalarGridSpec(
        num_scalar_prefetch=1,
        grid=(tiles,),
        in_specs=[pl.BlockSpec(v.shape, lambda n, at: (0, 0)) for v in vs]
        + [pl.BlockSpec((tile, w.shape[1]), lambda n, at: (at[0] * tiles + n, 0))],
        out_specs=pl.BlockSpec((tokens, tile), lambda n, at: (0, n)),
    )
    return pl.pallas_call(
        input_kernel,
        grid_spec=spec,
        out_shape=jax.ShapeDtypeStruct((tokens, rows_here), dtype),
        compiler_params=PARAMS,
        name="input_part",
    )(at, *vs, w)


def weight_kernel(side_ref, low_ref, a_ref, v00, v01, v10, v11, o_ref):
    total = None
    for i, vs in enumerate(((v00, v01), (v10, v11))):
        for j, v in enumerate(vs):
            part = dot(a_ref[0, i, j, 0], v[...], ((1,), (0,)))
            total = part if total is None else total + part
    o_ref[0] = total.astype(o_ref.dtype)


def weight_part(side, low, a, vs, dtype):
    blocks, width = side.shape[0], vs[0].shape[1]
    rows, tokens = a.shape[4:]
    spec = pltpu.PrefetchScalarGridSpec(
        num_scalar_prefetch=2,
        grid=(blocks,),
        in_specs=[pl.BlockSpec((1, 2, 2, 1, rows, tokens), lambda n, side, low: (side[n], 0, 0, low[n], 0, 0))]
        + [pl.BlockSpec(v.shape, lambda n, side, low: (0, 0)) for v in vs],
        out_specs=pl.BlockSpec((1, rows, width), lambda n, side, low: (n, 0, 0)),
    )
    return pl.pallas_call(
        weight_kernel,
        grid_spec=spec,
        out_shape=jax.ShapeDtypeStruct((blocks, rows, width), dtype),
        compiler_params=PARAMS,
        name="weight_part",
    )(side, low, a, *vs)


def swap_with(x, axis, bit):
    return lax.ppermute(x, axis, [(i, i ^ bit) for i in range(lax.axis_size(axis))])


def from_later(x, axis, shift):
    return lax.ppermute(x, axis, [(i, i - shift) for i in range(shift, lax.axis_size(axis))])


def pick(x, at, axis):
    return lax.dynamic_index_in_dim(x, at, axis, keepdims=False)


def local(inputs, value_weight, cotangent, spikes_q, spikes_k, log_decay):
    seqs, sides, dps = lax.axis_size("seq"), lax.axis_size("head"), lax.axis_size("dp")
    seq, side, dp = lax.axis_index("seq"), lax.axis_index("head"), lax.axis_index("dp")
    y, z = seq % 2, seq // 2
    tokens, rows_here = inputs.shape[1:]
    features = value_weight.shape[1]
    heads_here = log_decay.shape[1]
    seq_length = tokens * seqs
    grad_scale = 1.0 / (2.25 * HD * math.sqrt(seq_length))
    groups = 2 if heads_here % 2 == 0 else 1
    heads = heads_here // groups
    chunks = (heads - heads // 2, heads // 2)
    rows = rows_here * sides // (seqs * dps)
    lows = rows_here // (2 * dps * rows)
    stages = (seqs // 2).bit_length() - 1
    y_flag = y.astype(jnp.int32).reshape(1)
    zero_flag = jnp.zeros((1,), jnp.int32)
    first_flag = 1 - y_flag

    q, k, c, ld = spikes_q[0], spikes_k[0], cotangent[0], log_decay[0]

    own = [state_terms(g, heads, q, c, ld) for g in range(groups)]
    other = [swap_with(own[g][0], "seq", 1) for g in range(groups)]

    a = transposed(inputs[0]).reshape(lows, 2, dps, rows, tokens)
    a = jnp.stack([pick(a, y, 1), swap_with(pick(a, 1 - y, 1), "seq", 1)])
    a = jnp.stack([pick(a, dp, 2), swap_with(pick(a, 1 - dp, 2), "dp", 1)])
    a = jnp.stack([a] + [swap_with(a, "head", i) for i in range(1, sides)])

    joined = [append(heads, y_flag, own[g][1], other[g]) for g in range(groups)]
    locals_ = [local_part(g, heads, q, k, c, own[g][2], own[g][3]) for g in range(groups)]
    values = []
    for g in range(groups):
        pay, mine = joined[g]
        e = None
        for stage in range(stages):
            later = from_later(pay, "seq", 2 << stage)
            if stage == 0:
                e = later
            elif stage < stages - 1:
                e = append(heads, zero_flag, e, later)[1]
            if stage < stages - 1:
                pay, mine = append(heads, zero_flag, mine, later)
        last = later if stages > 1 else jnp.zeros_like(later)
        values.append(
            value_grads(g, heads, chunks, grad_scale, first_flag, k, locals_[g], own[g][3], other[g], e, last)
        )
    values = [v for vs in values for v in vs]

    order = [0]
    for stage in range(stages):
        order = [o for o in order] + [o | (1 << stage) for o in order]
    order = [int(format(o, "b").zfill(stages)[::-1], 2) for o in order]
    at_z = jnp.stack([z ^ o for o in order]).astype(jnp.int32)
    block_side = (at_z // lows) ^ side
    block_low = at_z % lows
    half = len(order) // 2

    results = []
    for v in values:
        from_y = swap_with(v, "seq", 1)
        parts = (v, from_y, swap_with(v, "dp", 1), swap_with(from_y, "dp", 1))
        away = weight_part(block_side[half:], block_low[half:], a, parts, BF)
        came = swap_with(away, "seq", 2)
        keep = weight_part(block_side[:half], block_low[:half], a, parts, F32)
        for stage in range(1, stages):
            n = keep.shape[0] // 2
            away = (keep[n:] + came[n:].astype(F32)).astype(BF)
            keep = keep[:n] + came[:n].astype(F32)
            came = swap_with(away, "seq", 2 << stage)
        results.append(keep[0] + came[0].astype(F32))
    grad_weight = jnp.concatenate(results, axis=1) * (1.0 / math.sqrt(dps * seq_length))

    total = None
    at = [(side ^ i).astype(jnp.int32).reshape(1) for i in range(sides)]
    sent = [swap_with(input_part(at[i], values, value_weight, rows_here, BF), "head", i) for i in range(1, sides)]
    total = input_part(at[0], values, value_weight, rows_here, F32)
    for s in sent:
        total = total + s.astype(F32)
    return total.astype(BF)[None], grad_weight


def solution(mesh):
    return jax.shard_map(
        local,
        mesh=mesh,
        in_specs=(
            P("dp", "seq", "head"),
            P(None, "head"),
            P("dp", "seq", "head"),
            P("dp", "seq", "head"),
            P("dp", "seq", "head"),
            P("dp", "head", "seq"),
        ),
        out_specs=(P("dp", "seq", "head"), P(("seq", "dp"), "head")),
        check_vma=False,
    )
```

time: 549 us -> 225 us (0.41)
  waiting for transfers between devices: 387 us -> 71.5 us
  Pallas kernels: 0 us -> 99.8 us
  matrix products: 44.6 us -> 0 us
  local copies, waits for them, and re-layouts: 47.6 us -> 11 us
  starting transfers between devices: 0.38 us -> 28.7 us
  blocking collectives: 23.9 us -> 0 us
  other arithmetic: 29.6 us -> 12.4 us
  between operations: 14.5 us -> 0.92 us
    unnamed x5 -> x0, waiting for transfers between devices: 250 us -> none
    pallas_call x0 -> x21, Pallas kernels: none -> 99.8 us  [the longest x8 35.8 us: weight_part(): pl.pallas_call(weight_kernel, grid_spec=spec, out_shape=jax.ShapeDtypeStr...]
    all_gather x2 -> x0, waiting for transfers between devices: 88.3 us -> none  [the longest x1 68.4 us: carried_in(): everything = jax.tree.map(lambda part: lax.all_gather(part, axis), array)]
    ppermute x0 -> x30, waiting for transfers between devices: none -> 71.5 us  [the longest x26 69.8 us: swap_with(): lax.ppermute(x, axis, [(i, i ^ bit) for i in range(lax.axis_size(axis))])]
    reduce_scatter x1 -> x0, waiting for transfers between devices: 48.2 us -> none  [local(): lax.psum_scatter(input_term, 'head', scatter_dimension=1, tiled=True)]
    dot_general x5 -> x0, matrix products: 44.6 us -> none  [the longest x1 14.9 us: local(): lax.dot_general(all_features, value_grad, (((0,), (0,)), ((), ())), prefe...]
    unnamed x16 -> x49, local copies, waits for them, and re-layouts: 46 us -> 8.05 us
    ppermute x0 -> x30, starting transfers between devices: none -> 28.7 us  [the longest x26 23.5 us: swap_with(): lax.ppermute(x, axis, [(i, i ^ bit) for i in range(lax.axis_size(axis))])]
  transfers between devices with their start and end apart: 4 -> 30, of which waited for: 4 -> 12; matrix products, arithmetic and copies ran while one was open for 18% -> 5% of each run, Pallas kernels for 0% -> 42%
where the time goes in v1:
time: 225 us; the launch traced here: 224 us
  Pallas kernels  99.8 us (44%)
  waiting for transfers between devices  71.5 us (32%)
  starting transfers between devices  28.7 us (13%)
  other arithmetic  12.4 us (6%)
  local copies, waits for them, and re-layouts  11 us (5%)
    ppermute x26, waiting for transfers between devices, swap_with(): lax.ppermute(x, axis, [(i, i ^ bit) for i in range(lax.axis_size(axis))])  69.8 us
    pallas_call x8, Pallas kernels, weight_part(): pl.pallas_call(weight_kernel, grid_spec=spec, out_shape=jax.ShapeDtypeStr...  35.8 us
    ppermute x26, starting transfers between devices, swap_with(): lax.ppermute(x, axis, [(i, i ^ bit) for i in range(lax.axis_size(axis))])  23.5 us
    pallas_call x2, Pallas kernels, input_part(): pl.pallas_call(input_kernel, grid_spec=spec, out_shape=jax.ShapeDtypeStru...  19.2 us
    pallas_call x2, Pallas kernels, local_part(): pl.pallas_call(functools.partial(local_kernel, heads), grid=(1,), in_spec...  15.1 us
    pallas_call x2, Pallas kernels, state_terms(): pl.pallas_call(functools.partial(state_kernel, group * heads, heads), gri...  8.53 us
    pallas_call x4, Pallas kernels, append(): pl.pallas_call(functools.partial(append_kernel, heads), in_specs=[SM, VM,...  8.13 us
    unnamed x49, local copies, waits for them, and re-layouts  8.05 us
  transfers between devices with their start and end apart: 30, of which 12 were waited for; matrix products, arithmetic and copies ran while one was open for 5% of the time, Pallas kernels for 42%

profile of v1, /device:TPU:0, one launch (start us, length us, event | category | flops | bytes accessed | tf_op | source)
XLA Modules:
  0.0 224.2 jit_solution(14952942792089812649)
XLA Ops:
  0.6 5.4 %transpose_inputs.1 = bf16[1792,512]{1,0:T(8,128)(2,1)} custom-call(bf16[512,1792]{1,0:T(8,128)(2,1)} %bitcast.54), custom_call_target="tpu_custom_call" | custom-call | tf_op jit(solution)/shard_map/transpose_inputs/pallas_call | solution.py:37
  6.1 1.6 constant_dynamic-slice_fusion
  7.7 3.0 %collective-permute-start.7 = (bf16[2,2,224,512]{3,2,0,1:T(8,128)(2,1)S(1)}, bf16[2,2,224,512]{3,2,0,1:T(8,128)(2,1)}, u32[]{:S(2)}, u32[]{:S(2)}) collective-permute-start(bf16[2,2,224,512]{3,2,0,1:T(8,128)(2,1)S(1)} %bitcast.55), channel_id=1, source_target_pairs={{0,4},{4,0},{8,12},{12,8},{16,20},{20,16},{24,28},{28,24},{1,5},{5... | collective-permute-start | bytes 2752520 | tf_op jit(solution)/shard_map/ppermute | solution.py:269
  10.8 20.4 %collective-permute-done.7 = bf16[2,2,224,512]{3,2,0,1:T(8,128)(2,1)} collective-permute-done((bf16[2,2,224,512]{3,2,0,1:T(8,128)(2,1)S(1)}, bf16[2,2,224,512]{3,2,0,1:T(8,128)(2,1)}, u32[]{:S(2)}, u32[]{:S(2)}) %collective-permute-start.7) | collective-permute-done | bytes 917536 | tf_op jit(solution)/shard_map/ppermute | solution.py:269
  31.2 1.3 fusion.4
  33.3 4.2 %state_terms.2 = (bf16[944,128]{1,0:T(8,128)(2,1)}, f32[944,128]{1,0:T(8,128)}, f32[16,512]{1,0:T(8,128)}, f32[512,128]{1,0:T(8,128)}) custom-call(s32[512,1792]{1,0:T(8,128)} %bitcast.40, bf16[512,1792]{1,0:T(8,128)(2,1)} %bitcast.48, f32[14,512]{1,0:T(8,128)} %bitcast.57), custom_call_target="tpu_custom_call" | custom-call | tf_op jit(solution)/shard_map/state_terms/pallas_call | solution.py:85
  37.5 1.7 collective-permute-start
  39.2 4.3 %state_terms.3 = (bf16[944,128]{1,0:T(8,128)(2,1)}, f32[944,128]{1,0:T(8,128)}, f32[16,512]{1,0:T(8,128)}, f32[512,128]{1,0:T(8,128)}) custom-call(s32[512,1792]{1,0:T(8,128)} %bitcast.41, bf16[512,1792]{1,0:T(8,128)(2,1)} %bitcast.49, f32[14,512]{1,0:T(8,128)} %bitcast.58), custom_call_target="tpu_custom_call" | custom-call | tf_op jit(solution)/shard_map/state_terms/pallas_call | solution.py:85
  43.8 2.1 collective-permute-done.b_ref.oth_ref
  46.0 0.7 copy-done.17
  46.7 2.0 join_states.4
  48.7 1.3 collective-permute-start.1
  50.0 1.7 collective-permute-done.3.b_ref.oth_ref
  52.4 2.0 join_states.6
  54.5 1.3 collective-permute-start.4
  55.8 1.5 fusion.18
  57.2 1.5 collective-permute-start.9
  58.7 0.7 copy-done.18
  59.5 2.0 join_states.5
  61.5 1.3 collective-permute-start.2
  62.8 1.0 collective-permute-done.4.b_ref.e_ref
  63.7 0.7 copy-done.19
  64.4 2.0 join_states.7
  66.5 1.3 collective-permute-start.5
  67.8 7.6 %local_part.2.l_ref = f32[512,896]{1,0:T(8,128)} custom-call(s32[512,1792]{1,0:T(8,128)} %bitcast.42, s32[512,1792]{1,0:T(8,128)} %bitcast.44, bf16[512,1792]{1,0:T(8,128)(2,1)} %bitcast.50, f32[16,512]{1,0:T(8,128)} %get-tuple-element.20.cum_ref, f32[512,128]{1,0:T(8,128)} %get-tuple-element.21.cumt_ref), custom_call_target="tpu_custom_call" | custom-call | tf_op jit(solution)/shard_map/local_part/pallas_call | solution.py:161
  75.3 7.6 %local_part.3.l_ref = f32[512,896]{1,0:T(8,128)} custom-call(s32[512,1792]{1,0:T(8,128)} %bitcast.43, s32[512,1792]{1,0:T(8,128)} %bitcast.45, bf16[512,1792]{1,0:T(8,128)(2,1)} %bitcast.51, f32[16,512]{1,0:T(8,128)} %get-tuple-element.29.cum_ref, f32[512,128]{1,0:T(8,128)} %get-tuple-element.30.cumt_ref), custom_call_target="tpu_custom_call" | custom-call | tf_op jit(solution)/shard_map/local_part/pallas_call | solution.py:161
  82.9 0.8 collective-permute-done.2.r_ref
  83.7 0.7 copy-done.21
  84.4 3.7 %value_grad.2 = (bf16[512,512]{1,0:T(8,128)(2,1)}, bf16[512,384]{1,0:T(8,128)(2,1)}) custom-call(s32[1]{0:T(128)S(6)} %sub.17.first_ref, s32[512,1792]{1,0:T(8,128)} %bitcast.46, f32[512,896]{1,0:T(8,128)} %local_part.2.l_ref, f32[512,128]{1,0:T(8,128)} %get-tuple-element.21.cumt_ref, bf16[944,128]{1,0:T(8,128)(2,1)} %copy-done.17, ...), custom_call_target="tpu_custom_call" | custom-call | tf_op jit(solution)/shard_map/value_grad/pallas_call | solution.py:198
  88.8 3.8 %value_grad.3 = (bf16[512,512]{1,0:T(8,128)(2,1)}, bf16[512,384]{1,0:T(8,128)(2,1)}) custom-call(s32[1]{0:T(128)S(6)} %sub.17.first_ref, s32[512,1792]{1,0:T(8,128)} %bitcast.47, f32[512,896]{1,0:T(8,128)} %local_part.3.l_ref, f32[512,128]{1,0:T(8,128)} %get-tuple-element.30.cumt_ref, bf16[944,128]{1,0:T(8,128)(2,1)} %copy-done.16, ...), custom_call_target="tpu_custom_call" | custom-call | tf_op jit(solution)/shard_map/value_grad/pallas_call | solution.py:198
  92.6 9.6 %input_part.3 = bf16[512,1792]{1,0:T(8,128)(2,1)} custom-call(s32[1]{0:T(128)} %bitcast.5.at_ref, bf16[512,512]{1,0:T(8,128)(2,1)} %get-tuple-element.27.refs_0_.v00, bf16[512,384]{1,0:T(8,128)(2,1)} %get-tuple-element.28.refs_1_.v00, bf16[512,512]{1,0:T(8,128)(2,1)} %get-tuple-element.36.refs_2_.v00, bf16[512,384]{1,0:T(8,128)(2,1)} %get-tuple-element.37.refs_3_.v00, ...), custom_call_target="tpu_custom_call" | custom-call | tf_op jit(solution)/shard_map/input_part/pallas_call | solution.py:231
  102.2 0.8 collective-permute-start.6
  103.0 1.5 collective-permute-start.15
  105.0 10.1 %collective-permute-done.15.v01 = bf16[512,384]{1,0:T(8,128)(2,1)} collective-permute-done((bf16[512,384]{1,0:T(8,128)(2,1)S(1)}, bf16[512,384]{1,0:T(8,128)(2,1)}, u32[]{:S(2)}, u32[]{:S(2)}) %collective-permute-start.15) | collective-permute-done | bytes 393248 | tf_op jit(solution)/shard_map/ppermute | solution.py:269
  115.1 0.8 copy-done.15
  116.5 4.3 %collective-permute-done.25.v01 = bf16[512,384]{1,0:T(8,128)(2,1)S(1)} collective-permute-done((bf16[512,384]{1,0:T(8,128)(2,1)}, bf16[512,384]{1,0:T(8,128)(2,1)S(1)}, u32[]{:S(2)}, u32[]{:S(2)}) %collective-permute-start.25) | collective-permute-done | bytes 393248 | tf_op jit(solution)/shard_map/ppermute | solution.py:269
  120.8 1.7 collective-permute-start.10
  124.4 9.6 %input_part.2 = f32[512,1792]{1,0:T(8,128)} custom-call(s32[1]{0:T(128)} %bitcast.at_ref, bf16[512,512]{1,0:T(8,128)(2,1)} %get-tuple-element.27.refs_0_.v00, bf16[512,384]{1,0:T(8,128)(2,1)} %get-tuple-element.28.refs_1_.v00, bf16[512,512]{1,0:T(8,128)(2,1)} %get-tuple-element.36.refs_2_.v00, bf16[512,384]{1,0:T(8,128)(2,1)} %get-tuple-element.37.refs_3_.v00, ...), custom_call_target="tpu_custom_call" | custom-call | tf_op jit(solution)/shard_map/input_part/pallas_call | solution.py:231
  134.0 3.6 %pad_maximum_fusion.a_ref = bf16[2,2,2,2,224,512]{5,4,3,2,1,0:T(8,128)(2,1)} fusion(bf16[1,2,2,2,224,512]{5,4,3,2,1,0:T(8,128)(2,1)} %bitcast.20, bf16[1,2,2,2,224,512]{5,4,3,2,1,0:T(8,128)(2,1)S(1)} %get-tuple-element.40), kind=kLoop, calls=%fused_computation | loop fusion | flops 1835008 | bytes 7340032 | tf_op jit(solution)/shard_map/stack | solution.py:307
  137.6 4.5 %weight_part.11 = bf16[2,224,384]{2,1,0:T(8,128)(2,1)} custom-call(s32[2]{0:T(128)} %get-tuple-element.48.side_ref, s32[2]{0:T(128)} %get-tuple-element.46.low_ref, bf16[2,2,2,2,224,512]{5,4,3,2,1,0:T(8,128)(2,1)} %pad_maximum_fusion.a_ref, bf16[512,384]{1,0:T(8,128)(2,1)} %get-tuple-element.28.refs_1_.v00, bf16[512,384]{1,0:T(8,128)(2,1)} %collective-permute-done.15.v01, ...), custom_call_target="tpu_custom_call" | custom-call | tf_op jit(solution)/shard_map/weight_part/pallas_call | solution.py:259
  142.5 1.2 collective-permute-done.20.v01
  144.3 4.3 %weight_part.15 = bf16[2,224,384]{2,1,0:T(8,128)(2,1)} custom-call(s32[2]{0:T(128)} %get-tuple-element.48.side_ref, s32[2]{0:T(128)} %get-tuple-element.46.low_ref, bf16[2,2,2,2,224,512]{5,4,3,2,1,0:T(8,128)(2,1)} %pad_maximum_fusion.a_ref, bf16[512,384]{1,0:T(8,128)(2,1)} %get-tuple-element.37.refs_3_.v00, bf16[512,384]{1,0:T(8,128)(2,1)} %copy-done.14, ...), custom_call_target="tpu_custom_call" | custom-call | tf_op jit(solution)/shard_map/weight_part/pallas_call | solution.py:259
  148.6 0.9 collective-permute-start.18
  149.6 1.2 collective-permute-start.28
  150.7 3.1 %fusion = bf16[1,512,1792]{2,1,0:T(8,128)(2,1)} fusion(f32[512,1792]{1,0:T(8,128)S(1)} %copy-done, bf16[512,1792]{1,0:T(8,128)(2,1)} %collective-permute-done.6), kind=kLoop, calls=%fused_computation.6 | loop fusion | flops 2752512 | bytes 7340032 | tf_op jit(solution)/shard_map/broadcast_in_dim | solution.py:359
  153.8 0.8 copy-done.13
  154.6 4.5 %weight_part.9 = bf16[2,224,512]{2,1,0:T(8,128)(2,1)} custom-call(s32[2]{0:T(128)} %get-tuple-element.48.side_ref, s32[2]{0:T(128)} %get-tuple-element.46.low_ref, bf16[2,2,2,2,224,512]{5,4,3,2,1,0:T(8,128)(2,1)} %pad_maximum_fusion.a_ref, bf16[512,512]{1,0:T(8,128)(2,1)} %get-tuple-element.27.refs_0_.v00, bf16[512,512]{1,0:T(8,128)(2,1)} %copy-done.9, ...), custom_call_target="tpu_custom_call" | custom-call | tf_op jit(solution)/shard_map/weight_part/pallas_call | solution.py:259
  159.1 0.9 collective-permute-start.13
  160.0 0.8 copy-done.11
  160.8 0.8 copy-done.12
  161.6 4.5 %weight_part.13 = bf16[2,224,512]{2,1,0:T(8,128)(2,1)} custom-call(s32[2]{0:T(128)} %get-tuple-element.48.side_ref, s32[2]{0:T(128)} %get-tuple-element.46.low_ref, bf16[2,2,2,2,224,512]{5,4,3,2,1,0:T(8,128)(2,1)} %pad_maximum_fusion.a_ref, bf16[512,512]{1,0:T(8,128)(2,1)} %get-tuple-element.36.refs_2_.v00, bf16[512,512]{1,0:T(8,128)(2,1)} %copy-done.10, ...), custom_call_target="tpu_custom_call" | custom-call | tf_op jit(solution)/shard_map/weight_part/pallas_call | solution.py:259
  166.1 1.1 collective-permute-start.23
  167.3 4.6 %weight_part.8 = f32[2,224,512]{2,1,0:T(8,128)} custom-call(s32[2]{0:T(128)} %get-tuple-element.49.side_ref, s32[2]{0:T(128)} %get-tuple-element.47.low_ref, bf16[2,2,2,2,224,512]{5,4,3,2,1,0:T(8,128)(2,1)} %pad_maximum_fusion.a_ref, bf16[512,512]{1,0:T(8,128)(2,1)} %get-tuple-element.27.refs_0_.v00, bf16[512,512]{1,0:T(8,128)(2,1)} %copy-done.9, ...), custom_call_target="tpu_custom_call" | custom-call | tf_op jit(solution)/shard_map/weight_part/pallas_call | solution.py:259
  171.9 4.4 %weight_part.10 = f32[2,224,384]{2,1,0:T(8,128)} custom-call(s32[2]{0:T(128)} %get-tuple-element.49.side_ref, s32[2]{0:T(128)} %get-tuple-element.47.low_ref, bf16[2,2,2,2,224,512]{5,4,3,2,1,0:T(8,128)(2,1)} %pad_maximum_fusion.a_ref, bf16[512,384]{1,0:T(8,128)(2,1)} %get-tuple-element.28.refs_1_.v00, bf16[512,384]{1,0:T(8,128)(2,1)} %collective-permute-done.15.v01, ...), custom_call_target="tpu_custom_call" | custom-call | tf_op jit(solution)/shard_map/weight_part/pallas_call | solution.py:259
  176.2 4.6 %weight_part.12 = f32[2,224,512]{2,1,0:T(8,128)} custom-call(s32[2]{0:T(128)} %get-tuple-element.49.side_ref, s32[2]{0:T(128)} %get-tuple-element.47.low_ref, bf16[2,2,2,2,224,512]{5,4,3,2,1,0:T(8,128)(2,1)} %pad_maximum_fusion.a_ref, bf16[512,512]{1,0:T(8,128)(2,1)} %get-tuple-element.36.refs_2_.v00, bf16[512,512]{1,0:T(8,128)(2,1)} %copy-done.10, ...), custom_call_target="tpu_custom_call" | custom-call | tf_op jit(solution)/shard_map/weight_part/pallas_call | solution.py:259
  180.8 4.5 %weight_part.14 = f32[2,224,384]{2,1,0:T(8,128)} custom-call(s32[2]{0:T(128)} %get-tuple-element.49.side_ref, s32[2]{0:T(128)} %get-tuple-element.47.low_ref, bf16[2,2,2,2,224,512]{5,4,3,2,1,0:T(8,128)(2,1)} %pad_maximum_fusion.a_ref, bf16[512,384]{1,0:T(8,128)(2,1)} %get-tuple-element.37.refs_3_.v00, bf16[512,384]{1,0:T(8,128)(2,1)} %copy-done.14, ...), custom_call_target="tpu_custom_call" | custom-call | tf_op jit(solution)/shard_map/weight_part/pallas_call | solution.py:259
  185.4 3.1 %collective-permute-start.19 = (bf16[1,224,384]{2,1,0:T(8,128)(2,1)S(1)}, bf16[1,224,384]{2,1,0:T(8,128)(2,1)S(1)}, u32[]{:S(2)}, u32[]{:S(2)}) collective-permute-start(bf16[1,224,384]{2,1,0:T(8,128)(2,1)S(1)} %fusion.14), channel_id=1, source_target_pairs={{0,16},{4,20},{8,24},{12,28},{16,0},{20,4},{24,8},{28,12},{1,17},{... | collective-permute-start | bytes 516104 | tf_op jit(solution)/shard_map/ppermute | solution.py:269
  188.5 1.0 fusion.11
  189.7 2.9 %collective-permute-start.14 = (bf16[1,224,512]{2,1,0:T(8,128)(2,1)S(1)}, bf16[1,224,512]{2,1,0:T(8,128)(2,1)S(1)}, u32[]{:S(2)}, u32[]{:S(2)}) collective-permute-start(bf16[1,224,512]{2,1,0:T(8,128)(2,1)S(1)} %fusion.8), channel_id=1, source_target_pairs={{0,16},{4,20},{8,24},{12,28},{16,0},{20,4},{24,8},{28,12},{1,17},{... | collective-permute-start | bytes 688136 | tf_op jit(solution)/shard_map/ppermute | solution.py:269
  192.9 17.2 %collective-permute-done.19 = bf16[1,224,384]{2,1,0:T(8,128)(2,1)S(1)} collective-permute-done((bf16[1,224,384]{2,1,0:T(8,128)(2,1)S(1)}, bf16[1,224,384]{2,1,0:T(8,128)(2,1)S(1)}, u32[]{:S(2)}, u32[]{:S(2)}) %collective-permute-start.19) | collective-permute-done | bytes 172064 | tf_op jit(solution)/shard_map/ppermute | solution.py:269
  210.1 3.6 %collective-permute-done.29 = bf16[1,224,384]{2,1,0:T(8,128)(2,1)S(1)} collective-permute-done((bf16[1,224,384]{2,1,0:T(8,128)(2,1)S(1)}, bf16[1,224,384]{2,1,0:T(8,128)(2,1)S(1)}, u32[]{:S(2)}, u32[]{:S(2)}) %collective-permute-start.29) | collective-permute-done | bytes 172064 | tf_op jit(solution)/shard_map/ppermute | solution.py:269
  213.8 4.8 %collective-permute-done.14 = bf16[1,224,512]{2,1,0:T(8,128)(2,1)S(1)} collective-permute-done((bf16[1,224,512]{2,1,0:T(8,128)(2,1)S(1)}, bf16[1,224,512]{2,1,0:T(8,128)(2,1)S(1)}, u32[]{:S(2)}, u32[]{:S(2)}) %collective-permute-start.14) | collective-permute-done | bytes 229408 | tf_op jit(solution)/shard_map/ppermute | solution.py:269
  218.7 4.1 %collective-permute-done.24 = bf16[1,224,512]{2,1,0:T(8,128)(2,1)S(1)} collective-permute-done((bf16[1,224,512]{2,1,0:T(8,128)(2,1)S(1)}, bf16[1,224,512]{2,1,0:T(8,128)(2,1)S(1)}, u32[]{:S(2)}, u32[]{:S(2)}) %collective-permute-start.24) | collective-permute-done | bytes 229408 | tf_op jit(solution)/shard_map/ppermute | solution.py:269
  222.9 1.3 maximum_multiply_fusion
  (86 shorter events, 7.2 us)
Async XLA Ops:
  7.7 23.5 %collective-permute-start.7 = (bf16[2,2,224,512]{3,2,0,1:T(8,128)(2,1)S(1)}, bf16[2,2,224,512]{3,2,0,1:T(8,128)(2,1)}, u32[]{:S(2)}, u32[]{:S(2)}) collective-permute-start(bf16[2,2,224,512]{3,2,0,1:T(8,128)(2,1)S(1)} %bitcast.55), channel_id=1, source_target_pairs={{0,4},{4,0},{8,12},{12,8},{16,20},{20,16},{24,28},{28,24},{1,5},{5... | collective-permute-start | bytes 2752520 | tf_op jit(solution)/shard_map/ppermute | solution.py:269
  31.2 1.4 copy-start.23
  32.6 23.2 %collective-permute-start.8 = (bf16[2,2,224,512]{3,2,1,0:T(8,128)(2,1)S(1)}, bf16[2,2,224,512]{3,2,1,0:T(8,128)(2,1)S(1)}, u32[]{:S(2)}, u32[]{:S(2)}) collective-permute-start(bf16[2,2,224,512]{3,2,1,0:T(8,128)(2,1)S(1)} %get-tuple-element.43), channel_id=1, source_target_pairs={{0,1},{1,0},{2,3},{3,2},{4,5},{5,4},{6,7},{7,6},{8,9},{9,8},{10,11... | collective-permute-start | bytes 2752520 | tf_op jit(solution)/shard_map/ppermute | solution.py:269
  37.5 8.5 %collective-permute-start = (bf16[944,128]{1,0:T(8,128)(2,1)}, bf16[944,128]{1,0:T(8,128)(2,1)S(1)}, u32[]{:S(2)}, u32[]{:S(2)}) collective-permute-start(bf16[944,128]{1,0:T(8,128)(2,1)} %get-tuple-element.22), channel_id=1, source_target_pairs={{0,4},{4,0},{8,12},{12,8},{16,20},{20,16},{24,28},{28,24},{1,5},{5... | collective-permute-start | bytes 725000 | tf_op jit(solution)/shard_map/ppermute | solution.py:269
  43.5 8.2 %collective-permute-start.3 = (bf16[944,128]{1,0:T(8,128)(2,1)}, bf16[944,128]{1,0:T(8,128)(2,1)S(1)}, u32[]{:S(2)}, u32[]{:S(2)}) collective-permute-start(bf16[944,128]{1,0:T(8,128)(2,1)} %get-tuple-element.31), channel_id=1, source_target_pairs={{0,4},{4,0},{8,12},{12,8},{16,20},{20,16},{24,28},{28,24},{1,5},{5... | collective-permute-start | bytes 725000 | tf_op jit(solution)/shard_map/ppermute | solution.py:269
  46.0 0.7 copy-start.17
  48.7 10.0 %collective-permute-start.1 = (bf16[944,128]{1,0:T(8,128)(2,1)}, bf16[944,128]{1,0:T(8,128)(2,1)S(1)}, u32[]{:S(2)}, u32[]{:S(2)}) collective-permute-start(bf16[944,128]{1,0:T(8,128)(2,1)} %get-tuple-element.24), channel_id=1, source_target_pairs={{8,0},{12,4},{16,8},{20,12},{24,16},{28,20},{9,1},{13,5},{17,9},{2... | collective-permute-start | bytes 725000 | tf_op jit(solution)/shard_map/ppermute | solution.py:273
  51.7 0.7 copy-start.16
  54.5 9.3 %collective-permute-start.4 = (bf16[944,128]{1,0:T(8,128)(2,1)}, bf16[944,128]{1,0:T(8,128)(2,1)S(1)}, u32[]{:S(2)}, u32[]{:S(2)}) collective-permute-start(bf16[944,128]{1,0:T(8,128)(2,1)} %get-tuple-element.33), channel_id=1, source_target_pairs={{8,0},{12,4},{16,8},{20,12},{24,16},{28,20},{9,1},{13,5},{17,9},{2... | collective-permute-start | bytes 725000 | tf_op jit(solution)/shard_map/ppermute | solution.py:273
  57.2 66.3 %collective-permute-start.9 = (bf16[2,2,2,224,512]{4,3,2,1,0:T(8,128)(2,1)}, bf16[2,2,2,224,512]{4,3,2,1,0:T(8,128)(2,1)}, u32[]{:S(2)}, u32[]{:S(2)}) collective-permute-start(bf16[2,2,2,224,512]{4,3,2,1,0:T(8,128)(2,1)} %get-tuple-element.41), channel_id=1, source_target_pairs={{0,2},{2,0},{1,3},{3,1},{4,6},{6,4},{5,7},{7,5},{8,10},{10,8},{9,1... | collective-permute-start | bytes 5505032 | tf_op jit(solution)/shard_map/ppermute | solution.py:269
  58.7 0.7 copy-start.18
  61.5 22.2 %collective-permute-start.2 = (bf16[944,128]{1,0:T(8,128)(2,1)}, bf16[944,128]{1,0:T(8,128)(2,1)S(1)}, u32[]{:S(2)}, u32[]{:S(2)}) collective-permute-start(bf16[944,128]{1,0:T(8,128)(2,1)} %get-tuple-element.26), channel_id=1, source_target_pairs={{16,0},{20,4},{24,8},{28,12},{17,1},{21,5},{25,9},{29,13},{18,2},{... | collective-permute-start | bytes 725000 | tf_op jit(solution)/shard_map/ppermute | solution.py:273
  63.7 0.7 copy-start.19
  66.5 21.6 %collective-permute-start.5 = (bf16[944,128]{1,0:T(8,128)(2,1)}, bf16[944,128]{1,0:T(8,128)(2,1)S(1)}, u32[]{:S(2)}, u32[]{:S(2)}) collective-permute-start(bf16[944,128]{1,0:T(8,128)(2,1)} %get-tuple-element.35), channel_id=1, source_target_pairs={{16,0},{20,4},{24,8},{28,12},{17,1},{21,5},{25,9},{29,13},{18,2},{... | collective-permute-start | bytes 725000 | tf_op jit(solution)/shard_map/ppermute | solution.py:273
  83.7 0.7 copy-start.21
  88.1 0.7 copy-start.22
  92.6 10.4 %copy-start.4 = (bf16[512,384]{1,0:T(8,128)(2,1)S(1)}, bf16[512,384]{1,0:T(8,128)(2,1)}, u32[]{:S(2)}) copy-start(bf16[512,384]{1,0:T(8,128)(2,1)} %get-tuple-element.28.refs_1_.v00) | copy-start | bytes 1179652
  92.6 28.3 %copy-start.1 = (bf16[512,512]{1,0:T(8,128)(2,1)S(1)}, bf16[512,512]{1,0:T(8,128)(2,1)}, u32[]{:S(2)}) copy-start(bf16[512,512]{1,0:T(8,128)(2,1)} %get-tuple-element.27.refs_0_.v00) | copy-start | bytes 1572868
  92.6 30.0 %copy-start.2 = (bf16[512,512]{1,0:T(8,128)(2,1)S(1)}, bf16[512,512]{1,0:T(8,128)(2,1)}, u32[]{:S(2)}) copy-start(bf16[512,512]{1,0:T(8,128)(2,1)} %get-tuple-element.36.refs_2_.v00) | copy-start | bytes 1572868
  102.2 47.4 %collective-permute-start.6 = (bf16[512,1792]{1,0:T(8,128)(2,1)}, bf16[512,1792]{1,0:T(8,128)(2,1)}, u32[]{:S(2)}, u32[]{:S(2)}) collective-permute-start(bf16[512,1792]{1,0:T(8,128)(2,1)} %input_part.3), channel_id=1, source_target_pairs={{0,2},{2,0},{1,3},{3,1},{4,6},{6,4},{5,7},{7,5},{8,10},{10,8},{9,1... | collective-permute-start | bytes 5505032 | tf_op jit(solution)/shard_map/ppermute | solution.py:269
  103.0 12.2 %collective-permute-start.15 = (bf16[512,384]{1,0:T(8,128)(2,1)S(1)}, bf16[512,384]{1,0:T(8,128)(2,1)}, u32[]{:S(2)}, u32[]{:S(2)}) collective-permute-start(bf16[512,384]{1,0:T(8,128)(2,1)S(1)} %copy-done.4), channel_id=1, source_target_pairs={{0,4},{4,0},{8,12},{12,8},{16,20},{20,16},{24,28},{28,24},{1,5},{5... | collective-permute-start | bytes 1179656 | tf_op jit(solution)/shard_map/ppermute | solution.py:269
  104.5 10.7 %collective-permute-start.16 = (bf16[512,384]{1,0:T(8,128)(2,1)S(1)}, bf16[512,384]{1,0:T(8,128)(2,1)S(1)}, u32[]{:S(2)}, u32[]{:S(2)}) collective-permute-start(bf16[512,384]{1,0:T(8,128)(2,1)S(1)} %copy-done.4), channel_id=1, source_target_pairs={{0,1},{1,0},{2,3},{3,2},{4,5},{5,4},{6,7},{7,6},{8,9},{9,8},{10,11... | collective-permute-start | bytes 1179656 | tf_op jit(solution)/shard_map/ppermute | solution.py:269
  104.5 16.4 %collective-permute-start.25 = (bf16[512,384]{1,0:T(8,128)(2,1)}, bf16[512,384]{1,0:T(8,128)(2,1)S(1)}, u32[]{:S(2)}, u32[]{:S(2)}) collective-permute-start(bf16[512,384]{1,0:T(8,128)(2,1)} %get-tuple-element.37.refs_3_.v00), channel_id=1, source_target_pairs={{0,4},{4,0},{8,12},{12,8},{16,20},{20,16},{24,28},{28,24},{1,5},{5... | collective-permute-start | bytes 1179656 | tf_op jit(solution)/shard_map/ppermute | solution.py:269
  115.1 7.5 %collective-permute-start.26 = (bf16[512,384]{1,0:T(8,128)(2,1)}, bf16[512,384]{1,0:T(8,128)(2,1)}, u32[]{:S(2)}, u32[]{:S(2)}) collective-permute-start(bf16[512,384]{1,0:T(8,128)(2,1)} %get-tuple-element.37.refs_3_.v00), channel_id=1, source_target_pairs={{0,1},{1,0},{2,3},{3,2},{4,5},{5,4},{6,7},{7,6},{8,9},{9,8},{10,11... | collective-permute-start | bytes 1179656 | tf_op jit(solution)/shard_map/ppermute | solution.py:269
  115.1 0.8 copy-start.15
  115.9 6.7 %collective-permute-start.17 = (bf16[512,384]{1,0:T(8,128)(2,1)}, bf16[512,384]{1,0:T(8,128)(2,1)}, u32[]{:S(2)}, u32[]{:S(2)}) collective-permute-start(bf16[512,384]{1,0:T(8,128)(2,1)} %collective-permute-done.15.v01), channel_id=1, source_target_pairs={{0,1},{1,0},{2,3},{3,2},{4,5},{5,4},{6,7},{7,6},{8,9},{9,8},{10,11... | collective-permute-start | bytes 1179656 | tf_op jit(solution)/shard_map/ppermute | solution.py:269
  120.8 13.2 %copy-start.14 = (bf16[512,384]{1,0:T(8,128)(2,1)}, bf16[512,384]{1,0:T(8,128)(2,1)S(1)}, u32[]{:S(2)}) copy-start(bf16[512,384]{1,0:T(8,128)(2,1)S(1)} %collective-permute-done.25.v01) | copy-start | bytes 1179652
  120.8 21.3 %collective-permute-start.10 = (bf16[512,512]{1,0:T(8,128)(2,1)S(1)}, bf16[512,512]{1,0:T(8,128)(2,1)S(1)}, u32[]{:S(2)}, u32[]{:S(2)}) collective-permute-start(bf16[512,512]{1,0:T(8,128)(2,1)S(1)} %copy-done.1), channel_id=1, source_target_pairs={{0,4},{4,0},{8,12},{12,8},{16,20},{20,16},{24,28},{28,24},{1,5},{5... | collective-permute-start | bytes 1572872 | tf_op jit(solution)/shard_map/ppermute | solution.py:269
  122.6 26.0 %collective-permute-start.11 = (bf16[512,512]{1,0:T(8,128)(2,1)S(1)}, bf16[512,512]{1,0:T(8,128)(2,1)}, u32[]{:S(2)}, u32[]{:S(2)}) collective-permute-start(bf16[512,512]{1,0:T(8,128)(2,1)S(1)} %copy-done.1), channel_id=1, source_target_pairs={{0,1},{1,0},{2,3},{3,2},{4,5},{5,4},{6,7},{7,6},{8,9},{9,8},{10,11... | collective-permute-start | bytes 1572872 | tf_op jit(solution)/shard_map/ppermute | solution.py:269
  122.6 21.2 %collective-permute-start.20 = (bf16[512,512]{1,0:T(8,128)(2,1)S(1)}, bf16[512,512]{1,0:T(8,128)(2,1)S(1)}, u32[]{:S(2)}, u32[]{:S(2)}) collective-permute-start(bf16[512,512]{1,0:T(8,128)(2,1)S(1)} %copy-done.2), channel_id=1, source_target_pairs={{0,4},{4,0},{8,12},{12,8},{16,20},{20,16},{24,28},{28,24},{1,5},{5... | collective-permute-start | bytes 1572872 | tf_op jit(solution)/shard_map/ppermute | solution.py:269
  123.6 20.2 %collective-permute-start.27 = (bf16[512,384]{1,0:T(8,128)(2,1)S(1)}, bf16[512,384]{1,0:T(8,128)(2,1)}, u32[]{:S(2)}, u32[]{:S(2)}) collective-permute-start(bf16[512,384]{1,0:T(8,128)(2,1)S(1)} %collective-permute-done.25.v01), channel_id=1, source_target_pairs={{0,1},{1,0},{2,3},{3,2},{4,5},{5,4},{6,7},{7,6},{8,9},{9,8},{10,11... | collective-permute-start | bytes 1179656 | tf_op jit(solution)/shard_map/ppermute | solution.py:269
  137.6 4.5 %copy-start.3 = (bf16[512,512]{1,0:T(8,128)(2,1)S(1)}, bf16[512,512]{1,0:T(8,128)(2,1)}, u32[]{:S(2)}) copy-start(bf16[512,512]{1,0:T(8,128)(2,1)} %get-tuple-element.36.refs_2_.v00) | copy-start | bytes 1572868
  142.1 8.6 %copy-start = (f32[512,1792]{1,0:T(8,128)S(1)}, f32[512,1792]{1,0:T(8,128)}, u32[]{:S(2)}) copy-start(f32[512,1792]{1,0:T(8,128)} %input_part.2) | copy-start | bytes 11010052
  142.1 6.5 %copy-start.9 = (bf16[512,512]{1,0:T(8,128)(2,1)}, bf16[512,512]{1,0:T(8,128)(2,1)S(1)}, u32[]{:S(2)}) copy-start(bf16[512,512]{1,0:T(8,128)(2,1)S(1)} %collective-permute-done.10.v01) | copy-start | bytes 1572868
  142.1 17.9 %collective-permute-start.21 = (bf16[512,512]{1,0:T(8,128)(2,1)S(1)}, bf16[512,512]{1,0:T(8,128)(2,1)S(1)}, u32[]{:S(2)}, u32[]{:S(2)}) collective-permute-start(bf16[512,512]{1,0:T(8,128)(2,1)S(1)} %copy-done.3), channel_id=1, source_target_pairs={{0,1},{1,0},{2,3},{3,2},{4,5},{5,4},{6,7},{7,6},{8,9},{9,8},{10,11... | collective-permute-start | bytes 1572872 | tf_op jit(solution)/shard_map/ppermute | solution.py:269
  143.8 4.8 %copy-start.10 = (bf16[512,512]{1,0:T(8,128)(2,1)}, bf16[512,512]{1,0:T(8,128)(2,1)S(1)}, u32[]{:S(2)}) copy-start(bf16[512,512]{1,0:T(8,128)(2,1)S(1)} %collective-permute-done.20.v01) | copy-start | bytes 1572868
  143.8 10.0 %collective-permute-start.12 = (bf16[512,512]{1,0:T(8,128)(2,1)S(1)}, bf16[512,512]{1,0:T(8,128)(2,1)S(1)}, u32[]{:S(2)}, u32[]{:S(2)}) collective-permute-start(bf16[512,512]{1,0:T(8,128)(2,1)S(1)} %collective-permute-done.10.v01), channel_id=1, source_target_pairs={{0,1},{1,0},{2,3},{3,2},{4,5},{5,4},{6,7},{7,6},{8,9},{9,8},{10,11... | collective-permute-start | bytes 1572872 | tf_op jit(solution)/shard_map/ppermute | solution.py:269
  143.8 4.8 %copy-start.20 = (bf16[2,224,384]{2,1,0:T(8,128)(2,1)S(1)}, bf16[2,224,384]{2,1,0:T(8,128)(2,1)}, u32[]{:S(2)}) copy-start(bf16[2,224,384]{2,1,0:T(8,128)(2,1)} %weight_part.11) | copy-start | bytes 1032196
  143.8 16.2 %collective-permute-start.22 = (bf16[512,512]{1,0:T(8,128)(2,1)S(1)}, bf16[512,512]{1,0:T(8,128)(2,1)S(1)}, u32[]{:S(2)}, u32[]{:S(2)}) collective-permute-start(bf16[512,512]{1,0:T(8,128)(2,1)S(1)} %collective-permute-done.20.v01), channel_id=1, source_target_pairs={{0,1},{1,0},{2,3},{3,2},{4,5},{5,4},{6,7},{7,6},{8,9},{9,8},{10,11... | collective-permute-start | bytes 1572872 | tf_op jit(solution)/shard_map/ppermute | solution.py:269
  148.6 36.7 %collective-permute-start.18 = (bf16[2,224,384]{2,1,0:T(8,128)(2,1)S(1)}, bf16[2,224,384]{2,1,0:T(8,128)(2,1)S(1)}, u32[]{:S(2)}, u32[]{:S(2)}) collective-permute-start(bf16[2,224,384]{2,1,0:T(8,128)(2,1)S(1)} %copy-done.20), channel_id=1, source_target_pairs={{0,8},{4,12},{8,0},{12,4},{16,24},{20,28},{24,16},{28,20},{1,9},{5... | collective-permute-start | bytes 1032200 | tf_op jit(solution)/shard_map/ppermute | solution.py:269
  149.6 38.9 %collective-permute-start.28 = (bf16[2,224,384]{2,1,0:T(8,128)(2,1)}, bf16[2,224,384]{2,1,0:T(8,128)(2,1)S(1)}, u32[]{:S(2)}, u32[]{:S(2)}) collective-permute-start(bf16[2,224,384]{2,1,0:T(8,128)(2,1)} %weight_part.15), channel_id=1, source_target_pairs={{0,8},{4,12},{8,0},{12,4},{16,24},{20,28},{24,16},{28,20},{1,9},{5... | collective-permute-start | bytes 1032200 | tf_op jit(solution)/shard_map/ppermute | solution.py:269
  153.8 0.8 copy-start.13
  159.1 30.6 %collective-permute-start.13 = (bf16[2,224,512]{2,1,0:T(8,128)(2,1)}, bf16[2,224,512]{2,1,0:T(8,128)(2,1)S(1)}, u32[]{:S(2)}, u32[]{:S(2)}) collective-permute-start(bf16[2,224,512]{2,1,0:T(8,128)(2,1)} %weight_part.9), channel_id=1, source_target_pairs={{0,8},{4,12},{8,0},{12,4},{16,24},{20,28},{24,16},{28,20},{1,9},{5... | collective-permute-start | bytes 1376264 | tf_op jit(solution)/shard_map/ppermute | solution.py:269
  160.0 0.8 copy-start.11
  160.8 0.8 copy-start.12
  166.1 26.5 %collective-permute-start.23 = (bf16[2,224,512]{2,1,0:T(8,128)(2,1)}, bf16[2,224,512]{2,1,0:T(8,128)(2,1)S(1)}, u32[]{:S(2)}, u32[]{:S(2)}) collective-permute-start(bf16[2,224,512]{2,1,0:T(8,128)(2,1)} %weight_part.13), channel_id=1, source_target_pairs={{0,8},{4,12},{8,0},{12,4},{16,24},{20,28},{24,16},{28,20},{1,9},{5... | collective-permute-start | bytes 1376264 | tf_op jit(solution)/shard_map/ppermute | solution.py:269
  180.8 4.5 %copy-start.7 = (f32[2,224,384]{2,1,0:T(8,128)S(1)}, f32[2,224,384]{2,1,0:T(8,128)}, u32[]{:S(2)}) copy-start(f32[2,224,384]{2,1,0:T(8,128)} %weight_part.10) | copy-start | bytes 2064388
  180.8 8.9 %copy-start.5 = (f32[2,224,512]{2,1,0:T(8,128)S(1)}, f32[2,224,512]{2,1,0:T(8,128)}, u32[]{:S(2)}) copy-start(f32[2,224,512]{2,1,0:T(8,128)} %weight_part.8) | copy-start | bytes 2752516
  185.3 7.3 %copy-start.6 = (f32[2,224,512]{2,1,0:T(8,128)S(1)}, f32[2,224,512]{2,1,0:T(8,128)}, u32[]{:S(2)}) copy-start(f32[2,224,512]{2,1,0:T(8,128)} %weight_part.12) | copy-start | bytes 2752516
  185.4 28.3 %copy-start.8 = (f32[2,224,384]{2,1,0:T(8,128)S(1)}, f32[2,224,384]{2,1,0:T(8,128)}, u32[]{:S(2)}) copy-start(f32[2,224,384]{2,1,0:T(8,128)} %weight_part.14) | copy-start | bytes 2064388
  185.4 24.6 %collective-permute-start.19 = (bf16[1,224,384]{2,1,0:T(8,128)(2,1)S(1)}, bf16[1,224,384]{2,1,0:T(8,128)(2,1)S(1)}, u32[]{:S(2)}, u32[]{:S(2)}) collective-permute-start(bf16[1,224,384]{2,1,0:T(8,128)(2,1)S(1)} %fusion.14), channel_id=1, source_target_pairs={{0,16},{4,20},{8,24},{12,28},{16,0},{20,4},{24,8},{28,12},{1,17},{... | collective-permute-start | bytes 516104 | tf_op jit(solution)/shard_map/ppermute | solution.py:269
  189.5 24.2 %collective-permute-start.29 = (bf16[1,224,384]{2,1,0:T(8,128)(2,1)S(1)}, bf16[1,224,384]{2,1,0:T(8,128)(2,1)S(1)}, u32[]{:S(2)}, u32[]{:S(2)}) collective-permute-start(bf16[1,224,384]{2,1,0:T(8,128)(2,1)S(1)} %fusion.11), channel_id=1, source_target_pairs={{0,16},{4,20},{8,24},{12,28},{16,0},{20,4},{24,8},{28,12},{1,17},{... | collective-permute-start | bytes 516104 | tf_op jit(solution)/shard_map/ppermute | solution.py:269
  189.7 28.9 %collective-permute-start.14 = (bf16[1,224,512]{2,1,0:T(8,128)(2,1)S(1)}, bf16[1,224,512]{2,1,0:T(8,128)(2,1)S(1)}, u32[]{:S(2)}, u32[]{:S(2)}) collective-permute-start(bf16[1,224,512]{2,1,0:T(8,128)(2,1)S(1)} %fusion.8), channel_id=1, source_target_pairs={{0,16},{4,20},{8,24},{12,28},{16,0},{20,4},{24,8},{28,12},{1,17},{... | collective-permute-start | bytes 688136 | tf_op jit(solution)/shard_map/ppermute | solution.py:269
  192.7 30.1 %collective-permute-start.24 = (bf16[1,224,512]{2,1,0:T(8,128)(2,1)S(1)}, bf16[1,224,512]{2,1,0:T(8,128)(2,1)S(1)}, u32[]{:S(2)}, u32[]{:S(2)}) collective-permute-start(bf16[1,224,512]{2,1,0:T(8,128)(2,1)S(1)} %fusion.5), channel_id=1, source_target_pairs={{0,16},{4,20},{8,24},{12,28},{16,0},{20,4},{24,8},{28,12},{1,17},{... | collective-permute-start | bytes 688136 | tf_op jit(solution)/shard_map/ppermute | solution.py:269

commit v2 on v0

v2 whole, which is shorter than its diff:
```python
import functools
import math

import jax
import jax.numpy as jnp
from jax import lax
from jax.experimental import pallas as pl
from jax.experimental.pallas import tpu as pltpu
from jax.sharding import PartitionSpec as P

BF = jnp.bfloat16
F32 = jnp.float32
HD = 128
PLANE = 16
EXTRA = 3 * PLANE
PARAMS = pltpu.CompilerParams(vmem_limit_bytes=20 * 1024 * 1024)
VM = pl.BlockSpec(memory_space=pltpu.VMEM)
SM = pl.BlockSpec(memory_space=pltpu.SMEM)
ANY = pl.BlockSpec(memory_space=pl.ANY)


def dot(a, b, contract):
    return lax.dot_general(a, b, (contract, ((), ())), preferred_element_type=F32)


def hi_lo(x):
    hi = x.astype(BF)
    return hi, (x - hi.astype(F32)).astype(BF)


def cost(microseconds):
    return pl.CostEstimate(flops=int(microseconds * 1.15e9), transcendentals=0, bytes_accessed=0)


def call(kernel, name, us, outs, smalls, arrays, after=(), scratch=(), far=()):
    def body(*refs):
        refs = list(refs)
        first = len(smalls) + len(arrays) + len(far)
        kernel(*refs[:first], *refs[first + len(after) :])

    return pl.pallas_call(
        body,
        in_specs=[SM] * len(smalls) + [VM] * len(arrays) + [ANY] * (len(far) + len(after)),
        out_specs=[VM] * len(outs),
        out_shape=[jax.ShapeDtypeStruct(shape, dtype) for shape, dtype in outs],
        scratch_shapes=list(scratch),
        compiler_params=PARAMS,
        cost_estimate=cost(us),
        name=name,
    )(*smalls, *arrays, *far, *after)


def transpose_kernel(lows, rows, at_ref, a_ref, near_ref, far_ref, flat):
    flat[...] = a_ref[...].T.astype(flat.dtype)
    for yr, out in enumerate((near_ref, far_ref)):
        for dr in range(2):
            for low in range(lows):
                start = ((low * 2 + (at_ref[0] ^ yr)) * 2 + (at_ref[1] ^ dr)) * rows
                out[low, dr] = flat[pl.ds(pl.multiple_of(start, 8), rows), :].astype(BF)


def transposed(at, a, lows, rows, after):
    tokens, cols = a.shape
    outs = [((lows, 2, rows, tokens), BF)] * 2
    scratch = [pltpu.VMEM((cols, tokens), BF if rows % 16 == 0 else F32)]
    return call(functools.partial(transpose_kernel, lows, rows), "transpose_inputs", 1.2, outs, [at], [a], after, scratch)


def state_kernel(group, heads, cols, q_ref, c_ref, ld_ref, pay_ref, own_ref, cum_ref, cumt_ref):
    tokens = ld_ref.shape[1]
    x = ld_ref[group * heads : (group + 1) * heads, :]
    x = jnp.concatenate([x, jnp.zeros((PLANE - heads, tokens), F32)], axis=0)
    lane = lax.broadcasted_iota(jnp.int32, x.shape, 1)
    shift = 1
    while shift < tokens:
        x = x + jnp.where(lane >= shift, pltpu.roll(x, shift, 1), 0.0)
        shift *= 2
    cum_ref[...] = x
    xt = jnp.concatenate([x, jnp.zeros((HD - PLANE, tokens), F32)], axis=0).T
    cumt_ref[...] = xt
    et = jnp.exp(xt)
    d = jnp.broadcast_to(jnp.exp(x[:, tokens - 1 : tokens]), (PLANE, HD))
    put_decays(d, heads, pay_ref, own_ref)
    for h in range(heads):
        s = slice(h * HD, (h + 1) * HD)
        f = slice(cols + h * HD, cols + (h + 1) * HD)
        q = q_ref[:, f].astype(F32).astype(BF)
        hi, lo = hi_lo(c_ref[:, f].astype(F32) * et[:, h : h + 1])
        both = dot(q, jnp.concatenate([hi, lo], axis=1), ((0,), (0,)))
        term = both[:, :HD] + both[:, HD:]
        own_ref[s, :] = term
        pay_ref[s, :] = term.astype(BF)


def state_outs(heads, tokens):
    rows = heads * HD + EXTRA
    return [((rows, HD), BF), ((rows, HD), F32), ((PLANE, tokens), F32), ((tokens, HD), F32)]


def first_state_terms(heads, q, c, ld, after):
    tokens = q.shape[0]
    cols = pl.BlockSpec((tokens, heads * HD), lambda i: (0, 0))
    whole = lambda shape: pl.BlockSpec(shape, lambda i: (0, 0))
    outs = state_outs(heads, tokens)
    return pl.pallas_call(
        lambda q, c, ld, after, *outs: state_kernel(0, heads, 0, q, c, ld, *outs),
        grid=(1,),
        in_specs=[cols, cols, whole(ld.shape), ANY],
        out_specs=[whole(shape) for shape, _ in outs],
        out_shape=[jax.ShapeDtypeStruct(shape, dtype) for shape, dtype in outs],
        compiler_params=PARAMS,
        cost_estimate=cost(2.0),
        name="state_terms",
    )(q, c, ld, after)


def later_state_terms(group, heads, q, c, ld, after):
    kernel = functools.partial(state_kernel, group, heads, group * heads * HD)
    return call(kernel, "state_terms", 1.6, state_outs(heads, q.shape[0]), [], [q, c, ld], after)


def put_decays(d, heads, pay_ref, own_ref):
    d_hi, d_mid = hi_lo(d)
    d_lo = (d - d_hi.astype(F32) - d_mid.astype(F32)).astype(BF)
    at = heads * HD
    pay_ref[at : at + PLANE, :] = d_hi
    pay_ref[at + PLANE : at + 2 * PLANE, :] = d_mid
    pay_ref[at + 2 * PLANE : at + EXTRA, :] = d_lo
    own_ref[at : at + PLANE, :] = d
    own_ref[at + PLANE : at + EXTRA, :] = jnp.zeros((EXTRA - PLANE, HD), F32)


def decays(ref, heads):
    p = ref[heads * HD :, :].astype(F32)
    return p[:PLANE] + p[PLANE : 2 * PLANE] + p[2 * PLANE :]


def append_kernel(heads, swap_ref, a_ref, b_ref, pay_ref, own_ref):
    swap = swap_ref[0] != 0
    da, db = decays(a_ref, heads), decays(b_ref, heads)
    one = jnp.ones_like(da)
    scale_a = jnp.where(swap, db, one)
    scale_b = jnp.where(swap, one, da)
    put_decays(da * db, heads, pay_ref, own_ref)
    for h in range(heads):
        s = slice(h * HD, (h + 1) * HD)
        term = scale_a[h : h + 1] * a_ref[s, :].astype(F32) + scale_b[h : h + 1] * b_ref[s, :].astype(F32)
        own_ref[s, :] = term
        pay_ref[s, :] = term.astype(BF)


def append(heads, swap, a, b, after=()):
    outs = [(a.shape, BF), (a.shape, F32)]
    return call(functools.partial(append_kernel, heads), "join_states", 0.9, outs, [swap], [a, b], after)


def local_kernel(heads, cols, q_ref, k_ref, c_ref, cum_ref, cumt_ref, o_ref):
    tokens = q_ref.shape[0]
    tile = 256
    row = lax.broadcasted_iota(jnp.int32, (tile, tile), 0)
    col = lax.broadcasted_iota(jnp.int32, (tile, tile), 1)
    causal = col >= row
    for h in range(heads):
        f = slice(cols + h * HD, cols + (h + 1) * HD)
        q = q_ref[:, f].astype(F32).astype(BF)
        k = k_ref[:, f].astype(F32).astype(BF)
        scores = dot(k, q, ((1,), (1,)))
        strips = []
        for at in range(0, tokens, tile):
            end = at + tile
            before = cumt_ref[at:end, h : h + 1]
            gap = jnp.where(causal, cum_ref[h : h + 1, at:end] - before, -jnp.inf)
            strip = [jnp.zeros((tile, at), BF)] if at else []
            strip.append((scores[at:end, at:end] * jnp.exp(gap)).astype(BF))
            if end < tokens:
                middle = cum_ref[h : h + 1, end - 1 : end]
                to_t = jnp.exp(cum_ref[h : h + 1, end:] - middle)
                from_s = jnp.exp(middle - before)
                strip.append((scores[at:end, end:] * to_t * from_s).astype(BF))
            strips.append(jnp.concatenate(strip, axis=1))
        weighted = jnp.concatenate(strips, axis=0)
        o_ref[:, h * HD : (h + 1) * HD] = dot(weighted, c_ref[:, f], ((1,), (0,)))


def local_part(group, heads, q, k, c, cum, cumt, after):
    kernel = functools.partial(local_kernel, heads, group * heads * HD)
    return call(kernel, "local_part", 2.2, [((q.shape[0], heads * HD), F32)], [], [q, k, c, cum, cumt], after)[0]


def value_kernel(heads, cols, scale, first_ref, k_ref, l_ref, cumt_ref, oth_ref, e_ref, r_ref, o_ref):
    tokens = k_ref.shape[0]
    first = first_ref[0] != 0
    de = decays(e_ref, heads)
    do = decays(oth_ref, heads)
    use_oth = jnp.where(first, 1.0, 0.0)
    scale_e = jnp.where(first, do, jnp.ones_like(do))
    fall = jnp.exp(cumt_ref[tokens - 1 : tokens, :] - cumt_ref[...])
    for h in range(heads):
        s = slice(h * HD, (h + 1) * HD)
        e = e_ref[s, :].astype(F32) + de[h : h + 1] * r_ref[s, :].astype(F32)
        carry = use_oth * oth_ref[s, :].astype(F32) + scale_e[h : h + 1] * e
        hi, lo = hi_lo(carry)
        k = k_ref[:, cols + h * HD : cols + (h + 1) * HD].astype(F32).astype(BF)
        both = dot(k, jnp.concatenate([hi, lo], axis=1), ((1,), (0,)))
        carried = fall[:, h : h + 1] * (both[:, :HD] + both[:, HD:])
        o_ref[:, s] = (scale * (l_ref[:, s] + carried)).astype(BF)


def value_grads(group, heads, scale, first, k, local, cumt, oth, e, r, after):
    kernel = functools.partial(value_kernel, heads, group * heads * HD, scale)
    outs = [((k.shape[0], heads * HD), BF)]
    return call(kernel, "value_grad", 0.8, outs, [first], [k, local, cumt, oth, e, r], after)[0]


def input_kernel(rows, sides, side_ref, *refs):
    vs, w_ref, outs, v_all, w_all, sems = refs[: -(4 + sides)], refs[-(4 + sides)], refs[-(3 + sides) : -3], *refs[-3:]
    half = rows // 2
    copies = []
    for i in range(2 * sides):
        start = ((side_ref[0] ^ ((i // 2 + 1) % sides)) * 2 + i % 2) * half
        start = pl.multiple_of(start, 64)
        copies.append(pltpu.make_async_copy(w_ref.at[pl.ds(start, half)], w_all.at[i], sems.at[i]))
        copies[-1].start()
    start = 0
    for v in vs:
        v_all[:, start : start + v.shape[1]] = v[...]
        start += v.shape[1]
    for i, copy in enumerate(copies):
        copy.wait()
        out = outs[i // 2]
        part = dot(v_all[...], w_all[i], ((1,), (1,)))
        out[:, i % 2 * half : (i % 2 + 1) * half] = part.astype(out.dtype)


def input_parts(side, sides, vs, w, after):
    tokens, features, rows = vs[0].shape[0], w.shape[1], w.shape[0] // sides
    outs = [((tokens, rows), BF)] * (sides - 1) + [((tokens, rows), F32)]
    scratch = [
        pltpu.VMEM((tokens, features), BF),
        pltpu.VMEM((2 * sides, rows // 2, features), BF),
        pltpu.SemaphoreType.DMA((2 * sides,)),
    ]
    kernel = functools.partial(input_kernel, rows, sides)
    return call(kernel, "input_part", 8.0, outs, [side], vs, after, scratch, [w])


def weight_kernel(blocks, sides, start, side_ref, low_ref, *refs):
    pieces = [refs[2 * s : 2 * s + 2] for s in range(sides)]
    v_ref, v_y_ref, away_ref, keep_ref, all_v = refs[2 * sides :]
    tokens, width = v_ref.shape[0], away_ref.shape[2]
    all_v[:tokens, :] = v_ref[:, start : start + width]
    all_v[tokens:, :] = v_y_ref[:, start : start + width]
    for n in range(blocks):
        for s in range(sides):

            @pl.when(side_ref[n] == s)
            def _(n=n, s=s):
                a = [p[low_ref[n]] for p in pieces[s]]
                rows = a[0].shape[1]
                a = jnp.concatenate([jnp.concatenate([p[1], p[0]], axis=0) for p in a], axis=1)
                total = dot(a, all_v[...], ((1,), (0,)))
                away_ref[n] = total[:rows].astype(BF)
                keep_ref[n] = total[rows:]


def weight_part(side, low, pieces, vs, start, width, after):
    blocks, sides = side.shape[0], len(pieces)
    rows = pieces[0][0].shape[2]
    shape = (blocks, rows, width)
    scratch = [pltpu.VMEM((2 * vs[0].shape[0], width), BF)]
    arrays = [p for side_pieces in pieces for p in side_pieces] + list(vs)
    kernel = functools.partial(weight_kernel, blocks, sides, start)
    return call(kernel, "weight_part", 3.2, [(shape, BF), (shape, F32)], [side, low], arrays, after, scratch)


def fold_kernel(keep_ref, came_ref, away_ref, left_ref):
    half = away_ref.shape[0]
    left_ref[...] = keep_ref[:half] + came_ref[:half].astype(F32)
    away_ref[...] = (keep_ref[half:] + came_ref[half:].astype(F32)).astype(BF)


def fold(keep, came, after):
    blocks, rows, width = keep.shape
    shape = (blocks // 2, rows, width)
    return call(fold_kernel, "fold_weight", 1.0, [(shape, BF), (shape, F32)], [], [keep, came], after)


def tied(x, *after):
    return lax.optimization_barrier((x, *after))[0]


def swap_with(x, axis, bit):
    return lax.ppermute(x, axis, [(i, i ^ bit) for i in range(lax.axis_size(axis))])


def from_later(x, axis, shift):
    return lax.ppermute(x, axis, [(i, i - shift) for i in range(shift, lax.axis_size(axis))])


def local(inputs, value_weight, cotangent, spikes_q, spikes_k, log_decay):
    seqs, sides, dps = lax.axis_size("seq"), lax.axis_size("head"), lax.axis_size("dp")
    seq, side, dp = lax.axis_index("seq"), lax.axis_index("head"), lax.axis_index("dp")
    y, z = seq % 2, seq // 2
    tokens, rows_here = inputs.shape[1:]
    features = value_weight.shape[1]
    heads_here = log_decay.shape[1]
    seq_length = tokens * seqs
    grad_scale = 1.0 / (2.25 * HD * math.sqrt(seq_length))
    groups = 2 if heads_here % 2 == 0 else 1
    heads = heads_here // groups
    chunks = (heads - heads // 2, heads // 2)
    rows = rows_here * sides // (seqs * dps)
    lows = rows_here // (2 * dps * rows)
    stages = (seqs // 2).bit_length() - 1
    y_flag = y.astype(jnp.int32).reshape(1)
    zero_flag = jnp.zeros((1,), jnp.int32)
    first_flag = 1 - y_flag
    place = jnp.stack([y, dp]).astype(jnp.int32)

    q, k, c, ld = spikes_q[0], spikes_k[0], cotangent[0], log_decay[0]

    near, far = transposed(place, inputs[0], lows, rows, ())
    near_x = [swap_with(near, "head", i) for i in range(1, sides)]

    own = [first_state_terms(heads, q, c, ld, near)]
    for g in range(1, groups):
        own.append(later_state_terms(g, heads, q, c, ld, [own[-1][0]]))
    other = [swap_with(o[0], "seq", 1) for o in own]
    far = swap_with(tied(far, other[-1]), "seq", 1)
    pieces = [[near, far]] + [[n, swap_with(far, "head", i + 1)] for i, n in enumerate(near_x)]

    last = own[-1][0]
    locals_, joined = [], []
    for g in range(groups):
        joined.append(append(heads, y_flag, own[g][1], other[g], [last]))
        last = joined[g][0]
    for g in range(groups):
        locals_.append(local_part(g, heads, q, k, c, own[g][2], own[g][3], [last, *near_x]))
        last = locals_[g]
    values = []
    for g in range(groups):
        pay, ours = joined[g]
        e = None
        for stage in range(stages):
            later = from_later(pay, "seq", 2 << stage)
            if stage == 0:
                e = later
            elif stage < stages - 1:
                e = append(heads, zero_flag, e, later)[1]
            if stage < stages - 1:
                pay, ours = append(heads, zero_flag, ours, later)
        if stages == 1:
            later = jnp.zeros_like(later)
        values.append(
            value_grads(g, heads, grad_scale, first_flag, k, locals_[g], own[g][3], other[g], e, later, [far])
        )

    order = [0]
    for stage in range(stages):
        order = order + [o | (1 << stage) for o in order]
    order = [int(format(o, "b").zfill(stages)[::-1], 2) for o in order]
    at_z = jnp.stack([z ^ o for o in order]).astype(jnp.int32)
    block_side = (at_z // lows) ^ side
    block_low = at_z % lows

    from_y = [swap_with(v, "seq", 1) for v in values]
    *others, total = input_parts(side.astype(jnp.int32).reshape(1), sides, values, value_weight, [])
    sent = [swap_with(o, "head", i + 1) for i, o in enumerate(others)]

    parts = [(g, start, n) for g in range(groups) for start, n in ((0, chunks[0]), (chunks[0], chunks[1]))]
    kept, last = [None] * len(parts), total
    for i in range(len(parts) + stages - 1):
        if i < len(parts):
            g, start, n = parts[i]
            away, keep = weight_part(
                block_side, block_low, pieces, (values[g], from_y[g]), start * HD, n * HD, [last]
            )
            came = swap_with(away, "dp", 1)
            away, keep = fold(keep, came, [])
            kept[i] = (keep, swap_with(away, "seq", 2))
            last = away
        for stage in range(1, stages):
            j = i - stage
            if 0 <= j < len(parts):
                away, keep = fold(*kept[j], [last])
                kept[j] = (keep, swap_with(away, "seq", 2 << stage))
                last = away
    results = [keep[0] + came[0].astype(F32) for keep, came in kept]
    grad_weight = jnp.concatenate(results, axis=1) * (1.0 / math.sqrt(dps * seq_length))

    for s in sent:
        total = total + s.astype(F32)
    return total.astype(BF)[None], grad_weight


def solution(mesh):
    return jax.shard_map(
        local,
        mesh=mesh,
        in_specs=(
            P("dp", "seq", "head"),
            P(None, "head"),
            P("dp", "seq", "head"),
            P("dp", "seq", "head"),
            P("dp", "seq", "head"),
            P("dp", "head", "seq"),
        ),
        out_specs=(P("dp", "seq", "head"), P(("seq", "dp"), "head")),
        check_vma=False,
    )
```

time: 549 us -> 154 us (0.28)
  waiting for transfers between devices: 387 us -> 83.4 us
  matrix products: 44.6 us -> 0 us
  local copies, waits for them, and re-layouts: 47.6 us -> 6.55 us
  Pallas kernels: 0 us -> 35.8 us
  other arithmetic: 29.6 us -> 3.35 us
  blocking collectives: 23.9 us -> 0 us
  starting transfers between devices: 0.38 us -> 23.3 us
  between operations: 14.5 us -> 1.02 us
    unnamed x5 -> x0, waiting for transfers between devices: 250 us -> none
    all_gather x2 -> x0, waiting for transfers between devices: 88.3 us -> none  [the longest x1 68.4 us: carried_in(): everything = jax.tree.map(lambda part: lax.all_gather(part, axis), array)]
    ppermute x0 -> x24, waiting for transfers between devices: none -> 83.4 us  [the longest x20 66.5 us: swap_with(): lax.ppermute(x, axis, [(i, i ^ bit) for i in range(lax.axis_size(axis))])]
    reduce_scatter x1 -> x0, waiting for transfers between devices: 48.2 us -> none  [local(): lax.psum_scatter(input_term, 'head', scatter_dimension=1, tiled=True)]
    dot_general x5 -> x0, matrix products: 44.6 us -> none  [the longest x1 14.9 us: local(): lax.dot_general(all_features, value_grad, (((0,), (0,)), ((), ())), prefe...]
    unnamed x16 -> x35, local copies, waits for them, and re-layouts: 46 us -> 6.55 us
    pallas_call x0 -> x24, Pallas kernels: none -> 35.8 us  [the longest x23 34.3 us: call(): pl.pallas_call(body, in_specs=[SM] * len(smalls) + [VM] * len(arrays) + [...]
    unnamed x1 -> x0, blocking collectives: 23.9 us -> none
  transfers between devices with their start and end apart: 4 -> 24, of which waited for: 4 -> 18; matrix products, arithmetic and copies ran while one was open for 18% -> 1% of each run, Pallas kernels for 0% -> 20%
where the time goes in v2:
time: 154 us; the launch traced here: 153 us
  waiting for transfers between devices  83.4 us (54%)
  Pallas kernels  35.8 us (23%)
  starting transfers between devices  23.3 us (15%)
  local copies, waits for them, and re-layouts  6.55 us (4%)
  other arithmetic  3.35 us (2%)
    ppermute x20, waiting for transfers between devices, swap_with(): lax.ppermute(x, axis, [(i, i ^ bit) for i in range(lax.axis_size(axis))])  66.5 us
    pallas_call x23, Pallas kernels, call(): pl.pallas_call(body, in_specs=[SM] * len(smalls) + [VM] * len(arrays) + [...  34.3 us
    ppermute x20, starting transfers between devices, swap_with(): lax.ppermute(x, axis, [(i, i ^ bit) for i in range(lax.axis_size(axis))])  17.4 us
    ppermute x4, waiting for transfers between devices, from_later(): lax.ppermute(x, axis, [(i, i - shift) for i in range(shift, lax.axis_size...  16.9 us
    unnamed x35, local copies, waits for them, and re-layouts  6.55 us
    ppermute x4, starting transfers between devices, from_later(): lax.ppermute(x, axis, [(i, i - shift) for i in range(shift, lax.axis_size...  5.85 us
  transfers between devices with their start and end apart: 24, of which 18 were waited for; matrix products, arithmetic and copies ran while one was open for 1% of the time, Pallas kernels for 20%

profile of v2, /device:TPU:0, one launch (start us, length us, event | category | flops | bytes accessed | tf_op | source)
XLA Modules:
  0.0 153.5 jit_solution(3018979509168663616)
XLA Ops:
  0.7 1.5 copy-done.5
  2.2 1.2 transpose_inputs.1
  3.4 0.9 copy-done.6
  4.3 2.9 %collective-permute-start.2 = (bf16[2,2,224,512]{3,2,1,0:T(8,128)(2,1)S(1)}, bf16[2,2,224,512]{3,2,1,0:T(8,128)(2,1)S(1)}, u32[]{:S(2)}, u32[]{:S(2)}) collective-permute-start(bf16[2,2,224,512]{3,2,1,0:T(8,128)(2,1)S(1)} %get-tuple-element.45.after.refs_2_), channel_id=1, source_target_pairs={{0,2},{2,0},{1,3},{3,1},{4,6},{6,4},{5,7},{7,5},{8,10},{10,8},{9,1... | collective-permute-start | bytes 2752520 | tf_op jit(solution)/shard_map/ppermute | solution.py:293
  7.3 1.5 copy-done.3
  8.8 1.6 %state_terms.2 = (bf16[944,128]{1,0:T(8,128)(2,1)S(1)}, f32[944,128]{1,0:T(8,128)S(1)}, f32[16,512]{1,0:T(8,128)S(1)}, f32[512,128]{1,0:T(8,128)S(1)}) custom-call(s32[512,1792]{1,0:T(8,128)S(1)} %bitcast.28, bf16[512,1792]{1,0:T(8,128)(2,1)S(1)} %bitcast.32, f32[14,512]{1,0:T(8,128)S(1)} %bitcast.36, ...), custom_call_target="tpu_custom_call" | custom-call | flops 2300000000 | tf_op jit(solution)/shard_map/state_terms/pallas_call | solution.py:105
  10.4 0.8 copy-done.10
  11.2 1.5 collective-permute-start.1
  12.7 1.6 %state_terms.3 = (bf16[944,128]{1,0:T(8,128)(2,1)S(1)}, f32[944,128]{1,0:T(8,128)S(1)}, f32[16,512]{1,0:T(8,128)S(1)}, f32[512,128]{1,0:T(8,128)S(1)}) custom-call(s32[512,1792]{1,0:T(8,128)S(1)} %bitcast.29, bf16[512,1792]{1,0:T(8,128)(2,1)S(1)} %bitcast.33, f32[14,512]{1,0:T(8,128)S(1)} %bitcast.37, bf16[944,128]{1,0:T(8,128)(2,1)S(1)} %get-tuple-element.48.refs_3_), custom_call_target="tpu_custom_call" | custom-call | flops 1840000000 | tf_op jit(solution)/shard_map/state_terms/pallas_call | solution.py:41
  14.3 0.8 copy-done.8
  15.1 0.5 collective-permute-start
  15.7 4.3 %collective-permute-done.1.refs_2_.refs_4_ = bf16[944,128]{1,0:T(8,128)(2,1)S(1)} collective-permute-done((bf16[944,128]{1,0:T(8,128)(2,1)S(1)}, bf16[944,128]{1,0:T(8,128)(2,1)S(1)}, u32[]{:S(2)}, u32[]{:S(2)}) %collective-permute-start.1) | collective-permute-done | bytes 241696 | tf_op jit(solution)/shard_map/ppermute | solution.py:293
  20.0 1.0 copy-done.11
  21.0 0.1 join_states.4
  21.1 1.4 collective-permute-start.3
  22.5 1.2 collective-permute-done.refs_2_.refs_4_
  23.7 1.5 collective-permute-start.5
  25.3 1.4 collective-permute-start.6
  26.7 3.4 %collective-permute-done.3.refs_2_.refs_5_ = bf16[944,128]{1,0:T(8,128)(2,1)S(1)} collective-permute-done((bf16[944,128]{1,0:T(8,128)(2,1)S(1)}, bf16[944,128]{1,0:T(8,128)(2,1)S(1)}, u32[]{:S(2)}, u32[]{:S(2)}) %collective-permute-start.3) | collective-permute-done | bytes 241696 | tf_op jit(solution)/shard_map/ppermute | solution.py:297
  30.2 0.8 join_states.6
  31.0 1.4 collective-permute-start.4
  32.5 2.5 %collective-permute-done.6.refs_2_.refs_5_ = bf16[944,128]{1,0:T(8,128)(2,1)S(1)} collective-permute-done((bf16[944,128]{1,0:T(8,128)(2,1)S(1)}, bf16[944,128]{1,0:T(8,128)(2,1)S(1)}, u32[]{:S(2)}, u32[]{:S(2)}) %collective-permute-start.6) | collective-permute-done | bytes 241696 | tf_op jit(solution)/shard_map/ppermute | solution.py:297
  35.0 0.9 join_states.7
  35.9 1.6 %collective-permute-start.7 = (bf16[944,128]{1,0:T(8,128)(2,1)S(1)}, bf16[944,128]{1,0:T(8,128)(2,1)S(1)}, u32[]{:S(2)}, u32[]{:S(2)}) collective-permute-start(bf16[944,128]{1,0:T(8,128)(2,1)S(1)} %get-tuple-element.61), channel_id=1, source_target_pairs={{16,0},{20,4},{24,8},{28,12},{17,1},{21,5},{25,9},{29,13},{18,2},{... | collective-permute-start | bytes 725000 | tf_op jit(solution)/shard_map/ppermute | solution.py:297
  37.5 2.2 %local_part.2.refs_2_.refs_5_ = f32[512,896]{1,0:T(8,128)S(1)} custom-call(s32[512,1792]{1,0:T(8,128)S(1)} %bitcast.30, s32[512,1792]{1,0:T(8,128)S(1)} %bitcast.24, bf16[512,1792]{1,0:T(8,128)(2,1)S(1)} %bitcast.34, f32[16,512]{1,0:T(8,128)S(1)} %get-tuple-element.46.refs_3_, f32[512,128]{1,0:T(8,128)S(1)} %get-tuple-element.47.refs_4_.refs_3_, ...), custom_call_target="tpu_custom_call" | custom-call | flops 2529999872 | tf_op jit(solution)/shard_map/local_part/pallas_call | solution.py:41
  39.8 2.2 %local_part.3.refs_2_ = f32[512,896]{1,0:T(8,128)S(1)} custom-call(s32[512,1792]{1,0:T(8,128)S(1)} %bitcast.31, s32[512,1792]{1,0:T(8,128)S(1)} %bitcast.25, bf16[512,1792]{1,0:T(8,128)(2,1)S(1)} %bitcast.35, f32[16,512]{1,0:T(8,128)S(1)} %get-tuple-element.58.refs_3_, f32[512,128]{1,0:T(8,128)S(1)} %get-tuple-element.59.refs_4_.refs_3_, ...), custom_call_target="tpu_custom_call" | custom-call | flops 2529999872 | tf_op jit(solution)/shard_map/local_part/pallas_call | solution.py:41
  42.0 8.1 %collective-permute-done.4.refs_6_ = bf16[944,128]{1,0:T(8,128)(2,1)S(1)} collective-permute-done((bf16[944,128]{1,0:T(8,128)(2,1)S(1)}, bf16[944,128]{1,0:T(8,128)(2,1)S(1)}, u32[]{:S(2)}, u32[]{:S(2)}) %collective-permute-start.4) | collective-permute-done | bytes 241696 | tf_op jit(solution)/shard_map/ppermute | solution.py:297
  50.1 0.7 value_grad.2.refs_1_.refs_6_
  50.8 2.0 %collective-permute-start.10 = (bf16[512,896]{1,0:T(8,128)(2,1)S(1)}, bf16[512,896]{1,0:T(8,128)(2,1)S(1)}, u32[]{:S(2)}, u32[]{:S(2)}) collective-permute-start(bf16[512,896]{1,0:T(8,128)(2,1)S(1)} %value_grad.2.refs_1_.refs_6_), channel_id=1, source_target_pairs={{0,4},{4,0},{8,12},{12,8},{16,20},{20,16},{24,28},{28,24},{1,5},{5... | collective-permute-start | bytes 2752520 | tf_op jit(solution)/shard_map/ppermute | solution.py:293
  52.8 0.5 collective-permute-start.9
  53.3 2.8 %collective-permute-done.7.refs_6_ = bf16[944,128]{1,0:T(8,128)(2,1)S(1)} collective-permute-done((bf16[944,128]{1,0:T(8,128)(2,1)S(1)}, bf16[944,128]{1,0:T(8,128)(2,1)S(1)}, u32[]{:S(2)}, u32[]{:S(2)}) %collective-permute-start.7) | collective-permute-done | bytes 241696 | tf_op jit(solution)/shard_map/ppermute | solution.py:297
  56.2 0.7 value_grad.3.refs_2_.refs_6_
  57.0 9.7 %input_part.1 = (bf16[512,1792]{1,0:T(8,128)(2,1)S(1)}, f32[512,1792]{1,0:T(8,128)S(1)}) custom-call(s32[1]{0:T(128)} %bitcast.refs_0_, bf16[512,896]{1,0:T(8,128)(2,1)S(1)} %value_grad.2.refs_1_.refs_6_, bf16[512,896]{1,0:T(8,128)(2,1)S(1)} %value_grad.3.refs_2_.refs_6_, bf16[3584,1792]{1,0:T(8,128)(2,1)S(1)} %bitcast.39), custom_call_target="tpu_custom_call" | custom-call | flops 9200000000 | tf_op jit(solution)/shard_map/input_part/pallas_call | solution.py:41
  66.7 4.1 %collective-permute-done.9.refs_5_ = bf16[2,2,224,512]{3,2,1,0:T(8,128)(2,1)S(1)} collective-permute-done((bf16[2,2,224,512]{3,2,1,0:T(8,128)(2,1)S(1)}, bf16[2,2,224,512]{3,2,1,0:T(8,128)(2,1)S(1)}, u32[]{:S(2)}, u32[]{:S(2)}) %collective-permute-start.9) | collective-permute-done | bytes 917536 | tf_op jit(solution)/shard_map/ppermute | solution.py:293
  70.8 3.4 %weight_part.4 = (bf16[4,224,512]{2,1,0:T(8,128)(2,1)S(1)}, f32[4,224,512]{2,1,0:T(8,128)S(1)}) custom-call(s32[4]{0:T(128)S(1)} %fusion.1.refs_0_, s32[4]{0:T(128)S(1)} %get-tuple-element.88.refs_1_, bf16[2,2,224,512]{3,2,1,0:T(8,128)(2,1)S(1)} %get-tuple-element.45.after.refs_2_, bf16[2,2,224,512]{3,2,1,0:T(8,128)(2,1)S(1)} %collective-permute-done.5.refs_7_.refs_3_, ...), custom_call_target="tpu_custom_call" | custom-call | flops 3680000000 | tf_op jit(solution)/shard_map/weight_part/pallas_call | solution.py:41
  74.3 0.9 collective-permute-start.16
  75.2 1.5 collective-permute-done.11.refs_1_
  76.7 0.2 fold_weight.8
  76.9 3.2 %weight_part.5 = (bf16[4,224,384]{2,1,0:T(8,128)(2,1)S(1)}, f32[4,224,384]{2,1,0:T(8,128)S(1)}) custom-call(s32[4]{0:T(128)S(1)} %fusion.1.refs_0_, s32[4]{0:T(128)S(1)} %get-tuple-element.88.refs_1_, bf16[2,2,224,512]{3,2,1,0:T(8,128)(2,1)S(1)} %get-tuple-element.45.after.refs_2_, bf16[2,2,224,512]{3,2,1,0:T(8,128)(2,1)S(1)} %collective-permute-done.5.refs_7_.refs_3_, ...), custom_call_target="tpu_custom_call" | custom-call | flops 3680000000 | tf_op jit(solution)/shard_map/weight_part/pallas_call | solution.py:41
  80.1 0.2 collective-permute-start.13
  80.3 0.5 collective-permute-start.8
  80.9 1.5 collective-permute-done.13.refs_1_
  82.3 0.2 fold_weight.9
  82.5 10.6 %collective-permute-done.12.refs_1_ = bf16[2,224,512]{2,1,0:T(8,128)(2,1)S(1)} collective-permute-done((bf16[2,224,512]{2,1,0:T(8,128)(2,1)S(1)}, bf16[2,224,512]{2,1,0:T(8,128)(2,1)S(1)}, u32[]{:S(2)}, u32[]{:S(2)}) %collective-permute-start.12) | collective-permute-done | bytes 458784 | tf_op jit(solution)/shard_map/ppermute | solution.py:293
  93.2 3.8 %collective-permute-done.16.refs_7_ = bf16[512,896]{1,0:T(8,128)(2,1)S(1)} collective-permute-done((bf16[512,896]{1,0:T(8,128)(2,1)S(1)}, bf16[512,896]{1,0:T(8,128)(2,1)S(1)}, u32[]{:S(2)}, u32[]{:S(2)}) %collective-permute-start.16) | collective-permute-done | bytes 917536 | tf_op jit(solution)/shard_map/ppermute | solution.py:293
  97.0 3.2 %weight_part.6 = (bf16[4,224,512]{2,1,0:T(8,128)(2,1)S(1)}, f32[4,224,512]{2,1,0:T(8,128)S(1)}) custom-call(s32[4]{0:T(128)S(1)} %fusion.1.refs_0_, s32[4]{0:T(128)S(1)} %get-tuple-element.88.refs_1_, bf16[2,2,224,512]{3,2,1,0:T(8,128)(2,1)S(1)} %get-tuple-element.45.after.refs_2_, bf16[2,2,224,512]{3,2,1,0:T(8,128)(2,1)S(1)} %collective-permute-done.5.refs_7_.refs_3_, ...), custom_call_target="tpu_custom_call" | custom-call | flops 3680000000 | tf_op jit(solution)/shard_map/weight_part/pallas_call | solution.py:41
  100.4 1.3 collective-permute-start.14
  101.7 1.0 collective-permute-done.17.refs_1_
  102.7 0.2 fold_weight.11
  103.0 13.1 %collective-permute-done.15.refs_1_ = bf16[2,224,384]{2,1,0:T(8,128)(2,1)S(1)} collective-permute-done((bf16[2,224,384]{2,1,0:T(8,128)(2,1)S(1)}, bf16[2,224,384]{2,1,0:T(8,128)(2,1)S(1)}, u32[]{:S(2)}, u32[]{:S(2)}) %collective-permute-start.15) | collective-permute-done | bytes 344096 | tf_op jit(solution)/shard_map/ppermute | solution.py:293
  116.2 3.2 %weight_part.7 = (bf16[4,224,384]{2,1,0:T(8,128)(2,1)S(1)}, f32[4,224,384]{2,1,0:T(8,128)S(1)}) custom-call(s32[4]{0:T(128)S(1)} %fusion.1.refs_0_, s32[4]{0:T(128)S(1)} %get-tuple-element.88.refs_1_, bf16[2,2,224,512]{3,2,1,0:T(8,128)(2,1)S(1)} %get-tuple-element.45.after.refs_2_, bf16[2,2,224,512]{3,2,1,0:T(8,128)(2,1)S(1)} %collective-permute-done.5.refs_7_.refs_3_, ...), custom_call_target="tpu_custom_call" | custom-call | flops 3680000000 | tf_op jit(solution)/shard_map/weight_part/pallas_call | solution.py:41
  119.5 3.2 %collective-permute-done.8 = bf16[512,1792]{1,0:T(8,128)(2,1)S(1)} collective-permute-done((bf16[512,1792]{1,0:T(8,128)(2,1)S(1)}, bf16[512,1792]{1,0:T(8,128)(2,1)S(1)}, u32[]{:S(2)}, u32[]{:S(2)}) %collective-permute-start.8) | collective-permute-done | bytes 1835040 | tf_op jit(solution)/shard_map/ppermute | solution.py:293
  122.6 1.7 %fusion = bf16[1,512,1792]{2,1,0:T(8,128)(2,1)} fusion(f32[512,1792]{1,0:T(8,128)S(1)} %get-tuple-element.62.refs_8_, bf16[512,1792]{1,0:T(8,128)(2,1)S(1)} %collective-permute-done.8), kind=kLoop, calls=%fused_computation.1 | loop fusion | flops 2752512 | bytes 7340032 | tf_op jit(solution)/shard_map/broadcast_in_dim | solution.py:393
  124.4 1.1 collective-permute-start.18
  125.5 0.1 fold_weight.13
  125.7 0.8 collective-permute-start.22
  126.4 0.1 fold_weight.14
  126.5 3.0 %collective-permute-start.21 = (bf16[1,224,512]{2,1,0:T(8,128)(2,1)S(1)}, bf16[1,224,512]{2,1,0:T(8,128)(2,1)S(1)}, u32[]{:S(2)}, u32[]{:S(2)}) collective-permute-start(bf16[1,224,512]{2,1,0:T(8,128)(2,1)S(1)} %get-tuple-element.84.refs_2_), channel_id=1, source_target_pairs={{0,16},{4,20},{8,24},{12,28},{16,0},{20,4},{24,8},{28,12},{1,17},{... | collective-permute-start | bytes 688136 | tf_op jit(solution)/shard_map/ppermute | solution.py:293
  129.5 6.5 %collective-permute-done.18 = bf16[1,224,384]{2,1,0:T(8,128)(2,1)S(1)} collective-permute-done((bf16[1,224,384]{2,1,0:T(8,128)(2,1)S(1)}, bf16[1,224,384]{2,1,0:T(8,128)(2,1)S(1)}, u32[]{:S(2)}, u32[]{:S(2)}) %collective-permute-start.18) | collective-permute-done | bytes 172064 | tf_op jit(solution)/shard_map/ppermute | solution.py:293
  136.0 7.0 %collective-permute-done.22.refs_1_ = bf16[2,224,384]{2,1,0:T(8,128)(2,1)S(1)} collective-permute-done((bf16[2,224,384]{2,1,0:T(8,128)(2,1)S(1)}, bf16[2,224,384]{2,1,0:T(8,128)(2,1)S(1)}, u32[]{:S(2)}, u32[]{:S(2)}) %collective-permute-start.22) | collective-permute-done | bytes 344096 | tf_op jit(solution)/shard_map/ppermute | solution.py:293
  143.1 0.2 collective-permute-start.23
  143.3 3.3 %collective-permute-done.21 = bf16[1,224,512]{2,1,0:T(8,128)(2,1)S(1)} collective-permute-done((bf16[1,224,512]{2,1,0:T(8,128)(2,1)S(1)}, bf16[1,224,512]{2,1,0:T(8,128)(2,1)S(1)}, u32[]{:S(2)}, u32[]{:S(2)}) %collective-permute-start.21) | collective-permute-done | bytes 229408 | tf_op jit(solution)/shard_map/ppermute | solution.py:293
  146.7 5.4 %collective-permute-done.23 = bf16[1,224,384]{2,1,0:T(8,128)(2,1)S(1)} collective-permute-done((bf16[1,224,384]{2,1,0:T(8,128)(2,1)S(1)}, bf16[1,224,384]{2,1,0:T(8,128)(2,1)S(1)}, u32[]{:S(2)}, u32[]{:S(2)}) %collective-permute-start.23) | collective-permute-done | bytes 172064 | tf_op jit(solution)/shard_map/ppermute | solution.py:293
  152.2 1.3 maximum_multiply_fusion
  (53 shorter events, 1.1 us)
Async XLA Ops:
  0.7 1.5 copy-start.5
  2.2 5.1 %copy-start.12 = (f32[1,14,512]{2,0,1:T(1,128)S(1)}, f32[1,14,512]{2,0,1:T(1,128)}, u32[]{:S(2)}) copy-start(f32[1,14,512]{2,0,1:T(1,128)} %param.11) | copy-start | bytes 86020
  2.2 5.1 %copy-start.1 = (s32[1,512,1792]{2,1,0:T(8,128)S(1)}, s32[1,512,1792]{2,1,0:T(8,128)}, u32[]{:S(2)}) copy-start(s32[1,512,1792]{2,1,0:T(8,128)} %param.9) | copy-start | bytes 11010052
  3.4 0.9 copy-start.6
  4.3 33.1 %collective-permute-start.2 = (bf16[2,2,224,512]{3,2,1,0:T(8,128)(2,1)S(1)}, bf16[2,2,224,512]{3,2,1,0:T(8,128)(2,1)S(1)}, u32[]{:S(2)}, u32[]{:S(2)}) collective-permute-start(bf16[2,2,224,512]{3,2,1,0:T(8,128)(2,1)S(1)} %get-tuple-element.45.after.refs_2_), channel_id=1, source_target_pairs={{0,2},{2,0},{1,3},{3,1},{4,6},{6,4},{5,7},{7,5},{8,10},{10,8},{9,1... | collective-permute-start | bytes 2752520 | tf_op jit(solution)/shard_map/ppermute | solution.py:293
  7.3 1.5 copy-start.3
  10.4 0.8 copy-start.10
  11.2 8.8 %collective-permute-start.1 = (bf16[944,128]{1,0:T(8,128)(2,1)S(1)}, bf16[944,128]{1,0:T(8,128)(2,1)S(1)}, u32[]{:S(2)}, u32[]{:S(2)}) collective-permute-start(bf16[944,128]{1,0:T(8,128)(2,1)S(1)} %get-tuple-element.48.refs_3_), channel_id=1, source_target_pairs={{0,4},{4,0},{8,12},{12,8},{16,20},{20,16},{24,28},{28,24},{1,5},{5... | collective-permute-start | bytes 725000 | tf_op jit(solution)/shard_map/ppermute | solution.py:293
  14.3 0.8 copy-start.8
  15.1 8.6 %collective-permute-start = (bf16[944,128]{1,0:T(8,128)(2,1)S(1)}, bf16[944,128]{1,0:T(8,128)(2,1)S(1)}, u32[]{:S(2)}, u32[]{:S(2)}) collective-permute-start(bf16[944,128]{1,0:T(8,128)(2,1)S(1)} %get-tuple-element.50.refs_3_), channel_id=1, source_target_pairs={{0,4},{4,0},{8,12},{12,8},{16,20},{20,16},{24,28},{28,24},{1,5},{5... | collective-permute-start | bytes 725000 | tf_op jit(solution)/shard_map/ppermute | solution.py:293
  20.0 1.0 copy-start.11
  21.0 2.7 %copy-start.7 = (bf16[2,2,224,512]{3,2,1,0:T(8,128)(2,1)S(1)}, bf16[2,2,224,512]{3,2,1,0:T(8,128)(2,1)}, u32[]{:S(2)}) copy-start(bf16[2,2,224,512]{3,2,1,0:T(8,128)(2,1)} %copy-done.6) | copy-start | bytes 2752516
  21.0 4.2 %copy-start.9 = (f32[944,128]{1,0:T(8,128)S(1)}, f32[944,128]{1,0:T(8,128)}, u32[]{:S(2)}) copy-start(f32[944,128]{1,0:T(8,128)} %copy-done.8) | copy-start | bytes 1449988
  21.1 9.1 %collective-permute-start.3 = (bf16[944,128]{1,0:T(8,128)(2,1)S(1)}, bf16[944,128]{1,0:T(8,128)(2,1)S(1)}, u32[]{:S(2)}, u32[]{:S(2)}) collective-permute-start(bf16[944,128]{1,0:T(8,128)(2,1)S(1)} %get-tuple-element.52.refs_3_), channel_id=1, source_target_pairs={{8,0},{12,4},{16,8},{20,12},{24,16},{28,20},{9,1},{13,5},{17,9},{2... | collective-permute-start | bytes 725000 | tf_op jit(solution)/shard_map/ppermute | solution.py:297
  23.7 26.4 %collective-permute-start.5 = (bf16[2,2,224,512]{3,2,1,0:T(8,128)(2,1)S(1)}, bf16[2,2,224,512]{3,2,1,0:T(8,128)(2,1)S(1)}, u32[]{:S(2)}, u32[]{:S(2)}) collective-permute-start(bf16[2,2,224,512]{3,2,1,0:T(8,128)(2,1)S(1)} %copy-done.7), channel_id=1, source_target_pairs={{0,4},{4,0},{8,12},{12,8},{16,20},{20,16},{24,28},{28,24},{1,5},{5... | collective-permute-start | bytes 2752520 | tf_op jit(solution)/shard_map/ppermute | solution.py:293
  25.2 12.3 %copy-start.4 = (bf16[1,512,1792]{2,1,0:T(8,128)(2,1)S(1)}, bf16[1,512,1792]{2,1,0:T(8,128)(2,1)}, u32[]{:S(2)}) copy-start(bf16[1,512,1792]{2,1,0:T(8,128)(2,1)} %param.8) | copy-start | bytes 5505028
  25.3 9.7 %collective-permute-start.6 = (bf16[944,128]{1,0:T(8,128)(2,1)S(1)}, bf16[944,128]{1,0:T(8,128)(2,1)S(1)}, u32[]{:S(2)}, u32[]{:S(2)}) collective-permute-start(bf16[944,128]{1,0:T(8,128)(2,1)S(1)} %get-tuple-element.53.refs_5_), channel_id=1, source_target_pairs={{8,0},{12,4},{16,8},{20,12},{24,16},{28,20},{9,1},{13,5},{17,9},{2... | collective-permute-start | bytes 725000 | tf_op jit(solution)/shard_map/ppermute | solution.py:297
  30.2 7.3 %copy-start.2 = (s32[1,512,1792]{2,1,0:T(8,128)S(1)}, s32[1,512,1792]{2,1,0:T(8,128)}, u32[]{:S(2)}) copy-start(s32[1,512,1792]{2,1,0:T(8,128)} %param.9) | copy-start | bytes 11010052
  31.0 19.0 %collective-permute-start.4 = (bf16[944,128]{1,0:T(8,128)(2,1)S(1)}, bf16[944,128]{1,0:T(8,128)(2,1)S(1)}, u32[]{:S(2)}, u32[]{:S(2)}) collective-permute-start(bf16[944,128]{1,0:T(8,128)(2,1)S(1)} %get-tuple-element.55), channel_id=1, source_target_pairs={{16,0},{20,4},{24,8},{28,12},{17,1},{21,5},{25,9},{29,13},{18,2},{... | collective-permute-start | bytes 725000 | tf_op jit(solution)/shard_map/ppermute | solution.py:297
  35.0 2.5 %copy-start = (s32[1,512,1792]{2,1,0:T(8,128)S(1)}, s32[1,512,1792]{2,1,0:T(8,128)}, u32[]{:S(2)}) copy-start(s32[1,512,1792]{2,1,0:T(8,128)} %param.10) | copy-start | bytes 11010052
  35.9 20.3 %collective-permute-start.7 = (bf16[944,128]{1,0:T(8,128)(2,1)S(1)}, bf16[944,128]{1,0:T(8,128)(2,1)S(1)}, u32[]{:S(2)}, u32[]{:S(2)}) collective-permute-start(bf16[944,128]{1,0:T(8,128)(2,1)S(1)} %get-tuple-element.61), channel_id=1, source_target_pairs={{16,0},{20,4},{24,8},{28,12},{17,1},{21,5},{25,9},{29,13},{18,2},{... | collective-permute-start | bytes 725000 | tf_op jit(solution)/shard_map/ppermute | solution.py:297
  39.7 17.2 %slice-start = ((s8[12845056]{0:T(1024)(128)(4,1)}), s8[4194304]{0:T(1024)(128)(4,1)S(1)}, s32[]{:S(2)}) async-start(s8[12845056]{0:T(1024)(128)(4,1)} %bitcast.38), calls=%async_computation | async-start | bytes 8388608
  39.7 17.2 %slice-start.1 = ((s8[12845056]{0:T(1024)(128)(4,1)}), s8[4194304]{0:T(1024)(128)(4,1)S(1)}, s32[]{:S(2)}) async-start(s8[12845056]{0:T(1024)(128)(4,1)} %bitcast.38), calls=%async_computation.1 | async-start | bytes 8388608
  42.0 15.0 %slice-start.2 = ((s8[12845056]{0:T(1024)(128)(4,1)}), s8[4194304]{0:T(1024)(128)(4,1)S(1)}, s32[]{:S(2)}) async-start(s8[12845056]{0:T(1024)(128)(4,1)} %bitcast.38), calls=%async_computation.2 | async-start | bytes 8388608
  50.8 6.1 %slice-start.3 = ((s8[12845056]{0:T(1024)(128)(4,1)}), s8[262144]{0:T(1024)(128)(4,1)S(1)}, s32[]{:S(2)}) async-start(s8[12845056]{0:T(1024)(128)(4,1)} %bitcast.38), calls=%async_computation.3 | async-start | bytes 524288
  50.8 19.9 %collective-permute-start.10 = (bf16[512,896]{1,0:T(8,128)(2,1)S(1)}, bf16[512,896]{1,0:T(8,128)(2,1)S(1)}, u32[]{:S(2)}, u32[]{:S(2)}) collective-permute-start(bf16[512,896]{1,0:T(8,128)(2,1)S(1)} %value_grad.2.refs_1_.refs_6_), channel_id=1, source_target_pairs={{0,4},{4,0},{8,12},{12,8},{16,20},{20,16},{24,28},{28,24},{1,5},{5... | collective-permute-start | bytes 2752520 | tf_op jit(solution)/shard_map/ppermute | solution.py:293
  52.8 18.0 %collective-permute-start.9 = (bf16[2,2,224,512]{3,2,1,0:T(8,128)(2,1)S(1)}, bf16[2,2,224,512]{3,2,1,0:T(8,128)(2,1)S(1)}, u32[]{:S(2)}, u32[]{:S(2)}) collective-permute-start(bf16[2,2,224,512]{3,2,1,0:T(8,128)(2,1)S(1)} %collective-permute-done.5.refs_7_.refs_3_), channel_id=1, source_target_pairs={{0,2},{2,0},{1,3},{3,1},{4,6},{6,4},{5,7},{7,5},{8,10},{10,8},{9,1... | collective-permute-start | bytes 2752520 | tf_op jit(solution)/shard_map/ppermute | solution.py:293
  74.2 2.5 %collective-permute-start.11 = (bf16[4,224,512]{2,1,0:T(8,128)(2,1)S(1)}, bf16[4,224,512]{2,1,0:T(8,128)(2,1)S(1)}, u32[]{:S(2)}, u32[]{:S(2)}) collective-permute-start(bf16[4,224,512]{2,1,0:T(8,128)(2,1)S(1)} %get-tuple-element.65), channel_id=1, source_target_pairs={{0,1},{1,0},{2,3},{3,2},{4,5},{5,4},{6,7},{7,6},{8,9},{9,8},{10,11... | collective-permute-start | bytes 2752520 | tf_op jit(solution)/shard_map/ppermute | solution.py:293
  74.3 22.8 %collective-permute-start.16 = (bf16[512,896]{1,0:T(8,128)(2,1)S(1)}, bf16[512,896]{1,0:T(8,128)(2,1)S(1)}, u32[]{:S(2)}, u32[]{:S(2)}) collective-permute-start(bf16[512,896]{1,0:T(8,128)(2,1)S(1)} %value_grad.3.refs_2_.refs_6_), channel_id=1, source_target_pairs={{0,4},{4,0},{8,12},{12,8},{16,20},{20,16},{24,28},{28,24},{1,5},{5... | collective-permute-start | bytes 2752520 | tf_op jit(solution)/shard_map/ppermute | solution.py:293
  80.1 2.2 %collective-permute-start.13 = (bf16[4,224,384]{2,1,0:T(8,128)(2,1)S(1)}, bf16[4,224,384]{2,1,0:T(8,128)(2,1)S(1)}, u32[]{:S(2)}, u32[]{:S(2)}) collective-permute-start(bf16[4,224,384]{2,1,0:T(8,128)(2,1)S(1)} %get-tuple-element.69), channel_id=1, source_target_pairs={{0,1},{1,0},{2,3},{3,2},{4,5},{5,4},{6,7},{7,6},{8,9},{9,8},{10,11... | collective-permute-start | bytes 2064392 | tf_op jit(solution)/shard_map/ppermute | solution.py:293
  80.3 12.8 %collective-permute-start.12 = (bf16[2,224,512]{2,1,0:T(8,128)(2,1)S(1)}, bf16[2,224,512]{2,1,0:T(8,128)(2,1)S(1)}, u32[]{:S(2)}, u32[]{:S(2)}) collective-permute-start(bf16[2,224,512]{2,1,0:T(8,128)(2,1)S(1)} %get-tuple-element.67.refs_8_), channel_id=1, source_target_pairs={{0,8},{4,12},{8,0},{12,4},{16,24},{20,28},{24,16},{28,20},{1,9},{5... | collective-permute-start | bytes 1376264 | tf_op jit(solution)/shard_map/ppermute | solution.py:293
  80.3 42.3 %collective-permute-start.8 = (bf16[512,1792]{1,0:T(8,128)(2,1)S(1)}, bf16[512,1792]{1,0:T(8,128)(2,1)S(1)}, u32[]{:S(2)}, u32[]{:S(2)}) collective-permute-start(bf16[512,1792]{1,0:T(8,128)(2,1)S(1)} %get-tuple-element.63), channel_id=1, source_target_pairs={{0,2},{2,0},{1,3},{3,1},{4,6},{6,4},{5,7},{7,5},{8,10},{10,8},{9,1... | collective-permute-start | bytes 5505032 | tf_op jit(solution)/shard_map/ppermute | solution.py:293
  100.2 2.5 %collective-permute-start.17 = (bf16[4,224,512]{2,1,0:T(8,128)(2,1)S(1)}, bf16[4,224,512]{2,1,0:T(8,128)(2,1)S(1)}, u32[]{:S(2)}, u32[]{:S(2)}) collective-permute-start(bf16[4,224,512]{2,1,0:T(8,128)(2,1)S(1)} %get-tuple-element.75), channel_id=1, source_target_pairs={{0,1},{1,0},{2,3},{3,2},{4,5},{5,4},{6,7},{7,6},{8,9},{9,8},{10,11... | collective-permute-start | bytes 2752520 | tf_op jit(solution)/shard_map/ppermute | solution.py:293
  100.3 15.8 %collective-permute-start.15 = (bf16[2,224,384]{2,1,0:T(8,128)(2,1)S(1)}, bf16[2,224,384]{2,1,0:T(8,128)(2,1)S(1)}, u32[]{:S(2)}, u32[]{:S(2)}) collective-permute-start(bf16[2,224,384]{2,1,0:T(8,128)(2,1)S(1)} %get-tuple-element.70.refs_2_), channel_id=1, source_target_pairs={{0,8},{4,12},{8,0},{12,4},{16,24},{20,28},{24,16},{28,20},{1,9},{5... | collective-permute-start | bytes 1032200 | tf_op jit(solution)/shard_map/ppermute | solution.py:293
  100.4 23.9 %collective-permute-start.14 = (bf16[1,224,512]{2,1,0:T(8,128)(2,1)S(1)}, bf16[1,224,512]{2,1,0:T(8,128)(2,1)S(1)}, u32[]{:S(2)}, u32[]{:S(2)}) collective-permute-start(bf16[1,224,512]{2,1,0:T(8,128)(2,1)S(1)} %get-tuple-element.72.refs_8_), channel_id=1, source_target_pairs={{0,16},{4,20},{8,24},{12,28},{16,0},{20,4},{24,8},{28,12},{1,17},{... | collective-permute-start | bytes 688136 | tf_op jit(solution)/shard_map/ppermute | solution.py:293
  103.0 23.5 %collective-permute-start.19 = (bf16[2,224,512]{2,1,0:T(8,128)(2,1)S(1)}, bf16[2,224,512]{2,1,0:T(8,128)(2,1)S(1)}, u32[]{:S(2)}, u32[]{:S(2)}) collective-permute-start(bf16[2,224,512]{2,1,0:T(8,128)(2,1)S(1)} %get-tuple-element.76.refs_2_), channel_id=1, source_target_pairs={{0,8},{4,12},{8,0},{12,4},{16,24},{20,28},{24,16},{28,20},{1,9},{5... | collective-permute-start | bytes 1376264 | tf_op jit(solution)/shard_map/ppermute | solution.py:293
  119.4 6.1 %collective-permute-start.20 = (bf16[4,224,384]{2,1,0:T(8,128)(2,1)S(1)}, bf16[4,224,384]{2,1,0:T(8,128)(2,1)S(1)}, u32[]{:S(2)}, u32[]{:S(2)}) collective-permute-start(bf16[4,224,384]{2,1,0:T(8,128)(2,1)S(1)} %get-tuple-element.81), channel_id=1, source_target_pairs={{0,1},{1,0},{2,3},{3,2},{4,5},{5,4},{6,7},{7,6},{8,9},{9,8},{10,11... | collective-permute-start | bytes 2064392 | tf_op jit(solution)/shard_map/ppermute | solution.py:293
  124.4 11.6 %collective-permute-start.18 = (bf16[1,224,384]{2,1,0:T(8,128)(2,1)S(1)}, bf16[1,224,384]{2,1,0:T(8,128)(2,1)S(1)}, u32[]{:S(2)}, u32[]{:S(2)}) collective-permute-start(bf16[1,224,384]{2,1,0:T(8,128)(2,1)S(1)} %get-tuple-element.78.refs_8_), channel_id=1, source_target_pairs={{0,16},{4,20},{8,24},{12,28},{16,0},{20,4},{24,8},{28,12},{1,17},{... | collective-permute-start | bytes 516104 | tf_op jit(solution)/shard_map/ppermute | solution.py:293
  125.7 17.3 %collective-permute-start.22 = (bf16[2,224,384]{2,1,0:T(8,128)(2,1)S(1)}, bf16[2,224,384]{2,1,0:T(8,128)(2,1)S(1)}, u32[]{:S(2)}, u32[]{:S(2)}) collective-permute-start(bf16[2,224,384]{2,1,0:T(8,128)(2,1)S(1)} %get-tuple-element.82.refs_2_), channel_id=1, source_target_pairs={{0,8},{4,12},{8,0},{12,4},{16,24},{20,28},{24,16},{28,20},{1,9},{5... | collective-permute-start | bytes 1032200 | tf_op jit(solution)/shard_map/ppermute | solution.py:293
  126.5 20.1 %collective-permute-start.21 = (bf16[1,224,512]{2,1,0:T(8,128)(2,1)S(1)}, bf16[1,224,512]{2,1,0:T(8,128)(2,1)S(1)}, u32[]{:S(2)}, u32[]{:S(2)}) collective-permute-start(bf16[1,224,512]{2,1,0:T(8,128)(2,1)S(1)} %get-tuple-element.84.refs_2_), channel_id=1, source_target_pairs={{0,16},{4,20},{8,24},{12,28},{16,0},{20,4},{24,8},{28,12},{1,17},{... | collective-permute-start | bytes 688136 | tf_op jit(solution)/shard_map/ppermute | solution.py:293
  143.1 9.0 %collective-permute-start.23 = (bf16[1,224,384]{2,1,0:T(8,128)(2,1)S(1)}, bf16[1,224,384]{2,1,0:T(8,128)(2,1)S(1)}, u32[]{:S(2)}, u32[]{:S(2)}) collective-permute-start(bf16[1,224,384]{2,1,0:T(8,128)(2,1)S(1)} %get-tuple-element.87), channel_id=1, source_target_pairs={{0,16},{4,20},{8,24},{12,28},{16,0},{20,4},{24,8},{28,12},{1,17},{... | collective-permute-start | bytes 516104 | tf_op jit(solution)/shard_map/ppermute | solution.py:293

commit v3 on v2

v3 whole, which is shorter than its diff:
```python
import functools
import math

import jax
import jax.numpy as jnp
from jax import lax
from jax.experimental import pallas as pl
from jax.experimental.pallas import tpu as pltpu
from jax.sharding import PartitionSpec as P

BF = jnp.bfloat16
F32 = jnp.float32
HD = 128
PLANE = 16
EXTRA = 3 * PLANE
PARAMS = pltpu.CompilerParams(vmem_limit_bytes=12 * 1024 * 1024)
VM = pl.BlockSpec(memory_space=pltpu.VMEM)
SM = pl.BlockSpec(memory_space=pltpu.SMEM)
ANY = pl.BlockSpec(memory_space=pl.ANY)


def dot(a, b, contract):
    return lax.dot_general(a, b, (contract, ((), ())), preferred_element_type=F32)


def hi_lo(x):
    hi = x.astype(BF)
    return hi, (x - hi.astype(F32)).astype(BF)


LONG = pl.CostEstimate(flops=2 * 10**10, transcendentals=0, bytes_accessed=0)


class Line:
    def __init__(self):
        self.last = []

    def __call__(self, kernel, name, outs, smalls, arrays, after=(), scratch=(), cost=LONG, last=0):
        waits = [*self.last, *after]
        first = len(smalls) + len(arrays)

        def body(*refs):
            kernel(*refs[:first], *refs[first + len(waits) :])

        results = pl.pallas_call(
            body,
            in_specs=[SM] * len(smalls) + [VM] * len(arrays) + [ANY] * len(waits),
            out_specs=[VM] * len(outs),
            out_shape=[jax.ShapeDtypeStruct(shape, dtype) for shape, dtype in outs],
            scratch_shapes=list(scratch),
            compiler_params=PARAMS,
            cost_estimate=cost,
            name=name,
        )(*smalls, *arrays, *waits)
        self.last = [results[last]]
        return results


def pause_kernel(o_ref):
    o_ref[...] = jnp.zeros_like(o_ref)


def pause(line, after=(), cost=LONG):
    line(pause_kernel, "pause", [((8, HD), F32)], [], [], after, (), cost)


def copy_kernel(*refs):
    outs = refs[len(refs) // 2 :]
    for ref, out in zip(refs, outs):
        out[...] = ref[...]


def merge_kernel(counts, *refs):
    first = 0
    for count, out in zip(counts, refs[sum(counts) :]):
        start = 0
        for ref in refs[first : first + count]:
            out[start : start + ref.shape[0]] = ref[...]
            start += ref.shape[0]
        first += count


def merged(line, groups):
    outs = [((sum(p.shape[0] for p in g), *g[0].shape[1:]), g[0].dtype) for g in groups]
    kernel = functools.partial(merge_kernel, [len(g) for g in groups])
    return line(kernel, "merge_inputs", outs, [], [p for g in groups for p in g])


def transpose_kernel(order, rows, at_ref, a_ref, near_ref, *refs):
    far_refs, flat = refs[:-1], refs[-1]
    flat[...] = a_ref[...].T.astype(flat.dtype)
    each = len(order) // len(far_refs)
    for yr in range(2):
        for dr in range(2):
            for i, low in enumerate(order):
                start = (((at_ref[2] ^ low) * 2 + (at_ref[0] ^ yr)) * 2 + (at_ref[1] ^ dr)) * rows
                piece = flat[pl.ds(pl.multiple_of(start, 8), rows), :].astype(BF)
                if yr == 0:
                    near_ref[i, dr] = piece
                else:
                    far_refs[i // each][i % each, dr] = piece


def transposed(line, at, a, order, rows):
    tokens, cols = a.shape
    halves = 2 if len(order) % 2 == 0 else 1
    outs = [((len(order), 2, rows, tokens), BF)] + [((len(order) // halves, 2, rows, tokens), BF)] * halves
    scratch = [pltpu.VMEM((cols, tokens), BF if rows % 16 == 0 else F32)]
    kernel = functools.partial(transpose_kernel, order, rows)
    return line(kernel, "transpose_inputs", outs, [at], [a], (), scratch)


def state_kernel(first, heads, ld_ref, q_ref, c_ref, pay_ref, own_ref, cum_ref, cumt_ref, qbf_ref):
    tokens = ld_ref.shape[1]
    x = ld_ref[first : first + heads, :]
    x = jnp.concatenate([x, jnp.zeros((PLANE - heads, tokens), F32)], axis=0)
    lane = lax.broadcasted_iota(jnp.int32, x.shape, 1)
    shift = 1
    while shift < tokens:
        x = x + jnp.where(lane >= shift, pltpu.roll(x, shift, 1), 0.0)
        shift *= 2
    cum_ref[...] = x
    xt = jnp.concatenate([x, jnp.zeros((HD - PLANE, tokens), F32)], axis=0).T
    cumt_ref[...] = xt
    et = jnp.exp(xt)
    d = jnp.broadcast_to(jnp.exp(x[:, tokens - 1 : tokens]), (PLANE, HD))
    put_decays(d, heads, pay_ref, own_ref)
    for h in range(heads):
        s = slice(h * HD, (h + 1) * HD)
        f = slice((first + h) * HD, (first + h + 1) * HD)
        q = q_ref[:, f].astype(F32).astype(BF)
        qbf_ref[:, s] = q
        hi, lo = hi_lo(c_ref[:, f].astype(F32) * et[:, h : h + 1])
        both = dot(q, jnp.concatenate([hi, lo], axis=1), ((0,), (0,)))
        term = both[:, :HD] + both[:, HD:]
        own_ref[s, :] = term
        pay_ref[s, :] = term.astype(BF)


def state_terms(line, first, heads, q, c, ld):
    tokens = q.shape[0]
    rows = heads * HD + EXTRA
    outs = [((rows, HD), BF), ((rows, HD), F32), ((PLANE, tokens), F32), ((tokens, HD), F32)]
    outs.append(((tokens, heads * HD), BF))
    return line(functools.partial(state_kernel, first, heads), "state_terms", outs, [], [ld, q, c])


def put_decays(d, heads, pay_ref, own_ref):
    d_hi, d_mid = hi_lo(d)
    d_lo = (d - d_hi.astype(F32) - d_mid.astype(F32)).astype(BF)
    at = heads * HD
    pay_ref[at : at + PLANE, :] = d_hi
    pay_ref[at + PLANE : at + 2 * PLANE, :] = d_mid
    pay_ref[at + 2 * PLANE : at + EXTRA, :] = d_lo
    own_ref[at : at + PLANE, :] = d
    own_ref[at + PLANE : at + EXTRA, :] = jnp.zeros((EXTRA - PLANE, HD), F32)


def decays(ref, heads):
    p = ref[heads * HD :, :].astype(F32)
    return p[:PLANE] + p[PLANE : 2 * PLANE] + p[2 * PLANE :]


def append_kernel(heads, at, flags_ref, a_ref, b_ref, pay_ref, own_ref):
    swap = flags_ref[at] != 0
    da, db = decays(a_ref, heads), decays(b_ref, heads)
    one = jnp.ones_like(da)
    scale_a = jnp.where(swap, db, one)
    scale_b = jnp.where(swap, one, da)
    put_decays(da * db, heads, pay_ref, own_ref)
    for h in range(heads):
        s = slice(h * HD, (h + 1) * HD)
        term = scale_a[h : h + 1] * a_ref[s, :].astype(F32) + scale_b[h : h + 1] * b_ref[s, :].astype(F32)
        own_ref[s, :] = term
        pay_ref[s, :] = term.astype(BF)


def append(line, heads, flags, at, a, b):
    outs = [(a.shape, BF), (a.shape, F32)]
    return line(functools.partial(append_kernel, heads, at), "join_states", outs, [flags], [a, b])


def local_kernel(heads, cols, q_ref, k_ref, c_ref, cum_ref, cumt_ref, o_ref, kbf_ref):
    tokens = q_ref.shape[0]
    tile = 256
    row = lax.broadcasted_iota(jnp.int32, (tile, tile), 0)
    col = lax.broadcasted_iota(jnp.int32, (tile, tile), 1)
    causal = col >= row
    for h in range(heads):
        f = slice(cols + h * HD, cols + (h + 1) * HD)
        k = k_ref[:, f].astype(F32).astype(BF)
        kbf_ref[:, h * HD : (h + 1) * HD] = k
        scores = dot(k, q_ref[:, h * HD : (h + 1) * HD], ((1,), (1,)))
        strips = []
        for at in range(0, tokens, tile):
            end = at + tile
            before = cumt_ref[at:end, h : h + 1]
            gap = jnp.where(causal, cum_ref[h : h + 1, at:end] - before, -jnp.inf)
            strip = [jnp.zeros((tile, at), BF)] if at else []
            strip.append((scores[at:end, at:end] * jnp.exp(gap)).astype(BF))
            if end < tokens:
                middle = cum_ref[h : h + 1, end - 1 : end]
                to_t = jnp.exp(cum_ref[h : h + 1, end:] - middle)
                from_s = jnp.exp(middle - before)
                strip.append((scores[at:end, end:] * to_t * from_s).astype(BF))
            strips.append(jnp.concatenate(strip, axis=1))
        weighted = jnp.concatenate(strips, axis=0)
        o_ref[:, h * HD : (h + 1) * HD] = dot(weighted, c_ref[:, f], ((1,), (0,)))


def local_part(line, first, heads, q, k, c, cum, cumt):
    kernel = functools.partial(local_kernel, heads, first * HD)
    shape = (q.shape[0], heads * HD)
    return line(kernel, "local_part", [(shape, F32), (shape, BF)], [], [q, k, c, cum, cumt])


def value_kernel(heads, first, count, scale, flags_ref, k_ref, l_ref, cumt_ref, oth_ref, e_ref, r_ref, o_ref):
    tokens = k_ref.shape[0]
    is_first = flags_ref[0] == 0
    de = decays(e_ref, heads)
    do = decays(oth_ref, heads)
    use_oth = jnp.where(is_first, 1.0, 0.0)
    scale_e = jnp.where(is_first, do, jnp.ones_like(do))
    fall = jnp.exp(cumt_ref[tokens - 1 : tokens, :] - cumt_ref[...])
    for h in range(first, first + count):
        s = slice(h * HD, (h + 1) * HD)
        e = e_ref[s, :].astype(F32) + de[h : h + 1] * r_ref[s, :].astype(F32)
        carry = use_oth * oth_ref[s, :].astype(F32) + scale_e[h : h + 1] * e
        hi, lo = hi_lo(carry)
        both = dot(k_ref[:, s], jnp.concatenate([hi, lo], axis=1), ((1,), (0,)))
        carried = fall[:, h : h + 1] * (both[:, :HD] + both[:, HD:])
        at = (h - first) * HD
        o_ref[:, at : at + HD] = (scale * (l_ref[:, s] + carried)).astype(BF)


def value_grads(line, heads, first, count, scale, flags, arrays, after):
    kernel = functools.partial(value_kernel, heads, first, count, scale)
    outs = [((arrays[0].shape[0], count * HD), BF)]
    return line(kernel, "value_grad", outs, [flags], arrays, after)[0]


def input_kernel(rows, at, flags_ref, *refs):
    vs, w_ref, o_ref, v_all = refs[:-3], *refs[-3:]
    start = 0
    for v in vs:
        v_all[:, start : start + v.shape[1]] = v[...]
        start += v.shape[1]
    w = w_ref[pl.ds(pl.multiple_of(flags_ref[at] * rows, 128), rows), :]
    o_ref[...] = dot(v_all[...], w, ((1,), (1,))).astype(o_ref.dtype)


def input_part(line, flags, at, vs, w, rows, dtype, after=()):
    tokens, features = vs[0].shape[0], w.shape[1]
    scratch = [pltpu.VMEM((tokens, features), BF)]
    kernel = functools.partial(input_kernel, rows, at)
    return line(kernel, "input_part", [((tokens, rows), dtype)], [flags], [*vs, w], after, scratch)[0]


def last_input_kernel(total_ref, *refs):
    total = total_ref[...]
    for ref in refs[:-2]:
        total = total + ref[...].astype(F32)
    refs[-2][...] = total.astype(BF)
    refs[-1][...] = jnp.zeros_like(refs[-1])


def last_weight_kernel(scale, *refs):
    out = refs[-1]
    start = 0
    for keep, came in zip(refs[0:-1:2], refs[1:-1:2]):
        width = keep.shape[2]
        out[:, start : start + width] = scale * (keep[0] + came[0].astype(F32))
        start += width


def weight_kernel(sides, *refs):
    *pieces, v_ref, v_y_ref, away_ref, keep_ref = refs
    for s in range(sides):
        own, other = pieces[2 * s : 2 * s + 2]
        lows, _, rows, tokens = own.shape
        total = dot(own[...].reshape(-1, tokens), v_ref[...], ((1,), (0,)))
        total = total + dot(other[...].reshape(-1, tokens), v_y_ref[...], ((1,), (0,)))
        for low in range(lows):
            at = low * 2 * rows
            keep_ref[low * sides + s] = total[at : at + rows]
            away_ref[low * sides + s] = total[at + rows : at + 2 * rows].astype(BF)


def weight_part(line, pieces, vs, after):
    sides, (lows, _, rows, _) = len(pieces), pieces[0][0].shape
    shape = (lows * sides, rows, vs[0].shape[1])
    arrays = [p for side_pieces in pieces for p in side_pieces] + list(vs)
    kernel = functools.partial(weight_kernel, sides)
    return line(kernel, "weight_part", [(shape, BF), (shape, F32)], [], arrays, after, last=1)


def fold_kernel(at, start, flags_ref, keep_ref, came_ref, away_ref, left_ref):
    half, _, width = away_ref.shape
    cols = slice(start, start + width)
    kept = pl.ds(flags_ref[at] * half, half)
    sent = pl.ds((1 - flags_ref[at]) * half, half)
    left_ref[...] = keep_ref[kept, :, cols] + came_ref[kept, :, cols].astype(F32)
    away_ref[...] = (keep_ref[sent, :, cols] + came_ref[sent, :, cols].astype(F32)).astype(BF)


def fold(line, flags, at, keep, came, start=0, width=None):
    blocks, rows, all_columns = keep.shape
    shape = (blocks // 2, rows, width or all_columns)
    kernel = functools.partial(fold_kernel, at, start)
    return line(kernel, "fold_weight", [(shape, BF), (shape, F32)], [flags], [keep, came])


def tied(x, *after):
    return lax.optimization_barrier((x, *after))[0]


def swap_with(x, axis, bit):
    return lax.ppermute(x, axis, [(i, i ^ bit) for i in range(lax.axis_size(axis))])


def from_later(x, axis, shift):
    return lax.ppermute(x, axis, [(i, i - shift) for i in range(shift, lax.axis_size(axis))])


def local(inputs, value_weight, cotangent, spikes_q, spikes_k, log_decay):
    seqs, sides, dps = lax.axis_size("seq"), lax.axis_size("head"), lax.axis_size("dp")
    seq, side, dp = lax.axis_index("seq"), lax.axis_index("head"), lax.axis_index("dp")
    y, z = seq % 2, seq // 2
    tokens, rows_here = inputs.shape[1:]
    features = value_weight.shape[1]
    heads_here = log_decay.shape[1]
    seq_length = tokens * seqs
    grad_scale = 1.0 / (2.25 * HD * math.sqrt(seq_length))
    third = (heads_here + 2) // 4
    splits = [(third - 1,) * 2, (third, heads_here - 3 * third + 2)] if heads_here > 8 else [(third, heads_here - third)]
    sizes = [sum(split) for split in splits]
    starts = [sum(sizes[:g]) for g in range(len(sizes))]
    groups = len(sizes)
    rows = rows_here * sides // (seqs * dps)
    lows = rows_here // (2 * dps * rows)
    stages = (seqs // 2).bit_length() - 1

    q, k, c, ld = spikes_q[0], spikes_k[0], cotangent[0], log_decay[0]

    low_bits = lows.bit_length() - 1
    order = [int("0" + format(i, "b").zfill(low_bits)[::-1], 2) for i in range(lows)] if low_bits else [0]
    here = (z // lows) ^ side
    bits = list(range(low_bits)) + list(reversed(range(low_bits, stages)))

    at_sides = 4
    at_steps = at_sides + sides
    places = [y, dp, z % lows, jnp.zeros_like(y)] + [side ^ i for i in range(sides)]
    places += [(here >> max(b - low_bits, 0)) & int(b >= low_bits) for b in bits]
    flags = jnp.stack([p.astype(jnp.int32) for p in places])

    line = Line()
    own, other, joined, locals_, values, from_y = [], [], [], [], [], []

    def states(g):
        own.append(state_terms(line, starts[g], sizes[g], q, c, ld))
        other.append(swap_with(own[g][0], "seq", 1))

    def join(g):
        joined.append(append(line, sizes[g], flags, 0, own[g][1], other[g]))

    def spread(g):
        pay, ours = joined[g]
        e = None
        for stage in range(stages):
            later = from_later(pay, "seq", 2 << stage)
            if stage == 0:
                e = later
            elif stage < stages - 1:
                e = append(line, sizes[g], flags, 3, e, later)[1]
            if stage < stages - 1:
                pay, ours = append(line, sizes[g], flags, 3, ours, later)
        if stages == 1:
            later = jnp.zeros_like(later)
        joined[g] = (e, later)

    def local(g):
        _, _, cum, cumt, q_bf = own[g]
        locals_.append(local_part(line, starts[g], sizes[g], q_bf, k, c, cum, cumt))

    def value(g, *after):
        part, k_bf = locals_[g]
        arrays = [k_bf, part, own[g][3], other[g], *joined[g]]
        first = 0
        for count in splits[g]:
            v = value_grads(line, sizes[g], first, count, grad_scale, flags, arrays, after)
            values.append(v)
            from_y.append(swap_with(v, "seq", 1))
            first, after = first + count, ()

    kept, parts = {}, {}

    def matmul(i, *after):
        away, keep = weight_part(line, pieces, (values[i], from_y[i]), after)
        parts[i] = (keep, swap_with(away, "dp", 1))

    def over_dp(i, *widths):
        start = 0
        for j, width in enumerate(widths or [None]):
            away, keep = fold(line, flags, at_steps, *parts[i], start, width)
            kept[i, j] = (keep, swap_with(away, "seq", 2 << bits[0]))
            start += width or 0

    def over_z(i, j=0):
        for step, bit in enumerate(bits[1:], 1):
            away, keep = fold(line, flags, at_steps + step, *kept[i, j])
            kept[i, j] = (keep, swap_with(away, "seq", 2 << bit))

    others = []

    def input_others():
        for i in range(1, sides):
            part = input_part(line, flags, at_sides + i, values, value_weight, rows_here, BF)
            others.append(swap_with(part, "head", i))

    def input_own(*after):
        return input_part(line, flags, at_sides, values, value_weight, rows_here, F32, after)

    near, *far = transposed(line, flags, inputs[0], order, rows)
    near_x = [swap_with(near, "head", i) for i in range(1, sides)]
    for g in range(groups):
        states(g)
    far_x = [[] for _ in near_x]

    def send_far(i):
        piece = far[i]
        far[i] = swap_with(tied(piece, *line.last), "seq", 1)
        line.last.append(piece)

    def far_to_x(i):
        far[i] = line(copy_kernel, "pass_on", [(far[i].shape, BF)], [], [far[i]])[0]
        for j in range(1, sides):
            far_x[j - 1].append(swap_with(far[i], "head", j))

    join(0)
    send_far(0)
    if groups == 2:
        join(1)
    if len(far) == 2:
        send_far(1)
    local(0)
    spread(0)
    if groups == 2:
        local(1)
    for i in range(len(far)):
        far_to_x(i)
    value(0, *near_x)
    if groups == 2:
        spread(1)
    everything = [[p] for p in (near, *near_x)] + [far, *far_x]
    everything = merged(line, everything)
    pieces = list(zip(everything[:sides], everything[sides:]))
    if groups == 2:
        matmul(0)
        pause(line)
        over_dp(0)
        value(1)
        matmul(1)
        pause(line)
        over_dp(1)
        over_z(0)
        input_others()
        matmul(2)
        pause(line)
        over_dp(2)
        over_z(1)
        matmul(3)
        pause(line, [kept[0, 0][1]])
        over_dp(3, splits[1][1] // 2 * HD, (splits[1][1] + 1) // 2 * HD)
        over_z(2)
        over_z(3, 0)
        over_z(3, 1)
        total = input_own()
    else:
        matmul(0)
        matmul(1)
        over_dp(0)
        over_dp(1)
        over_z(0)
        input_others()
        total = input_own()
        over_z(1)
    outs = [(total.shape, BF), ((8, HD), F32)]
    grad_input = line(last_input_kernel, "grad_input", outs, [], [total, *others], last=1)[0]
    arrays = [a for i in sorted(kept) for a in kept[i]]
    kernel = functools.partial(last_weight_kernel, 1.0 / math.sqrt(dps * seq_length))
    grad_weight = line(kernel, "grad_weight", [((rows, features), F32)], [], arrays)[0]
    return grad_input[None], grad_weight


def solution(mesh):
    return jax.shard_map(
        local,
        mesh=mesh,
        in_specs=(
            P("dp", "seq", "head"),
            P(None, "head"),
            P("dp", "seq", "head"),
            P("dp", "seq", "head"),
            P("dp", "seq", "head"),
            P("dp", "head", "seq"),
        ),
        out_specs=(P("dp", "seq", "head"), P(("seq", "dp"), "head")),
        check_vma=False,
    )
```

time: 154 us -> 137 us (0.89)
  waiting for transfers between devices: 83.4 us -> 42 us
  Pallas kernels: 35.8 us -> 52.8 us
  starting transfers between devices: 23.3 us -> 36.9 us
  other arithmetic: 3.35 us -> 0.01 us
  local copies, waits for them, and re-layouts: 6.55 us -> 3.21 us
    ppermute x20 -> x26, waiting for transfers between devices: 66.5 us -> 42 us  [swap_with(): lax.ppermute(x, axis, [(i, i ^ bit) for i in range(lax.axis_size(axis))])]
    pallas_call x24 -> x38, Pallas kernels: 35.8 us -> 52.8 us  [__call__(): pl.pallas_call(body, in_specs=[SM] * len(smalls) + [VM] * len(arrays) + [...]
    ppermute x4, waiting for transfers between devices: 16.9 us -> 0.01 us  [from_later(): lax.ppermute(x, axis, [(i, i - shift) for i in range(shift, lax.axis_size...]
    ppermute x20 -> x26, starting transfers between devices: 17.4 us -> 31.5 us  [swap_with(): lax.ppermute(x, axis, [(i, i ^ bit) for i in range(lax.axis_size(axis))])]
    unnamed x35 -> x53, local copies, waits for them, and re-layouts: 6.55 us -> 3.13 us
    broadcast_in_dim x1 -> x0, other arithmetic: 1.68 us -> none  [local(): return (total.astype(BF)[None], grad_weight)]
  transfers between devices with their start and end apart: 24 -> 30, of which waited for: 18 -> 12; matrix products, arithmetic and copies ran while one was open for 1% -> 0% of each run, Pallas kernels for 20% -> 36%
where the time goes in v3:
time: 137 us; the launch traced here: 136 us
  Pallas kernels  52.8 us (39%)
  waiting for transfers between devices  42 us (31%)
  starting transfers between devices  36.9 us (27%)
  local copies, waits for them, and re-layouts  3.21 us (2%)
    pallas_call x38, Pallas kernels, __call__(): pl.pallas_call(body, in_specs=[SM] * len(smalls) + [VM] * len(arrays) + [...  52.8 us
    ppermute x26, waiting for transfers between devices, swap_with(): lax.ppermute(x, axis, [(i, i ^ bit) for i in range(lax.axis_size(axis))])  42 us
    ppermute x26, starting transfers between devices, swap_with(): lax.ppermute(x, axis, [(i, i ^ bit) for i in range(lax.axis_size(axis))])  31.5 us
    ppermute x4, starting transfers between devices, from_later(): lax.ppermute(x, axis, [(i, i - shift) for i in range(shift, lax.axis_size...  5.44 us
    unnamed x53, local copies, waits for them, and re-layouts  3.13 us
  transfers between devices with their start and end apart: 30, of which 12 were waited for; matrix products, arithmetic and copies ran while one was open for 0% of the time, Pallas kernels for 36%

profile of v3, /device:TPU:0, one launch (start us, length us, event | category | flops | bytes accessed | tf_op | source)
XLA Modules:
  0.0 136.2 jit_solution(8796001185615933757)
XLA Ops:
  0.8 1.5 %copy-done.2 = bf16[1,512,1792]{2,1,0:T(8,128)(2,1)S(1)} copy-done((bf16[1,512,1792]{2,1,0:T(8,128)(2,1)S(1)}, bf16[1,512,1792]{2,1,0:T(8,128)(2,1)}, u32[]{:S(2)}) %copy-start.2) | copy-done | bytes 1835032
  2.3 2.1 %transpose_inputs.1 = (bf16[2,2,224,512]{3,2,1,0:T(8,128)(2,1)}, bf16[1,2,224,512]{3,2,1,0:T(8,128)(2,1)S(1)}, bf16[1,2,224,512]{3,2,1,0:T(8,128)(2,1)S(1)}) custom-call(s32[8]{0:T(128)S(1)} %stack.27.refs_0_, bf16[512,1792]{1,0:T(8,128)(2,1)S(1)} %bitcast.24), custom_call_target="tpu_custom_call" | custom-call | flops 20000000000 | tf_op jit(solution)/shard_map/transpose_inputs/pallas_call | solution.py:45
  4.4 2.9 %collective-permute-start.6 = (bf16[2,2,224,512]{3,2,1,0:T(8,128)(2,1)}, bf16[2,2,224,512]{3,2,1,0:T(8,128)(2,1)}, u32[]{:S(2)}, u32[]{:S(2)}) collective-permute-start(bf16[2,2,224,512]{3,2,1,0:T(8,128)(2,1)} %get-tuple-element.61.refs_3_.refs_0_), channel_id=1, source_target_pairs={{0,2},{2,0},{1,3},{3,1},{4,6},{6,4},{5,7},{7,5},{8,10},{10,8},{9,1... | collective-permute-start | bytes 2752520 | tf_op jit(solution)/shard_map/ppermute | solution.py:318
  7.3 1.5 %state_terms.2 = (bf16[816,128]{1,0:T(8,128)(2,1)S(1)}, f32[816,128]{1,0:T(8,128)S(1)}, f32[16,512]{1,0:T(8,128)S(1)}, f32[512,128]{1,0:T(8,128)S(1)}, bf16[512,768]{1,0:T(8,128)(2,1)S(1)}) custom-call(f32[14,512]{1,0:T(8,128)S(1)} %bitcast.14, s32[512,1792]{1,0:T(8,128)S(1)} %bitcast.20, bf16[512,1792]{1,0:T(8,128)(2,1)S(1)} %bitcast.25, ...), custom_call_target="tpu_custom_call" | custom-call | flops 20000000000 | tf_op jit(solution)/shard_map/state_terms/pallas_call | solution.py:45
  8.9 1.6 %collective-permute-start.1 = (bf16[816,128]{1,0:T(8,128)(2,1)S(1)}, bf16[816,128]{1,0:T(8,128)(2,1)S(1)}, u32[]{:S(2)}, u32[]{:S(2)}) collective-permute-start(bf16[816,128]{1,0:T(8,128)(2,1)S(1)} %get-tuple-element.65.refs_3_), channel_id=1, source_target_pairs={{0,4},{4,0},{8,12},{12,8},{16,20},{20,16},{24,28},{28,24},{1,5},{5... | collective-permute-start | bytes 626696 | tf_op jit(solution)/shard_map/ppermute | solution.py:318
  10.5 1.8 %state_terms.3 = (bf16[1072,128]{1,0:T(8,128)(2,1)S(1)}, f32[1072,128]{1,0:T(8,128)S(1)}, f32[16,512]{1,0:T(8,128)S(1)}, f32[512,128]{1,0:T(8,128)S(1)}, bf16[512,1024]{1,0:T(8,128)(2,1)S(1)}) custom-call(f32[14,512]{1,0:T(8,128)S(1)} %bitcast.15, s32[512,1792]{1,0:T(8,128)S(1)} %bitcast.21, bf16[512,1792]{1,0:T(8,128)(2,1)S(1)} %bitcast.26, ...), custom_call_target="tpu_custom_call" | custom-call | flops 20000000000 | tf_op jit(solution)/shard_map/state_terms/pallas_call | solution.py:45
  12.8 4.1 %collective-permute-done.1.refs_2_.refs_4_ = bf16[816,128]{1,0:T(8,128)(2,1)S(1)} collective-permute-done((bf16[816,128]{1,0:T(8,128)(2,1)S(1)}, bf16[816,128]{1,0:T(8,128)(2,1)S(1)}, u32[]{:S(2)}, u32[]{:S(2)}) %collective-permute-start.1) | collective-permute-done | bytes 208928 | tf_op jit(solution)/shard_map/ppermute | solution.py:318
  17.5 1.3 collective-permute-start.2
  18.8 1.7 %collective-permute-start.5 = (bf16[1,2,224,512]{3,2,1,0:T(8,128)(2,1)S(1)}, bf16[1,2,224,512]{3,2,1,0:T(8,128)(2,1)S(1)}, u32[]{:S(2)}, u32[]{:S(2)}) collective-permute-start(bf16[1,2,224,512]{3,2,1,0:T(8,128)(2,1)S(1)} %get-tuple-element.78.refs_4_), channel_id=1, source_target_pairs={{0,4},{4,0},{8,12},{12,8},{16,20},{20,16},{24,28},{28,24},{1,5},{5... | collective-permute-start | bytes 1376264 | tf_op jit(solution)/shard_map/ppermute | solution.py:318
  20.6 2.2 %collective-permute-done.refs_2_.refs_4_ = bf16[1072,128]{1,0:T(8,128)(2,1)S(1)} collective-permute-done((bf16[1072,128]{1,0:T(8,128)(2,1)S(1)}, bf16[1072,128]{1,0:T(8,128)(2,1)S(1)}, u32[]{:S(2)}, u32[]{:S(2)}) %collective-permute-start) | collective-permute-done | bytes 274464 | tf_op jit(solution)/shard_map/ppermute | solution.py:318
  22.8 0.6 join_states.5
  23.5 1.4 %collective-permute-start.7 = (bf16[1072,128]{1,0:T(8,128)(2,1)S(1)}, bf16[1072,128]{1,0:T(8,128)(2,1)S(1)}, u32[]{:S(2)}, u32[]{:S(2)}) collective-permute-start(bf16[1072,128]{1,0:T(8,128)(2,1)S(1)} %get-tuple-element.71.refs_5_), channel_id=1, source_target_pairs={{8,0},{12,4},{16,8},{20,12},{24,16},{28,20},{9,1},{13,5},{17,9},{2... | collective-permute-start | bytes 823304 | tf_op jit(solution)/shard_map/ppermute | solution.py:322
  24.9 1.7 %collective-permute-start.4 = (bf16[1,2,224,512]{3,2,1,0:T(8,128)(2,1)S(1)}, bf16[1,2,224,512]{3,2,1,0:T(8,128)(2,1)S(1)}, u32[]{:S(2)}, u32[]{:S(2)}) collective-permute-start(bf16[1,2,224,512]{3,2,1,0:T(8,128)(2,1)S(1)} %get-tuple-element.77.refs_6_), channel_id=1, source_target_pairs={{0,4},{4,0},{8,12},{12,8},{16,20},{20,16},{24,28},{28,24},{1,5},{5... | collective-permute-start | bytes 1376264 | tf_op jit(solution)/shard_map/ppermute | solution.py:318
  26.7 1.9 %local_part.2 = (f32[512,768]{1,0:T(8,128)S(1)}, bf16[512,768]{1,0:T(8,128)(2,1)S(1)}) custom-call(bf16[512,768]{1,0:T(8,128)(2,1)S(1)} %get-tuple-element.62.refs_0_, s32[512,1792]{1,0:T(8,128)S(1)} %bitcast.22, bf16[512,1792]{1,0:T(8,128)(2,1)S(1)} %bitcast.27, f32[16,512]{1,0:T(8,128)S(1)} %get-tuple-element.63.refs_3_, ...), custom_call_target="tpu_custom_call" | custom-call | flops 20000000000 | tf_op jit(solution)/shard_map/local_part/pallas_call | solution.py:45
  28.6 1.4 %join_states.6 = (bf16[816,128]{1,0:T(8,128)(2,1)S(1)}, f32[816,128]{1,0:T(8,128)}) custom-call(s32[8]{0:T(128)S(1)} %stack.27.refs_0_, f32[816,128]{1,0:T(8,128)S(1)} %get-tuple-element.75.refs_1_, bf16[816,128]{1,0:T(8,128)(2,1)S(1)} %collective-permute-done.2.refs_2_.refs_5_, f32[512,768]{1,0:T(8,128)S(1)} %get-tuple-element.74.refs_3_.refs_2_), custom_call_target="tpu_custom_call" | custom-call | flops 20000000000 | tf_op jit(solution)/shard_map/join_states/pallas_call | solution.py:45
  30.0 1.3 collective-permute-start.3
  31.3 2.5 %local_part.3 = (f32[512,1024]{1,0:T(8,128)S(1)}, bf16[512,1024]{1,0:T(8,128)(2,1)S(1)}) custom-call(bf16[512,1024]{1,0:T(8,128)(2,1)S(1)} %get-tuple-element.79.refs_0_, s32[512,1792]{1,0:T(8,128)S(1)} %bitcast.23, bf16[512,1792]{1,0:T(8,128)(2,1)S(1)} %bitcast.28, f32[16,512]{1,0:T(8,128)S(1)} %get-tuple-element.80.refs_3_, ...), custom_call_target="tpu_custom_call" | custom-call | flops 20000000000 | tf_op jit(solution)/shard_map/local_part/pallas_call | solution.py:45
  33.8 1.3 copy-done.13
  35.1 0.8 collective-permute-start.9
  35.9 5.2 %collective-permute-done.4.refs_0_ = bf16[1,2,224,512]{3,2,1,0:T(8,128)(2,1)S(1)} collective-permute-done((bf16[1,2,224,512]{3,2,1,0:T(8,128)(2,1)S(1)}, bf16[1,2,224,512]{3,2,1,0:T(8,128)(2,1)S(1)}, u32[]{:S(2)}, u32[]{:S(2)}) %collective-permute-start.4) | collective-permute-done | bytes 458784 | tf_op jit(solution)/shard_map/ppermute | solution.py:318
  41.2 1.2 collective-permute-start.10
  42.3 0.9 value_grad.4.refs_7_.refs_4_.refs_1_
  43.3 1.6 %collective-permute-start.11 = (bf16[512,384]{1,0:T(8,128)(2,1)S(1)}, bf16[512,384]{1,0:T(8,128)(2,1)S(1)}, u32[]{:S(2)}, u32[]{:S(2)}) collective-permute-start(bf16[512,384]{1,0:T(8,128)(2,1)S(1)} %value_grad.4.refs_7_.refs_4_.refs_1_), channel_id=1, source_target_pairs={{0,4},{4,0},{8,12},{12,8},{16,20},{20,16},{24,28},{28,24},{1,5},{5... | collective-permute-start | bytes 1179656 | tf_op jit(solution)/shard_map/ppermute | solution.py:318
  44.9 0.9 value_grad.5.refs_3_.refs_4_.refs_2_
  46.4 1.4 %join_states.7 = (bf16[1072,128]{1,0:T(8,128)(2,1)S(1)}, f32[1072,128]{1,0:T(8,128)}) custom-call(s32[8]{0:T(128)S(1)} %stack.27.refs_0_, f32[1072,128]{1,0:T(8,128)S(1)} %get-tuple-element.84.refs_1_, bf16[1072,128]{1,0:T(8,128)(2,1)S(1)} %collective-permute-done.7.refs_2_.refs_5_, bf16[512,384]{1,0:T(8,128)(2,1)S(1)} %value_grad.5.refs_3_.refs_4_.refs_2_), custom_call_target="tpu_custom_call" | custom-call | flops 20000000000 | tf_op jit(solution)/shard_map/join_states/pallas_call | solution.py:45
  47.8 1.5 %collective-permute-start.8 = (bf16[1072,128]{1,0:T(8,128)(2,1)S(1)}, bf16[1072,128]{1,0:T(8,128)(2,1)S(1)}, u32[]{:S(2)}, u32[]{:S(2)}) collective-permute-start(bf16[1072,128]{1,0:T(8,128)(2,1)S(1)} %get-tuple-element.85.refs_6_), channel_id=1, source_target_pairs={{16,0},{20,4},{24,8},{28,12},{17,1},{21,5},{25,9},{29,13},{18,2},{... | collective-permute-start | bytes 823304 | tf_op jit(solution)/shard_map/ppermute | solution.py:322
  49.3 5.1 %collective-permute-done.10.refs_5_ = bf16[1,2,224,512]{3,2,1,0:T(8,128)(2,1)S(1)} collective-permute-done((bf16[1,2,224,512]{3,2,1,0:T(8,128)(2,1)S(1)}, bf16[1,2,224,512]{3,2,1,0:T(8,128)(2,1)S(1)}, u32[]{:S(2)}, u32[]{:S(2)}) %collective-permute-start.10) | collective-permute-done | bytes 458784 | tf_op jit(solution)/shard_map/ppermute | solution.py:318
  54.4 1.7 %merge_inputs.1 = (bf16[2,2,224,512]{3,2,1,0:T(8,128)(2,1)S(1)}, bf16[2,2,224,512]{3,2,1,0:T(8,128)(2,1)S(1)}, bf16[2,2,224,512]{3,2,1,0:T(8,128)(2,1)S(1)}, bf16[2,2,224,512]{3,2,1,0:T(8,128)(2,1)S(1)}) custom-call(bf16[2,2,224,512]{3,2,1,0:T(8,128)(2,1)} %get-tuple-element.61.refs_3_.refs_0_, ...), custom_call_target="tpu_custom_call" | custom-call | flops 20000000000 | tf_op jit(solution)/shard_map/merge_inputs/pallas_call | solution.py:45
  56.1 2.1 %weight_part.4 = (bf16[4,224,384]{2,1,0:T(8,128)(2,1)S(1)}, f32[4,224,384]{2,1,0:T(8,128)S(1)}) custom-call(bf16[2,2,224,512]{3,2,1,0:T(8,128)(2,1)S(1)} %get-tuple-element.86.refs_0_.refs_6_, bf16[2,2,224,512]{3,2,1,0:T(8,128)(2,1)S(1)} %get-tuple-element.87.refs_1_, bf16[2,2,224,512]{3,2,1,0:T(8,128)(2,1)S(1)} %get-tuple-element.88.refs_2_, ...), custom_call_target="tpu_custom_call" | custom-call | flops 20000000000 | tf_op jit(solution)/shard_map/weight_part/pallas_call | solution.py:45
  58.3 2.1 %collective-permute-done.12.refs_2_ = bf16[4,224,384]{2,1,0:T(8,128)(2,1)S(1)} collective-permute-done((bf16[4,224,384]{2,1,0:T(8,128)(2,1)S(1)}, bf16[4,224,384]{2,1,0:T(8,128)(2,1)S(1)}, u32[]{:S(2)}, u32[]{:S(2)}) %collective-permute-start.12) | collective-permute-done | bytes 688160 | tf_op jit(solution)/shard_map/ppermute | solution.py:318
  60.4 0.7 fold_weight.10
  61.1 2.4 %collective-permute-start.18 = (bf16[2,224,384]{2,1,0:T(8,128)(2,1)S(1)}, bf16[2,224,384]{2,1,0:T(8,128)(2,1)S(1)}, u32[]{:S(2)}, u32[]{:S(2)}) collective-permute-start(bf16[2,224,384]{2,1,0:T(8,128)(2,1)S(1)} %get-tuple-element.92.refs_7_), channel_id=1, source_target_pairs={{0,8},{4,12},{8,0},{12,4},{16,24},{20,28},{24,16},{28,20},{1,9},{5... | collective-permute-start | bytes 1032200 | tf_op jit(solution)/shard_map/ppermute | solution.py:318
  63.5 1.0 value_grad.6.refs_7_.refs_3_.refs_4_
  64.6 1.2 collective-permute-start.17
  65.7 1.9 %value_grad.7.refs_6_.refs_4_ = bf16[512,512]{1,0:T(8,128)(2,1)} custom-call(s32[8]{0:T(128)S(1)} %stack.27.refs_0_, bf16[512,1024]{1,0:T(8,128)(2,1)S(1)} %get-tuple-element.83.refs_1_, f32[512,1024]{1,0:T(8,128)S(1)} %copy-done.14, f32[512,128]{1,0:T(8,128)S(1)} %copy-done.16, bf16[1072,128]{1,0:T(8,128)(2,1)S(1)} %copy-done.12, ...), custom_call_target="tpu_custom_call" | custom-call | flops 20000000000 | tf_op jit(solution)/shard_map/value_grad/pallas_call | solution.py:45
  67.6 0.9 collective-permute-start.13
  68.5 2.1 %weight_part.5 = (bf16[4,224,384]{2,1,0:T(8,128)(2,1)S(1)}, f32[4,224,384]{2,1,0:T(8,128)S(1)}) custom-call(bf16[2,2,224,512]{3,2,1,0:T(8,128)(2,1)S(1)} %get-tuple-element.86.refs_0_.refs_6_, bf16[2,2,224,512]{3,2,1,0:T(8,128)(2,1)S(1)} %get-tuple-element.87.refs_1_, bf16[2,2,224,512]{3,2,1,0:T(8,128)(2,1)S(1)} %get-tuple-element.88.refs_2_, ...), custom_call_target="tpu_custom_call" | custom-call | flops 20000000000 | tf_op jit(solution)/shard_map/weight_part/pallas_call | solution.py:45
  70.7 2.1 %collective-permute-done.15.refs_2_ = bf16[4,224,384]{2,1,0:T(8,128)(2,1)S(1)} collective-permute-done((bf16[4,224,384]{2,1,0:T(8,128)(2,1)S(1)}, bf16[4,224,384]{2,1,0:T(8,128)(2,1)S(1)}, u32[]{:S(2)}, u32[]{:S(2)}) %collective-permute-start.15) | collective-permute-done | bytes 688160 | tf_op jit(solution)/shard_map/ppermute | solution.py:318
  72.8 0.7 fold_weight.11
  74.3 3.3 %collective-permute-start.21 = (bf16[1,224,384]{2,1,0:T(8,128)(2,1)S(1)}, bf16[1,224,384]{2,1,0:T(8,128)(2,1)S(1)}, u32[]{:S(2)}, u32[]{:S(2)}) collective-permute-start(bf16[1,224,384]{2,1,0:T(8,128)(2,1)S(1)} %get-tuple-element.98.refs_6_), channel_id=1, source_target_pairs={{0,16},{4,20},{8,24},{12,28},{16,0},{20,4},{24,8},{28,12},{1,17},{... | collective-permute-start | bytes 516104 | tf_op jit(solution)/shard_map/ppermute | solution.py:318
  77.7 5.8 %input_part.2.refs_6_ = bf16[512,1792]{1,0:T(8,128)(2,1)} custom-call(s32[8]{0:T(128)S(1)} %stack.27.refs_0_, bf16[512,384]{1,0:T(8,128)(2,1)S(1)} %copy-done.7, bf16[512,384]{1,0:T(8,128)(2,1)S(1)} %value_grad.5.refs_3_.refs_4_.refs_2_, bf16[512,512]{1,0:T(8,128)(2,1)S(1)} %value_grad.6.refs_7_.refs_3_.refs_4_, bf16[512,512]{1,0:T(8,128)(2,1)} %value_grad.7.refs_6_.refs_4_, ...), custom_call_target="tpu_custom_call" | custom-call | flops 20000000000 | tf_op jit(solution)/shard_map/input_part/pallas_call | solution.py:45
  83.6 1.4 %collective-permute-start.25 = (bf16[512,1792]{1,0:T(8,128)(2,1)}, bf16[512,1792]{1,0:T(8,128)(2,1)}, u32[]{:S(2)}, u32[]{:S(2)}) collective-permute-start(bf16[512,1792]{1,0:T(8,128)(2,1)} %input_part.2.refs_6_), channel_id=1, source_target_pairs={{0,2},{2,0},{1,3},{3,1},{4,6},{6,4},{5,7},{7,5},{8,10},{10,8},{9,1... | collective-permute-start | bytes 5505032 | tf_op jit(solution)/shard_map/ppermute | solution.py:318
  85.0 2.1 %weight_part.6 = (bf16[4,224,512]{2,1,0:T(8,128)(2,1)S(1)}, f32[4,224,512]{2,1,0:T(8,128)S(1)}) custom-call(bf16[2,2,224,512]{3,2,1,0:T(8,128)(2,1)S(1)} %get-tuple-element.86.refs_0_.refs_6_, bf16[2,2,224,512]{3,2,1,0:T(8,128)(2,1)S(1)} %get-tuple-element.87.refs_1_, bf16[2,2,224,512]{3,2,1,0:T(8,128)(2,1)S(1)} %get-tuple-element.88.refs_2_, ...), custom_call_target="tpu_custom_call" | custom-call | flops 20000000000 | tf_op jit(solution)/shard_map/weight_part/pallas_call | solution.py:45
  87.1 2.4 %collective-permute-done.19.refs_2_ = bf16[4,224,512]{2,1,0:T(8,128)(2,1)S(1)} collective-permute-done((bf16[4,224,512]{2,1,0:T(8,128)(2,1)S(1)}, bf16[4,224,512]{2,1,0:T(8,128)(2,1)S(1)}, u32[]{:S(2)}, u32[]{:S(2)}) %collective-permute-start.19) | collective-permute-done | bytes 917536 | tf_op jit(solution)/shard_map/ppermute | solution.py:318
  89.6 0.7 fold_weight.13
  90.3 1.9 %collective-permute-start.24 = (bf16[2,224,512]{2,1,0:T(8,128)(2,1)S(1)}, bf16[2,224,512]{2,1,0:T(8,128)(2,1)S(1)}, u32[]{:S(2)}, u32[]{:S(2)}) collective-permute-start(bf16[2,224,512]{2,1,0:T(8,128)(2,1)S(1)} %get-tuple-element.101.refs_3_), channel_id=1, source_target_pairs={{0,8},{4,12},{8,0},{12,4},{16,24},{20,28},{24,16},{28,20},{1,9},{5... | collective-permute-start | bytes 1376264 | tf_op jit(solution)/shard_map/ppermute | solution.py:318
  92.2 1.3 fold_weight.14
  93.5 1.7 %collective-permute-start.26 = (bf16[1,224,384]{2,1,0:T(8,128)(2,1)}, bf16[1,224,384]{2,1,0:T(8,128)(2,1)}, u32[]{:S(2)}, u32[]{:S(2)}) collective-permute-start(bf16[1,224,384]{2,1,0:T(8,128)(2,1)} %get-tuple-element.102.refs_6_), channel_id=1, source_target_pairs={{0,16},{4,20},{8,24},{12,28},{16,0},{20,4},{24,8},{28,12},{1,17},{... | collective-permute-start | bytes 516104 | tf_op jit(solution)/shard_map/ppermute | solution.py:318
  95.2 3.3 %weight_part.7 = (bf16[4,224,512]{2,1,0:T(8,128)(2,1)S(1)}, f32[4,224,512]{2,1,0:T(8,128)S(1)}) custom-call(bf16[2,2,224,512]{3,2,1,0:T(8,128)(2,1)S(1)} %get-tuple-element.86.refs_0_.refs_6_, bf16[2,2,224,512]{3,2,1,0:T(8,128)(2,1)S(1)} %get-tuple-element.87.refs_1_, bf16[2,2,224,512]{3,2,1,0:T(8,128)(2,1)S(1)} %get-tuple-element.88.refs_2_, ...), custom_call_target="tpu_custom_call" | custom-call | flops 20000000000 | tf_op jit(solution)/shard_map/weight_part/pallas_call | solution.py:45
  98.6 2.4 %collective-permute-done.20.refs_2_ = bf16[4,224,512]{2,1,0:T(8,128)(2,1)S(1)} collective-permute-done((bf16[4,224,512]{2,1,0:T(8,128)(2,1)S(1)}, bf16[4,224,512]{2,1,0:T(8,128)(2,1)S(1)}, u32[]{:S(2)}, u32[]{:S(2)}) %collective-permute-start.20) | collective-permute-done | bytes 917536 | tf_op jit(solution)/shard_map/ppermute | solution.py:318
  101.0 0.6 fold_weight.15
  101.7 1.8 %collective-permute-start.23 = (bf16[2,224,256]{2,1,0:T(8,128)(2,1)S(1)}, bf16[2,224,256]{2,1,0:T(8,128)(2,1)S(1)}, u32[]{:S(2)}, u32[]{:S(2)}) collective-permute-start(bf16[2,224,256]{2,1,0:T(8,128)(2,1)S(1)} %get-tuple-element.105.refs_3_), channel_id=1, source_target_pairs={{0,8},{4,12},{8,0},{12,4},{16,24},{20,28},{24,16},{28,20},{1,9},{5... | collective-permute-start | bytes 688136 | tf_op jit(solution)/shard_map/ppermute | solution.py:318
  103.4 0.7 fold_weight.16
  104.5 2.9 %collective-permute-done.24.refs_2_ = bf16[2,224,512]{2,1,0:T(8,128)(2,1)S(1)} collective-permute-done((bf16[2,224,512]{2,1,0:T(8,128)(2,1)S(1)}, bf16[2,224,512]{2,1,0:T(8,128)(2,1)S(1)}, u32[]{:S(2)}, u32[]{:S(2)}) %collective-permute-start.24) | collective-permute-done | bytes 458784 | tf_op jit(solution)/shard_map/ppermute | solution.py:318
  107.4 0.7 fold_weight.17
  108.0 1.2 collective-permute-start.27
  109.2 8.0 %collective-permute-done.23.refs_2_ = bf16[2,224,256]{2,1,0:T(8,128)(2,1)S(1)} collective-permute-done((bf16[2,224,256]{2,1,0:T(8,128)(2,1)S(1)}, bf16[2,224,256]{2,1,0:T(8,128)(2,1)S(1)}, u32[]{:S(2)}, u32[]{:S(2)}) %collective-permute-start.23) | collective-permute-done | bytes 229408 | tf_op jit(solution)/shard_map/ppermute | solution.py:318
  117.8 1.2 collective-permute-start.28
  119.0 2.6 %collective-permute-done.22.refs_2_ = bf16[2,224,256]{2,1,0:T(8,128)(2,1)S(1)} collective-permute-done((bf16[2,224,256]{2,1,0:T(8,128)(2,1)S(1)}, bf16[2,224,256]{2,1,0:T(8,128)(2,1)S(1)}, u32[]{:S(2)}, u32[]{:S(2)}) %collective-permute-start.22) | collective-permute-done | bytes 229408 | tf_op jit(solution)/shard_map/ppermute | solution.py:318
  122.2 1.0 collective-permute-start.29
  123.3 4.6 %input_part.3.refs_0_.refs_2_ = f32[512,1792]{1,0:T(8,128)S(1)} custom-call(s32[8]{0:T(128)S(1)} %stack.27.refs_0_, bf16[512,384]{1,0:T(8,128)(2,1)S(1)} %copy-done.8, bf16[512,384]{1,0:T(8,128)(2,1)S(1)} %copy-done.10, bf16[512,512]{1,0:T(8,128)(2,1)S(1)} %copy-done.5, bf16[512,512]{1,0:T(8,128)(2,1)} %value_grad.7.refs_6_.refs_4_, ...), custom_call_target="tpu_custom_call" | custom-call | flops 20000000000 | tf_op jit(solution)/shard_map/input_part/pallas_call | solution.py:45
  127.9 3.2 %grad_input.1 = (bf16[512,1792]{1,0:T(8,128)(2,1)}, f32[8,128]{1,0:T(8,128)S(1)}) custom-call(f32[512,1792]{1,0:T(8,128)S(1)} %input_part.3.refs_0_.refs_2_, bf16[512,1792]{1,0:T(8,128)(2,1)} %collective-permute-done.25.refs_1_, f32[512,1792]{1,0:T(8,128)S(1)} %input_part.3.refs_0_.refs_2_), custom_call_target="tpu_custom_call" | custom-call | flops 20000000000 | tf_op jit(solution)/shard_map/grad_input/pallas_call | solution.py:45
  131.1 2.8 %collective-permute-done.29.refs_9_ = bf16[1,224,256]{2,1,0:T(8,128)(2,1)S(1)} collective-permute-done((bf16[1,224,256]{2,1,0:T(8,128)(2,1)S(1)}, bf16[1,224,256]{2,1,0:T(8,128)(2,1)S(1)}, u32[]{:S(2)}, u32[]{:S(2)}) %collective-permute-start.29) | collective-permute-done | bytes 114720 | tf_op jit(solution)/shard_map/ppermute | solution.py:318
  133.9 2.3 %grad_weight.1 = f32[224,1792]{1,0:T(8,128)} custom-call(f32[1,224,384]{2,1,0:T(8,128)S(1)} %get-tuple-element.114.refs_0_, bf16[1,224,384]{2,1,0:T(8,128)(2,1)S(1)} %collective-permute-done.21.refs_1_, f32[1,224,384]{2,1,0:T(8,128)S(1)} %get-tuple-element.115.refs_2_, bf16[1,224,384]{2,1,0:T(8,128)(2,1)} %collective-permute-done.26.refs_3_, ...), custom_call_target="tpu_custom_call" | custom-call | flops 20000000000 | tf_op jit(solution)/shard_map/grad_weight/pallas_call | solution.py:45
  (90 shorter events, 4.8 us)
Async XLA Ops:
  0.8 1.5 %copy-start.2 = (bf16[1,512,1792]{2,1,0:T(8,128)(2,1)S(1)}, bf16[1,512,1792]{2,1,0:T(8,128)(2,1)}, u32[]{:S(2)}) copy-start(bf16[1,512,1792]{2,1,0:T(8,128)(2,1)} %param.6) | copy-start | bytes 5505028
  2.3 5.1 %copy-start.17 = (f32[1,14,512]{2,0,1:T(1,128)S(1)}, f32[1,14,512]{2,0,1:T(1,128)}, u32[]{:S(2)}) copy-start(f32[1,14,512]{2,0,1:T(1,128)} %param.11) | copy-start | bytes 86020
  2.3 5.1 %copy-start = (s32[1,512,1792]{2,1,0:T(8,128)S(1)}, s32[1,512,1792]{2,1,0:T(8,128)}, u32[]{:S(2)}) copy-start(s32[1,512,1792]{2,1,0:T(8,128)} %param.9) | copy-start | bytes 11010052
  2.3 5.1 %copy-start.3 = (bf16[1,512,1792]{2,1,0:T(8,128)(2,1)S(1)}, bf16[1,512,1792]{2,1,0:T(8,128)(2,1)}, u32[]{:S(2)}) copy-start(bf16[1,512,1792]{2,1,0:T(8,128)(2,1)} %param.8) | copy-start | bytes 5505028
  4.4 37.9 %collective-permute-start.6 = (bf16[2,2,224,512]{3,2,1,0:T(8,128)(2,1)}, bf16[2,2,224,512]{3,2,1,0:T(8,128)(2,1)}, u32[]{:S(2)}, u32[]{:S(2)}) collective-permute-start(bf16[2,2,224,512]{3,2,1,0:T(8,128)(2,1)} %get-tuple-element.61.refs_3_.refs_0_), channel_id=1, source_target_pairs={{0,2},{2,0},{1,3},{3,1},{4,6},{6,4},{5,7},{7,5},{8,10},{10,8},{9,1... | collective-permute-start | bytes 2752520 | tf_op jit(solution)/shard_map/ppermute | solution.py:318
  8.9 8.0 %collective-permute-start.1 = (bf16[816,128]{1,0:T(8,128)(2,1)S(1)}, bf16[816,128]{1,0:T(8,128)(2,1)S(1)}, u32[]{:S(2)}, u32[]{:S(2)}) collective-permute-start(bf16[816,128]{1,0:T(8,128)(2,1)S(1)} %get-tuple-element.65.refs_3_), channel_id=1, source_target_pairs={{0,4},{4,0},{8,12},{12,8},{16,20},{20,16},{24,28},{28,24},{1,5},{5... | collective-permute-start | bytes 626696 | tf_op jit(solution)/shard_map/ppermute | solution.py:318
  12.2 19.0 %copy-start.15 = (f32[512,128]{1,0:T(8,128)}, f32[512,128]{1,0:T(8,128)S(1)}, u32[]{:S(2)}) copy-start(f32[512,128]{1,0:T(8,128)S(1)} %get-tuple-element.81.refs_4_.refs_3_) | copy-start | bytes 786436
  12.3 10.5 %collective-permute-start = (bf16[1072,128]{1,0:T(8,128)(2,1)S(1)}, bf16[1072,128]{1,0:T(8,128)(2,1)S(1)}, u32[]{:S(2)}, u32[]{:S(2)}) collective-permute-start(bf16[1072,128]{1,0:T(8,128)(2,1)S(1)} %get-tuple-element.67.refs_3_), channel_id=1, source_target_pairs={{0,4},{4,0},{8,12},{12,8},{16,20},{20,16},{24,28},{28,24},{1,5},{5... | collective-permute-start | bytes 823304 | tf_op jit(solution)/shard_map/ppermute | solution.py:318
  17.5 11.1 %collective-permute-start.2 = (bf16[816,128]{1,0:T(8,128)(2,1)S(1)}, bf16[816,128]{1,0:T(8,128)(2,1)S(1)}, u32[]{:S(2)}, u32[]{:S(2)}) collective-permute-start(bf16[816,128]{1,0:T(8,128)(2,1)S(1)} %get-tuple-element.69.refs_3_), channel_id=1, source_target_pairs={{8,0},{12,4},{16,8},{20,12},{24,16},{28,20},{9,1},{13,5},{17,9},{2... | collective-permute-start | bytes 626696 | tf_op jit(solution)/shard_map/ppermute | solution.py:322
  18.8 15.0 %collective-permute-start.5 = (bf16[1,2,224,512]{3,2,1,0:T(8,128)(2,1)S(1)}, bf16[1,2,224,512]{3,2,1,0:T(8,128)(2,1)S(1)}, u32[]{:S(2)}, u32[]{:S(2)}) collective-permute-start(bf16[1,2,224,512]{3,2,1,0:T(8,128)(2,1)S(1)} %get-tuple-element.78.refs_4_), channel_id=1, source_target_pairs={{0,4},{4,0},{8,12},{12,8},{16,20},{20,16},{24,28},{28,24},{1,5},{5... | collective-permute-start | bytes 1376264 | tf_op jit(solution)/shard_map/ppermute | solution.py:318
  22.8 0.7 copy-start.11
  22.8 3.9 %copy-start.1 = (s32[1,512,1792]{2,1,0:T(8,128)S(1)}, s32[1,512,1792]{2,1,0:T(8,128)}, u32[]{:S(2)}) copy-start(s32[1,512,1792]{2,1,0:T(8,128)} %param.10) | copy-start | bytes 11010052
  23.5 22.9 %collective-permute-start.7 = (bf16[1072,128]{1,0:T(8,128)(2,1)S(1)}, bf16[1072,128]{1,0:T(8,128)(2,1)S(1)}, u32[]{:S(2)}, u32[]{:S(2)}) collective-permute-start(bf16[1072,128]{1,0:T(8,128)(2,1)S(1)} %get-tuple-element.71.refs_5_), channel_id=1, source_target_pairs={{8,0},{12,4},{16,8},{20,12},{24,16},{28,20},{9,1},{13,5},{17,9},{2... | collective-permute-start | bytes 823304 | tf_op jit(solution)/shard_map/ppermute | solution.py:322
  24.9 16.2 %collective-permute-start.4 = (bf16[1,2,224,512]{3,2,1,0:T(8,128)(2,1)S(1)}, bf16[1,2,224,512]{3,2,1,0:T(8,128)(2,1)S(1)}, u32[]{:S(2)}, u32[]{:S(2)}) collective-permute-start(bf16[1,2,224,512]{3,2,1,0:T(8,128)(2,1)S(1)} %get-tuple-element.77.refs_6_), channel_id=1, source_target_pairs={{0,4},{4,0},{8,12},{12,8},{16,20},{20,16},{24,28},{28,24},{1,5},{5... | collective-permute-start | bytes 1376264 | tf_op jit(solution)/shard_map/ppermute | solution.py:318
  30.0 12.3 %collective-permute-start.3 = (bf16[816,128]{1,0:T(8,128)(2,1)S(1)}, bf16[816,128]{1,0:T(8,128)(2,1)S(1)}, u32[]{:S(2)}, u32[]{:S(2)}) collective-permute-start(bf16[816,128]{1,0:T(8,128)(2,1)S(1)} %get-tuple-element.76.refs_5_), channel_id=1, source_target_pairs={{16,0},{20,4},{24,8},{28,12},{17,1},{21,5},{25,9},{29,13},{18,2},{... | collective-permute-start | bytes 626696 | tf_op jit(solution)/shard_map/ppermute | solution.py:322
  33.8 1.4 %copy-start.13 = (f32[512,1024]{1,0:T(8,128)}, f32[512,1024]{1,0:T(8,128)S(1)}, u32[]{:S(2)}) copy-start(f32[512,1024]{1,0:T(8,128)S(1)} %get-tuple-element.82.refs_1_.refs_2_) | copy-start | bytes 6291460
  35.1 14.2 %collective-permute-start.9 = (bf16[1,2,224,512]{3,2,1,0:T(8,128)(2,1)S(1)}, bf16[1,2,224,512]{3,2,1,0:T(8,128)(2,1)S(1)}, u32[]{:S(2)}, u32[]{:S(2)}) collective-permute-start(bf16[1,2,224,512]{3,2,1,0:T(8,128)(2,1)S(1)} %pass_on.2.refs_1_.refs_2_), channel_id=1, source_target_pairs={{0,2},{2,0},{1,3},{3,1},{4,6},{6,4},{5,7},{7,5},{8,10},{10,8},{9,1... | collective-permute-start | bytes 1376264 | tf_op jit(solution)/shard_map/ppermute | solution.py:318
  41.2 13.2 %collective-permute-start.10 = (bf16[1,2,224,512]{3,2,1,0:T(8,128)(2,1)S(1)}, bf16[1,2,224,512]{3,2,1,0:T(8,128)(2,1)S(1)}, u32[]{:S(2)}, u32[]{:S(2)}) collective-permute-start(bf16[1,2,224,512]{3,2,1,0:T(8,128)(2,1)S(1)} %pass_on.3.refs_7_.refs_3_), channel_id=1, source_target_pairs={{0,2},{2,0},{1,3},{3,1},{4,6},{6,4},{5,7},{7,5},{8,10},{10,8},{9,1... | collective-permute-start | bytes 1376264 | tf_op jit(solution)/shard_map/ppermute | solution.py:318
  43.3 12.8 %copy-start.6 = (bf16[512,384]{1,0:T(8,128)(2,1)}, bf16[512,384]{1,0:T(8,128)(2,1)S(1)}, u32[]{:S(2)}) copy-start(bf16[512,384]{1,0:T(8,128)(2,1)S(1)} %value_grad.4.refs_7_.refs_4_.refs_1_) | copy-start | bytes 1179652
  43.3 12.8 %collective-permute-start.11 = (bf16[512,384]{1,0:T(8,128)(2,1)S(1)}, bf16[512,384]{1,0:T(8,128)(2,1)S(1)}, u32[]{:S(2)}, u32[]{:S(2)}) collective-permute-start(bf16[512,384]{1,0:T(8,128)(2,1)S(1)} %value_grad.4.refs_7_.refs_4_.refs_1_), channel_id=1, source_target_pairs={{0,4},{4,0},{8,12},{12,8},{16,20},{20,16},{24,28},{28,24},{1,5},{5... | collective-permute-start | bytes 1179656 | tf_op jit(solution)/shard_map/ppermute | solution.py:318
  45.8 31.8 %copy-start.9 = (bf16[512,384]{1,0:T(8,128)(2,1)}, bf16[512,384]{1,0:T(8,128)(2,1)S(1)}, u32[]{:S(2)}) copy-start(bf16[512,384]{1,0:T(8,128)(2,1)S(1)} %value_grad.5.refs_3_.refs_4_.refs_2_) | copy-start | bytes 1179652
  45.8 22.7 %collective-permute-start.14 = (bf16[512,384]{1,0:T(8,128)(2,1)S(1)}, bf16[512,384]{1,0:T(8,128)(2,1)S(1)}, u32[]{:S(2)}, u32[]{:S(2)}) collective-permute-start(bf16[512,384]{1,0:T(8,128)(2,1)S(1)} %value_grad.5.refs_3_.refs_4_.refs_2_), channel_id=1, source_target_pairs={{0,4},{4,0},{8,12},{12,8},{16,20},{20,16},{24,28},{28,24},{1,5},{5... | collective-permute-start | bytes 1179656 | tf_op jit(solution)/shard_map/ppermute | solution.py:318
  47.8 15.6 %collective-permute-start.8 = (bf16[1072,128]{1,0:T(8,128)(2,1)S(1)}, bf16[1072,128]{1,0:T(8,128)(2,1)S(1)}, u32[]{:S(2)}, u32[]{:S(2)}) collective-permute-start(bf16[1072,128]{1,0:T(8,128)(2,1)S(1)} %get-tuple-element.85.refs_6_), channel_id=1, source_target_pairs={{16,0},{20,4},{24,8},{28,12},{17,1},{21,5},{25,9},{29,13},{18,2},{... | collective-permute-start | bytes 823304 | tf_op jit(solution)/shard_map/ppermute | solution.py:322
  58.2 2.2 %collective-permute-start.12 = (bf16[4,224,384]{2,1,0:T(8,128)(2,1)S(1)}, bf16[4,224,384]{2,1,0:T(8,128)(2,1)S(1)}, u32[]{:S(2)}, u32[]{:S(2)}) collective-permute-start(bf16[4,224,384]{2,1,0:T(8,128)(2,1)S(1)} %get-tuple-element.91), channel_id=1, source_target_pairs={{0,1},{1,0},{2,3},{3,2},{4,5},{5,4},{6,7},{7,6},{8,9},{9,8},{10,11... | collective-permute-start | bytes 2064392 | tf_op jit(solution)/shard_map/ppermute | solution.py:318
  58.3 5.2 %copy-start.12 = (bf16[1072,128]{1,0:T(8,128)(2,1)S(1)}, bf16[1072,128]{1,0:T(8,128)(2,1)}, u32[]{:S(2)}) copy-start(bf16[1072,128]{1,0:T(8,128)(2,1)} %copy-done.11) | copy-start | bytes 823300
  58.3 5.2 %copy-start.14 = (f32[512,1024]{1,0:T(8,128)S(1)}, f32[512,1024]{1,0:T(8,128)}, u32[]{:S(2)}) copy-start(f32[512,1024]{1,0:T(8,128)} %copy-done.13) | copy-start | bytes 6291460
  58.3 5.2 %copy-start.16 = (f32[512,128]{1,0:T(8,128)S(1)}, f32[512,128]{1,0:T(8,128)}, u32[]{:S(2)}) copy-start(f32[512,128]{1,0:T(8,128)} %copy-done.15) | copy-start | bytes 786436
  61.1 12.6 %collective-permute-start.18 = (bf16[2,224,384]{2,1,0:T(8,128)(2,1)S(1)}, bf16[2,224,384]{2,1,0:T(8,128)(2,1)S(1)}, u32[]{:S(2)}, u32[]{:S(2)}) collective-permute-start(bf16[2,224,384]{2,1,0:T(8,128)(2,1)S(1)} %get-tuple-element.92.refs_7_), channel_id=1, source_target_pairs={{0,8},{4,12},{8,0},{12,4},{16,24},{20,28},{24,16},{28,20},{1,9},{5... | collective-permute-start | bytes 1032200 | tf_op jit(solution)/shard_map/ppermute | solution.py:318
  64.5 20.4 %copy-start.4 = (bf16[512,512]{1,0:T(8,128)(2,1)}, bf16[512,512]{1,0:T(8,128)(2,1)S(1)}, u32[]{:S(2)}) copy-start(bf16[512,512]{1,0:T(8,128)(2,1)S(1)} %value_grad.6.refs_7_.refs_3_.refs_4_) | copy-start | bytes 1572868
  64.6 20.4 %collective-permute-start.17 = (bf16[512,512]{1,0:T(8,128)(2,1)S(1)}, bf16[512,512]{1,0:T(8,128)(2,1)S(1)}, u32[]{:S(2)}, u32[]{:S(2)}) collective-permute-start(bf16[512,512]{1,0:T(8,128)(2,1)S(1)} %value_grad.6.refs_7_.refs_3_.refs_4_), channel_id=1, source_target_pairs={{0,4},{4,0},{8,12},{12,8},{16,20},{20,16},{24,28},{28,24},{1,5},{5... | collective-permute-start | bytes 1572872 | tf_op jit(solution)/shard_map/ppermute | solution.py:318
  67.6 27.6 %collective-permute-start.13 = (bf16[512,512]{1,0:T(8,128)(2,1)}, bf16[512,512]{1,0:T(8,128)(2,1)}, u32[]{:S(2)}, u32[]{:S(2)}) collective-permute-start(bf16[512,512]{1,0:T(8,128)(2,1)} %value_grad.7.refs_6_.refs_4_), channel_id=1, source_target_pairs={{0,4},{4,0},{8,12},{12,8},{16,20},{20,16},{24,28},{28,24},{1,5},{5... | collective-permute-start | bytes 1572872 | tf_op jit(solution)/shard_map/ppermute | solution.py:318
  70.6 2.2 %collective-permute-start.15 = (bf16[4,224,384]{2,1,0:T(8,128)(2,1)S(1)}, bf16[4,224,384]{2,1,0:T(8,128)(2,1)S(1)}, u32[]{:S(2)}, u32[]{:S(2)}) collective-permute-start(bf16[4,224,384]{2,1,0:T(8,128)(2,1)S(1)} %get-tuple-element.94), channel_id=1, source_target_pairs={{0,1},{1,0},{2,3},{3,2},{4,5},{5,4},{6,7},{7,6},{8,9},{9,8},{10,11... | collective-permute-start | bytes 2064392 | tf_op jit(solution)/shard_map/ppermute | solution.py:318
  72.8 4.8 %slice-start = ((s8[12845056]{0:T(1024)(128)(4,1)}), s8[262144]{0:T(1024)(128)(4,1)S(1)}, s32[]{:S(2)}) async-start(s8[12845056]{0:T(1024)(128)(4,1)} %bitcast.16), calls=%async_computation | async-start | bytes 524288
  72.8 4.8 %slice-start.1 = ((s8[12845056]{0:T(1024)(128)(4,1)}), s8[4194304]{0:T(1024)(128)(4,1)S(1)}, s32[]{:S(2)}) async-start(s8[12845056]{0:T(1024)(128)(4,1)} %bitcast.16), calls=%async_computation.1 | async-start | bytes 8388608
  73.5 4.1 %slice-start.2 = ((s8[12845056]{0:T(1024)(128)(4,1)}), s8[4194304]{0:T(1024)(128)(4,1)S(1)}, s32[]{:S(2)}) async-start(s8[12845056]{0:T(1024)(128)(4,1)} %bitcast.16), calls=%async_computation.2 | async-start | bytes 8388608
  73.5 18.7 %collective-permute-start.16 = (bf16[2,224,384]{2,1,0:T(8,128)(2,1)S(1)}, bf16[2,224,384]{2,1,0:T(8,128)(2,1)S(1)}, u32[]{:S(2)}, u32[]{:S(2)}) collective-permute-start(bf16[2,224,384]{2,1,0:T(8,128)(2,1)S(1)} %get-tuple-element.96.refs_3_), channel_id=1, source_target_pairs={{0,8},{4,12},{8,0},{12,4},{16,24},{20,28},{24,16},{28,20},{1,9},{5... | collective-permute-start | bytes 1032200 | tf_op jit(solution)/shard_map/ppermute | solution.py:318
  73.6 4.1 %slice-start.3 = ((s8[12845056]{0:T(1024)(128)(4,1)}), s8[4194304]{0:T(1024)(128)(4,1)S(1)}, s32[]{:S(2)}) async-start(s8[12845056]{0:T(1024)(128)(4,1)} %bitcast.16), calls=%async_computation.3 | async-start | bytes 8388608
  73.6 4.1 %copy-start.7 = (bf16[512,384]{1,0:T(8,128)(2,1)S(1)}, bf16[512,384]{1,0:T(8,128)(2,1)}, u32[]{:S(2)}) copy-start(bf16[512,384]{1,0:T(8,128)(2,1)} %copy-done.6) | copy-start | bytes 1179652
  74.3 24.3 %collective-permute-start.21 = (bf16[1,224,384]{2,1,0:T(8,128)(2,1)S(1)}, bf16[1,224,384]{2,1,0:T(8,128)(2,1)S(1)}, u32[]{:S(2)}, u32[]{:S(2)}) collective-permute-start(bf16[1,224,384]{2,1,0:T(8,128)(2,1)S(1)} %get-tuple-element.98.refs_6_), channel_id=1, source_target_pairs={{0,16},{4,20},{8,24},{12,28},{16,0},{20,4},{24,8},{28,12},{1,17},{... | collective-permute-start | bytes 516104 | tf_op jit(solution)/shard_map/ppermute | solution.py:318
  83.6 44.3 %collective-permute-start.25 = (bf16[512,1792]{1,0:T(8,128)(2,1)}, bf16[512,1792]{1,0:T(8,128)(2,1)}, u32[]{:S(2)}, u32[]{:S(2)}) collective-permute-start(bf16[512,1792]{1,0:T(8,128)(2,1)} %input_part.2.refs_6_), channel_id=1, source_target_pairs={{0,2},{2,0},{1,3},{3,1},{4,6},{6,4},{5,7},{7,5},{8,10},{10,8},{9,1... | collective-permute-start | bytes 5505032 | tf_op jit(solution)/shard_map/ppermute | solution.py:318
  87.0 2.5 %collective-permute-start.19 = (bf16[4,224,512]{2,1,0:T(8,128)(2,1)S(1)}, bf16[4,224,512]{2,1,0:T(8,128)(2,1)S(1)}, u32[]{:S(2)}, u32[]{:S(2)}) collective-permute-start(bf16[4,224,512]{2,1,0:T(8,128)(2,1)S(1)} %get-tuple-element.100), channel_id=1, source_target_pairs={{0,1},{1,0},{2,3},{3,2},{4,5},{5,4},{6,7},{7,6},{8,9},{9,8},{10,11... | collective-permute-start | bytes 2752520 | tf_op jit(solution)/shard_map/ppermute | solution.py:318
  90.3 17.1 %collective-permute-start.24 = (bf16[2,224,512]{2,1,0:T(8,128)(2,1)S(1)}, bf16[2,224,512]{2,1,0:T(8,128)(2,1)S(1)}, u32[]{:S(2)}, u32[]{:S(2)}) collective-permute-start(bf16[2,224,512]{2,1,0:T(8,128)(2,1)S(1)} %get-tuple-element.101.refs_3_), channel_id=1, source_target_pairs={{0,8},{4,12},{8,0},{12,4},{16,24},{20,28},{24,16},{28,20},{1,9},{5... | collective-permute-start | bytes 1376264 | tf_op jit(solution)/shard_map/ppermute | solution.py:318
  93.5 37.6 %collective-permute-start.26 = (bf16[1,224,384]{2,1,0:T(8,128)(2,1)}, bf16[1,224,384]{2,1,0:T(8,128)(2,1)}, u32[]{:S(2)}, u32[]{:S(2)}) collective-permute-start(bf16[1,224,384]{2,1,0:T(8,128)(2,1)} %get-tuple-element.102.refs_6_), channel_id=1, source_target_pairs={{0,16},{4,20},{8,24},{12,28},{16,0},{20,4},{24,8},{28,12},{1,17},{... | collective-permute-start | bytes 516104 | tf_op jit(solution)/shard_map/ppermute | solution.py:318
  98.5 2.5 %collective-permute-start.20 = (bf16[4,224,512]{2,1,0:T(8,128)(2,1)S(1)}, bf16[4,224,512]{2,1,0:T(8,128)(2,1)S(1)}, u32[]{:S(2)}, u32[]{:S(2)}) collective-permute-start(bf16[4,224,512]{2,1,0:T(8,128)(2,1)S(1)} %get-tuple-element.104), channel_id=1, source_target_pairs={{0,1},{1,0},{2,3},{3,2},{4,5},{5,4},{6,7},{7,6},{8,9},{9,8},{10,11... | collective-permute-start | bytes 2752520 | tf_op jit(solution)/shard_map/ppermute | solution.py:318
  101.7 15.6 %collective-permute-start.23 = (bf16[2,224,256]{2,1,0:T(8,128)(2,1)S(1)}, bf16[2,224,256]{2,1,0:T(8,128)(2,1)S(1)}, u32[]{:S(2)}, u32[]{:S(2)}) collective-permute-start(bf16[2,224,256]{2,1,0:T(8,128)(2,1)S(1)} %get-tuple-element.105.refs_3_), channel_id=1, source_target_pairs={{0,8},{4,12},{8,0},{12,4},{16,24},{20,28},{24,16},{28,20},{1,9},{5... | collective-permute-start | bytes 688136 | tf_op jit(solution)/shard_map/ppermute | solution.py:318
  104.1 17.5 %collective-permute-start.22 = (bf16[2,224,256]{2,1,0:T(8,128)(2,1)S(1)}, bf16[2,224,256]{2,1,0:T(8,128)(2,1)S(1)}, u32[]{:S(2)}, u32[]{:S(2)}) collective-permute-start(bf16[2,224,256]{2,1,0:T(8,128)(2,1)S(1)} %get-tuple-element.107.refs_3_), channel_id=1, source_target_pairs={{0,8},{4,12},{8,0},{12,4},{16,24},{20,28},{24,16},{28,20},{1,9},{5... | collective-permute-start | bytes 688136 | tf_op jit(solution)/shard_map/ppermute | solution.py:318
  108.0 23.0 %collective-permute-start.27 = (bf16[1,224,512]{2,1,0:T(8,128)(2,1)S(1)}, bf16[1,224,512]{2,1,0:T(8,128)(2,1)S(1)}, u32[]{:S(2)}, u32[]{:S(2)}) collective-permute-start(bf16[1,224,512]{2,1,0:T(8,128)(2,1)S(1)} %get-tuple-element.110.refs_3_), channel_id=1, source_target_pairs={{0,16},{4,20},{8,24},{12,28},{16,0},{20,4},{24,8},{28,12},{1,17},{... | collective-permute-start | bytes 688136 | tf_op jit(solution)/shard_map/ppermute | solution.py:318
  117.2 6.0 %slice-start.4 = ((s8[12845056]{0:T(1024)(128)(4,1)}), s8[4194304]{0:T(1024)(128)(4,1)S(1)}, s32[]{:S(2)}) async-start(s8[12845056]{0:T(1024)(128)(4,1)} %bitcast.18), calls=%async_computation.4 | async-start | bytes 8388608
  117.2 6.0 %slice-start.5 = ((s8[12845056]{0:T(1024)(128)(4,1)}), s8[4194304]{0:T(1024)(128)(4,1)S(1)}, s32[]{:S(2)}) async-start(s8[12845056]{0:T(1024)(128)(4,1)} %bitcast.18), calls=%async_computation.5 | async-start | bytes 8388608
  117.8 5.4 %slice-start.6 = ((s8[12845056]{0:T(1024)(128)(4,1)}), s8[4194304]{0:T(1024)(128)(4,1)S(1)}, s32[]{:S(2)}) async-start(s8[12845056]{0:T(1024)(128)(4,1)} %bitcast.18), calls=%async_computation.6 | async-start | bytes 8388608
  117.8 16.0 %collective-permute-start.28 = (bf16[1,224,256]{2,1,0:T(8,128)(2,1)S(1)}, bf16[1,224,256]{2,1,0:T(8,128)(2,1)S(1)}, u32[]{:S(2)}, u32[]{:S(2)}) collective-permute-start(bf16[1,224,256]{2,1,0:T(8,128)(2,1)S(1)} %get-tuple-element.111.refs_3_), channel_id=1, source_target_pairs={{0,16},{4,20},{8,24},{12,28},{16,0},{20,4},{24,8},{28,12},{1,17},{... | collective-permute-start | bytes 344072 | tf_op jit(solution)/shard_map/ppermute | solution.py:318
  121.6 1.7 %slice-start.7 = ((s8[12845056]{0:T(1024)(128)(4,1)}), s8[262144]{0:T(1024)(128)(4,1)S(1)}, s32[]{:S(2)}) async-start(s8[12845056]{0:T(1024)(128)(4,1)} %bitcast.18), calls=%async_computation.7 | async-start | bytes 524288
  121.6 1.7 %copy-start.5 = (bf16[512,512]{1,0:T(8,128)(2,1)S(1)}, bf16[512,512]{1,0:T(8,128)(2,1)}, u32[]{:S(2)}) copy-start(bf16[512,512]{1,0:T(8,128)(2,1)} %copy-done.4) | copy-start | bytes 1572868
  121.6 1.7 %copy-start.8 = (bf16[512,384]{1,0:T(8,128)(2,1)S(1)}, bf16[512,384]{1,0:T(8,128)(2,1)}, u32[]{:S(2)}) copy-start(bf16[512,384]{1,0:T(8,128)(2,1)} %copy-done.6) | copy-start | bytes 1179652
  121.6 1.7 %copy-start.10 = (bf16[512,384]{1,0:T(8,128)(2,1)S(1)}, bf16[512,384]{1,0:T(8,128)(2,1)}, u32[]{:S(2)}) copy-start(bf16[512,384]{1,0:T(8,128)(2,1)} %copy-done.9) | copy-start | bytes 1179652
  122.2 11.7 %collective-permute-start.29 = (bf16[1,224,256]{2,1,0:T(8,128)(2,1)S(1)}, bf16[1,224,256]{2,1,0:T(8,128)(2,1)S(1)}, u32[]{:S(2)}, u32[]{:S(2)}) collective-permute-start(bf16[1,224,256]{2,1,0:T(8,128)(2,1)S(1)} %get-tuple-element.112.refs_6_), channel_id=1, source_target_pairs={{0,16},{4,20},{8,24},{12,28},{16,0},{20,4},{24,8},{28,12},{1,17},{... | collective-permute-start | bytes 344072 | tf_op jit(solution)/shard_map/ppermute | solution.py:318

commit v4 on v3

--- a/solution.py
+++ b/solution.py
@@ -110,8 +110,10 @@
     return line(kernel, "transpose_inputs", outs, [at], [a], (), scratch)
 
 
-def state_kernel(first, heads, ld_ref, q_ref, c_ref, pay_ref, own_ref, cum_ref, cumt_ref, qbf_ref):
+def state_kernel(first, heads, flags_ref, ld_ref, q_ref, c_ref, pay_ref, own_ref, cum_ref, cumt_ref, qbf_ref):
     tokens = ld_ref.shape[1]
+    half = (heads + 1) // 2
+    y = flags_ref[0]
     x = ld_ref[first : first + heads, :]
     x = jnp.concatenate([x, jnp.zeros((PLANE - heads, tokens), F32)], axis=0)
     lane = lax.broadcasted_iota(jnp.int32, x.shape, 1)
@@ -124,7 +126,16 @@
     cumt_ref[...] = xt
     et = jnp.exp(xt)
     d = jnp.broadcast_to(jnp.exp(x[:, tokens - 1 : tokens]), (PLANE, HD))
-    put_decays(d, heads, pay_ref, own_ref)
+    later = jnp.concatenate([d[half:], d[:half]], axis=0)
+    put_decays(jnp.where(y == 0, later, d), half, pay_ref, None)
+    put_decays(jnp.where(y == 0, d, later), half, None, own_ref)
+
+    def put_terms(low, high, at):
+        s = slice(at * HD, (at + 1) * HD)
+        own_ref[s, :] = jnp.where(y == 0, low, high)
+        pay_ref[s, :] = jnp.where(y == 0, high, low).astype(BF)
+
+    terms = []
     for h in range(heads):
         s = slice(h * HD, (h + 1) * HD)
         f = slice((first + h) * HD, (first + h + 1) * HD)
@@ -132,28 +143,31 @@
         qbf_ref[:, s] = q
         hi, lo = hi_lo(c_ref[:, f].astype(F32) * et[:, h : h + 1])
         both = dot(q, jnp.concatenate([hi, lo], axis=1), ((0,), (0,)))
-        term = both[:, :HD] + both[:, HD:]
-        own_ref[s, :] = term
-        pay_ref[s, :] = term.astype(BF)
-
-
-def state_terms(line, first, heads, q, c, ld):
+        terms.append(both[:, :HD] + both[:, HD:])
+        if h >= half:
+            put_terms(terms[h - half], terms[h], h - half)
+    if heads % 2:
+        put_terms(terms[half - 1], jnp.zeros((HD, HD), F32), half - 1)
+
+
+def state_terms(line, first, heads, flags, q, c, ld):
     tokens = q.shape[0]
-    rows = heads * HD + EXTRA
+    rows = (heads + 1) // 2 * HD + EXTRA
     outs = [((rows, HD), BF), ((rows, HD), F32), ((PLANE, tokens), F32), ((tokens, HD), F32)]
     outs.append(((tokens, heads * HD), BF))
-    return line(functools.partial(state_kernel, first, heads), "state_terms", outs, [], [ld, q, c])
+    return line(functools.partial(state_kernel, first, heads), "state_terms", outs, [flags], [ld, q, c])
 
 
 def put_decays(d, heads, pay_ref, own_ref):
-    d_hi, d_mid = hi_lo(d)
-    d_lo = (d - d_hi.astype(F32) - d_mid.astype(F32)).astype(BF)
     at = heads * HD
-    pay_ref[at : at + PLANE, :] = d_hi
-    pay_ref[at + PLANE : at + 2 * PLANE, :] = d_mid
-    pay_ref[at + 2 * PLANE : at + EXTRA, :] = d_lo
-    own_ref[at : at + PLANE, :] = d
-    own_ref[at + PLANE : at + EXTRA, :] = jnp.zeros((EXTRA - PLANE, HD), F32)
+    if pay_ref is not None:
+        d_hi, d_mid = hi_lo(d)
+        pay_ref[at : at + PLANE, :] = d_hi
+        pay_ref[at + PLANE : at + 2 * PLANE, :] = d_mid
+        pay_ref[at + 2 * PLANE : at + EXTRA, :] = (d - d_hi.astype(F32) - d_mid.astype(F32)).astype(BF)
+    if own_ref is not None:
+        own_ref[at : at + PLANE, :] = d
+        own_ref[at + PLANE : at + EXTRA, :] = jnp.zeros((EXTRA - PLANE, HD), F32)
 
 
 def decays(ref, heads):
@@ -214,18 +228,32 @@
     return line(kernel, "local_part", [(shape, F32), (shape, BF)], [], [q, k, c, cum, cumt])
 
 
-def value_kernel(heads, first, count, scale, flags_ref, k_ref, l_ref, cumt_ref, oth_ref, e_ref, r_ref, o_ref):
-    tokens = k_ref.shape[0]
+def carry_kernel(heads, flags_ref, own_ref, oth_ref, e_ref, r_ref, theirs_ref, mine_ref):
     is_first = flags_ref[0] == 0
     de = decays(e_ref, heads)
-    do = decays(oth_ref, heads)
-    use_oth = jnp.where(is_first, 1.0, 0.0)
-    scale_e = jnp.where(is_first, do, jnp.ones_like(do))
+    d_second = jnp.where(is_first, decays(oth_ref, heads), decays(own_ref, heads))
+    for h in range(heads):
+        s = slice(h * HD, (h + 1) * HD)
+        second = e_ref[s, :].astype(F32) + de[h : h + 1] * r_ref[s, :].astype(F32)
+        term = jnp.where(is_first, oth_ref[s, :].astype(F32), own_ref[s, :])
+        first = term + d_second[h : h + 1] * second
+        mine_ref[s, :] = jnp.where(is_first, first, second)
+        theirs_ref[s, :] = jnp.where(is_first, second, first).astype(BF)
+
+
+def carries(line, heads, flags, arrays):
+    shape = (heads * HD, HD)
+    kernel = functools.partial(carry_kernel, heads)
+    return line(kernel, "carries", [(shape, BF), (shape, F32)], [flags], arrays)
+
+
+def value_kernel(half, first, count, scale, flags_ref, k_ref, l_ref, cumt_ref, mine_ref, theirs_ref, o_ref):
+    tokens = k_ref.shape[0]
     fall = jnp.exp(cumt_ref[tokens - 1 : tokens, :] - cumt_ref[...])
     for h in range(first, first + count):
         s = slice(h * HD, (h + 1) * HD)
-        e = e_ref[s, :].astype(F32) + de[h : h + 1] * r_ref[s, :].astype(F32)
-        carry = use_oth * oth_ref[s, :].astype(F32) + scale_e[h : h + 1] * e
+        at = slice(h % half * HD, (h % half + 1) * HD)
+        carry = jnp.where(flags_ref[0] == h // half, mine_ref[at, :], theirs_ref[at, :].astype(F32))
         hi, lo = hi_lo(carry)
         both = dot(k_ref[:, s], jnp.concatenate([hi, lo], axis=1), ((1,), (0,)))
         carried = fall[:, h : h + 1] * (both[:, :HD] + both[:, HD:])
@@ -233,27 +261,32 @@
         o_ref[:, at : at + HD] = (scale * (l_ref[:, s] + carried)).astype(BF)
 
 
-def value_grads(line, heads, first, count, scale, flags, arrays, after):
-    kernel = functools.partial(value_kernel, heads, first, count, scale)
+def value_grads(line, half, first, count, scale, flags, arrays, after):
+    kernel = functools.partial(value_kernel, half, first, count, scale)
     outs = [((arrays[0].shape[0], count * HD), BF)]
     return line(kernel, "value_grad", outs, [flags], arrays, after)[0]
 
 
-def input_kernel(rows, at, flags_ref, *refs):
-    vs, w_ref, o_ref, v_all = refs[:-3], *refs[-3:]
+def input_kernel(rows, at, first, count, flags_ref, *refs):
+    *vs, w_ref, o_ref, v_all = refs[count:]
     start = 0
     for v in vs:
         v_all[:, start : start + v.shape[1]] = v[...]
         start += v.shape[1]
-    w = w_ref[pl.ds(pl.multiple_of(flags_ref[at] * rows, 128), rows), :]
-    o_ref[...] = dot(v_all[...], w, ((1,), (1,))).astype(o_ref.dtype)
-
-
-def input_part(line, flags, at, vs, w, rows, dtype, after=()):
+    cols = o_ref.shape[1] - first
+    w = w_ref[pl.ds(pl.multiple_of(flags_ref[at] * rows + first, 128), cols), :]
+    for before in refs[:count]:
+        o_ref[:, :first] = before[...]
+    o_ref[:, first:] = dot(v_all[...], w, ((1,), (1,))).astype(o_ref.dtype)
+
+
+def input_part(line, flags, at, vs, w, rows, dtype, end, before=()):
     tokens, features = vs[0].shape[0], w.shape[1]
+    first = before[0].shape[1] if before else 0
     scratch = [pltpu.VMEM((tokens, features), BF)]
-    kernel = functools.partial(input_kernel, rows, at)
-    return line(kernel, "input_part", [((tokens, rows), dtype)], [flags], [*vs, w], after, scratch)[0]
+    kernel = functools.partial(input_kernel, rows, at, first, len(before))
+    outs = [((tokens, end), dtype)]
+    return line(kernel, "input_part", outs, [flags], [*before, *vs, w], (), scratch)[0]
 
 
 def last_input_kernel(total_ref, *refs):
@@ -354,14 +387,15 @@
     flags = jnp.stack([p.astype(jnp.int32) for p in places])
 
     line = Line()
-    own, other, joined, locals_, values, from_y = [], [], [], [], [], []
+    own, other, joined, locals_, carried, values, from_y = [], [], [], [], [], [], []
+    halves = [(size + 1) // 2 for size in sizes]
 
     def states(g):
-        own.append(state_terms(line, starts[g], sizes[g], q, c, ld))
+        own.append(state_terms(line, starts[g], sizes[g], flags, q, c, ld))
         other.append(swap_with(own[g][0], "seq", 1))
 
     def join(g):
-        joined.append(append(line, sizes[g], flags, 0, own[g][1], other[g]))
+        joined.append(append(line, halves[g], flags, 0, own[g][1], other[g]))
 
     def spread(g):
         pay, ours = joined[g]
@@ -371,23 +405,27 @@
             if stage == 0:
                 e = later
             elif stage < stages - 1:
-                e = append(line, sizes[g], flags, 3, e, later)[1]
+                e = append(line, halves[g], flags, 3, e, later)[1]
             if stage < stages - 1:
-                pay, ours = append(line, sizes[g], flags, 3, ours, later)
+                pay, ours = append(line, halves[g], flags, 3, ours, later)
         if stages == 1:
             later = jnp.zeros_like(later)
         joined[g] = (e, later)
 
+    def carry(g):
+        theirs, mine = carries(line, halves[g], flags, [own[g][1], other[g], *joined[g]])
+        carried.append((mine, swap_with(theirs, "seq", 1)))
+
     def local(g):
         _, _, cum, cumt, q_bf = own[g]
         locals_.append(local_part(line, starts[g], sizes[g], q_bf, k, c, cum, cumt))
 
     def value(g, *after):
         part, k_bf = locals_[g]
-        arrays = [k_bf, part, own[g][3], other[g], *joined[g]]
+        arrays = [k_bf, part, own[g][3], *carried[g]]
         first = 0
         for count in splits[g]:
-            v = value_grads(line, sizes[g], first, count, grad_scale, flags, arrays, after)
+            v = value_grads(line, halves[g], first, count, grad_scale, flags, arrays, after)
             values.append(v)
             from_y.append(swap_with(v, "seq", 1))
             first, after = first + count, ()
@@ -411,14 +449,24 @@
             kept[i, j] = (keep, swap_with(away, "seq", 2 << bit))
 
     others = []
-
-    def input_others():
+    middle = rows_here // 2 if rows_here % 256 == 0 else 0
+
+    def input_parts(at, dtype, step):
+        if step == 0:
+            if not middle:
+                return pause(line)
+            halves_done[at] = [input_part(line, flags, at, values, value_weight, rows_here, dtype, middle)]
+        else:
+            before = halves_done.get(at, ())
+            return input_part(line, flags, at, values, value_weight, rows_here, dtype, rows_here, before)
+
+    halves_done = {}
+
+    def input_others(step):
         for i in range(1, sides):
-            part = input_part(line, flags, at_sides + i, values, value_weight, rows_here, BF)
-            others.append(swap_with(part, "head", i))
-
-    def input_own(*after):
-        return input_part(line, flags, at_sides, values, value_weight, rows_here, F32, after)
+            part = input_parts(at_sides + i, BF, step)
+            if step:
+                others.append(swap_with(part, "head", i))
 
     near, *far = transposed(line, flags, inputs[0], order, rows)
     near_x = [swap_with(near, "head", i) for i in range(1, sides)]
@@ -446,43 +494,49 @@
     spread(0)
     if groups == 2:
         local(1)
-    for i in range(len(far)):
-        far_to_x(i)
+        spread(1)
+    far_to_x(0)
+    carry(0)
+    if len(far) == 2:
+        far_to_x(1)
+    if groups == 2:
+        carry(1)
     value(0, *near_x)
     if groups == 2:
-        spread(1)
+        value(1, *[f[0] for f in far_x])
     everything = [[p] for p in (near, *near_x)] + [far, *far_x]
     everything = merged(line, everything)
     pieces = list(zip(everything[:sides], everything[sides:]))
     if groups == 2:
         matmul(0)
-        pause(line)
+        input_others(0)
         over_dp(0)
-        value(1)
         matmul(1)
-        pause(line)
+        input_others(1)
         over_dp(1)
         over_z(0)
-        input_others()
         matmul(2)
-        pause(line)
+        input_parts(at_sides, F32, 0)
         over_dp(2)
         over_z(1)
         matmul(3)
         pause(line, [kept[0, 0][1]])
         over_dp(3, splits[1][1] // 2 * HD, (splits[1][1] + 1) // 2 * HD)
         over_z(2)
+        pause(line)
+        total = input_parts(at_sides, F32, 1)
         over_z(3, 0)
         over_z(3, 1)
-        total = input_own()
     else:
         matmul(0)
         matmul(1)
         over_dp(0)
         over_dp(1)
         over_z(0)
-        input_others()
-        total = input_own()
+        input_others(0)
+        input_others(1)
+        input_parts(at_sides, F32, 0)
+        total = input_parts(at_sides, F32, 1)
         over_z(1)
     outs = [(total.shape, BF), ((8, HD), F32)]
     grad_input = line(last_input_kernel, "grad_input", outs, [], [total, *others], last=1)[0]

time: 137 us -> 129 us (0.942)
  waiting for transfers between devices: 42 us -> 25.4 us
  Pallas kernels: 52.8 us -> 61.4 us
  local copies, waits for them, and re-layouts: 3.21 us -> 7 us
  starting transfers between devices: 36.9 us -> 34.2 us
    ppermute x26 -> x28, waiting for transfers between devices: 42 us -> 25 us  [swap_with(): lax.ppermute(x, axis, [(i, i ^ bit) for i in range(lax.axis_size(axis))])]
    pallas_call x38 -> x40, Pallas kernels: 52.8 us -> 61.4 us  [__call__(): pl.pallas_call(body, in_specs=[SM] * len(smalls) + [VM] * len(arrays) + [...]
    unnamed x53 -> x39, local copies, waits for them, and re-layouts: 3.13 us -> 6.91 us
    ppermute x26 -> x28, starting transfers between devices: 31.5 us -> 28.7 us  [swap_with(): lax.ppermute(x, axis, [(i, i ^ bit) for i in range(lax.axis_size(axis))])]
  transfers between devices with their start and end apart: 30 -> 32, of which waited for: 12 -> 15; matrix products, arithmetic and copies ran while one was open for 0% -> 0% of each run, Pallas kernels for 36% -> 44%
where the time goes in v4:
time: 129 us
  Pallas kernels  61.4 us (48%)
  starting transfers between devices  34.2 us (27%)
  waiting for transfers between devices  25.4 us (20%)
  local copies, waits for them, and re-layouts  7 us (5%)
    pallas_call x40, Pallas kernels, __call__(): pl.pallas_call(body, in_specs=[SM] * len(smalls) + [VM] * len(arrays) + [...  61.4 us
    ppermute x28, starting transfers between devices, swap_with(): lax.ppermute(x, axis, [(i, i ^ bit) for i in range(lax.axis_size(axis))])  28.7 us
    ppermute x28, waiting for transfers between devices, swap_with(): lax.ppermute(x, axis, [(i, i ^ bit) for i in range(lax.axis_size(axis))])  25 us
    unnamed x39, local copies, waits for them, and re-layouts  6.91 us
    ppermute x4, starting transfers between devices, from_later(): lax.ppermute(x, axis, [(i, i - shift) for i in range(shift, lax.axis_size...  5.46 us
  transfers between devices with their start and end apart: 32, of which 15 were waited for; matrix products, arithmetic and copies ran while one was open for 0% of the time, Pallas kernels for 44%

profile of v4, /device:TPU:0, one launch (start us, length us, event | category | flops | bytes accessed | tf_op | source)
XLA Modules:
  0.0 129.0 jit_solution(8803267781289333186)
XLA Ops:
  0.8 1.5 %copy-done.2 = bf16[1,512,1792]{2,1,0:T(8,128)(2,1)S(1)} copy-done((bf16[1,512,1792]{2,1,0:T(8,128)(2,1)S(1)}, bf16[1,512,1792]{2,1,0:T(8,128)(2,1)}, u32[]{:S(2)}) %copy-start.2) | copy-done | bytes 1835032
  2.3 2.1 %transpose_inputs.1 = (bf16[2,2,224,512]{3,2,1,0:T(8,128)(2,1)}, bf16[1,2,224,512]{3,2,1,0:T(8,128)(2,1)S(1)}, bf16[1,2,224,512]{3,2,1,0:T(8,128)(2,1)S(1)}) custom-call(s32[8]{0:T(128)S(1)} %stack.27.refs_0_, bf16[512,1792]{1,0:T(8,128)(2,1)S(1)} %bitcast.24), custom_call_target="tpu_custom_call" | custom-call | flops 20000000000 | tf_op jit(solution)/shard_map/transpose_inputs/pallas_call | solution.py:45
  4.4 2.9 %collective-permute-start.9 = (bf16[2,2,224,512]{3,2,1,0:T(8,128)(2,1)}, bf16[2,2,224,512]{3,2,1,0:T(8,128)(2,1)}, u32[]{:S(2)}, u32[]{:S(2)}) collective-permute-start(bf16[2,2,224,512]{3,2,1,0:T(8,128)(2,1)} %get-tuple-element.65.refs_4_.refs_0_), channel_id=1, source_target_pairs={{0,2},{2,0},{1,3},{3,1},{4,6},{6,4},{5,7},{7,5},{8,10},{10,8},{9,1... | collective-permute-start | bytes 2752520 | tf_op jit(solution)/shard_map/ppermute | solution.py:351
  7.3 2.1 %state_terms.2 = (bf16[432,128]{1,0:T(8,128)(2,1)S(1)}, f32[432,128]{1,0:T(8,128)S(1)}, f32[16,512]{1,0:T(8,128)S(1)}, f32[512,128]{1,0:T(8,128)S(1)}, bf16[512,768]{1,0:T(8,128)(2,1)S(1)}) custom-call(s32[8]{0:T(128)S(1)} %stack.27.refs_0_, f32[14,512]{1,0:T(8,128)S(1)} %bitcast.14, s32[512,1792]{1,0:T(8,128)S(1)} %bitcast.20, ...), custom_call_target="tpu_custom_call" | custom-call | flops 20000000000 | tf_op jit(solution)/shard_map/state_terms/pallas_call | solution.py:45
  9.5 1.6 %collective-permute-start.1 = (bf16[432,128]{1,0:T(8,128)(2,1)S(1)}, bf16[432,128]{1,0:T(8,128)(2,1)S(1)}, u32[]{:S(2)}, u32[]{:S(2)}) collective-permute-start(bf16[432,128]{1,0:T(8,128)(2,1)S(1)} %get-tuple-element.69.refs_4_), channel_id=1, source_target_pairs={{0,4},{4,0},{8,12},{12,8},{16,20},{20,16},{24,28},{28,24},{1,5},{5... | collective-permute-start | bytes 331784 | tf_op jit(solution)/shard_map/ppermute | solution.py:351
  11.0 2.3 %state_terms.3 = (bf16[560,128]{1,0:T(8,128)(2,1)S(1)}, f32[560,128]{1,0:T(8,128)S(1)}, f32[16,512]{1,0:T(8,128)S(1)}, f32[512,128]{1,0:T(8,128)S(1)}, bf16[512,1024]{1,0:T(8,128)(2,1)S(1)}) custom-call(s32[8]{0:T(128)S(1)} %stack.27.refs_0_, f32[14,512]{1,0:T(8,128)S(1)} %bitcast.15, s32[512,1792]{1,0:T(8,128)S(1)} %bitcast.21, ...), custom_call_target="tpu_custom_call" | custom-call | flops 20000000000 | tf_op jit(solution)/shard_map/state_terms/pallas_call | solution.py:45
  14.9 1.3 %collective-permute-start.2 = (bf16[432,128]{1,0:T(8,128)(2,1)S(1)}, bf16[432,128]{1,0:T(8,128)(2,1)S(1)}, u32[]{:S(2)}, u32[]{:S(2)}) collective-permute-start(bf16[432,128]{1,0:T(8,128)(2,1)S(1)} %get-tuple-element.73.refs_3_), channel_id=1, source_target_pairs={{8,0},{12,4},{16,8},{20,12},{24,16},{28,20},{9,1},{13,5},{17,9},{2... | collective-permute-start | bytes 331784 | tf_op jit(solution)/shard_map/ppermute | solution.py:355
  16.2 1.6 %collective-permute-start.4 = (bf16[1,2,224,512]{3,2,1,0:T(8,128)(2,1)S(1)}, bf16[1,2,224,512]{3,2,1,0:T(8,128)(2,1)S(1)}, u32[]{:S(2)}, u32[]{:S(2)}) collective-permute-start(bf16[1,2,224,512]{3,2,1,0:T(8,128)(2,1)S(1)} %get-tuple-element.81.refs_4_), channel_id=1, source_target_pairs={{0,4},{4,0},{8,12},{12,8},{16,20},{20,16},{24,28},{28,24},{1,5},{5... | collective-permute-start | bytes 1376264 | tf_op jit(solution)/shard_map/ppermute | solution.py:351
  17.7 1.7 %collective-permute-done.refs_2_ = bf16[560,128]{1,0:T(8,128)(2,1)S(1)} collective-permute-done((bf16[560,128]{1,0:T(8,128)(2,1)S(1)}, bf16[560,128]{1,0:T(8,128)(2,1)S(1)}, u32[]{:S(2)}, u32[]{:S(2)}) %collective-permute-start) | collective-permute-done | bytes 143392 | tf_op jit(solution)/shard_map/ppermute | solution.py:351
  20.1 1.4 %collective-permute-start.5 = (bf16[560,128]{1,0:T(8,128)(2,1)S(1)}, bf16[560,128]{1,0:T(8,128)(2,1)S(1)}, u32[]{:S(2)}, u32[]{:S(2)}) collective-permute-start(bf16[560,128]{1,0:T(8,128)(2,1)S(1)} %get-tuple-element.75.refs_5_), channel_id=1, source_target_pairs={{8,0},{12,4},{16,8},{20,12},{24,16},{28,20},{9,1},{13,5},{17,9},{2... | collective-permute-start | bytes 430088 | tf_op jit(solution)/shard_map/ppermute | solution.py:355
  21.6 1.9 %local_part.2 = (f32[512,768]{1,0:T(8,128)S(1)}, bf16[512,768]{1,0:T(8,128)(2,1)S(1)}) custom-call(bf16[512,768]{1,0:T(8,128)(2,1)S(1)} %get-tuple-element.66.refs_0_, s32[512,1792]{1,0:T(8,128)S(1)} %bitcast.22, bf16[512,1792]{1,0:T(8,128)(2,1)S(1)} %bitcast.27, f32[16,512]{1,0:T(8,128)S(1)} %get-tuple-element.67.refs_3_, ...), custom_call_target="tpu_custom_call" | custom-call | flops 20000000000 | tf_op jit(solution)/shard_map/local_part/pallas_call | solution.py:45
  23.5 1.3 join_states.6
  24.8 1.3 collective-permute-start.3
  26.1 2.5 %local_part.3 = (f32[512,1024]{1,0:T(8,128)S(1)}, bf16[512,1024]{1,0:T(8,128)(2,1)S(1)}) custom-call(bf16[512,1024]{1,0:T(8,128)(2,1)S(1)} %get-tuple-element.83.refs_0_, s32[512,1792]{1,0:T(8,128)S(1)} %bitcast.23, bf16[512,1792]{1,0:T(8,128)(2,1)S(1)} %bitcast.28, f32[16,512]{1,0:T(8,128)S(1)} %get-tuple-element.84.refs_3_, ...), custom_call_target="tpu_custom_call" | custom-call | flops 20000000000 | tf_op jit(solution)/shard_map/local_part/pallas_call | solution.py:45
  28.6 1.3 %join_states.7 = (bf16[560,128]{1,0:T(8,128)(2,1)S(1)}, f32[560,128]{1,0:T(8,128)}) custom-call(s32[8]{0:T(128)S(1)} %stack.27.refs_0_, f32[560,128]{1,0:T(8,128)S(1)} %get-tuple-element.82.refs_1_, bf16[560,128]{1,0:T(8,128)(2,1)S(1)} %collective-permute-done.5.refs_2_.refs_3_, f32[512,1024]{1,0:T(8,128)S(1)} %get-tuple-element.86.refs_3_.refs_2_), custom_call_target="tpu_custom_call" | custom-call | flops 20000000000 | tf_op jit(solution)/shard_map/join_states/pallas_call | solution.py:45
  29.9 1.5 %collective-permute-start.7 = (bf16[560,128]{1,0:T(8,128)(2,1)S(1)}, bf16[560,128]{1,0:T(8,128)(2,1)S(1)}, u32[]{:S(2)}, u32[]{:S(2)}) collective-permute-start(bf16[560,128]{1,0:T(8,128)(2,1)S(1)} %get-tuple-element.87.refs_1_), channel_id=1, source_target_pairs={{16,0},{20,4},{24,8},{28,12},{17,1},{21,5},{25,9},{29,13},{18,2},{... | collective-permute-start | bytes 430088 | tf_op jit(solution)/shard_map/ppermute | solution.py:355
  31.5 0.8 collective-permute-start.11
  33.0 2.1 %collective-permute-start.6 = (bf16[384,128]{1,0:T(8,128)(2,1)S(1)}, bf16[384,128]{1,0:T(8,128)(2,1)S(1)}, u32[]{:S(2)}, u32[]{:S(2)}) collective-permute-start(bf16[384,128]{1,0:T(8,128)(2,1)S(1)} %get-tuple-element.89.refs_1_), channel_id=1, source_target_pairs={{0,4},{4,0},{8,12},{12,8},{16,20},{20,16},{24,28},{28,24},{1,5},{5... | collective-permute-start | bytes 294920 | tf_op jit(solution)/shard_map/ppermute | solution.py:351
  35.0 4.2 %collective-permute-done.8.refs_0_ = bf16[1,2,224,512]{3,2,1,0:T(8,128)(2,1)S(1)} collective-permute-done((bf16[1,2,224,512]{3,2,1,0:T(8,128)(2,1)S(1)}, bf16[1,2,224,512]{3,2,1,0:T(8,128)(2,1)S(1)}, u32[]{:S(2)}, u32[]{:S(2)}) %collective-permute-start.8) | collective-permute-done | bytes 458784 | tf_op jit(solution)/shard_map/ppermute | solution.py:351
  39.3 1.0 collective-permute-start.12
  41.2 1.6 %collective-permute-start.10 = (bf16[512,128]{1,0:T(8,128)(2,1)S(1)}, bf16[512,128]{1,0:T(8,128)(2,1)S(1)}, u32[]{:S(2)}, u32[]{:S(2)}) collective-permute-start(bf16[512,128]{1,0:T(8,128)(2,1)S(1)} %get-tuple-element.91.refs_6_), channel_id=1, source_target_pairs={{0,4},{4,0},{8,12},{12,8},{16,20},{20,16},{24,28},{28,24},{1,5},{5... | collective-permute-start | bytes 393224 | tf_op jit(solution)/shard_map/ppermute | solution.py:351
  42.8 0.9 value_grad.4.refs_6_.refs_4_.refs_1_.refs_2_
  44.3 0.9 value_grad.5.refs_6_.refs_2_.refs_4_.refs_3_
  45.2 1.6 %collective-permute-start.17 = (bf16[512,384]{1,0:T(8,128)(2,1)S(1)}, bf16[512,384]{1,0:T(8,128)(2,1)S(1)}, u32[]{:S(2)}, u32[]{:S(2)}) collective-permute-start(bf16[512,384]{1,0:T(8,128)(2,1)S(1)} %value_grad.5.refs_6_.refs_2_.refs_4_.refs_3_), channel_id=1, source_target_pairs={{0,4},{4,0},{8,12},{12,8},{16,20},{20,16},{24,28},{28,24},{1,5},{5... | collective-permute-start | bytes 1179656 | tf_op jit(solution)/shard_map/ppermute | solution.py:351
  46.8 0.8 collective-permute-done.10.refs_5_
  47.6 1.8 %value_grad.6.refs_6_.refs_3_.refs_4_ = bf16[512,512]{1,0:T(8,128)(2,1)} custom-call(s32[8]{0:T(128)S(1)} %stack.27.refs_0_, bf16[512,1024]{1,0:T(8,128)(2,1)S(1)} %get-tuple-element.92.refs_1_, f32[512,1024]{1,0:T(8,128)S(1)} %get-tuple-element.86.refs_3_.refs_2_, f32[512,128]{1,0:T(8,128)S(1)} %get-tuple-element.85.refs_4_.refs_3_, ...), custom_call_target="tpu_custom_call" | custom-call | flops 20000000000 | tf_op jit(solution)/shard_map/value_grad/pallas_call | solution.py:45
  49.4 1.6 %collective-permute-start.13 = (bf16[512,512]{1,0:T(8,128)(2,1)}, bf16[512,512]{1,0:T(8,128)(2,1)}, u32[]{:S(2)}, u32[]{:S(2)}) collective-permute-start(bf16[512,512]{1,0:T(8,128)(2,1)} %value_grad.6.refs_6_.refs_3_.refs_4_), channel_id=1, source_target_pairs={{0,4},{4,0},{8,12},{12,8},{16,20},{20,16},{24,28},{28,24},{1,5},{5... | collective-permute-start | bytes 1572872 | tf_op jit(solution)/shard_map/ppermute | solution.py:351
  51.0 1.8 %value_grad.7.refs_6_.refs_4_.refs_5_ = bf16[512,512]{1,0:T(8,128)(2,1)} custom-call(s32[8]{0:T(128)S(1)} %stack.27.refs_0_, bf16[512,1024]{1,0:T(8,128)(2,1)S(1)} %get-tuple-element.92.refs_1_, f32[512,1024]{1,0:T(8,128)S(1)} %get-tuple-element.86.refs_3_.refs_2_, f32[512,128]{1,0:T(8,128)S(1)} %get-tuple-element.85.refs_4_.refs_3_, ...), custom_call_target="tpu_custom_call" | custom-call | flops 20000000000 | tf_op jit(solution)/shard_map/value_grad/pallas_call | solution.py:45
  53.3 1.8 %merge_inputs.1 = (bf16[2,2,224,512]{3,2,1,0:T(8,128)(2,1)S(1)}, bf16[2,2,224,512]{3,2,1,0:T(8,128)(2,1)S(1)}, bf16[2,2,224,512]{3,2,1,0:T(8,128)(2,1)S(1)}, bf16[2,2,224,512]{3,2,1,0:T(8,128)(2,1)S(1)}) custom-call(bf16[2,2,224,512]{3,2,1,0:T(8,128)(2,1)} %get-tuple-element.65.refs_4_.refs_0_, ...), custom_call_target="tpu_custom_call" | custom-call | flops 20000000000 | tf_op jit(solution)/shard_map/merge_inputs/pallas_call | solution.py:45
  55.1 0.9 collective-permute-done.14.refs_5_
  56.1 2.1 %weight_part.4 = (bf16[4,224,384]{2,1,0:T(8,128)(2,1)S(1)}, f32[4,224,384]{2,1,0:T(8,128)S(1)}) custom-call(bf16[2,2,224,512]{3,2,1,0:T(8,128)(2,1)S(1)} %get-tuple-element.94.refs_0_.refs_6_, bf16[2,2,224,512]{3,2,1,0:T(8,128)(2,1)S(1)} %get-tuple-element.95.refs_1_, bf16[2,2,224,512]{3,2,1,0:T(8,128)(2,1)S(1)} %get-tuple-element.96.refs_2_, ...), custom_call_target="tpu_custom_call" | custom-call | flops 20000000000 | tf_op jit(solution)/shard_map/weight_part/pallas_call | solution.py:45
  58.7 3.3 %input_part.4.refs_3_.refs_1_ = bf16[512,896]{1,0:T(8,128)(2,1)S(1)} custom-call(s32[8]{0:T(128)S(1)} %stack.27.refs_0_, bf16[512,384]{1,0:T(8,128)(2,1)S(1)} %value_grad.4.refs_6_.refs_4_.refs_1_.refs_2_, bf16[512,384]{1,0:T(8,128)(2,1)S(1)} %value_grad.5.refs_6_.refs_2_.refs_4_.refs_3_, bf16[512,512]{1,0:T(8,128)(2,1)} %value_grad.6.refs_6_.refs_3_.refs_4_, ...), custom_call_target="tpu_custom_call" | custom-call | flops 20000000000 | tf_op jit(solution)/shard_map/input_part/pallas_call | solution.py:45
  62.0 0.7 fold_weight.10
  62.7 1.5 %collective-permute-start.16 = (bf16[2,224,384]{2,1,0:T(8,128)(2,1)S(1)}, bf16[2,224,384]{2,1,0:T(8,128)(2,1)S(1)}, u32[]{:S(2)}, u32[]{:S(2)}) collective-permute-start(bf16[2,224,384]{2,1,0:T(8,128)(2,1)S(1)} %get-tuple-element.101.refs_6_), channel_id=1, source_target_pairs={{0,8},{4,12},{8,0},{12,4},{16,24},{20,28},{24,16},{28,20},{1,9},{5... | collective-permute-start | bytes 1032200 | tf_op jit(solution)/shard_map/ppermute | solution.py:351
  64.5 2.1 %weight_part.5 = (bf16[4,224,384]{2,1,0:T(8,128)(2,1)S(1)}, f32[4,224,384]{2,1,0:T(8,128)S(1)}) custom-call(bf16[2,2,224,512]{3,2,1,0:T(8,128)(2,1)S(1)} %get-tuple-element.94.refs_0_.refs_6_, bf16[2,2,224,512]{3,2,1,0:T(8,128)(2,1)S(1)} %get-tuple-element.95.refs_1_, bf16[2,2,224,512]{3,2,1,0:T(8,128)(2,1)S(1)} %get-tuple-element.96.refs_2_, ...), custom_call_target="tpu_custom_call" | custom-call | flops 20000000000 | tf_op jit(solution)/shard_map/weight_part/pallas_call | solution.py:45
  66.6 4.6 %input_part.5.refs_3_ = bf16[512,1792]{1,0:T(8,128)(2,1)} custom-call(s32[8]{0:T(128)S(1)} %stack.27.refs_0_, bf16[512,896]{1,0:T(8,128)(2,1)S(1)} %input_part.4.refs_3_.refs_1_, bf16[512,384]{1,0:T(8,128)(2,1)S(1)} %value_grad.4.refs_6_.refs_4_.refs_1_.refs_2_, bf16[512,384]{1,0:T(8,128)(2,1)S(1)} %value_grad.5.refs_6_.refs_2_.refs_4_.refs_3_, ...), custom_call_target="tpu_custom_call" | custom-call | flops 20000000000 | tf_op jit(solution)/shard_map/input_part/pallas_call | solution.py:45
  71.2 0.9 collective-permute-start.25
  72.1 0.7 fold_weight.11
  72.8 1.6 %collective-permute-start.22 = (bf16[2,224,384]{2,1,0:T(8,128)(2,1)S(1)}, bf16[2,224,384]{2,1,0:T(8,128)(2,1)S(1)}, u32[]{:S(2)}, u32[]{:S(2)}) collective-permute-start(bf16[2,224,384]{2,1,0:T(8,128)(2,1)S(1)} %get-tuple-element.104.refs_3_), channel_id=1, source_target_pairs={{0,8},{4,12},{8,0},{12,4},{16,24},{20,28},{24,16},{28,20},{1,9},{5... | collective-permute-start | bytes 1032200 | tf_op jit(solution)/shard_map/ppermute | solution.py:351
  75.0 2.6 %collective-permute-start.24 = (bf16[1,224,384]{2,1,0:T(8,128)(2,1)S(1)}, bf16[1,224,384]{2,1,0:T(8,128)(2,1)S(1)}, u32[]{:S(2)}, u32[]{:S(2)}) collective-permute-start(bf16[1,224,384]{2,1,0:T(8,128)(2,1)S(1)} %get-tuple-element.105.refs_6_), channel_id=1, source_target_pairs={{0,16},{4,20},{8,24},{12,28},{16,0},{20,4},{24,8},{28,12},{1,17},{... | collective-permute-start | bytes 516104 | tf_op jit(solution)/shard_map/ppermute | solution.py:351
  77.7 3.3 %weight_part.6 = (bf16[4,224,512]{2,1,0:T(8,128)(2,1)S(1)}, f32[4,224,512]{2,1,0:T(8,128)S(1)}) custom-call(bf16[2,2,224,512]{3,2,1,0:T(8,128)(2,1)S(1)} %get-tuple-element.94.refs_0_.refs_6_, bf16[2,2,224,512]{3,2,1,0:T(8,128)(2,1)S(1)} %get-tuple-element.95.refs_1_, bf16[2,2,224,512]{3,2,1,0:T(8,128)(2,1)S(1)} %get-tuple-element.96.refs_2_, ...), custom_call_target="tpu_custom_call" | custom-call | flops 20000000000 | tf_op jit(solution)/shard_map/weight_part/pallas_call | solution.py:45
  81.0 3.3 %input_part.6.refs_3_.refs_1_ = f32[512,896]{1,0:T(8,128)S(1)} custom-call(s32[8]{0:T(128)S(1)} %stack.27.refs_0_, bf16[512,384]{1,0:T(8,128)(2,1)S(1)} %value_grad.4.refs_6_.refs_4_.refs_1_.refs_2_, bf16[512,384]{1,0:T(8,128)(2,1)S(1)} %value_grad.5.refs_6_.refs_2_.refs_4_.refs_3_, bf16[512,512]{1,0:T(8,128)(2,1)} %value_grad.6.refs_6_.refs_3_.refs_4_, ...), custom_call_target="tpu_custom_call" | custom-call | flops 20000000000 | tf_op jit(solution)/shard_map/input_part/pallas_call | solution.py:45
  84.4 0.8 fold_weight.13
  85.6 1.1 collective-permute-done.22.refs_2_
  86.7 1.3 fold_weight.14
  88.0 1.9 %collective-permute-start.28 = (bf16[1,224,384]{2,1,0:T(8,128)(2,1)}, bf16[1,224,384]{2,1,0:T(8,128)(2,1)}, u32[]{:S(2)}, u32[]{:S(2)}) collective-permute-start(bf16[1,224,384]{2,1,0:T(8,128)(2,1)} %get-tuple-element.111.refs_6_), channel_id=1, source_target_pairs={{0,16},{4,20},{8,24},{12,28},{16,0},{20,4},{24,8},{28,12},{1,17},{... | collective-permute-start | bytes 516104 | tf_op jit(solution)/shard_map/ppermute | solution.py:351
  89.9 3.5 %weight_part.7 = (bf16[4,224,512]{2,1,0:T(8,128)(2,1)S(1)}, f32[4,224,512]{2,1,0:T(8,128)S(1)}) custom-call(bf16[2,2,224,512]{3,2,1,0:T(8,128)(2,1)S(1)} %get-tuple-element.94.refs_0_.refs_6_, bf16[2,2,224,512]{3,2,1,0:T(8,128)(2,1)S(1)} %get-tuple-element.95.refs_1_, bf16[2,2,224,512]{3,2,1,0:T(8,128)(2,1)S(1)} %get-tuple-element.96.refs_2_, ...), custom_call_target="tpu_custom_call" | custom-call | flops 20000000000 | tf_op jit(solution)/shard_map/weight_part/pallas_call | solution.py:45
  93.5 0.7 copy-done.8
  94.2 1.8 %collective-permute-done.23.refs_2_ = bf16[4,224,512]{2,1,0:T(8,128)(2,1)S(1)} collective-permute-done((bf16[4,224,512]{2,1,0:T(8,128)(2,1)S(1)}, bf16[4,224,512]{2,1,0:T(8,128)(2,1)S(1)}, u32[]{:S(2)}, u32[]{:S(2)}) %collective-permute-start.23) | collective-permute-done | bytes 917536 | tf_op jit(solution)/shard_map/ppermute | solution.py:351
  96.0 0.6 fold_weight.15
  96.6 2.5 %collective-permute-start.27 = (bf16[2,224,256]{2,1,0:T(8,128)(2,1)S(1)}, bf16[2,224,256]{2,1,0:T(8,128)(2,1)S(1)}, u32[]{:S(2)}, u32[]{:S(2)}) collective-permute-start(bf16[2,224,256]{2,1,0:T(8,128)(2,1)S(1)} %get-tuple-element.114.refs_3_), channel_id=1, source_target_pairs={{0,8},{4,12},{8,0},{12,4},{16,24},{20,28},{24,16},{28,20},{1,9},{5... | collective-permute-start | bytes 688136 | tf_op jit(solution)/shard_map/ppermute | solution.py:351
  99.2 0.7 fold_weight.16
  99.9 2.3 %collective-permute-done.20.refs_2_ = bf16[2,224,512]{2,1,0:T(8,128)(2,1)S(1)} collective-permute-done((bf16[2,224,512]{2,1,0:T(8,128)(2,1)S(1)}, bf16[2,224,512]{2,1,0:T(8,128)(2,1)S(1)}, u32[]{:S(2)}, u32[]{:S(2)}) %collective-permute-start.20) | collective-permute-done | bytes 458784 | tf_op jit(solution)/shard_map/ppermute | solution.py:351
  102.2 0.7 fold_weight.17
  103.1 1.3 %slice-done.5 = s8[4194304]{0:T(1024)(128)(4,1)S(1)} async-done(((s8[12845056]{0:T(1024)(128)(4,1)}), s8[4194304]{0:T(1024)(128)(4,1)S(1)}, s32[]{:S(2)}) %slice-start.5) | async-done | bytes 4194328
  104.5 1.4 %slice-done.6 = s8[4194304]{0:T(1024)(128)(4,1)S(1)} async-done(((s8[12845056]{0:T(1024)(128)(4,1)}), s8[4194304]{0:T(1024)(128)(4,1)S(1)}, s32[]{:S(2)}) %slice-start.6) | async-done | bytes 4194328
  105.9 1.2 slice-done.7
  107.2 3.4 %input_part.7.refs_3_.refs_0_ = f32[512,1792]{1,0:T(8,128)S(1)} custom-call(s32[8]{0:T(128)S(1)} %stack.27.refs_0_, f32[512,896]{1,0:T(8,128)S(1)} %input_part.6.refs_3_.refs_1_, bf16[512,384]{1,0:T(8,128)(2,1)S(1)} %copy-done.5, bf16[512,384]{1,0:T(8,128)(2,1)S(1)} %copy-done.7, bf16[512,512]{1,0:T(8,128)(2,1)} %value_grad.6.refs_6_.refs_3_.refs_4_, ...), custom_call_target="tpu_custom_call" | custom-call | flops 20000000000 | tf_op jit(solution)/shard_map/input_part/pallas_call | solution.py:45
  110.6 1.4 %collective-permute-done.27.refs_2_ = bf16[2,224,256]{2,1,0:T(8,128)(2,1)S(1)} collective-permute-done((bf16[2,224,256]{2,1,0:T(8,128)(2,1)S(1)}, bf16[2,224,256]{2,1,0:T(8,128)(2,1)S(1)}, u32[]{:S(2)}, u32[]{:S(2)}) %collective-permute-start.27) | collective-permute-done | bytes 229408 | tf_op jit(solution)/shard_map/ppermute | solution.py:351
  112.7 3.9 %collective-permute-done.26.refs_2_ = bf16[2,224,256]{2,1,0:T(8,128)(2,1)S(1)} collective-permute-done((bf16[2,224,256]{2,1,0:T(8,128)(2,1)S(1)}, bf16[2,224,256]{2,1,0:T(8,128)(2,1)S(1)}, u32[]{:S(2)}, u32[]{:S(2)}) %collective-permute-start.26) | collective-permute-done | bytes 229408 | tf_op jit(solution)/shard_map/ppermute | solution.py:351
  117.4 3.1 %grad_input.1 = (bf16[512,1792]{1,0:T(8,128)(2,1)}, f32[8,128]{1,0:T(8,128)S(1)}) custom-call(f32[512,1792]{1,0:T(8,128)S(1)} %input_part.7.refs_3_.refs_0_, bf16[512,1792]{1,0:T(8,128)(2,1)} %collective-permute-done.25.refs_1_, bf16[1,224,256]{2,1,0:T(8,128)(2,1)S(1)} %get-tuple-element.120.refs_2_), custom_call_target="tpu_custom_call" | custom-call | flops 20000000000 | tf_op jit(solution)/shard_map/grad_input/pallas_call | solution.py:45
  120.6 3.9 %collective-permute-done.30.refs_7_ = bf16[1,224,256]{2,1,0:T(8,128)(2,1)S(1)} collective-permute-done((bf16[1,224,256]{2,1,0:T(8,128)(2,1)S(1)}, bf16[1,224,256]{2,1,0:T(8,128)(2,1)S(1)}, u32[]{:S(2)}, u32[]{:S(2)}) %collective-permute-start.30) | collective-permute-done | bytes 114720 | tf_op jit(solution)/shard_map/ppermute | solution.py:351
  124.4 2.4 %collective-permute-done.31.refs_9_ = bf16[1,224,256]{2,1,0:T(8,128)(2,1)S(1)} collective-permute-done((bf16[1,224,256]{2,1,0:T(8,128)(2,1)S(1)}, bf16[1,224,256]{2,1,0:T(8,128)(2,1)S(1)}, u32[]{:S(2)}, u32[]{:S(2)}) %collective-permute-start.31) | collective-permute-done | bytes 114720 | tf_op jit(solution)/shard_map/ppermute | solution.py:351
  126.8 2.3 %grad_weight.1 = f32[224,1792]{1,0:T(8,128)} custom-call(f32[1,224,384]{2,1,0:T(8,128)S(1)} %get-tuple-element.122.refs_0_, bf16[1,224,384]{2,1,0:T(8,128)(2,1)S(1)} %copy-done.9, f32[1,224,384]{2,1,0:T(8,128)S(1)} %get-tuple-element.123.refs_2_, bf16[1,224,384]{2,1,0:T(8,128)(2,1)} %collective-permute-done.28.refs_3_, ...), custom_call_target="tpu_custom_call" | custom-call | flops 20000000000 | tf_op jit(solution)/shard_map/grad_weight/pallas_call | solution.py:45
  (82 shorter events, 9.0 us)
Async XLA Ops:
  0.8 1.5 %copy-start.2 = (bf16[1,512,1792]{2,1,0:T(8,128)(2,1)S(1)}, bf16[1,512,1792]{2,1,0:T(8,128)(2,1)}, u32[]{:S(2)}) copy-start(bf16[1,512,1792]{2,1,0:T(8,128)(2,1)} %param.6) | copy-start | bytes 5505028
  2.3 5.1 %copy-start.10 = (f32[1,14,512]{2,0,1:T(1,128)S(1)}, f32[1,14,512]{2,0,1:T(1,128)}, u32[]{:S(2)}) copy-start(f32[1,14,512]{2,0,1:T(1,128)} %param.11) | copy-start | bytes 86020
  2.3 5.1 %copy-start = (s32[1,512,1792]{2,1,0:T(8,128)S(1)}, s32[1,512,1792]{2,1,0:T(8,128)}, u32[]{:S(2)}) copy-start(s32[1,512,1792]{2,1,0:T(8,128)} %param.9) | copy-start | bytes 11010052
  2.3 5.1 %copy-start.3 = (bf16[1,512,1792]{2,1,0:T(8,128)(2,1)S(1)}, bf16[1,512,1792]{2,1,0:T(8,128)(2,1)}, u32[]{:S(2)}) copy-start(bf16[1,512,1792]{2,1,0:T(8,128)(2,1)} %param.8) | copy-start | bytes 5505028
  4.4 38.4 %collective-permute-start.9 = (bf16[2,2,224,512]{3,2,1,0:T(8,128)(2,1)}, bf16[2,2,224,512]{3,2,1,0:T(8,128)(2,1)}, u32[]{:S(2)}, u32[]{:S(2)}) collective-permute-start(bf16[2,2,224,512]{3,2,1,0:T(8,128)(2,1)} %get-tuple-element.65.refs_4_.refs_0_), channel_id=1, source_target_pairs={{0,2},{2,0},{1,3},{3,1},{4,6},{6,4},{5,7},{7,5},{8,10},{10,8},{9,1... | collective-permute-start | bytes 2752520 | tf_op jit(solution)/shard_map/ppermute | solution.py:351
  9.5 4.8 %collective-permute-start.1 = (bf16[432,128]{1,0:T(8,128)(2,1)S(1)}, bf16[432,128]{1,0:T(8,128)(2,1)S(1)}, u32[]{:S(2)}, u32[]{:S(2)}) collective-permute-start(bf16[432,128]{1,0:T(8,128)(2,1)S(1)} %get-tuple-element.69.refs_4_), channel_id=1, source_target_pairs={{0,4},{4,0},{8,12},{12,8},{16,20},{20,16},{24,28},{28,24},{1,5},{5... | collective-permute-start | bytes 331784 | tf_op jit(solution)/shard_map/ppermute | solution.py:351
  13.4 6.1 %collective-permute-start = (bf16[560,128]{1,0:T(8,128)(2,1)S(1)}, bf16[560,128]{1,0:T(8,128)(2,1)S(1)}, u32[]{:S(2)}, u32[]{:S(2)}) collective-permute-start(bf16[560,128]{1,0:T(8,128)(2,1)S(1)} %get-tuple-element.71.refs_3_), channel_id=1, source_target_pairs={{0,4},{4,0},{8,12},{12,8},{16,20},{20,16},{24,28},{28,24},{1,5},{5... | collective-permute-start | bytes 430088 | tf_op jit(solution)/shard_map/ppermute | solution.py:351
  14.9 8.7 %collective-permute-start.2 = (bf16[432,128]{1,0:T(8,128)(2,1)S(1)}, bf16[432,128]{1,0:T(8,128)(2,1)S(1)}, u32[]{:S(2)}, u32[]{:S(2)}) collective-permute-start(bf16[432,128]{1,0:T(8,128)(2,1)S(1)} %get-tuple-element.73.refs_3_), channel_id=1, source_target_pairs={{8,0},{12,4},{16,8},{20,12},{24,16},{28,20},{9,1},{13,5},{17,9},{2... | collective-permute-start | bytes 331784 | tf_op jit(solution)/shard_map/ppermute | solution.py:355
  16.2 15.2 %collective-permute-start.4 = (bf16[1,2,224,512]{3,2,1,0:T(8,128)(2,1)S(1)}, bf16[1,2,224,512]{3,2,1,0:T(8,128)(2,1)S(1)}, u32[]{:S(2)}, u32[]{:S(2)}) collective-permute-start(bf16[1,2,224,512]{3,2,1,0:T(8,128)(2,1)S(1)} %get-tuple-element.81.refs_4_), channel_id=1, source_target_pairs={{0,4},{4,0},{8,12},{12,8},{16,20},{20,16},{24,28},{28,24},{1,5},{5... | collective-permute-start | bytes 1376264 | tf_op jit(solution)/shard_map/ppermute | solution.py:351
  19.5 2.1 %copy-start.1 = (s32[1,512,1792]{2,1,0:T(8,128)S(1)}, s32[1,512,1792]{2,1,0:T(8,128)}, u32[]{:S(2)}) copy-start(s32[1,512,1792]{2,1,0:T(8,128)} %param.10) | copy-start | bytes 11010052
  20.1 8.6 %collective-permute-start.5 = (bf16[560,128]{1,0:T(8,128)(2,1)S(1)}, bf16[560,128]{1,0:T(8,128)(2,1)S(1)}, u32[]{:S(2)}, u32[]{:S(2)}) collective-permute-start(bf16[560,128]{1,0:T(8,128)(2,1)S(1)} %get-tuple-element.75.refs_5_), channel_id=1, source_target_pairs={{8,0},{12,4},{16,8},{20,12},{24,16},{28,20},{9,1},{13,5},{17,9},{2... | collective-permute-start | bytes 430088 | tf_op jit(solution)/shard_map/ppermute | solution.py:355
  21.5 17.7 %collective-permute-start.8 = (bf16[1,2,224,512]{3,2,1,0:T(8,128)(2,1)S(1)}, bf16[1,2,224,512]{3,2,1,0:T(8,128)(2,1)S(1)}, u32[]{:S(2)}, u32[]{:S(2)}) collective-permute-start(bf16[1,2,224,512]{3,2,1,0:T(8,128)(2,1)S(1)} %get-tuple-element.90.refs_6_), channel_id=1, source_target_pairs={{0,4},{4,0},{8,12},{12,8},{16,20},{20,16},{24,28},{28,24},{1,5},{5... | collective-permute-start | bytes 1376264 | tf_op jit(solution)/shard_map/ppermute | solution.py:351
  24.8 7.5 %collective-permute-start.3 = (bf16[432,128]{1,0:T(8,128)(2,1)S(1)}, bf16[432,128]{1,0:T(8,128)(2,1)S(1)}, u32[]{:S(2)}, u32[]{:S(2)}) collective-permute-start(bf16[432,128]{1,0:T(8,128)(2,1)S(1)} %get-tuple-element.80.refs_5_), channel_id=1, source_target_pairs={{16,0},{20,4},{24,8},{28,12},{17,1},{21,5},{25,9},{29,13},{18,2},{... | collective-permute-start | bytes 331784 | tf_op jit(solution)/shard_map/ppermute | solution.py:355
  29.9 10.6 %collective-permute-start.7 = (bf16[560,128]{1,0:T(8,128)(2,1)S(1)}, bf16[560,128]{1,0:T(8,128)(2,1)S(1)}, u32[]{:S(2)}, u32[]{:S(2)}) collective-permute-start(bf16[560,128]{1,0:T(8,128)(2,1)S(1)} %get-tuple-element.87.refs_1_), channel_id=1, source_target_pairs={{16,0},{20,4},{24,8},{28,12},{17,1},{21,5},{25,9},{29,13},{18,2},{... | collective-permute-start | bytes 430088 | tf_op jit(solution)/shard_map/ppermute | solution.py:355
  31.5 16.2 %collective-permute-start.11 = (bf16[1,2,224,512]{3,2,1,0:T(8,128)(2,1)S(1)}, bf16[1,2,224,512]{3,2,1,0:T(8,128)(2,1)S(1)}, u32[]{:S(2)}, u32[]{:S(2)}) collective-permute-start(bf16[1,2,224,512]{3,2,1,0:T(8,128)(2,1)S(1)} %pass_on.2.refs_5_.refs_2_), channel_id=1, source_target_pairs={{0,2},{2,0},{1,3},{3,1},{4,6},{6,4},{5,7},{7,5},{8,10},{10,8},{9,1... | collective-permute-start | bytes 1376264 | tf_op jit(solution)/shard_map/ppermute | solution.py:351
  33.0 9.8 %collective-permute-start.6 = (bf16[384,128]{1,0:T(8,128)(2,1)S(1)}, bf16[384,128]{1,0:T(8,128)(2,1)S(1)}, u32[]{:S(2)}, u32[]{:S(2)}) collective-permute-start(bf16[384,128]{1,0:T(8,128)(2,1)S(1)} %get-tuple-element.89.refs_1_), channel_id=1, source_target_pairs={{0,4},{4,0},{8,12},{12,8},{16,20},{20,16},{24,28},{28,24},{1,5},{5... | collective-permute-start | bytes 294920 | tf_op jit(solution)/shard_map/ppermute | solution.py:351
  39.3 14.0 %collective-permute-start.12 = (bf16[1,2,224,512]{3,2,1,0:T(8,128)(2,1)S(1)}, bf16[1,2,224,512]{3,2,1,0:T(8,128)(2,1)S(1)}, u32[]{:S(2)}, u32[]{:S(2)}) collective-permute-start(bf16[1,2,224,512]{3,2,1,0:T(8,128)(2,1)S(1)} %pass_on.3.refs_5_.refs_3_), channel_id=1, source_target_pairs={{0,2},{2,0},{1,3},{3,1},{4,6},{6,4},{5,7},{7,5},{8,10},{10,8},{9,1... | collective-permute-start | bytes 1376264 | tf_op jit(solution)/shard_map/ppermute | solution.py:351
  41.2 6.4 %collective-permute-start.10 = (bf16[512,128]{1,0:T(8,128)(2,1)S(1)}, bf16[512,128]{1,0:T(8,128)(2,1)S(1)}, u32[]{:S(2)}, u32[]{:S(2)}) collective-permute-start(bf16[512,128]{1,0:T(8,128)(2,1)S(1)} %get-tuple-element.91.refs_6_), channel_id=1, source_target_pairs={{0,4},{4,0},{8,12},{12,8},{16,20},{20,16},{24,28},{28,24},{1,5},{5... | collective-permute-start | bytes 393224 | tf_op jit(solution)/shard_map/ppermute | solution.py:351
  43.7 37.3 %copy-start.4 = (bf16[512,384]{1,0:T(8,128)(2,1)}, bf16[512,384]{1,0:T(8,128)(2,1)S(1)}, u32[]{:S(2)}) copy-start(bf16[512,384]{1,0:T(8,128)(2,1)S(1)} %value_grad.4.refs_6_.refs_4_.refs_1_.refs_2_) | copy-start | bytes 1179652
  43.7 12.3 %collective-permute-start.14 = (bf16[512,384]{1,0:T(8,128)(2,1)S(1)}, bf16[512,384]{1,0:T(8,128)(2,1)S(1)}, u32[]{:S(2)}, u32[]{:S(2)}) collective-permute-start(bf16[512,384]{1,0:T(8,128)(2,1)S(1)} %value_grad.4.refs_6_.refs_4_.refs_1_.refs_2_), channel_id=1, source_target_pairs={{0,4},{4,0},{8,12},{12,8},{16,20},{20,16},{24,28},{28,24},{1,5},{5... | collective-permute-start | bytes 1179656 | tf_op jit(solution)/shard_map/ppermute | solution.py:351
  45.2 35.8 %copy-start.6 = (bf16[512,384]{1,0:T(8,128)(2,1)}, bf16[512,384]{1,0:T(8,128)(2,1)S(1)}, u32[]{:S(2)}) copy-start(bf16[512,384]{1,0:T(8,128)(2,1)S(1)} %value_grad.5.refs_6_.refs_2_.refs_4_.refs_3_) | copy-start | bytes 1179652
  45.2 19.2 %collective-permute-start.17 = (bf16[512,384]{1,0:T(8,128)(2,1)S(1)}, bf16[512,384]{1,0:T(8,128)(2,1)S(1)}, u32[]{:S(2)}, u32[]{:S(2)}) collective-permute-start(bf16[512,384]{1,0:T(8,128)(2,1)S(1)} %value_grad.5.refs_6_.refs_2_.refs_4_.refs_3_), channel_id=1, source_target_pairs={{0,4},{4,0},{8,12},{12,8},{16,20},{20,16},{24,28},{28,24},{1,5},{5... | collective-permute-start | bytes 1179656 | tf_op jit(solution)/shard_map/ppermute | solution.py:351
  49.4 28.2 %collective-permute-start.13 = (bf16[512,512]{1,0:T(8,128)(2,1)}, bf16[512,512]{1,0:T(8,128)(2,1)}, u32[]{:S(2)}, u32[]{:S(2)}) collective-permute-start(bf16[512,512]{1,0:T(8,128)(2,1)} %value_grad.6.refs_6_.refs_3_.refs_4_), channel_id=1, source_target_pairs={{0,4},{4,0},{8,12},{12,8},{16,20},{20,16},{24,28},{28,24},{1,5},{5... | collective-permute-start | bytes 1572872 | tf_op jit(solution)/shard_map/ppermute | solution.py:351
  52.9 37.1 %collective-permute-start.21 = (bf16[512,512]{1,0:T(8,128)(2,1)}, bf16[512,512]{1,0:T(8,128)(2,1)}, u32[]{:S(2)}, u32[]{:S(2)}) collective-permute-start(bf16[512,512]{1,0:T(8,128)(2,1)} %value_grad.7.refs_6_.refs_4_.refs_5_), channel_id=1, source_target_pairs={{0,4},{4,0},{8,12},{12,8},{16,20},{20,16},{24,28},{28,24},{1,5},{5... | collective-permute-start | bytes 1572872 | tf_op jit(solution)/shard_map/ppermute | solution.py:351
  53.3 4.9 %slice-start = ((s8[12845056]{0:T(1024)(128)(4,1)}), s8[4194304]{0:T(1024)(128)(4,1)S(1)}, s32[]{:S(2)}) async-start(s8[12845056]{0:T(1024)(128)(4,1)} %bitcast.16), calls=%async_computation | async-start | bytes 8388608
  53.3 4.9 %slice-start.1 = ((s8[12845056]{0:T(1024)(128)(4,1)}), s8[4194304]{0:T(1024)(128)(4,1)S(1)}, s32[]{:S(2)}) async-start(s8[12845056]{0:T(1024)(128)(4,1)} %bitcast.16), calls=%async_computation.1 | async-start | bytes 8388608
  56.1 2.7 %slice-start.2 = ((s8[12845056]{0:T(1024)(128)(4,1)}), s8[4194304]{0:T(1024)(128)(4,1)S(1)}, s32[]{:S(2)}) async-start(s8[12845056]{0:T(1024)(128)(4,1)} %bitcast.16), calls=%async_computation.2 | async-start | bytes 8388608
  56.1 2.7 %slice-start.3 = ((s8[12845056]{0:T(1024)(128)(4,1)}), s8[262144]{0:T(1024)(128)(4,1)S(1)}, s32[]{:S(2)}) async-start(s8[12845056]{0:T(1024)(128)(4,1)} %bitcast.16), calls=%async_computation.3 | async-start | bytes 524288
  58.1 3.9 %collective-permute-start.15 = (bf16[4,224,384]{2,1,0:T(8,128)(2,1)S(1)}, bf16[4,224,384]{2,1,0:T(8,128)(2,1)S(1)}, u32[]{:S(2)}, u32[]{:S(2)}) collective-permute-start(bf16[4,224,384]{2,1,0:T(8,128)(2,1)S(1)} %get-tuple-element.99), channel_id=1, source_target_pairs={{0,1},{1,0},{2,3},{3,2},{4,5},{5,4},{6,7},{7,6},{8,9},{9,8},{10,11... | collective-permute-start | bytes 2064392 | tf_op jit(solution)/shard_map/ppermute | solution.py:351
  62.7 11.6 %collective-permute-start.16 = (bf16[2,224,384]{2,1,0:T(8,128)(2,1)S(1)}, bf16[2,224,384]{2,1,0:T(8,128)(2,1)S(1)}, u32[]{:S(2)}, u32[]{:S(2)}) collective-permute-start(bf16[2,224,384]{2,1,0:T(8,128)(2,1)S(1)} %get-tuple-element.101.refs_6_), channel_id=1, source_target_pairs={{0,8},{4,12},{8,0},{12,4},{16,24},{20,28},{24,16},{28,20},{1,9},{5... | collective-permute-start | bytes 1032200 | tf_op jit(solution)/shard_map/ppermute | solution.py:351
  66.6 5.6 %collective-permute-start.18 = (bf16[4,224,384]{2,1,0:T(8,128)(2,1)S(1)}, bf16[4,224,384]{2,1,0:T(8,128)(2,1)S(1)}, u32[]{:S(2)}, u32[]{:S(2)}) collective-permute-start(bf16[4,224,384]{2,1,0:T(8,128)(2,1)S(1)} %get-tuple-element.103), channel_id=1, source_target_pairs={{0,1},{1,0},{2,3},{3,2},{4,5},{5,4},{6,7},{7,6},{8,9},{9,8},{10,11... | collective-permute-start | bytes 2064392 | tf_op jit(solution)/shard_map/ppermute | solution.py:351
  71.2 46.2 %collective-permute-start.25 = (bf16[512,1792]{1,0:T(8,128)(2,1)}, bf16[512,1792]{1,0:T(8,128)(2,1)}, u32[]{:S(2)}, u32[]{:S(2)}) collective-permute-start(bf16[512,1792]{1,0:T(8,128)(2,1)} %input_part.5.refs_3_), channel_id=1, source_target_pairs={{0,2},{2,0},{1,3},{3,1},{4,6},{6,4},{5,7},{7,5},{8,10},{10,8},{9,1... | collective-permute-start | bytes 5505032 | tf_op jit(solution)/shard_map/ppermute | solution.py:351
  72.8 13.9 %collective-permute-start.22 = (bf16[2,224,384]{2,1,0:T(8,128)(2,1)S(1)}, bf16[2,224,384]{2,1,0:T(8,128)(2,1)S(1)}, u32[]{:S(2)}, u32[]{:S(2)}) collective-permute-start(bf16[2,224,384]{2,1,0:T(8,128)(2,1)S(1)} %get-tuple-element.104.refs_3_), channel_id=1, source_target_pairs={{0,8},{4,12},{8,0},{12,4},{16,24},{20,28},{24,16},{28,20},{1,9},{5... | collective-permute-start | bytes 1032200 | tf_op jit(solution)/shard_map/ppermute | solution.py:351
  75.0 18.5 %collective-permute-start.24 = (bf16[1,224,384]{2,1,0:T(8,128)(2,1)S(1)}, bf16[1,224,384]{2,1,0:T(8,128)(2,1)S(1)}, u32[]{:S(2)}, u32[]{:S(2)}) collective-permute-start(bf16[1,224,384]{2,1,0:T(8,128)(2,1)S(1)} %get-tuple-element.105.refs_6_), channel_id=1, source_target_pairs={{0,16},{4,20},{8,24},{12,28},{16,0},{20,4},{24,8},{28,12},{1,17},{... | collective-permute-start | bytes 516104 | tf_op jit(solution)/shard_map/ppermute | solution.py:351
  80.9 3.4 %collective-permute-start.19 = (bf16[4,224,512]{2,1,0:T(8,128)(2,1)S(1)}, bf16[4,224,512]{2,1,0:T(8,128)(2,1)S(1)}, u32[]{:S(2)}, u32[]{:S(2)}) collective-permute-start(bf16[4,224,512]{2,1,0:T(8,128)(2,1)S(1)} %get-tuple-element.107), channel_id=1, source_target_pairs={{0,1},{1,0},{2,3},{3,2},{4,5},{5,4},{6,7},{7,6},{8,9},{9,8},{10,11... | collective-permute-start | bytes 2752520 | tf_op jit(solution)/shard_map/ppermute | solution.py:351
  85.1 17.1 %collective-permute-start.20 = (bf16[2,224,512]{2,1,0:T(8,128)(2,1)S(1)}, bf16[2,224,512]{2,1,0:T(8,128)(2,1)S(1)}, u32[]{:S(2)}, u32[]{:S(2)}) collective-permute-start(bf16[2,224,512]{2,1,0:T(8,128)(2,1)S(1)} %get-tuple-element.109.refs_3_), channel_id=1, source_target_pairs={{0,8},{4,12},{8,0},{12,4},{16,24},{20,28},{24,16},{28,20},{1,9},{5... | collective-permute-start | bytes 1376264 | tf_op jit(solution)/shard_map/ppermute | solution.py:351
  88.0 32.6 %collective-permute-start.28 = (bf16[1,224,384]{2,1,0:T(8,128)(2,1)}, bf16[1,224,384]{2,1,0:T(8,128)(2,1)}, u32[]{:S(2)}, u32[]{:S(2)}) collective-permute-start(bf16[1,224,384]{2,1,0:T(8,128)(2,1)} %get-tuple-element.111.refs_6_), channel_id=1, source_target_pairs={{0,16},{4,20},{8,24},{12,28},{16,0},{20,4},{24,8},{28,12},{1,17},{... | collective-permute-start | bytes 516104 | tf_op jit(solution)/shard_map/ppermute | solution.py:351
  93.4 2.5 %collective-permute-start.23 = (bf16[4,224,512]{2,1,0:T(8,128)(2,1)S(1)}, bf16[4,224,512]{2,1,0:T(8,128)(2,1)S(1)}, u32[]{:S(2)}, u32[]{:S(2)}) collective-permute-start(bf16[4,224,512]{2,1,0:T(8,128)(2,1)S(1)} %get-tuple-element.113), channel_id=1, source_target_pairs={{0,1},{1,0},{2,3},{3,2},{4,5},{5,4},{6,7},{7,6},{8,9},{9,8},{10,11... | collective-permute-start | bytes 2752520 | tf_op jit(solution)/shard_map/ppermute | solution.py:351
  93.5 0.7 copy-start.8
  96.6 15.4 %collective-permute-start.27 = (bf16[2,224,256]{2,1,0:T(8,128)(2,1)S(1)}, bf16[2,224,256]{2,1,0:T(8,128)(2,1)S(1)}, u32[]{:S(2)}, u32[]{:S(2)}) collective-permute-start(bf16[2,224,256]{2,1,0:T(8,128)(2,1)S(1)} %get-tuple-element.114.refs_3_), channel_id=1, source_target_pairs={{0,8},{4,12},{8,0},{12,4},{16,24},{20,28},{24,16},{28,20},{1,9},{5... | collective-permute-start | bytes 688136 | tf_op jit(solution)/shard_map/ppermute | solution.py:351
  99.8 16.8 %collective-permute-start.26 = (bf16[2,224,256]{2,1,0:T(8,128)(2,1)S(1)}, bf16[2,224,256]{2,1,0:T(8,128)(2,1)S(1)}, u32[]{:S(2)}, u32[]{:S(2)}) collective-permute-start(bf16[2,224,256]{2,1,0:T(8,128)(2,1)S(1)} %get-tuple-element.115.refs_3_), channel_id=1, source_target_pairs={{0,8},{4,12},{8,0},{12,4},{16,24},{20,28},{24,16},{28,20},{1,9},{5... | collective-permute-start | bytes 688136 | tf_op jit(solution)/shard_map/ppermute | solution.py:351
  102.2 1.0 slice-start.4
  102.2 2.3 %slice-start.5 = ((s8[12845056]{0:T(1024)(128)(4,1)}), s8[4194304]{0:T(1024)(128)(4,1)S(1)}, s32[]{:S(2)}) async-start(s8[12845056]{0:T(1024)(128)(4,1)} %bitcast.18), calls=%async_computation.5 | async-start | bytes 8388608
  102.8 3.0 %slice-start.6 = ((s8[12845056]{0:T(1024)(128)(4,1)}), s8[4194304]{0:T(1024)(128)(4,1)S(1)}, s32[]{:S(2)}) async-start(s8[12845056]{0:T(1024)(128)(4,1)} %bitcast.18), calls=%async_computation.6 | async-start | bytes 8388608
  102.9 4.2 %slice-start.7 = ((s8[12845056]{0:T(1024)(128)(4,1)}), s8[4194304]{0:T(1024)(128)(4,1)S(1)}, s32[]{:S(2)}) async-start(s8[12845056]{0:T(1024)(128)(4,1)} %bitcast.18), calls=%async_computation.7 | async-start | bytes 8388608
  102.9 4.2 %copy-start.5 = (bf16[512,384]{1,0:T(8,128)(2,1)S(1)}, bf16[512,384]{1,0:T(8,128)(2,1)}, u32[]{:S(2)}) copy-start(bf16[512,384]{1,0:T(8,128)(2,1)} %copy-done.4) | copy-start | bytes 1179652
  102.9 4.3 %copy-start.7 = (bf16[512,384]{1,0:T(8,128)(2,1)S(1)}, bf16[512,384]{1,0:T(8,128)(2,1)}, u32[]{:S(2)}) copy-start(bf16[512,384]{1,0:T(8,128)(2,1)} %copy-done.6) | copy-start | bytes 1179652
  102.9 17.6 %collective-permute-start.29 = (bf16[1,224,512]{2,1,0:T(8,128)(2,1)S(1)}, bf16[1,224,512]{2,1,0:T(8,128)(2,1)S(1)}, u32[]{:S(2)}, u32[]{:S(2)}) collective-permute-start(bf16[1,224,512]{2,1,0:T(8,128)(2,1)S(1)} %get-tuple-element.116.refs_0_), channel_id=1, source_target_pairs={{0,16},{4,20},{8,24},{12,28},{16,0},{20,4},{24,8},{28,12},{1,17},{... | collective-permute-start | bytes 688136 | tf_op jit(solution)/shard_map/ppermute | solution.py:351
  112.6 11.8 %collective-permute-start.30 = (bf16[1,224,256]{2,1,0:T(8,128)(2,1)S(1)}, bf16[1,224,256]{2,1,0:T(8,128)(2,1)S(1)}, u32[]{:S(2)}, u32[]{:S(2)}) collective-permute-start(bf16[1,224,256]{2,1,0:T(8,128)(2,1)S(1)} %get-tuple-element.119.refs_3_), channel_id=1, source_target_pairs={{0,16},{4,20},{8,24},{12,28},{16,0},{20,4},{24,8},{28,12},{1,17},{... | collective-permute-start | bytes 344072 | tf_op jit(solution)/shard_map/ppermute | solution.py:351
  117.2 9.6 %copy-start.9 = (bf16[1,224,384]{2,1,0:T(8,128)(2,1)S(1)}, bf16[1,224,384]{2,1,0:T(8,128)(2,1)}, u32[]{:S(2)}) copy-start(bf16[1,224,384]{2,1,0:T(8,128)(2,1)} %copy-done.8) | copy-start | bytes 516100
  117.2 9.6 %collective-permute-start.31 = (bf16[1,224,256]{2,1,0:T(8,128)(2,1)S(1)}, bf16[1,224,256]{2,1,0:T(8,128)(2,1)S(1)}, u32[]{:S(2)}, u32[]{:S(2)}) collective-permute-start(bf16[1,224,256]{2,1,0:T(8,128)(2,1)S(1)} %get-tuple-element.120.refs_2_), channel_id=1, source_target_pairs={{0,16},{4,20},{8,24},{12,28},{16,0},{20,4},{24,8},{28,12},{1,17},{... | collective-permute-start | bytes 344072 | tf_op jit(solution)/shard_map/ppermute | solution.py:351

commit v5 on v4

--- a/solution.py
+++ b/solution.py
@@ -13,7 +13,7 @@
 HD = 128
 PLANE = 16
 EXTRA = 3 * PLANE
-PARAMS = pltpu.CompilerParams(vmem_limit_bytes=12 * 1024 * 1024)
+PARAMS = pltpu.CompilerParams(vmem_limit_bytes=6 * 1024 * 1024)
 VM = pl.BlockSpec(memory_space=pltpu.VMEM)
 SM = pl.BlockSpec(memory_space=pltpu.SMEM)
 ANY = pl.BlockSpec(memory_space=pl.ANY)
@@ -267,26 +267,35 @@
     return line(kernel, "value_grad", outs, [flags], arrays, after)[0]
 
 
-def input_kernel(rows, at, first, count, flags_ref, *refs):
-    *vs, w_ref, o_ref, v_all = refs[count:]
+def join_and_input_kernel(rows, at, flags_ref, *refs):
+    *vs, w_ref, o_ref, v_all = refs
     start = 0
     for v in vs:
         v_all[:, start : start + v.shape[1]] = v[...]
         start += v.shape[1]
+    input_kernel(rows, at, 0, flags_ref, v_all, w_ref, o_ref)
+
+
+def input_kernel(rows, at, first, flags_ref, *refs):
+    *before, v_ref, w_ref, o_ref = refs
+    for done in before:
+        o_ref[:, :first] = done[...]
     cols = o_ref.shape[1] - first
     w = w_ref[pl.ds(pl.multiple_of(flags_ref[at] * rows + first, 128), cols), :]
-    for before in refs[:count]:
-        o_ref[:, :first] = before[...]
-    o_ref[:, first:] = dot(v_all[...], w, ((1,), (1,))).astype(o_ref.dtype)
-
-
-def input_part(line, flags, at, vs, w, rows, dtype, end, before=()):
+    o_ref[:, first:] = dot(v_ref[...], w, ((1,), (1,))).astype(o_ref.dtype)
+
+
+def first_input_part(line, flags, at, vs, w, rows, dtype, end):
     tokens, features = vs[0].shape[0], w.shape[1]
+    outs = [((tokens, end), dtype), ((tokens, features), BF)]
+    kernel = functools.partial(join_and_input_kernel, rows, at)
+    return line(kernel, "input_part", outs, [flags], [*vs, w])
+
+
+def input_part(line, flags, at, v, w, rows, dtype, end, before=()):
     first = before[0].shape[1] if before else 0
-    scratch = [pltpu.VMEM((tokens, features), BF)]
-    kernel = functools.partial(input_kernel, rows, at, first, len(before))
-    outs = [((tokens, end), dtype)]
-    return line(kernel, "input_part", outs, [flags], [*before, *vs, w], (), scratch)[0]
+    kernel = functools.partial(input_kernel, rows, at, first)
+    return line(kernel, "input_part", [((v.shape[0], end), dtype)], [flags], [*before, v, w])[0]
 
 
 def last_input_kernel(total_ref, *refs):
@@ -436,12 +445,9 @@
         away, keep = weight_part(line, pieces, (values[i], from_y[i]), after)
         parts[i] = (keep, swap_with(away, "dp", 1))
 
-    def over_dp(i, *widths):
-        start = 0
-        for j, width in enumerate(widths or [None]):
-            away, keep = fold(line, flags, at_steps, *parts[i], start, width)
-            kept[i, j] = (keep, swap_with(away, "seq", 2 << bits[0]))
-            start += width or 0
+    def over_dp(i, j=0, start=0, width=None):
+        away, keep = fold(line, flags, at_steps, *parts[i], start, width)
+        kept[i, j] = (keep, swap_with(away, "seq", 2 << bits[0]))
 
     def over_z(i, j=0):
         for step, bit in enumerate(bits[1:], 1):
@@ -452,14 +458,23 @@
     middle = rows_here // 2 if rows_here % 256 == 0 else 0
 
     def input_parts(at, dtype, step):
-        if step == 0:
-            if not middle:
-                return pause(line)
-            halves_done[at] = [input_part(line, flags, at, values, value_weight, rows_here, dtype, middle)]
+        common = (value_weight, rows_here, dtype)
+        if step == 0 and not middle:
+            return pause(line)
+        if step == 0 and not all_values:
+            part, v = first_input_part(line, flags, at, values, *common, middle)
+            all_values.append(v)
+            halves_done[at] = [part]
+        elif step == 0:
+            halves_done[at] = [input_part(line, flags, at, all_values[0], *common, middle)]
+        elif not all_values:
+            part, v = first_input_part(line, flags, at, values, *common, rows_here)
+            all_values.append(v)
+            return part
         else:
-            before = halves_done.get(at, ())
-            return input_part(line, flags, at, values, value_weight, rows_here, dtype, rows_here, before)
-
+            return input_part(line, flags, at, all_values[0], *common, rows_here, halves_done.get(at, ()))
+
+    all_values = []
     halves_done = {}
 
     def input_others(step):
@@ -518,15 +533,15 @@
         matmul(2)
         input_parts(at_sides, F32, 0)
         over_dp(2)
-        over_z(1)
         matmul(3)
         pause(line, [kept[0, 0][1]])
-        over_dp(3, splits[1][1] // 2 * HD, (splits[1][1] + 1) // 2 * HD)
+        over_z(1)
+        over_dp(3, 0, 0, splits[1][1] // 2 * HD)
+        over_dp(3, 1, splits[1][1] // 2 * HD, (splits[1][1] + 1) // 2 * HD)
         over_z(2)
-        pause(line)
-        total = input_parts(at_sides, F32, 1)
         over_z(3, 0)
         over_z(3, 1)
+        total = input_parts(at_sides, F32, 1)
     else:
         matmul(0)
         matmul(1)

time: 129 us -> 128 us (level)
  waiting for transfers between devices: 25.4 us -> 30.4 us
  local copies, waits for them, and re-layouts: 7 us -> 2.13 us
  Pallas kernels: 61.4 us -> 57.6 us
  starting transfers between devices: 34.2 us -> 36.3 us
    ppermute x28, waiting for transfers between devices: 25 us -> 30 us  [swap_with(): lax.ppermute(x, axis, [(i, i ^ bit) for i in range(lax.axis_size(axis))])]
    unnamed x39 -> x27, local copies, waits for them, and re-layouts: 6.91 us -> 2.04 us
    pallas_call x40 -> x39, Pallas kernels: 61.4 us -> 57.6 us  [__call__(): pl.pallas_call(body, in_specs=[SM] * len(smalls) + [VM] * len(arrays) + [...]
    ppermute x28, starting transfers between devices: 28.7 us -> 30.8 us  [swap_with(): lax.ppermute(x, axis, [(i, i ^ bit) for i in range(lax.axis_size(axis))])]
  transfers between devices with their start and end apart: 32 -> 32, of which waited for: 15 -> 13; matrix products, arithmetic and copies ran while one was open for 0% -> 0% of each run, Pallas kernels for 44% -> 42%
where the time goes in v5:
time: 128 us; the launch traced here: 127 us
  Pallas kernels  57.6 us (45%)
  starting transfers between devices  36.3 us (28%)
  waiting for transfers between devices  30.4 us (24%)
  local copies, waits for them, and re-layouts  2.13 us (2%)
    pallas_call x39, Pallas kernels, __call__(): pl.pallas_call(body, in_specs=[SM] * len(smalls) + [VM] * len(arrays) + [...  57.6 us
    ppermute x28, starting transfers between devices, swap_with(): lax.ppermute(x, axis, [(i, i ^ bit) for i in range(lax.axis_size(axis))])  30.8 us
    ppermute x28, waiting for transfers between devices, swap_with(): lax.ppermute(x, axis, [(i, i ^ bit) for i in range(lax.axis_size(axis))])  30 us
    ppermute x4, starting transfers between devices, from_later(): lax.ppermute(x, axis, [(i, i - shift) for i in range(shift, lax.axis_size...  5.46 us
  transfers between devices with their start and end apart: 32, of which 13 were waited for; matrix products, arithmetic and copies ran while one was open for 0% of the time, Pallas kernels for 42%

profile of v5, /device:TPU:0, one launch (start us, length us, event | category | flops | bytes accessed | tf_op | source)
XLA Modules:
  0.0 127.4 jit_solution(6481383543065500297)
XLA Ops:
  0.8 1.5 %copy-done.2 = bf16[1,512,1792]{2,1,0:T(8,128)(2,1)S(1)} copy-done((bf16[1,512,1792]{2,1,0:T(8,128)(2,1)S(1)}, bf16[1,512,1792]{2,1,0:T(8,128)(2,1)}, u32[]{:S(2)}) %copy-start.2) | copy-done | bytes 1835032
  2.3 2.1 %transpose_inputs.1 = (bf16[2,2,224,512]{3,2,1,0:T(8,128)(2,1)}, bf16[1,2,224,512]{3,2,1,0:T(8,128)(2,1)S(1)}, bf16[1,2,224,512]{3,2,1,0:T(8,128)(2,1)S(1)}) custom-call(s32[8]{0:T(128)S(1)} %stack.27.refs_0_, bf16[512,1792]{1,0:T(8,128)(2,1)S(1)} %bitcast.24), custom_call_target="tpu_custom_call" | custom-call | flops 20000000000 | tf_op jit(solution)/shard_map/transpose_inputs/pallas_call | solution.py:45
  4.4 2.9 %collective-permute-start.9 = (bf16[2,2,224,512]{3,2,1,0:T(8,128)(2,1)}, bf16[2,2,224,512]{3,2,1,0:T(8,128)(2,1)}, u32[]{:S(2)}, u32[]{:S(2)}) collective-permute-start(bf16[2,2,224,512]{3,2,1,0:T(8,128)(2,1)} %get-tuple-element.67.refs_4_.refs_0_), channel_id=1, source_target_pairs={{0,2},{2,0},{1,3},{3,1},{4,6},{6,4},{5,7},{7,5},{8,10},{10,8},{9,1... | collective-permute-start | bytes 2752520 | tf_op jit(solution)/shard_map/ppermute | solution.py:360
  7.3 2.1 %state_terms.2 = (bf16[432,128]{1,0:T(8,128)(2,1)S(1)}, f32[432,128]{1,0:T(8,128)S(1)}, f32[16,512]{1,0:T(8,128)S(1)}, f32[512,128]{1,0:T(8,128)S(1)}, bf16[512,768]{1,0:T(8,128)(2,1)S(1)}) custom-call(s32[8]{0:T(128)S(1)} %stack.27.refs_0_, f32[14,512]{1,0:T(8,128)S(1)} %bitcast.14, s32[512,1792]{1,0:T(8,128)S(1)} %bitcast.20, ...), custom_call_target="tpu_custom_call" | custom-call | flops 20000000000 | tf_op jit(solution)/shard_map/state_terms/pallas_call | solution.py:45
  9.5 1.6 %collective-permute-start.1 = (bf16[432,128]{1,0:T(8,128)(2,1)S(1)}, bf16[432,128]{1,0:T(8,128)(2,1)S(1)}, u32[]{:S(2)}, u32[]{:S(2)}) collective-permute-start(bf16[432,128]{1,0:T(8,128)(2,1)S(1)} %get-tuple-element.71.refs_4_), channel_id=1, source_target_pairs={{0,4},{4,0},{8,12},{12,8},{16,20},{20,16},{24,28},{28,24},{1,5},{5... | collective-permute-start | bytes 331784 | tf_op jit(solution)/shard_map/ppermute | solution.py:360
  11.0 2.3 %state_terms.3 = (bf16[560,128]{1,0:T(8,128)(2,1)S(1)}, f32[560,128]{1,0:T(8,128)S(1)}, f32[16,512]{1,0:T(8,128)S(1)}, f32[512,128]{1,0:T(8,128)S(1)}, bf16[512,1024]{1,0:T(8,128)(2,1)S(1)}) custom-call(s32[8]{0:T(128)S(1)} %stack.27.refs_0_, f32[14,512]{1,0:T(8,128)S(1)} %bitcast.15, s32[512,1792]{1,0:T(8,128)S(1)} %bitcast.21, ...), custom_call_target="tpu_custom_call" | custom-call | flops 20000000000 | tf_op jit(solution)/shard_map/state_terms/pallas_call | solution.py:45
  14.9 1.3 %collective-permute-start.2 = (bf16[432,128]{1,0:T(8,128)(2,1)S(1)}, bf16[432,128]{1,0:T(8,128)(2,1)S(1)}, u32[]{:S(2)}, u32[]{:S(2)}) collective-permute-start(bf16[432,128]{1,0:T(8,128)(2,1)S(1)} %get-tuple-element.75.refs_3_), channel_id=1, source_target_pairs={{8,0},{12,4},{16,8},{20,12},{24,16},{28,20},{9,1},{13,5},{17,9},{2... | collective-permute-start | bytes 331784 | tf_op jit(solution)/shard_map/ppermute | solution.py:364
  16.2 1.6 %collective-permute-start.4 = (bf16[1,2,224,512]{3,2,1,0:T(8,128)(2,1)S(1)}, bf16[1,2,224,512]{3,2,1,0:T(8,128)(2,1)S(1)}, u32[]{:S(2)}, u32[]{:S(2)}) collective-permute-start(bf16[1,2,224,512]{3,2,1,0:T(8,128)(2,1)S(1)} %get-tuple-element.83.refs_4_), channel_id=1, source_target_pairs={{0,4},{4,0},{8,12},{12,8},{16,20},{20,16},{24,28},{28,24},{1,5},{5... | collective-permute-start | bytes 1376264 | tf_op jit(solution)/shard_map/ppermute | solution.py:360
  17.7 1.7 %collective-permute-done.refs_2_ = bf16[560,128]{1,0:T(8,128)(2,1)S(1)} collective-permute-done((bf16[560,128]{1,0:T(8,128)(2,1)S(1)}, bf16[560,128]{1,0:T(8,128)(2,1)S(1)}, u32[]{:S(2)}, u32[]{:S(2)}) %collective-permute-start) | collective-permute-done | bytes 143392 | tf_op jit(solution)/shard_map/ppermute | solution.py:360
  20.1 1.4 %collective-permute-start.5 = (bf16[560,128]{1,0:T(8,128)(2,1)S(1)}, bf16[560,128]{1,0:T(8,128)(2,1)S(1)}, u32[]{:S(2)}, u32[]{:S(2)}) collective-permute-start(bf16[560,128]{1,0:T(8,128)(2,1)S(1)} %get-tuple-element.77.refs_5_), channel_id=1, source_target_pairs={{8,0},{12,4},{16,8},{20,12},{24,16},{28,20},{9,1},{13,5},{17,9},{2... | collective-permute-start | bytes 430088 | tf_op jit(solution)/shard_map/ppermute | solution.py:364
  21.6 1.9 %local_part.2 = (f32[512,768]{1,0:T(8,128)S(1)}, bf16[512,768]{1,0:T(8,128)(2,1)S(1)}) custom-call(bf16[512,768]{1,0:T(8,128)(2,1)S(1)} %get-tuple-element.68.refs_0_, s32[512,1792]{1,0:T(8,128)S(1)} %bitcast.22, bf16[512,1792]{1,0:T(8,128)(2,1)S(1)} %bitcast.27, f32[16,512]{1,0:T(8,128)S(1)} %get-tuple-element.69.refs_3_, ...), custom_call_target="tpu_custom_call" | custom-call | flops 20000000000 | tf_op jit(solution)/shard_map/local_part/pallas_call | solution.py:45
  23.5 1.3 join_states.6
  24.8 1.3 %collective-permute-start.3 = (bf16[432,128]{1,0:T(8,128)(2,1)S(1)}, bf16[432,128]{1,0:T(8,128)(2,1)S(1)}, u32[]{:S(2)}, u32[]{:S(2)}) collective-permute-start(bf16[432,128]{1,0:T(8,128)(2,1)S(1)} %get-tuple-element.82.refs_5_), channel_id=1, source_target_pairs={{16,0},{20,4},{24,8},{28,12},{17,1},{21,5},{25,9},{29,13},{18,2},{... | collective-permute-start | bytes 331784 | tf_op jit(solution)/shard_map/ppermute | solution.py:364
  26.1 2.5 %local_part.3 = (f32[512,1024]{1,0:T(8,128)S(1)}, bf16[512,1024]{1,0:T(8,128)(2,1)S(1)}) custom-call(bf16[512,1024]{1,0:T(8,128)(2,1)S(1)} %get-tuple-element.85.refs_0_, s32[512,1792]{1,0:T(8,128)S(1)} %bitcast.23, bf16[512,1792]{1,0:T(8,128)(2,1)S(1)} %bitcast.28, f32[16,512]{1,0:T(8,128)S(1)} %get-tuple-element.86.refs_3_, ...), custom_call_target="tpu_custom_call" | custom-call | flops 20000000000 | tf_op jit(solution)/shard_map/local_part/pallas_call | solution.py:45
  28.6 1.3 %join_states.7 = (bf16[560,128]{1,0:T(8,128)(2,1)S(1)}, f32[560,128]{1,0:T(8,128)}) custom-call(s32[8]{0:T(128)S(1)} %stack.27.refs_0_, f32[560,128]{1,0:T(8,128)S(1)} %get-tuple-element.84.refs_1_, bf16[560,128]{1,0:T(8,128)(2,1)S(1)} %collective-permute-done.5.refs_2_.refs_3_, f32[512,1024]{1,0:T(8,128)S(1)} %get-tuple-element.88.refs_3_.refs_2_), custom_call_target="tpu_custom_call" | custom-call | flops 20000000000 | tf_op jit(solution)/shard_map/join_states/pallas_call | solution.py:45
  29.9 1.5 %collective-permute-start.7 = (bf16[560,128]{1,0:T(8,128)(2,1)S(1)}, bf16[560,128]{1,0:T(8,128)(2,1)S(1)}, u32[]{:S(2)}, u32[]{:S(2)}) collective-permute-start(bf16[560,128]{1,0:T(8,128)(2,1)S(1)} %get-tuple-element.89.refs_1_), channel_id=1, source_target_pairs={{16,0},{20,4},{24,8},{28,12},{17,1},{21,5},{25,9},{29,13},{18,2},{... | collective-permute-start | bytes 430088 | tf_op jit(solution)/shard_map/ppermute | solution.py:364
  31.4 0.8 collective-permute-start.11
  32.3 0.6 carries.2
  33.0 2.1 %collective-permute-start.6 = (bf16[384,128]{1,0:T(8,128)(2,1)S(1)}, bf16[384,128]{1,0:T(8,128)(2,1)S(1)}, u32[]{:S(2)}, u32[]{:S(2)}) collective-permute-start(bf16[384,128]{1,0:T(8,128)(2,1)S(1)} %get-tuple-element.91.refs_1_), channel_id=1, source_target_pairs={{0,4},{4,0},{8,12},{12,8},{16,20},{20,16},{24,28},{28,24},{1,5},{5... | collective-permute-start | bytes 294920 | tf_op jit(solution)/shard_map/ppermute | solution.py:360
  35.0 4.2 %collective-permute-done.8.refs_0_ = bf16[1,2,224,512]{3,2,1,0:T(8,128)(2,1)S(1)} collective-permute-done((bf16[1,2,224,512]{3,2,1,0:T(8,128)(2,1)S(1)}, bf16[1,2,224,512]{3,2,1,0:T(8,128)(2,1)S(1)}, u32[]{:S(2)}, u32[]{:S(2)}) %collective-permute-start.8) | collective-permute-done | bytes 458784 | tf_op jit(solution)/shard_map/ppermute | solution.py:360
  39.3 1.0 collective-permute-start.12
  40.5 0.6 carries.3
  41.2 1.6 %collective-permute-start.10 = (bf16[512,128]{1,0:T(8,128)(2,1)S(1)}, bf16[512,128]{1,0:T(8,128)(2,1)S(1)}, u32[]{:S(2)}, u32[]{:S(2)}) collective-permute-start(bf16[512,128]{1,0:T(8,128)(2,1)S(1)} %get-tuple-element.93.refs_6_), channel_id=1, source_target_pairs={{0,4},{4,0},{8,12},{12,8},{16,20},{20,16},{24,28},{28,24},{1,5},{5... | collective-permute-start | bytes 393224 | tf_op jit(solution)/shard_map/ppermute | solution.py:360
  42.8 0.9 value_grad.4.refs_6_.refs_4_.refs_1_
  44.3 0.9 value_grad.5.refs_6_.refs_2_.refs_4_
  45.2 1.6 %collective-permute-start.17 = (bf16[512,384]{1,0:T(8,128)(2,1)S(1)}, bf16[512,384]{1,0:T(8,128)(2,1)S(1)}, u32[]{:S(2)}, u32[]{:S(2)}) collective-permute-start(bf16[512,384]{1,0:T(8,128)(2,1)S(1)} %value_grad.5.refs_6_.refs_2_.refs_4_), channel_id=1, source_target_pairs={{0,4},{4,0},{8,12},{12,8},{16,20},{20,16},{24,28},{28,24},{1,5},{5... | collective-permute-start | bytes 1179656 | tf_op jit(solution)/shard_map/ppermute | solution.py:360
  46.8 0.8 collective-permute-done.10.refs_5_
  47.6 1.8 %value_grad.6.refs_6_.refs_3_.refs_4_ = bf16[512,512]{1,0:T(8,128)(2,1)} custom-call(s32[8]{0:T(128)S(1)} %stack.27.refs_0_, bf16[512,1024]{1,0:T(8,128)(2,1)S(1)} %get-tuple-element.94.refs_1_, f32[512,1024]{1,0:T(8,128)S(1)} %get-tuple-element.88.refs_3_.refs_2_, f32[512,128]{1,0:T(8,128)S(1)} %get-tuple-element.87.refs_4_.refs_3_, ...), custom_call_target="tpu_custom_call" | custom-call | flops 20000000000 | tf_op jit(solution)/shard_map/value_grad/pallas_call | solution.py:45
  49.4 1.6 %collective-permute-start.14 = (bf16[512,512]{1,0:T(8,128)(2,1)}, bf16[512,512]{1,0:T(8,128)(2,1)}, u32[]{:S(2)}, u32[]{:S(2)}) collective-permute-start(bf16[512,512]{1,0:T(8,128)(2,1)} %value_grad.6.refs_6_.refs_3_.refs_4_), channel_id=1, source_target_pairs={{0,4},{4,0},{8,12},{12,8},{16,20},{20,16},{24,28},{28,24},{1,5},{5... | collective-permute-start | bytes 1572872 | tf_op jit(solution)/shard_map/ppermute | solution.py:360
  51.0 1.8 %value_grad.7.refs_6_.refs_4_ = bf16[512,512]{1,0:T(8,128)(2,1)} custom-call(s32[8]{0:T(128)S(1)} %stack.27.refs_0_, bf16[512,1024]{1,0:T(8,128)(2,1)S(1)} %get-tuple-element.94.refs_1_, f32[512,1024]{1,0:T(8,128)S(1)} %get-tuple-element.88.refs_3_.refs_2_, f32[512,128]{1,0:T(8,128)S(1)} %get-tuple-element.87.refs_4_.refs_3_, ...), custom_call_target="tpu_custom_call" | custom-call | flops 20000000000 | tf_op jit(solution)/shard_map/value_grad/pallas_call | solution.py:45
  53.3 1.8 %merge_inputs.1 = (bf16[2,2,224,512]{3,2,1,0:T(8,128)(2,1)S(1)}, bf16[2,2,224,512]{3,2,1,0:T(8,128)(2,1)S(1)}, bf16[2,2,224,512]{3,2,1,0:T(8,128)(2,1)S(1)}, bf16[2,2,224,512]{3,2,1,0:T(8,128)(2,1)S(1)}) custom-call(bf16[2,2,224,512]{3,2,1,0:T(8,128)(2,1)} %get-tuple-element.67.refs_4_.refs_0_, ...), custom_call_target="tpu_custom_call" | custom-call | flops 20000000000 | tf_op jit(solution)/shard_map/merge_inputs/pallas_call | solution.py:45
  55.1 0.9 collective-permute-done.13.refs_5_
  56.0 2.1 %weight_part.4 = (bf16[4,224,384]{2,1,0:T(8,128)(2,1)S(1)}, f32[4,224,384]{2,1,0:T(8,128)S(1)}) custom-call(bf16[2,2,224,512]{3,2,1,0:T(8,128)(2,1)S(1)} %get-tuple-element.96.refs_0_.refs_6_, bf16[2,2,224,512]{3,2,1,0:T(8,128)(2,1)S(1)} %get-tuple-element.97.refs_1_, bf16[2,2,224,512]{3,2,1,0:T(8,128)(2,1)S(1)} %get-tuple-element.98.refs_2_, ...), custom_call_target="tpu_custom_call" | custom-call | flops 20000000000 | tf_op jit(solution)/shard_map/weight_part/pallas_call | solution.py:45
  58.7 3.3 %input_part.4 = (bf16[512,896]{1,0:T(8,128)(2,1)S(1)}, bf16[512,1792]{1,0:T(8,128)(2,1)S(1)}) custom-call(s32[8]{0:T(128)S(1)} %stack.27.refs_0_, bf16[512,384]{1,0:T(8,128)(2,1)S(1)} %value_grad.4.refs_6_.refs_4_.refs_1_, bf16[512,384]{1,0:T(8,128)(2,1)S(1)} %value_grad.5.refs_6_.refs_2_.refs_4_, bf16[512,512]{1,0:T(8,128)(2,1)} %value_grad.6.refs_6_.refs_3_.refs_4_, ...), custom_call_target="tpu_custom_call" | custom-call | flops 20000000000 | tf_op jit(solution)/shard_map/input_part/pallas_call | solution.py:45
  62.0 0.7 fold_weight.10
  62.7 1.5 %collective-permute-start.16 = (bf16[2,224,384]{2,1,0:T(8,128)(2,1)S(1)}, bf16[2,224,384]{2,1,0:T(8,128)(2,1)S(1)}, u32[]{:S(2)}, u32[]{:S(2)}) collective-permute-start(bf16[2,224,384]{2,1,0:T(8,128)(2,1)S(1)} %get-tuple-element.105.refs_6_), channel_id=1, source_target_pairs={{0,8},{4,12},{8,0},{12,4},{16,24},{20,28},{24,16},{28,20},{1,9},{5... | collective-permute-start | bytes 1032200 | tf_op jit(solution)/shard_map/ppermute | solution.py:360
  64.5 2.1 %weight_part.5 = (bf16[4,224,384]{2,1,0:T(8,128)(2,1)S(1)}, f32[4,224,384]{2,1,0:T(8,128)S(1)}) custom-call(bf16[2,2,224,512]{3,2,1,0:T(8,128)(2,1)S(1)} %get-tuple-element.96.refs_0_.refs_6_, bf16[2,2,224,512]{3,2,1,0:T(8,128)(2,1)S(1)} %get-tuple-element.97.refs_1_, bf16[2,2,224,512]{3,2,1,0:T(8,128)(2,1)S(1)} %get-tuple-element.98.refs_2_, ...), custom_call_target="tpu_custom_call" | custom-call | flops 20000000000 | tf_op jit(solution)/shard_map/weight_part/pallas_call | solution.py:45
  66.6 3.9 %input_part.5.refs_3_ = bf16[512,1792]{1,0:T(8,128)(2,1)} custom-call(s32[8]{0:T(128)S(1)} %stack.27.refs_0_, bf16[512,896]{1,0:T(8,128)(2,1)S(1)} %get-tuple-element.103.refs_3_.refs_1_, bf16[512,1792]{1,0:T(8,128)(2,1)S(1)} %get-tuple-element.101.refs_2_.refs_1_, bf16[3584,1792]{1,0:T(8,128)(2,1)S(1)} %bitcast.17, ...), custom_call_target="tpu_custom_call" | custom-call | flops 20000000000 | tf_op jit(solution)/shard_map/input_part/pallas_call | solution.py:45
  70.5 0.9 collective-permute-start.27
  71.4 0.7 fold_weight.11
  72.1 1.6 %collective-permute-start.22 = (bf16[2,224,384]{2,1,0:T(8,128)(2,1)S(1)}, bf16[2,224,384]{2,1,0:T(8,128)(2,1)S(1)}, u32[]{:S(2)}, u32[]{:S(2)}) collective-permute-start(bf16[2,224,384]{2,1,0:T(8,128)(2,1)S(1)} %get-tuple-element.108.refs_3_), channel_id=1, source_target_pairs={{0,8},{4,12},{8,0},{12,4},{16,24},{20,28},{24,16},{28,20},{1,9},{5... | collective-permute-start | bytes 1032200 | tf_op jit(solution)/shard_map/ppermute | solution.py:360
  73.7 0.6 fold_weight.12
  74.3 2.7 %collective-permute-start.23 = (bf16[1,224,384]{2,1,0:T(8,128)(2,1)S(1)}, bf16[1,224,384]{2,1,0:T(8,128)(2,1)S(1)}, u32[]{:S(2)}, u32[]{:S(2)}) collective-permute-start(bf16[1,224,384]{2,1,0:T(8,128)(2,1)S(1)} %get-tuple-element.109.refs_6_), channel_id=1, source_target_pairs={{0,16},{4,20},{8,24},{12,28},{16,0},{20,4},{24,8},{28,12},{1,17},{... | collective-permute-start | bytes 516104 | tf_op jit(solution)/shard_map/ppermute | solution.py:360
  77.0 3.3 %weight_part.6 = (bf16[4,224,512]{2,1,0:T(8,128)(2,1)S(1)}, f32[4,224,512]{2,1,0:T(8,128)S(1)}) custom-call(bf16[2,2,224,512]{3,2,1,0:T(8,128)(2,1)S(1)} %get-tuple-element.96.refs_0_.refs_6_, bf16[2,2,224,512]{3,2,1,0:T(8,128)(2,1)S(1)} %get-tuple-element.97.refs_1_, bf16[2,2,224,512]{3,2,1,0:T(8,128)(2,1)S(1)} %get-tuple-element.98.refs_2_, ...), custom_call_target="tpu_custom_call" | custom-call | flops 20000000000 | tf_op jit(solution)/shard_map/weight_part/pallas_call | solution.py:45
  80.3 2.6 %input_part.6.refs_3_.refs_1_ = f32[512,896]{1,0:T(8,128)S(1)} custom-call(s32[8]{0:T(128)S(1)} %stack.27.refs_0_, bf16[512,1792]{1,0:T(8,128)(2,1)S(1)} %get-tuple-element.101.refs_2_.refs_1_, bf16[3584,1792]{1,0:T(8,128)(2,1)S(1)} %bitcast.17, f32[4,224,512]{2,1,0:T(8,128)S(1)} %get-tuple-element.110.refs_3_.refs_1_), custom_call_target="tpu_custom_call" | custom-call | flops 20000000000 | tf_op jit(solution)/shard_map/input_part/pallas_call | solution.py:45
  83.0 0.8 fold_weight.13
  84.6 3.5 %weight_part.7 = (bf16[4,224,512]{2,1,0:T(8,128)(2,1)S(1)}, f32[4,224,512]{2,1,0:T(8,128)S(1)}) custom-call(bf16[2,2,224,512]{3,2,1,0:T(8,128)(2,1)S(1)} %get-tuple-element.96.refs_0_.refs_6_, bf16[2,2,224,512]{3,2,1,0:T(8,128)(2,1)S(1)} %get-tuple-element.97.refs_1_, bf16[2,2,224,512]{3,2,1,0:T(8,128)(2,1)S(1)} %get-tuple-element.98.refs_2_, ...), custom_call_target="tpu_custom_call" | custom-call | flops 20000000000 | tf_op jit(solution)/shard_map/weight_part/pallas_call | solution.py:45
  88.2 0.6 fold_weight.14
  88.8 2.3 %collective-permute-start.28 = (bf16[1,224,384]{2,1,0:T(8,128)(2,1)S(1)}, bf16[1,224,384]{2,1,0:T(8,128)(2,1)S(1)}, u32[]{:S(2)}, u32[]{:S(2)}) collective-permute-start(bf16[1,224,384]{2,1,0:T(8,128)(2,1)S(1)} %get-tuple-element.116.refs_3_), channel_id=1, source_target_pairs={{0,16},{4,20},{8,24},{12,28},{16,0},{20,4},{24,8},{28,12},{1,17},{... | collective-permute-start | bytes 516104 | tf_op jit(solution)/shard_map/ppermute | solution.py:360
  91.1 0.7 fold_weight.15
  91.8 0.8 collective-permute-start.25
  92.6 0.7 fold_weight.16
  93.2 1.4 %collective-permute-start.24 = (bf16[2,224,256]{2,1,0:T(8,128)(2,1)S(1)}, bf16[2,224,256]{2,1,0:T(8,128)(2,1)S(1)}, u32[]{:S(2)}, u32[]{:S(2)}) collective-permute-start(bf16[2,224,256]{2,1,0:T(8,128)(2,1)S(1)} %get-tuple-element.119.refs_3_), channel_id=1, source_target_pairs={{0,8},{4,12},{8,0},{12,4},{16,24},{20,28},{24,16},{28,20},{1,9},{5... | collective-permute-start | bytes 688136 | tf_op jit(solution)/shard_map/ppermute | solution.py:360
  94.6 6.2 %collective-permute-done.26.refs_2_ = bf16[2,224,512]{2,1,0:T(8,128)(2,1)S(1)} collective-permute-done((bf16[2,224,512]{2,1,0:T(8,128)(2,1)S(1)}, bf16[2,224,512]{2,1,0:T(8,128)(2,1)S(1)}, u32[]{:S(2)}, u32[]{:S(2)}) %collective-permute-start.26) | collective-permute-done | bytes 458784 | tf_op jit(solution)/shard_map/ppermute | solution.py:360
  100.8 0.7 fold_weight.17
  101.5 0.8 collective-permute-start.29
  102.2 8.4 %collective-permute-done.25.refs_2_ = bf16[2,224,256]{2,1,0:T(8,128)(2,1)S(1)} collective-permute-done((bf16[2,224,256]{2,1,0:T(8,128)(2,1)S(1)}, bf16[2,224,256]{2,1,0:T(8,128)(2,1)S(1)}, u32[]{:S(2)}, u32[]{:S(2)}) %collective-permute-start.25) | collective-permute-done | bytes 229408 | tf_op jit(solution)/shard_map/ppermute | solution.py:360
  111.2 0.8 collective-permute-start.30
  112.0 3.2 %collective-permute-done.24.refs_2_ = bf16[2,224,256]{2,1,0:T(8,128)(2,1)S(1)} collective-permute-done((bf16[2,224,256]{2,1,0:T(8,128)(2,1)S(1)}, bf16[2,224,256]{2,1,0:T(8,128)(2,1)S(1)}, u32[]{:S(2)}, u32[]{:S(2)}) %collective-permute-start.24) | collective-permute-done | bytes 229408 | tf_op jit(solution)/shard_map/ppermute | solution.py:360
  115.9 0.8 collective-permute-start.31
  116.7 2.7 %input_part.7.refs_0_.refs_2_ = f32[512,1792]{1,0:T(8,128)S(1)} custom-call(s32[8]{0:T(128)S(1)} %stack.27.refs_0_, f32[512,896]{1,0:T(8,128)S(1)} %input_part.6.refs_3_.refs_1_, bf16[512,1792]{1,0:T(8,128)(2,1)S(1)} %get-tuple-element.101.refs_2_.refs_1_, bf16[3584,1792]{1,0:T(8,128)(2,1)S(1)} %bitcast.19, bf16[1,224,256]{2,1,0:T(8,128)(2,1)S(1)} %get-tuple-element.124.refs_4_), custom_call_target="tpu_custom_call" | custom-call | flops 20000000000 | tf_op jit(solution)/shard_map/input_part/pallas_call | solution.py:45
  119.5 3.0 %grad_input.1 = (bf16[512,1792]{1,0:T(8,128)(2,1)}, f32[8,128]{1,0:T(8,128)S(1)}) custom-call(f32[512,1792]{1,0:T(8,128)S(1)} %input_part.7.refs_0_.refs_2_, bf16[512,1792]{1,0:T(8,128)(2,1)} %collective-permute-done.27.refs_1_, f32[512,1792]{1,0:T(8,128)S(1)} %input_part.7.refs_0_.refs_2_), custom_call_target="tpu_custom_call" | custom-call | flops 20000000000 | tf_op jit(solution)/shard_map/grad_input/pallas_call | solution.py:45
  122.5 3.6 %collective-permute-done.31.refs_9_ = bf16[1,224,256]{2,1,0:T(8,128)(2,1)S(1)} collective-permute-done((bf16[1,224,256]{2,1,0:T(8,128)(2,1)S(1)}, bf16[1,224,256]{2,1,0:T(8,128)(2,1)S(1)}, u32[]{:S(2)}, u32[]{:S(2)}) %collective-permute-start.31) | collective-permute-done | bytes 114720 | tf_op jit(solution)/shard_map/ppermute | solution.py:360
  126.1 1.3 %grad_weight.1 = f32[224,1792]{1,0:T(8,128)} custom-call(f32[1,224,384]{2,1,0:T(8,128)S(1)} %get-tuple-element.126.refs_0_, bf16[1,224,384]{2,1,0:T(8,128)(2,1)S(1)} %collective-permute-done.23.refs_1_, f32[1,224,384]{2,1,0:T(8,128)S(1)} %get-tuple-element.127.refs_2_, bf16[1,224,384]{2,1,0:T(8,128)(2,1)S(1)} %collective-permute-done.28.refs_3_, ...), custom_call_target="tpu_custom_call" | custom-call | flops 20000000000 | tf_op jit(solution)/shard_map/grad_weight/pallas_call | solution.py:45
  (69 shorter events, 6.8 us)
Async XLA Ops:
  0.8 1.5 %copy-start.2 = (bf16[1,512,1792]{2,1,0:T(8,128)(2,1)S(1)}, bf16[1,512,1792]{2,1,0:T(8,128)(2,1)}, u32[]{:S(2)}) copy-start(bf16[1,512,1792]{2,1,0:T(8,128)(2,1)} %param.6) | copy-start | bytes 5505028
  2.3 5.1 %copy-start.4 = (f32[1,14,512]{2,0,1:T(1,128)S(1)}, f32[1,14,512]{2,0,1:T(1,128)}, u32[]{:S(2)}) copy-start(f32[1,14,512]{2,0,1:T(1,128)} %param.11) | copy-start | bytes 86020
  2.3 5.1 %copy-start = (s32[1,512,1792]{2,1,0:T(8,128)S(1)}, s32[1,512,1792]{2,1,0:T(8,128)}, u32[]{:S(2)}) copy-start(s32[1,512,1792]{2,1,0:T(8,128)} %param.9) | copy-start | bytes 11010052
  2.3 5.1 %copy-start.3 = (bf16[1,512,1792]{2,1,0:T(8,128)(2,1)S(1)}, bf16[1,512,1792]{2,1,0:T(8,128)(2,1)}, u32[]{:S(2)}) copy-start(bf16[1,512,1792]{2,1,0:T(8,128)(2,1)} %param.8) | copy-start | bytes 5505028
  4.4 38.4 %collective-permute-start.9 = (bf16[2,2,224,512]{3,2,1,0:T(8,128)(2,1)}, bf16[2,2,224,512]{3,2,1,0:T(8,128)(2,1)}, u32[]{:S(2)}, u32[]{:S(2)}) collective-permute-start(bf16[2,2,224,512]{3,2,1,0:T(8,128)(2,1)} %get-tuple-element.67.refs_4_.refs_0_), channel_id=1, source_target_pairs={{0,2},{2,0},{1,3},{3,1},{4,6},{6,4},{5,7},{7,5},{8,10},{10,8},{9,1... | collective-permute-start | bytes 2752520 | tf_op jit(solution)/shard_map/ppermute | solution.py:360
  9.5 4.8 %collective-permute-start.1 = (bf16[432,128]{1,0:T(8,128)(2,1)S(1)}, bf16[432,128]{1,0:T(8,128)(2,1)S(1)}, u32[]{:S(2)}, u32[]{:S(2)}) collective-permute-start(bf16[432,128]{1,0:T(8,128)(2,1)S(1)} %get-tuple-element.71.refs_4_), channel_id=1, source_target_pairs={{0,4},{4,0},{8,12},{12,8},{16,20},{20,16},{24,28},{28,24},{1,5},{5... | collective-permute-start | bytes 331784 | tf_op jit(solution)/shard_map/ppermute | solution.py:360
  13.4 6.1 %collective-permute-start = (bf16[560,128]{1,0:T(8,128)(2,1)S(1)}, bf16[560,128]{1,0:T(8,128)(2,1)S(1)}, u32[]{:S(2)}, u32[]{:S(2)}) collective-permute-start(bf16[560,128]{1,0:T(8,128)(2,1)S(1)} %get-tuple-element.73.refs_3_), channel_id=1, source_target_pairs={{0,4},{4,0},{8,12},{12,8},{16,20},{20,16},{24,28},{28,24},{1,5},{5... | collective-permute-start | bytes 430088 | tf_op jit(solution)/shard_map/ppermute | solution.py:360
  14.9 8.7 %collective-permute-start.2 = (bf16[432,128]{1,0:T(8,128)(2,1)S(1)}, bf16[432,128]{1,0:T(8,128)(2,1)S(1)}, u32[]{:S(2)}, u32[]{:S(2)}) collective-permute-start(bf16[432,128]{1,0:T(8,128)(2,1)S(1)} %get-tuple-element.75.refs_3_), channel_id=1, source_target_pairs={{8,0},{12,4},{16,8},{20,12},{24,16},{28,20},{9,1},{13,5},{17,9},{2... | collective-permute-start | bytes 331784 | tf_op jit(solution)/shard_map/ppermute | solution.py:364
  16.2 15.2 %collective-permute-start.4 = (bf16[1,2,224,512]{3,2,1,0:T(8,128)(2,1)S(1)}, bf16[1,2,224,512]{3,2,1,0:T(8,128)(2,1)S(1)}, u32[]{:S(2)}, u32[]{:S(2)}) collective-permute-start(bf16[1,2,224,512]{3,2,1,0:T(8,128)(2,1)S(1)} %get-tuple-element.83.refs_4_), channel_id=1, source_target_pairs={{0,4},{4,0},{8,12},{12,8},{16,20},{20,16},{24,28},{28,24},{1,5},{5... | collective-permute-start | bytes 1376264 | tf_op jit(solution)/shard_map/ppermute | solution.py:360
  19.5 2.1 %copy-start.1 = (s32[1,512,1792]{2,1,0:T(8,128)S(1)}, s32[1,512,1792]{2,1,0:T(8,128)}, u32[]{:S(2)}) copy-start(s32[1,512,1792]{2,1,0:T(8,128)} %param.10) | copy-start | bytes 11010052
  20.1 8.5 %collective-permute-start.5 = (bf16[560,128]{1,0:T(8,128)(2,1)S(1)}, bf16[560,128]{1,0:T(8,128)(2,1)S(1)}, u32[]{:S(2)}, u32[]{:S(2)}) collective-permute-start(bf16[560,128]{1,0:T(8,128)(2,1)S(1)} %get-tuple-element.77.refs_5_), channel_id=1, source_target_pairs={{8,0},{12,4},{16,8},{20,12},{24,16},{28,20},{9,1},{13,5},{17,9},{2... | collective-permute-start | bytes 430088 | tf_op jit(solution)/shard_map/ppermute | solution.py:364
  21.5 17.7 %collective-permute-start.8 = (bf16[1,2,224,512]{3,2,1,0:T(8,128)(2,1)S(1)}, bf16[1,2,224,512]{3,2,1,0:T(8,128)(2,1)S(1)}, u32[]{:S(2)}, u32[]{:S(2)}) collective-permute-start(bf16[1,2,224,512]{3,2,1,0:T(8,128)(2,1)S(1)} %get-tuple-element.92.refs_6_), channel_id=1, source_target_pairs={{0,4},{4,0},{8,12},{12,8},{16,20},{20,16},{24,28},{28,24},{1,5},{5... | collective-permute-start | bytes 1376264 | tf_op jit(solution)/shard_map/ppermute | solution.py:360
  24.8 7.5 %collective-permute-start.3 = (bf16[432,128]{1,0:T(8,128)(2,1)S(1)}, bf16[432,128]{1,0:T(8,128)(2,1)S(1)}, u32[]{:S(2)}, u32[]{:S(2)}) collective-permute-start(bf16[432,128]{1,0:T(8,128)(2,1)S(1)} %get-tuple-element.82.refs_5_), channel_id=1, source_target_pairs={{16,0},{20,4},{24,8},{28,12},{17,1},{21,5},{25,9},{29,13},{18,2},{... | collective-permute-start | bytes 331784 | tf_op jit(solution)/shard_map/ppermute | solution.py:364
  29.9 10.6 %collective-permute-start.7 = (bf16[560,128]{1,0:T(8,128)(2,1)S(1)}, bf16[560,128]{1,0:T(8,128)(2,1)S(1)}, u32[]{:S(2)}, u32[]{:S(2)}) collective-permute-start(bf16[560,128]{1,0:T(8,128)(2,1)S(1)} %get-tuple-element.89.refs_1_), channel_id=1, source_target_pairs={{16,0},{20,4},{24,8},{28,12},{17,1},{21,5},{25,9},{29,13},{18,2},{... | collective-permute-start | bytes 430088 | tf_op jit(solution)/shard_map/ppermute | solution.py:364
  31.4 16.2 %collective-permute-start.11 = (bf16[1,2,224,512]{3,2,1,0:T(8,128)(2,1)S(1)}, bf16[1,2,224,512]{3,2,1,0:T(8,128)(2,1)S(1)}, u32[]{:S(2)}, u32[]{:S(2)}) collective-permute-start(bf16[1,2,224,512]{3,2,1,0:T(8,128)(2,1)S(1)} %pass_on.2.refs_5_.refs_2_), channel_id=1, source_target_pairs={{0,2},{2,0},{1,3},{3,1},{4,6},{6,4},{5,7},{7,5},{8,10},{10,8},{9,1... | collective-permute-start | bytes 1376264 | tf_op jit(solution)/shard_map/ppermute | solution.py:360
  33.0 9.8 %collective-permute-start.6 = (bf16[384,128]{1,0:T(8,128)(2,1)S(1)}, bf16[384,128]{1,0:T(8,128)(2,1)S(1)}, u32[]{:S(2)}, u32[]{:S(2)}) collective-permute-start(bf16[384,128]{1,0:T(8,128)(2,1)S(1)} %get-tuple-element.91.refs_1_), channel_id=1, source_target_pairs={{0,4},{4,0},{8,12},{12,8},{16,20},{20,16},{24,28},{28,24},{1,5},{5... | collective-permute-start | bytes 294920 | tf_op jit(solution)/shard_map/ppermute | solution.py:360
  39.3 14.0 %collective-permute-start.12 = (bf16[1,2,224,512]{3,2,1,0:T(8,128)(2,1)S(1)}, bf16[1,2,224,512]{3,2,1,0:T(8,128)(2,1)S(1)}, u32[]{:S(2)}, u32[]{:S(2)}) collective-permute-start(bf16[1,2,224,512]{3,2,1,0:T(8,128)(2,1)S(1)} %pass_on.3.refs_5_.refs_3_), channel_id=1, source_target_pairs={{0,2},{2,0},{1,3},{3,1},{4,6},{6,4},{5,7},{7,5},{8,10},{10,8},{9,1... | collective-permute-start | bytes 1376264 | tf_op jit(solution)/shard_map/ppermute | solution.py:360
  41.2 6.4 %collective-permute-start.10 = (bf16[512,128]{1,0:T(8,128)(2,1)S(1)}, bf16[512,128]{1,0:T(8,128)(2,1)S(1)}, u32[]{:S(2)}, u32[]{:S(2)}) collective-permute-start(bf16[512,128]{1,0:T(8,128)(2,1)S(1)} %get-tuple-element.93.refs_6_), channel_id=1, source_target_pairs={{0,4},{4,0},{8,12},{12,8},{16,20},{20,16},{24,28},{28,24},{1,5},{5... | collective-permute-start | bytes 393224 | tf_op jit(solution)/shard_map/ppermute | solution.py:360
  43.7 12.3 %collective-permute-start.13 = (bf16[512,384]{1,0:T(8,128)(2,1)S(1)}, bf16[512,384]{1,0:T(8,128)(2,1)S(1)}, u32[]{:S(2)}, u32[]{:S(2)}) collective-permute-start(bf16[512,384]{1,0:T(8,128)(2,1)S(1)} %value_grad.4.refs_6_.refs_4_.refs_1_), channel_id=1, source_target_pairs={{0,4},{4,0},{8,12},{12,8},{16,20},{20,16},{24,28},{28,24},{1,5},{5... | collective-permute-start | bytes 1179656 | tf_op jit(solution)/shard_map/ppermute | solution.py:360
  45.2 19.3 %collective-permute-start.17 = (bf16[512,384]{1,0:T(8,128)(2,1)S(1)}, bf16[512,384]{1,0:T(8,128)(2,1)S(1)}, u32[]{:S(2)}, u32[]{:S(2)}) collective-permute-start(bf16[512,384]{1,0:T(8,128)(2,1)S(1)} %value_grad.5.refs_6_.refs_2_.refs_4_), channel_id=1, source_target_pairs={{0,4},{4,0},{8,12},{12,8},{16,20},{20,16},{24,28},{28,24},{1,5},{5... | collective-permute-start | bytes 1179656 | tf_op jit(solution)/shard_map/ppermute | solution.py:360
  49.4 27.6 %collective-permute-start.14 = (bf16[512,512]{1,0:T(8,128)(2,1)}, bf16[512,512]{1,0:T(8,128)(2,1)}, u32[]{:S(2)}, u32[]{:S(2)}) collective-permute-start(bf16[512,512]{1,0:T(8,128)(2,1)} %value_grad.6.refs_6_.refs_3_.refs_4_), channel_id=1, source_target_pairs={{0,4},{4,0},{8,12},{12,8},{16,20},{20,16},{24,28},{28,24},{1,5},{5... | collective-permute-start | bytes 1572872 | tf_op jit(solution)/shard_map/ppermute | solution.py:360
  52.8 31.8 %collective-permute-start.19 = (bf16[512,512]{1,0:T(8,128)(2,1)}, bf16[512,512]{1,0:T(8,128)(2,1)}, u32[]{:S(2)}, u32[]{:S(2)}) collective-permute-start(bf16[512,512]{1,0:T(8,128)(2,1)} %value_grad.7.refs_6_.refs_4_), channel_id=1, source_target_pairs={{0,4},{4,0},{8,12},{12,8},{16,20},{20,16},{24,28},{28,24},{1,5},{5... | collective-permute-start | bytes 1572872 | tf_op jit(solution)/shard_map/ppermute | solution.py:360
  53.3 4.9 %slice-start = ((s8[12845056]{0:T(1024)(128)(4,1)}), s8[4194304]{0:T(1024)(128)(4,1)S(1)}, s32[]{:S(2)}) async-start(s8[12845056]{0:T(1024)(128)(4,1)} %bitcast.16), calls=%async_computation | async-start | bytes 8388608
  53.3 4.9 %slice-start.1 = ((s8[12845056]{0:T(1024)(128)(4,1)}), s8[4194304]{0:T(1024)(128)(4,1)S(1)}, s32[]{:S(2)}) async-start(s8[12845056]{0:T(1024)(128)(4,1)} %bitcast.16), calls=%async_computation.1 | async-start | bytes 8388608
  56.0 2.7 %slice-start.2 = ((s8[12845056]{0:T(1024)(128)(4,1)}), s8[4194304]{0:T(1024)(128)(4,1)S(1)}, s32[]{:S(2)}) async-start(s8[12845056]{0:T(1024)(128)(4,1)} %bitcast.16), calls=%async_computation.2 | async-start | bytes 8388608
  56.0 2.7 %slice-start.3 = ((s8[12845056]{0:T(1024)(128)(4,1)}), s8[262144]{0:T(1024)(128)(4,1)S(1)}, s32[]{:S(2)}) async-start(s8[12845056]{0:T(1024)(128)(4,1)} %bitcast.16), calls=%async_computation.3 | async-start | bytes 524288
  58.1 3.9 %collective-permute-start.15 = (bf16[4,224,384]{2,1,0:T(8,128)(2,1)S(1)}, bf16[4,224,384]{2,1,0:T(8,128)(2,1)S(1)}, u32[]{:S(2)}, u32[]{:S(2)}) collective-permute-start(bf16[4,224,384]{2,1,0:T(8,128)(2,1)S(1)} %get-tuple-element.102), channel_id=1, source_target_pairs={{0,1},{1,0},{2,3},{3,2},{4,5},{5,4},{6,7},{7,6},{8,9},{9,8},{10,11... | collective-permute-start | bytes 2064392 | tf_op jit(solution)/shard_map/ppermute | solution.py:360
  62.7 11.0 %collective-permute-start.16 = (bf16[2,224,384]{2,1,0:T(8,128)(2,1)S(1)}, bf16[2,224,384]{2,1,0:T(8,128)(2,1)S(1)}, u32[]{:S(2)}, u32[]{:S(2)}) collective-permute-start(bf16[2,224,384]{2,1,0:T(8,128)(2,1)S(1)} %get-tuple-element.105.refs_6_), channel_id=1, source_target_pairs={{0,8},{4,12},{8,0},{12,4},{16,24},{20,28},{24,16},{28,20},{1,9},{5... | collective-permute-start | bytes 1032200 | tf_op jit(solution)/shard_map/ppermute | solution.py:360
  66.5 4.9 %collective-permute-start.18 = (bf16[4,224,384]{2,1,0:T(8,128)(2,1)S(1)}, bf16[4,224,384]{2,1,0:T(8,128)(2,1)S(1)}, u32[]{:S(2)}, u32[]{:S(2)}) collective-permute-start(bf16[4,224,384]{2,1,0:T(8,128)(2,1)S(1)} %get-tuple-element.107), channel_id=1, source_target_pairs={{0,1},{1,0},{2,3},{3,2},{4,5},{5,4},{6,7},{7,6},{8,9},{9,8},{10,11... | collective-permute-start | bytes 2064392 | tf_op jit(solution)/shard_map/ppermute | solution.py:360
  70.5 49.0 %collective-permute-start.27 = (bf16[512,1792]{1,0:T(8,128)(2,1)}, bf16[512,1792]{1,0:T(8,128)(2,1)}, u32[]{:S(2)}, u32[]{:S(2)}) collective-permute-start(bf16[512,1792]{1,0:T(8,128)(2,1)} %input_part.5.refs_3_), channel_id=1, source_target_pairs={{0,2},{2,0},{1,3},{3,1},{4,6},{6,4},{5,7},{7,5},{8,10},{10,8},{9,1... | collective-permute-start | bytes 5505032 | tf_op jit(solution)/shard_map/ppermute | solution.py:360
  72.1 16.1 %collective-permute-start.22 = (bf16[2,224,384]{2,1,0:T(8,128)(2,1)S(1)}, bf16[2,224,384]{2,1,0:T(8,128)(2,1)S(1)}, u32[]{:S(2)}, u32[]{:S(2)}) collective-permute-start(bf16[2,224,384]{2,1,0:T(8,128)(2,1)S(1)} %get-tuple-element.108.refs_3_), channel_id=1, source_target_pairs={{0,8},{4,12},{8,0},{12,4},{16,24},{20,28},{24,16},{28,20},{1,9},{5... | collective-permute-start | bytes 1032200 | tf_op jit(solution)/shard_map/ppermute | solution.py:360
  74.3 13.8 %collective-permute-start.23 = (bf16[1,224,384]{2,1,0:T(8,128)(2,1)S(1)}, bf16[1,224,384]{2,1,0:T(8,128)(2,1)S(1)}, u32[]{:S(2)}, u32[]{:S(2)}) collective-permute-start(bf16[1,224,384]{2,1,0:T(8,128)(2,1)S(1)} %get-tuple-element.109.refs_6_), channel_id=1, source_target_pairs={{0,16},{4,20},{8,24},{12,28},{16,0},{20,4},{24,8},{28,12},{1,17},{... | collective-permute-start | bytes 516104 | tf_op jit(solution)/shard_map/ppermute | solution.py:360
  80.3 2.7 %collective-permute-start.20 = (bf16[4,224,512]{2,1,0:T(8,128)(2,1)S(1)}, bf16[4,224,512]{2,1,0:T(8,128)(2,1)S(1)}, u32[]{:S(2)}, u32[]{:S(2)}) collective-permute-start(bf16[4,224,512]{2,1,0:T(8,128)(2,1)S(1)} %get-tuple-element.111), channel_id=1, source_target_pairs={{0,1},{1,0},{2,3},{3,2},{4,5},{5,4},{6,7},{7,6},{8,9},{9,8},{10,11... | collective-permute-start | bytes 2752520 | tf_op jit(solution)/shard_map/ppermute | solution.py:360
  83.7 17.1 %collective-permute-start.26 = (bf16[2,224,512]{2,1,0:T(8,128)(2,1)S(1)}, bf16[2,224,512]{2,1,0:T(8,128)(2,1)S(1)}, u32[]{:S(2)}, u32[]{:S(2)}) collective-permute-start(bf16[2,224,512]{2,1,0:T(8,128)(2,1)S(1)} %get-tuple-element.112.refs_6_), channel_id=1, source_target_pairs={{0,8},{4,12},{8,0},{12,4},{16,24},{20,28},{24,16},{28,20},{1,9},{5... | collective-permute-start | bytes 1376264 | tf_op jit(solution)/shard_map/ppermute | solution.py:360
  88.1 3.1 %collective-permute-start.21 = (bf16[4,224,512]{2,1,0:T(8,128)(2,1)S(1)}, bf16[4,224,512]{2,1,0:T(8,128)(2,1)S(1)}, u32[]{:S(2)}, u32[]{:S(2)}) collective-permute-start(bf16[4,224,512]{2,1,0:T(8,128)(2,1)S(1)} %get-tuple-element.114), channel_id=1, source_target_pairs={{0,1},{1,0},{2,3},{3,2},{4,5},{5,4},{6,7},{7,6},{8,9},{9,8},{10,11... | collective-permute-start | bytes 2752520 | tf_op jit(solution)/shard_map/ppermute | solution.py:360
  88.8 33.7 %collective-permute-start.28 = (bf16[1,224,384]{2,1,0:T(8,128)(2,1)S(1)}, bf16[1,224,384]{2,1,0:T(8,128)(2,1)S(1)}, u32[]{:S(2)}, u32[]{:S(2)}) collective-permute-start(bf16[1,224,384]{2,1,0:T(8,128)(2,1)S(1)} %get-tuple-element.116.refs_3_), channel_id=1, source_target_pairs={{0,16},{4,20},{8,24},{12,28},{16,0},{20,4},{24,8},{28,12},{1,17},{... | collective-permute-start | bytes 516104 | tf_op jit(solution)/shard_map/ppermute | solution.py:360
  91.8 18.8 %collective-permute-start.25 = (bf16[2,224,256]{2,1,0:T(8,128)(2,1)S(1)}, bf16[2,224,256]{2,1,0:T(8,128)(2,1)S(1)}, u32[]{:S(2)}, u32[]{:S(2)}) collective-permute-start(bf16[2,224,256]{2,1,0:T(8,128)(2,1)S(1)} %get-tuple-element.117.refs_3_), channel_id=1, source_target_pairs={{0,8},{4,12},{8,0},{12,4},{16,24},{20,28},{24,16},{28,20},{1,9},{5... | collective-permute-start | bytes 688136 | tf_op jit(solution)/shard_map/ppermute | solution.py:360
  93.2 22.0 %collective-permute-start.24 = (bf16[2,224,256]{2,1,0:T(8,128)(2,1)S(1)}, bf16[2,224,256]{2,1,0:T(8,128)(2,1)S(1)}, u32[]{:S(2)}, u32[]{:S(2)}) collective-permute-start(bf16[2,224,256]{2,1,0:T(8,128)(2,1)S(1)} %get-tuple-element.119.refs_3_), channel_id=1, source_target_pairs={{0,8},{4,12},{8,0},{12,4},{16,24},{20,28},{24,16},{28,20},{1,9},{5... | collective-permute-start | bytes 688136 | tf_op jit(solution)/shard_map/ppermute | solution.py:360
  101.5 21.1 %collective-permute-start.29 = (bf16[1,224,512]{2,1,0:T(8,128)(2,1)S(1)}, bf16[1,224,512]{2,1,0:T(8,128)(2,1)S(1)}, u32[]{:S(2)}, u32[]{:S(2)}) collective-permute-start(bf16[1,224,512]{2,1,0:T(8,128)(2,1)S(1)} %get-tuple-element.122.refs_3_), channel_id=1, source_target_pairs={{0,16},{4,20},{8,24},{12,28},{16,0},{20,4},{24,8},{28,12},{1,17},{... | collective-permute-start | bytes 688136 | tf_op jit(solution)/shard_map/ppermute | solution.py:360
  110.6 6.1 %slice-start.4 = ((s8[12845056]{0:T(1024)(128)(4,1)}), s8[4194304]{0:T(1024)(128)(4,1)S(1)}, s32[]{:S(2)}) async-start(s8[12845056]{0:T(1024)(128)(4,1)} %bitcast.18), calls=%async_computation.4 | async-start | bytes 8388608
  110.6 6.1 %slice-start.5 = ((s8[12845056]{0:T(1024)(128)(4,1)}), s8[4194304]{0:T(1024)(128)(4,1)S(1)}, s32[]{:S(2)}) async-start(s8[12845056]{0:T(1024)(128)(4,1)} %bitcast.18), calls=%async_computation.5 | async-start | bytes 8388608
  111.2 5.5 %slice-start.6 = ((s8[12845056]{0:T(1024)(128)(4,1)}), s8[4194304]{0:T(1024)(128)(4,1)S(1)}, s32[]{:S(2)}) async-start(s8[12845056]{0:T(1024)(128)(4,1)} %bitcast.18), calls=%async_computation.6 | async-start | bytes 8388608
  111.2 14.9 %collective-permute-start.30 = (bf16[1,224,256]{2,1,0:T(8,128)(2,1)S(1)}, bf16[1,224,256]{2,1,0:T(8,128)(2,1)S(1)}, u32[]{:S(2)}, u32[]{:S(2)}) collective-permute-start(bf16[1,224,256]{2,1,0:T(8,128)(2,1)S(1)} %get-tuple-element.123.refs_3_), channel_id=1, source_target_pairs={{0,16},{4,20},{8,24},{12,28},{16,0},{20,4},{24,8},{28,12},{1,17},{... | collective-permute-start | bytes 344072 | tf_op jit(solution)/shard_map/ppermute | solution.py:360
  115.3 1.5 %slice-start.7 = ((s8[12845056]{0:T(1024)(128)(4,1)}), s8[262144]{0:T(1024)(128)(4,1)S(1)}, s32[]{:S(2)}) async-start(s8[12845056]{0:T(1024)(128)(4,1)} %bitcast.18), calls=%async_computation.7 | async-start | bytes 524288
  115.9 10.3 %collective-permute-start.31 = (bf16[1,224,256]{2,1,0:T(8,128)(2,1)S(1)}, bf16[1,224,256]{2,1,0:T(8,128)(2,1)S(1)}, u32[]{:S(2)}, u32[]{:S(2)}) collective-permute-start(bf16[1,224,256]{2,1,0:T(8,128)(2,1)S(1)} %get-tuple-element.124.refs_4_), channel_id=1, source_target_pairs={{0,16},{4,20},{8,24},{12,28},{16,0},{20,4},{24,8},{28,12},{1,17},{... | collective-permute-start | bytes 344072 | tf_op jit(solution)/shard_map/ppermute | solution.py:360

commit v6 on v5

--- a/solution.py
+++ b/solution.py
@@ -499,12 +499,12 @@
         for j in range(1, sides):
             far_x[j - 1].append(swap_with(far[i], "head", j))
 
+    send_far(0)
     join(0)
-    send_far(0)
+    if len(far) == 2:
+        send_far(1)
     if groups == 2:
         join(1)
-    if len(far) == 2:
-        send_far(1)
     local(0)
     spread(0)
     if groups == 2:

time: 128 us -> 128 us (level)
  transfers between devices with their start and end apart: 32 -> 32, of which waited for: 13 -> 10; matrix products, arithmetic and copies ran while one was open for 0% -> 0% of each run, Pallas kernels for 42% -> 43%
where the time goes in v6:
time: 128 us; the launch traced here: 127 us
  Pallas kernels  57.6 us (45%)
  starting transfers between devices  35.7 us (28%)
  waiting for transfers between devices  30.9 us (24%)
  local copies, waits for them, and re-layouts  2.13 us (2%)
    pallas_call x39, Pallas kernels, __call__(): pl.pallas_call(body, in_specs=[SM] * len(smalls) + [VM] * len(arrays) + [...  57.6 us
    ppermute x28, waiting for transfers between devices, swap_with(): lax.ppermute(x, axis, [(i, i ^ bit) for i in range(lax.axis_size(axis))])  30.7 us
    ppermute x28, starting transfers between devices, swap_with(): lax.ppermute(x, axis, [(i, i ^ bit) for i in range(lax.axis_size(axis))])  30.2 us
    ppermute x4, starting transfers between devices, from_later(): lax.ppermute(x, axis, [(i, i - shift) for i in range(shift, lax.axis_size...  5.46 us
  transfers between devices with their start and end apart: 32, of which 10 were waited for; matrix products, arithmetic and copies ran while one was open for 0% of the time, Pallas kernels for 43%

profile of v6, /device:TPU:0, one launch (start us, length us, event | category | flops | bytes accessed | tf_op | source)
XLA Modules:
  0.0 127.3 jit_solution(959195802598157095)
XLA Ops:
  0.8 1.5 %copy-done.2 = bf16[1,512,1792]{2,1,0:T(8,128)(2,1)S(1)} copy-done((bf16[1,512,1792]{2,1,0:T(8,128)(2,1)S(1)}, bf16[1,512,1792]{2,1,0:T(8,128)(2,1)}, u32[]{:S(2)}) %copy-start.2) | copy-done | bytes 1835032
  2.3 2.1 %transpose_inputs.1 = (bf16[2,2,224,512]{3,2,1,0:T(8,128)(2,1)}, bf16[1,2,224,512]{3,2,1,0:T(8,128)(2,1)S(1)}, bf16[1,2,224,512]{3,2,1,0:T(8,128)(2,1)S(1)}) custom-call(s32[8]{0:T(128)S(1)} %stack.27.refs_0_, bf16[512,1792]{1,0:T(8,128)(2,1)S(1)} %bitcast.24), custom_call_target="tpu_custom_call" | custom-call | flops 20000000000 | tf_op jit(solution)/shard_map/transpose_inputs/pallas_call | solution.py:45
  4.4 2.9 %collective-permute-start.9 = (bf16[2,2,224,512]{3,2,1,0:T(8,128)(2,1)}, bf16[2,2,224,512]{3,2,1,0:T(8,128)(2,1)}, u32[]{:S(2)}, u32[]{:S(2)}) collective-permute-start(bf16[2,2,224,512]{3,2,1,0:T(8,128)(2,1)} %get-tuple-element.67.refs_4_.refs_0_), channel_id=1, source_target_pairs={{0,2},{2,0},{1,3},{3,1},{4,6},{6,4},{5,7},{7,5},{8,10},{10,8},{9,1... | collective-permute-start | bytes 2752520 | tf_op jit(solution)/shard_map/ppermute | solution.py:360
  7.3 2.1 %state_terms.2 = (bf16[432,128]{1,0:T(8,128)(2,1)S(1)}, f32[432,128]{1,0:T(8,128)S(1)}, f32[16,512]{1,0:T(8,128)S(1)}, f32[512,128]{1,0:T(8,128)S(1)}, bf16[512,768]{1,0:T(8,128)(2,1)S(1)}) custom-call(s32[8]{0:T(128)S(1)} %stack.27.refs_0_, f32[14,512]{1,0:T(8,128)S(1)} %bitcast.14, s32[512,1792]{1,0:T(8,128)S(1)} %bitcast.20, ...), custom_call_target="tpu_custom_call" | custom-call | flops 20000000000 | tf_op jit(solution)/shard_map/state_terms/pallas_call | solution.py:45
  9.5 1.6 %collective-permute-start.1 = (bf16[432,128]{1,0:T(8,128)(2,1)S(1)}, bf16[432,128]{1,0:T(8,128)(2,1)S(1)}, u32[]{:S(2)}, u32[]{:S(2)}) collective-permute-start(bf16[432,128]{1,0:T(8,128)(2,1)S(1)} %get-tuple-element.71.refs_4_), channel_id=1, source_target_pairs={{0,4},{4,0},{8,12},{12,8},{16,20},{20,16},{24,28},{28,24},{1,5},{5... | collective-permute-start | bytes 331784 | tf_op jit(solution)/shard_map/ppermute | solution.py:360
  11.0 2.3 %state_terms.3 = (bf16[560,128]{1,0:T(8,128)(2,1)S(1)}, f32[560,128]{1,0:T(8,128)S(1)}, f32[16,512]{1,0:T(8,128)S(1)}, f32[512,128]{1,0:T(8,128)S(1)}, bf16[512,1024]{1,0:T(8,128)(2,1)S(1)}) custom-call(s32[8]{0:T(128)S(1)} %stack.27.refs_0_, f32[14,512]{1,0:T(8,128)S(1)} %bitcast.15, s32[512,1792]{1,0:T(8,128)S(1)} %bitcast.21, ...), custom_call_target="tpu_custom_call" | custom-call | flops 20000000000 | tf_op jit(solution)/shard_map/state_terms/pallas_call | solution.py:45
  13.9 1.5 %collective-permute-start.4 = (bf16[1,2,224,512]{3,2,1,0:T(8,128)(2,1)S(1)}, bf16[1,2,224,512]{3,2,1,0:T(8,128)(2,1)S(1)}, u32[]{:S(2)}, u32[]{:S(2)}) collective-permute-start(bf16[1,2,224,512]{3,2,1,0:T(8,128)(2,1)S(1)} %get-tuple-element.83.refs_4_), channel_id=1, source_target_pairs={{0,4},{4,0},{8,12},{12,8},{16,20},{20,16},{24,28},{28,24},{1,5},{5... | collective-permute-start | bytes 1376264 | tf_op jit(solution)/shard_map/ppermute | solution.py:360
  16.0 1.3 %collective-permute-start.2 = (bf16[432,128]{1,0:T(8,128)(2,1)S(1)}, bf16[432,128]{1,0:T(8,128)(2,1)S(1)}, u32[]{:S(2)}, u32[]{:S(2)}) collective-permute-start(bf16[432,128]{1,0:T(8,128)(2,1)S(1)} %get-tuple-element.76.refs_3_), channel_id=1, source_target_pairs={{8,0},{12,4},{16,8},{20,12},{24,16},{28,20},{9,1},{13,5},{17,9},{2... | collective-permute-start | bytes 331784 | tf_op jit(solution)/shard_map/ppermute | solution.py:364
  17.9 2.2 %collective-permute-done.refs_2_ = bf16[560,128]{1,0:T(8,128)(2,1)S(1)} collective-permute-done((bf16[560,128]{1,0:T(8,128)(2,1)S(1)}, bf16[560,128]{1,0:T(8,128)(2,1)S(1)}, u32[]{:S(2)}, u32[]{:S(2)}) %collective-permute-start) | collective-permute-done | bytes 143392 | tf_op jit(solution)/shard_map/ppermute | solution.py:360
  20.7 1.4 %collective-permute-start.5 = (bf16[560,128]{1,0:T(8,128)(2,1)S(1)}, bf16[560,128]{1,0:T(8,128)(2,1)S(1)}, u32[]{:S(2)}, u32[]{:S(2)}) collective-permute-start(bf16[560,128]{1,0:T(8,128)(2,1)S(1)} %get-tuple-element.78.refs_5_), channel_id=1, source_target_pairs={{8,0},{12,4},{16,8},{20,12},{24,16},{28,20},{9,1},{13,5},{17,9},{2... | collective-permute-start | bytes 430088 | tf_op jit(solution)/shard_map/ppermute | solution.py:364
  22.2 1.9 %local_part.2 = (f32[512,768]{1,0:T(8,128)S(1)}, bf16[512,768]{1,0:T(8,128)(2,1)S(1)}) custom-call(bf16[512,768]{1,0:T(8,128)(2,1)S(1)} %get-tuple-element.68.refs_0_, s32[512,1792]{1,0:T(8,128)S(1)} %bitcast.22, bf16[512,1792]{1,0:T(8,128)(2,1)S(1)} %bitcast.27, f32[16,512]{1,0:T(8,128)S(1)} %get-tuple-element.69.refs_3_, ...), custom_call_target="tpu_custom_call" | custom-call | flops 20000000000 | tf_op jit(solution)/shard_map/local_part/pallas_call | solution.py:45
  24.1 1.3 join_states.6
  25.4 1.3 %collective-permute-start.3 = (bf16[432,128]{1,0:T(8,128)(2,1)S(1)}, bf16[432,128]{1,0:T(8,128)(2,1)S(1)}, u32[]{:S(2)}, u32[]{:S(2)}) collective-permute-start(bf16[432,128]{1,0:T(8,128)(2,1)S(1)} %get-tuple-element.82.refs_5_), channel_id=1, source_target_pairs={{16,0},{20,4},{24,8},{28,12},{17,1},{21,5},{25,9},{29,13},{18,2},{... | collective-permute-start | bytes 331784 | tf_op jit(solution)/shard_map/ppermute | solution.py:364
  26.7 2.5 %local_part.3 = (f32[512,1024]{1,0:T(8,128)S(1)}, bf16[512,1024]{1,0:T(8,128)(2,1)S(1)}) custom-call(bf16[512,1024]{1,0:T(8,128)(2,1)S(1)} %get-tuple-element.85.refs_0_, s32[512,1792]{1,0:T(8,128)S(1)} %bitcast.23, bf16[512,1792]{1,0:T(8,128)(2,1)S(1)} %bitcast.28, f32[16,512]{1,0:T(8,128)S(1)} %get-tuple-element.86.refs_3_, ...), custom_call_target="tpu_custom_call" | custom-call | flops 20000000000 | tf_op jit(solution)/shard_map/local_part/pallas_call | solution.py:45
  29.2 1.3 %join_states.7 = (bf16[560,128]{1,0:T(8,128)(2,1)S(1)}, f32[560,128]{1,0:T(8,128)}) custom-call(s32[8]{0:T(128)S(1)} %stack.27.refs_0_, f32[560,128]{1,0:T(8,128)S(1)} %get-tuple-element.84.refs_1_, bf16[560,128]{1,0:T(8,128)(2,1)S(1)} %collective-permute-done.5.refs_2_.refs_3_, f32[512,1024]{1,0:T(8,128)S(1)} %get-tuple-element.88.refs_3_.refs_2_), custom_call_target="tpu_custom_call" | custom-call | flops 20000000000 | tf_op jit(solution)/shard_map/join_states/pallas_call | solution.py:45
  30.5 1.5 %collective-permute-start.7 = (bf16[560,128]{1,0:T(8,128)(2,1)S(1)}, bf16[560,128]{1,0:T(8,128)(2,1)S(1)}, u32[]{:S(2)}, u32[]{:S(2)}) collective-permute-start(bf16[560,128]{1,0:T(8,128)(2,1)S(1)} %get-tuple-element.89.refs_1_), channel_id=1, source_target_pairs={{16,0},{20,4},{24,8},{28,12},{17,1},{21,5},{25,9},{29,13},{18,2},{... | collective-permute-start | bytes 430088 | tf_op jit(solution)/shard_map/ppermute | solution.py:364
  32.0 0.9 collective-permute-start.11
  34.2 4.9 %collective-permute-done.8.refs_0_ = bf16[1,2,224,512]{3,2,1,0:T(8,128)(2,1)S(1)} collective-permute-done((bf16[1,2,224,512]{3,2,1,0:T(8,128)(2,1)S(1)}, bf16[1,2,224,512]{3,2,1,0:T(8,128)(2,1)S(1)}, u32[]{:S(2)}, u32[]{:S(2)}) %collective-permute-start.8) | collective-permute-done | bytes 458784 | tf_op jit(solution)/shard_map/ppermute | solution.py:360
  39.1 1.2 collective-permute-start.12
  40.3 0.6 carries.3
  40.9 1.4 %collective-permute-start.10 = (bf16[512,128]{1,0:T(8,128)(2,1)S(1)}, bf16[512,128]{1,0:T(8,128)(2,1)S(1)}, u32[]{:S(2)}, u32[]{:S(2)}) collective-permute-start(bf16[512,128]{1,0:T(8,128)(2,1)S(1)} %get-tuple-element.93.refs_6_), channel_id=1, source_target_pairs={{0,4},{4,0},{8,12},{12,8},{16,20},{20,16},{24,28},{28,24},{1,5},{5... | collective-permute-start | bytes 393224 | tf_op jit(solution)/shard_map/ppermute | solution.py:360
  42.4 0.9 value_grad.4.refs_6_.refs_4_.refs_1_
  43.3 0.7 collective-permute-start.13
  44.0 0.9 value_grad.5.refs_6_.refs_2_.refs_4_
  44.9 1.4 %collective-permute-start.17 = (bf16[512,384]{1,0:T(8,128)(2,1)S(1)}, bf16[512,384]{1,0:T(8,128)(2,1)S(1)}, u32[]{:S(2)}, u32[]{:S(2)}) collective-permute-start(bf16[512,384]{1,0:T(8,128)(2,1)S(1)} %value_grad.5.refs_6_.refs_2_.refs_4_), channel_id=1, source_target_pairs={{0,4},{4,0},{8,12},{12,8},{16,20},{20,16},{24,28},{28,24},{1,5},{5... | collective-permute-start | bytes 1179656 | tf_op jit(solution)/shard_map/ppermute | solution.py:360
  46.4 1.0 collective-permute-done.10.refs_5_
  47.4 1.8 %value_grad.6.refs_6_.refs_3_.refs_4_ = bf16[512,512]{1,0:T(8,128)(2,1)} custom-call(s32[8]{0:T(128)S(1)} %stack.27.refs_0_, bf16[512,1024]{1,0:T(8,128)(2,1)S(1)} %get-tuple-element.94.refs_1_, f32[512,1024]{1,0:T(8,128)S(1)} %get-tuple-element.88.refs_3_.refs_2_, f32[512,128]{1,0:T(8,128)S(1)} %get-tuple-element.87.refs_4_.refs_3_, ...), custom_call_target="tpu_custom_call" | custom-call | flops 20000000000 | tf_op jit(solution)/shard_map/value_grad/pallas_call | solution.py:45
  49.2 1.4 %collective-permute-start.14 = (bf16[512,512]{1,0:T(8,128)(2,1)}, bf16[512,512]{1,0:T(8,128)(2,1)}, u32[]{:S(2)}, u32[]{:S(2)}) collective-permute-start(bf16[512,512]{1,0:T(8,128)(2,1)} %value_grad.6.refs_6_.refs_3_.refs_4_), channel_id=1, source_target_pairs={{0,4},{4,0},{8,12},{12,8},{16,20},{20,16},{24,28},{28,24},{1,5},{5... | collective-permute-start | bytes 1572872 | tf_op jit(solution)/shard_map/ppermute | solution.py:360
  50.6 1.8 %value_grad.7.refs_6_.refs_4_ = bf16[512,512]{1,0:T(8,128)(2,1)} custom-call(s32[8]{0:T(128)S(1)} %stack.27.refs_0_, bf16[512,1024]{1,0:T(8,128)(2,1)S(1)} %get-tuple-element.94.refs_1_, f32[512,1024]{1,0:T(8,128)S(1)} %get-tuple-element.88.refs_3_.refs_2_, f32[512,128]{1,0:T(8,128)S(1)} %get-tuple-element.87.refs_4_.refs_3_, ...), custom_call_target="tpu_custom_call" | custom-call | flops 20000000000 | tf_op jit(solution)/shard_map/value_grad/pallas_call | solution.py:45
  53.0 1.8 %merge_inputs.1 = (bf16[2,2,224,512]{3,2,1,0:T(8,128)(2,1)S(1)}, bf16[2,2,224,512]{3,2,1,0:T(8,128)(2,1)S(1)}, bf16[2,2,224,512]{3,2,1,0:T(8,128)(2,1)S(1)}, bf16[2,2,224,512]{3,2,1,0:T(8,128)(2,1)S(1)}) custom-call(bf16[2,2,224,512]{3,2,1,0:T(8,128)(2,1)} %get-tuple-element.67.refs_4_.refs_0_, ...), custom_call_target="tpu_custom_call" | custom-call | flops 20000000000 | tf_op jit(solution)/shard_map/merge_inputs/pallas_call | solution.py:45
  54.9 0.9 collective-permute-done.13.refs_5_
  55.8 2.1 %weight_part.4 = (bf16[4,224,384]{2,1,0:T(8,128)(2,1)S(1)}, f32[4,224,384]{2,1,0:T(8,128)S(1)}) custom-call(bf16[2,2,224,512]{3,2,1,0:T(8,128)(2,1)S(1)} %get-tuple-element.96.refs_0_.refs_6_, bf16[2,2,224,512]{3,2,1,0:T(8,128)(2,1)S(1)} %get-tuple-element.97.refs_1_, bf16[2,2,224,512]{3,2,1,0:T(8,128)(2,1)S(1)} %get-tuple-element.98.refs_2_, ...), custom_call_target="tpu_custom_call" | custom-call | flops 20000000000 | tf_op jit(solution)/shard_map/weight_part/pallas_call | solution.py:45
  58.5 3.3 %input_part.4 = (bf16[512,896]{1,0:T(8,128)(2,1)S(1)}, bf16[512,1792]{1,0:T(8,128)(2,1)S(1)}) custom-call(s32[8]{0:T(128)S(1)} %stack.27.refs_0_, bf16[512,384]{1,0:T(8,128)(2,1)S(1)} %value_grad.4.refs_6_.refs_4_.refs_1_, bf16[512,384]{1,0:T(8,128)(2,1)S(1)} %value_grad.5.refs_6_.refs_2_.refs_4_, bf16[512,512]{1,0:T(8,128)(2,1)} %value_grad.6.refs_6_.refs_3_.refs_4_, ...), custom_call_target="tpu_custom_call" | custom-call | flops 20000000000 | tf_op jit(solution)/shard_map/input_part/pallas_call | solution.py:45
  61.8 0.7 fold_weight.10
  62.5 1.7 %collective-permute-start.16 = (bf16[2,224,384]{2,1,0:T(8,128)(2,1)S(1)}, bf16[2,224,384]{2,1,0:T(8,128)(2,1)S(1)}, u32[]{:S(2)}, u32[]{:S(2)}) collective-permute-start(bf16[2,224,384]{2,1,0:T(8,128)(2,1)S(1)} %get-tuple-element.105.refs_6_), channel_id=1, source_target_pairs={{0,8},{4,12},{8,0},{12,4},{16,24},{20,28},{24,16},{28,20},{1,9},{5... | collective-permute-start | bytes 1032200 | tf_op jit(solution)/shard_map/ppermute | solution.py:360
  64.2 2.1 %weight_part.5 = (bf16[4,224,384]{2,1,0:T(8,128)(2,1)S(1)}, f32[4,224,384]{2,1,0:T(8,128)S(1)}) custom-call(bf16[2,2,224,512]{3,2,1,0:T(8,128)(2,1)S(1)} %get-tuple-element.96.refs_0_.refs_6_, bf16[2,2,224,512]{3,2,1,0:T(8,128)(2,1)S(1)} %get-tuple-element.97.refs_1_, bf16[2,2,224,512]{3,2,1,0:T(8,128)(2,1)S(1)} %get-tuple-element.98.refs_2_, ...), custom_call_target="tpu_custom_call" | custom-call | flops 20000000000 | tf_op jit(solution)/shard_map/weight_part/pallas_call | solution.py:45
  66.4 3.9 %input_part.5.refs_3_ = bf16[512,1792]{1,0:T(8,128)(2,1)} custom-call(s32[8]{0:T(128)S(1)} %stack.27.refs_0_, bf16[512,896]{1,0:T(8,128)(2,1)S(1)} %get-tuple-element.103.refs_3_.refs_1_, bf16[512,1792]{1,0:T(8,128)(2,1)S(1)} %get-tuple-element.101.refs_2_.refs_1_, bf16[3584,1792]{1,0:T(8,128)(2,1)S(1)} %bitcast.17, ...), custom_call_target="tpu_custom_call" | custom-call | flops 20000000000 | tf_op jit(solution)/shard_map/input_part/pallas_call | solution.py:45
  70.2 1.2 collective-permute-start.27
  71.5 0.7 fold_weight.11
  72.1 1.4 %collective-permute-start.22 = (bf16[2,224,384]{2,1,0:T(8,128)(2,1)S(1)}, bf16[2,224,384]{2,1,0:T(8,128)(2,1)S(1)}, u32[]{:S(2)}, u32[]{:S(2)}) collective-permute-start(bf16[2,224,384]{2,1,0:T(8,128)(2,1)S(1)} %get-tuple-element.108.refs_3_), channel_id=1, source_target_pairs={{0,8},{4,12},{8,0},{12,4},{16,24},{20,28},{24,16},{28,20},{1,9},{5... | collective-permute-start | bytes 1032200 | tf_op jit(solution)/shard_map/ppermute | solution.py:360
  73.6 0.6 fold_weight.12
  74.2 2.7 %collective-permute-start.23 = (bf16[1,224,384]{2,1,0:T(8,128)(2,1)S(1)}, bf16[1,224,384]{2,1,0:T(8,128)(2,1)S(1)}, u32[]{:S(2)}, u32[]{:S(2)}) collective-permute-start(bf16[1,224,384]{2,1,0:T(8,128)(2,1)S(1)} %get-tuple-element.109.refs_6_), channel_id=1, source_target_pairs={{0,16},{4,20},{8,24},{12,28},{16,0},{20,4},{24,8},{28,12},{1,17},{... | collective-permute-start | bytes 516104 | tf_op jit(solution)/shard_map/ppermute | solution.py:360
  76.8 3.3 %weight_part.6 = (bf16[4,224,512]{2,1,0:T(8,128)(2,1)S(1)}, f32[4,224,512]{2,1,0:T(8,128)S(1)}) custom-call(bf16[2,2,224,512]{3,2,1,0:T(8,128)(2,1)S(1)} %get-tuple-element.96.refs_0_.refs_6_, bf16[2,2,224,512]{3,2,1,0:T(8,128)(2,1)S(1)} %get-tuple-element.97.refs_1_, bf16[2,2,224,512]{3,2,1,0:T(8,128)(2,1)S(1)} %get-tuple-element.98.refs_2_, ...), custom_call_target="tpu_custom_call" | custom-call | flops 20000000000 | tf_op jit(solution)/shard_map/weight_part/pallas_call | solution.py:45
  80.2 2.6 %input_part.6.refs_3_.refs_1_ = f32[512,896]{1,0:T(8,128)S(1)} custom-call(s32[8]{0:T(128)S(1)} %stack.27.refs_0_, bf16[512,1792]{1,0:T(8,128)(2,1)S(1)} %get-tuple-element.101.refs_2_.refs_1_, bf16[3584,1792]{1,0:T(8,128)(2,1)S(1)} %bitcast.17, f32[4,224,512]{2,1,0:T(8,128)S(1)} %get-tuple-element.110.refs_3_.refs_1_), custom_call_target="tpu_custom_call" | custom-call | flops 20000000000 | tf_op jit(solution)/shard_map/input_part/pallas_call | solution.py:45
  82.8 0.8 fold_weight.13
  83.6 0.7 collective-permute-start.26
  84.3 3.5 %weight_part.7 = (bf16[4,224,512]{2,1,0:T(8,128)(2,1)S(1)}, f32[4,224,512]{2,1,0:T(8,128)S(1)}) custom-call(bf16[2,2,224,512]{3,2,1,0:T(8,128)(2,1)S(1)} %get-tuple-element.96.refs_0_.refs_6_, bf16[2,2,224,512]{3,2,1,0:T(8,128)(2,1)S(1)} %get-tuple-element.97.refs_1_, bf16[2,2,224,512]{3,2,1,0:T(8,128)(2,1)S(1)} %get-tuple-element.98.refs_2_, ...), custom_call_target="tpu_custom_call" | custom-call | flops 20000000000 | tf_op jit(solution)/shard_map/weight_part/pallas_call | solution.py:45
  88.0 0.6 fold_weight.14
  88.6 2.4 %collective-permute-start.28 = (bf16[1,224,384]{2,1,0:T(8,128)(2,1)S(1)}, bf16[1,224,384]{2,1,0:T(8,128)(2,1)S(1)}, u32[]{:S(2)}, u32[]{:S(2)}) collective-permute-start(bf16[1,224,384]{2,1,0:T(8,128)(2,1)S(1)} %get-tuple-element.116.refs_3_), channel_id=1, source_target_pairs={{0,16},{4,20},{8,24},{12,28},{16,0},{20,4},{24,8},{28,12},{1,17},{... | collective-permute-start | bytes 516104 | tf_op jit(solution)/shard_map/ppermute | solution.py:360
  91.1 0.7 fold_weight.15
  91.7 0.7 collective-permute-start.25
  92.4 0.7 fold_weight.16
  93.1 1.5 %collective-permute-start.24 = (bf16[2,224,256]{2,1,0:T(8,128)(2,1)S(1)}, bf16[2,224,256]{2,1,0:T(8,128)(2,1)S(1)}, u32[]{:S(2)}, u32[]{:S(2)}) collective-permute-start(bf16[2,224,256]{2,1,0:T(8,128)(2,1)S(1)} %get-tuple-element.119.refs_3_), channel_id=1, source_target_pairs={{0,8},{4,12},{8,0},{12,4},{16,24},{20,28},{24,16},{28,20},{1,9},{5... | collective-permute-start | bytes 688136 | tf_op jit(solution)/shard_map/ppermute | solution.py:360
  94.5 6.1 %collective-permute-done.26.refs_2_ = bf16[2,224,512]{2,1,0:T(8,128)(2,1)S(1)} collective-permute-done((bf16[2,224,512]{2,1,0:T(8,128)(2,1)S(1)}, bf16[2,224,512]{2,1,0:T(8,128)(2,1)S(1)}, u32[]{:S(2)}, u32[]{:S(2)}) %collective-permute-start.26) | collective-permute-done | bytes 458784 | tf_op jit(solution)/shard_map/ppermute | solution.py:360
  100.7 0.7 fold_weight.17
  101.3 0.7 collective-permute-start.29
  102.0 8.5 %collective-permute-done.25.refs_2_ = bf16[2,224,256]{2,1,0:T(8,128)(2,1)S(1)} collective-permute-done((bf16[2,224,256]{2,1,0:T(8,128)(2,1)S(1)}, bf16[2,224,256]{2,1,0:T(8,128)(2,1)S(1)}, u32[]{:S(2)}, u32[]{:S(2)}) %collective-permute-start.25) | collective-permute-done | bytes 229408 | tf_op jit(solution)/shard_map/ppermute | solution.py:360
  111.1 0.7 collective-permute-start.30
  111.8 3.3 %collective-permute-done.24.refs_2_ = bf16[2,224,256]{2,1,0:T(8,128)(2,1)S(1)} collective-permute-done((bf16[2,224,256]{2,1,0:T(8,128)(2,1)S(1)}, bf16[2,224,256]{2,1,0:T(8,128)(2,1)S(1)}, u32[]{:S(2)}, u32[]{:S(2)}) %collective-permute-start.24) | collective-permute-done | bytes 229408 | tf_op jit(solution)/shard_map/ppermute | solution.py:360
  115.7 0.8 collective-permute-start.31
  116.6 2.7 %input_part.7.refs_0_.refs_2_ = f32[512,1792]{1,0:T(8,128)S(1)} custom-call(s32[8]{0:T(128)S(1)} %stack.27.refs_0_, f32[512,896]{1,0:T(8,128)S(1)} %input_part.6.refs_3_.refs_1_, bf16[512,1792]{1,0:T(8,128)(2,1)S(1)} %get-tuple-element.101.refs_2_.refs_1_, bf16[3584,1792]{1,0:T(8,128)(2,1)S(1)} %bitcast.19, bf16[1,224,256]{2,1,0:T(8,128)(2,1)S(1)} %get-tuple-element.124.refs_4_), custom_call_target="tpu_custom_call" | custom-call | flops 20000000000 | tf_op jit(solution)/shard_map/input_part/pallas_call | solution.py:45
  119.3 3.0 %grad_input.1 = (bf16[512,1792]{1,0:T(8,128)(2,1)}, f32[8,128]{1,0:T(8,128)S(1)}) custom-call(f32[512,1792]{1,0:T(8,128)S(1)} %input_part.7.refs_0_.refs_2_, bf16[512,1792]{1,0:T(8,128)(2,1)} %collective-permute-done.27.refs_1_, f32[512,1792]{1,0:T(8,128)S(1)} %input_part.7.refs_0_.refs_2_), custom_call_target="tpu_custom_call" | custom-call | flops 20000000000 | tf_op jit(solution)/shard_map/grad_input/pallas_call | solution.py:45
  122.4 3.6 %collective-permute-done.31.refs_9_ = bf16[1,224,256]{2,1,0:T(8,128)(2,1)S(1)} collective-permute-done((bf16[1,224,256]{2,1,0:T(8,128)(2,1)S(1)}, bf16[1,224,256]{2,1,0:T(8,128)(2,1)S(1)}, u32[]{:S(2)}, u32[]{:S(2)}) %collective-permute-start.31) | collective-permute-done | bytes 114720 | tf_op jit(solution)/shard_map/ppermute | solution.py:360
  126.0 1.3 %grad_weight.1 = f32[224,1792]{1,0:T(8,128)} custom-call(f32[1,224,384]{2,1,0:T(8,128)S(1)} %get-tuple-element.126.refs_0_, bf16[1,224,384]{2,1,0:T(8,128)(2,1)S(1)} %collective-permute-done.23.refs_1_, f32[1,224,384]{2,1,0:T(8,128)S(1)} %get-tuple-element.127.refs_2_, bf16[1,224,384]{2,1,0:T(8,128)(2,1)S(1)} %collective-permute-done.28.refs_3_, ...), custom_call_target="tpu_custom_call" | custom-call | flops 20000000000 | tf_op jit(solution)/shard_map/grad_weight/pallas_call | solution.py:45
  (69 shorter events, 6.7 us)
Async XLA Ops:
  0.8 1.5 %copy-start.2 = (bf16[1,512,1792]{2,1,0:T(8,128)(2,1)S(1)}, bf16[1,512,1792]{2,1,0:T(8,128)(2,1)}, u32[]{:S(2)}) copy-start(bf16[1,512,1792]{2,1,0:T(8,128)(2,1)} %param.6) | copy-start | bytes 5505028
  2.3 5.1 %copy-start.4 = (f32[1,14,512]{2,0,1:T(1,128)S(1)}, f32[1,14,512]{2,0,1:T(1,128)}, u32[]{:S(2)}) copy-start(f32[1,14,512]{2,0,1:T(1,128)} %param.11) | copy-start | bytes 86020
  2.3 5.1 %copy-start = (s32[1,512,1792]{2,1,0:T(8,128)S(1)}, s32[1,512,1792]{2,1,0:T(8,128)}, u32[]{:S(2)}) copy-start(s32[1,512,1792]{2,1,0:T(8,128)} %param.9) | copy-start | bytes 11010052
  2.3 5.1 %copy-start.3 = (bf16[1,512,1792]{2,1,0:T(8,128)(2,1)S(1)}, bf16[1,512,1792]{2,1,0:T(8,128)(2,1)}, u32[]{:S(2)}) copy-start(bf16[1,512,1792]{2,1,0:T(8,128)(2,1)} %param.8) | copy-start | bytes 5505028
  4.4 38.0 %collective-permute-start.9 = (bf16[2,2,224,512]{3,2,1,0:T(8,128)(2,1)}, bf16[2,2,224,512]{3,2,1,0:T(8,128)(2,1)}, u32[]{:S(2)}, u32[]{:S(2)}) collective-permute-start(bf16[2,2,224,512]{3,2,1,0:T(8,128)(2,1)} %get-tuple-element.67.refs_4_.refs_0_), channel_id=1, source_target_pairs={{0,2},{2,0},{1,3},{3,1},{4,6},{6,4},{5,7},{7,5},{8,10},{10,8},{9,1... | collective-permute-start | bytes 2752520 | tf_op jit(solution)/shard_map/ppermute | solution.py:360
  9.5 6.0 %collective-permute-start.1 = (bf16[432,128]{1,0:T(8,128)(2,1)S(1)}, bf16[432,128]{1,0:T(8,128)(2,1)S(1)}, u32[]{:S(2)}, u32[]{:S(2)}) collective-permute-start(bf16[432,128]{1,0:T(8,128)(2,1)S(1)} %get-tuple-element.71.refs_4_), channel_id=1, source_target_pairs={{0,4},{4,0},{8,12},{12,8},{16,20},{20,16},{24,28},{28,24},{1,5},{5... | collective-permute-start | bytes 331784 | tf_op jit(solution)/shard_map/ppermute | solution.py:360
  13.4 6.8 %collective-permute-start = (bf16[560,128]{1,0:T(8,128)(2,1)S(1)}, bf16[560,128]{1,0:T(8,128)(2,1)S(1)}, u32[]{:S(2)}, u32[]{:S(2)}) collective-permute-start(bf16[560,128]{1,0:T(8,128)(2,1)S(1)} %get-tuple-element.73.refs_3_), channel_id=1, source_target_pairs={{0,4},{4,0},{8,12},{12,8},{16,20},{20,16},{24,28},{28,24},{1,5},{5... | collective-permute-start | bytes 430088 | tf_op jit(solution)/shard_map/ppermute | solution.py:360
  13.9 18.0 %collective-permute-start.4 = (bf16[1,2,224,512]{3,2,1,0:T(8,128)(2,1)S(1)}, bf16[1,2,224,512]{3,2,1,0:T(8,128)(2,1)S(1)}, u32[]{:S(2)}, u32[]{:S(2)}) collective-permute-start(bf16[1,2,224,512]{3,2,1,0:T(8,128)(2,1)S(1)} %get-tuple-element.83.refs_4_), channel_id=1, source_target_pairs={{0,4},{4,0},{8,12},{12,8},{16,20},{20,16},{24,28},{28,24},{1,5},{5... | collective-permute-start | bytes 1376264 | tf_op jit(solution)/shard_map/ppermute | solution.py:360
  16.0 8.1 %collective-permute-start.2 = (bf16[432,128]{1,0:T(8,128)(2,1)S(1)}, bf16[432,128]{1,0:T(8,128)(2,1)S(1)}, u32[]{:S(2)}, u32[]{:S(2)}) collective-permute-start(bf16[432,128]{1,0:T(8,128)(2,1)S(1)} %get-tuple-element.76.refs_3_), channel_id=1, source_target_pairs={{8,0},{12,4},{16,8},{20,12},{24,16},{28,20},{9,1},{13,5},{17,9},{2... | collective-permute-start | bytes 331784 | tf_op jit(solution)/shard_map/ppermute | solution.py:364
  17.3 21.7 %collective-permute-start.8 = (bf16[1,2,224,512]{3,2,1,0:T(8,128)(2,1)S(1)}, bf16[1,2,224,512]{3,2,1,0:T(8,128)(2,1)S(1)}, u32[]{:S(2)}, u32[]{:S(2)}) collective-permute-start(bf16[1,2,224,512]{3,2,1,0:T(8,128)(2,1)S(1)} %get-tuple-element.92.refs_4_), channel_id=1, source_target_pairs={{0,4},{4,0},{8,12},{12,8},{16,20},{20,16},{24,28},{28,24},{1,5},{5... | collective-permute-start | bytes 1376264 | tf_op jit(solution)/shard_map/ppermute | solution.py:360
  20.1 2.0 %copy-start.1 = (s32[1,512,1792]{2,1,0:T(8,128)S(1)}, s32[1,512,1792]{2,1,0:T(8,128)}, u32[]{:S(2)}) copy-start(s32[1,512,1792]{2,1,0:T(8,128)} %param.10) | copy-start | bytes 11010052
  20.7 8.5 %collective-permute-start.5 = (bf16[560,128]{1,0:T(8,128)(2,1)S(1)}, bf16[560,128]{1,0:T(8,128)(2,1)S(1)}, u32[]{:S(2)}, u32[]{:S(2)}) collective-permute-start(bf16[560,128]{1,0:T(8,128)(2,1)S(1)} %get-tuple-element.78.refs_5_), channel_id=1, source_target_pairs={{8,0},{12,4},{16,8},{20,12},{24,16},{28,20},{9,1},{13,5},{17,9},{2... | collective-permute-start | bytes 430088 | tf_op jit(solution)/shard_map/ppermute | solution.py:364
  25.4 7.6 %collective-permute-start.3 = (bf16[432,128]{1,0:T(8,128)(2,1)S(1)}, bf16[432,128]{1,0:T(8,128)(2,1)S(1)}, u32[]{:S(2)}, u32[]{:S(2)}) collective-permute-start(bf16[432,128]{1,0:T(8,128)(2,1)S(1)} %get-tuple-element.82.refs_5_), channel_id=1, source_target_pairs={{16,0},{20,4},{24,8},{28,12},{17,1},{21,5},{25,9},{29,13},{18,2},{... | collective-permute-start | bytes 331784 | tf_op jit(solution)/shard_map/ppermute | solution.py:364
  30.5 9.8 %collective-permute-start.7 = (bf16[560,128]{1,0:T(8,128)(2,1)S(1)}, bf16[560,128]{1,0:T(8,128)(2,1)S(1)}, u32[]{:S(2)}, u32[]{:S(2)}) collective-permute-start(bf16[560,128]{1,0:T(8,128)(2,1)S(1)} %get-tuple-element.89.refs_1_), channel_id=1, source_target_pairs={{16,0},{20,4},{24,8},{28,12},{17,1},{21,5},{25,9},{29,13},{18,2},{... | collective-permute-start | bytes 430088 | tf_op jit(solution)/shard_map/ppermute | solution.py:364
  32.0 15.3 %collective-permute-start.11 = (bf16[1,2,224,512]{3,2,1,0:T(8,128)(2,1)S(1)}, bf16[1,2,224,512]{3,2,1,0:T(8,128)(2,1)S(1)}, u32[]{:S(2)}, u32[]{:S(2)}) collective-permute-start(bf16[1,2,224,512]{3,2,1,0:T(8,128)(2,1)S(1)} %pass_on.2.refs_5_.refs_2_), channel_id=1, source_target_pairs={{0,2},{2,0},{1,3},{3,1},{4,6},{6,4},{5,7},{7,5},{8,10},{10,8},{9,1... | collective-permute-start | bytes 1376264 | tf_op jit(solution)/shard_map/ppermute | solution.py:360
  33.6 8.7 %collective-permute-start.6 = (bf16[384,128]{1,0:T(8,128)(2,1)S(1)}, bf16[384,128]{1,0:T(8,128)(2,1)S(1)}, u32[]{:S(2)}, u32[]{:S(2)}) collective-permute-start(bf16[384,128]{1,0:T(8,128)(2,1)S(1)} %get-tuple-element.91.refs_1_), channel_id=1, source_target_pairs={{0,4},{4,0},{8,12},{12,8},{16,20},{20,16},{24,28},{28,24},{1,5},{5... | collective-permute-start | bytes 294920 | tf_op jit(solution)/shard_map/ppermute | solution.py:360
  39.1 13.9 %collective-permute-start.12 = (bf16[1,2,224,512]{3,2,1,0:T(8,128)(2,1)S(1)}, bf16[1,2,224,512]{3,2,1,0:T(8,128)(2,1)S(1)}, u32[]{:S(2)}, u32[]{:S(2)}) collective-permute-start(bf16[1,2,224,512]{3,2,1,0:T(8,128)(2,1)S(1)} %pass_on.3.refs_5_.refs_3_), channel_id=1, source_target_pairs={{0,2},{2,0},{1,3},{3,1},{4,6},{6,4},{5,7},{7,5},{8,10},{10,8},{9,1... | collective-permute-start | bytes 1376264 | tf_op jit(solution)/shard_map/ppermute | solution.py:360
  40.9 6.4 %collective-permute-start.10 = (bf16[512,128]{1,0:T(8,128)(2,1)S(1)}, bf16[512,128]{1,0:T(8,128)(2,1)S(1)}, u32[]{:S(2)}, u32[]{:S(2)}) collective-permute-start(bf16[512,128]{1,0:T(8,128)(2,1)S(1)} %get-tuple-element.93.refs_6_), channel_id=1, source_target_pairs={{0,4},{4,0},{8,12},{12,8},{16,20},{20,16},{24,28},{28,24},{1,5},{5... | collective-permute-start | bytes 393224 | tf_op jit(solution)/shard_map/ppermute | solution.py:360
  43.3 12.5 %collective-permute-start.13 = (bf16[512,384]{1,0:T(8,128)(2,1)S(1)}, bf16[512,384]{1,0:T(8,128)(2,1)S(1)}, u32[]{:S(2)}, u32[]{:S(2)}) collective-permute-start(bf16[512,384]{1,0:T(8,128)(2,1)S(1)} %value_grad.4.refs_6_.refs_4_.refs_1_), channel_id=1, source_target_pairs={{0,4},{4,0},{8,12},{12,8},{16,20},{20,16},{24,28},{28,24},{1,5},{5... | collective-permute-start | bytes 1179656 | tf_op jit(solution)/shard_map/ppermute | solution.py:360
  44.9 19.3 %collective-permute-start.17 = (bf16[512,384]{1,0:T(8,128)(2,1)S(1)}, bf16[512,384]{1,0:T(8,128)(2,1)S(1)}, u32[]{:S(2)}, u32[]{:S(2)}) collective-permute-start(bf16[512,384]{1,0:T(8,128)(2,1)S(1)} %value_grad.5.refs_6_.refs_2_.refs_4_), channel_id=1, source_target_pairs={{0,4},{4,0},{8,12},{12,8},{16,20},{20,16},{24,28},{28,24},{1,5},{5... | collective-permute-start | bytes 1179656 | tf_op jit(solution)/shard_map/ppermute | solution.py:360
  49.2 27.7 %collective-permute-start.14 = (bf16[512,512]{1,0:T(8,128)(2,1)}, bf16[512,512]{1,0:T(8,128)(2,1)}, u32[]{:S(2)}, u32[]{:S(2)}) collective-permute-start(bf16[512,512]{1,0:T(8,128)(2,1)} %value_grad.6.refs_6_.refs_3_.refs_4_), channel_id=1, source_target_pairs={{0,4},{4,0},{8,12},{12,8},{16,20},{20,16},{24,28},{28,24},{1,5},{5... | collective-permute-start | bytes 1572872 | tf_op jit(solution)/shard_map/ppermute | solution.py:360
  52.4 31.9 %collective-permute-start.19 = (bf16[512,512]{1,0:T(8,128)(2,1)}, bf16[512,512]{1,0:T(8,128)(2,1)}, u32[]{:S(2)}, u32[]{:S(2)}) collective-permute-start(bf16[512,512]{1,0:T(8,128)(2,1)} %value_grad.7.refs_6_.refs_4_), channel_id=1, source_target_pairs={{0,4},{4,0},{8,12},{12,8},{16,20},{20,16},{24,28},{28,24},{1,5},{5... | collective-permute-start | bytes 1572872 | tf_op jit(solution)/shard_map/ppermute | solution.py:360
  53.0 4.9 %slice-start = ((s8[12845056]{0:T(1024)(128)(4,1)}), s8[4194304]{0:T(1024)(128)(4,1)S(1)}, s32[]{:S(2)}) async-start(s8[12845056]{0:T(1024)(128)(4,1)} %bitcast.16), calls=%async_computation | async-start | bytes 8388608
  53.0 4.9 %slice-start.1 = ((s8[12845056]{0:T(1024)(128)(4,1)}), s8[4194304]{0:T(1024)(128)(4,1)S(1)}, s32[]{:S(2)}) async-start(s8[12845056]{0:T(1024)(128)(4,1)} %bitcast.16), calls=%async_computation.1 | async-start | bytes 8388608
  55.8 2.7 %slice-start.2 = ((s8[12845056]{0:T(1024)(128)(4,1)}), s8[4194304]{0:T(1024)(128)(4,1)S(1)}, s32[]{:S(2)}) async-start(s8[12845056]{0:T(1024)(128)(4,1)} %bitcast.16), calls=%async_computation.2 | async-start | bytes 8388608
  55.8 2.7 %slice-start.3 = ((s8[12845056]{0:T(1024)(128)(4,1)}), s8[262144]{0:T(1024)(128)(4,1)S(1)}, s32[]{:S(2)}) async-start(s8[12845056]{0:T(1024)(128)(4,1)} %bitcast.16), calls=%async_computation.3 | async-start | bytes 524288
  57.9 3.9 %collective-permute-start.15 = (bf16[4,224,384]{2,1,0:T(8,128)(2,1)S(1)}, bf16[4,224,384]{2,1,0:T(8,128)(2,1)S(1)}, u32[]{:S(2)}, u32[]{:S(2)}) collective-permute-start(bf16[4,224,384]{2,1,0:T(8,128)(2,1)S(1)} %get-tuple-element.102), channel_id=1, source_target_pairs={{0,1},{1,0},{2,3},{3,2},{4,5},{5,4},{6,7},{7,6},{8,9},{9,8},{10,11... | collective-permute-start | bytes 2064392 | tf_op jit(solution)/shard_map/ppermute | solution.py:360
  62.5 11.1 %collective-permute-start.16 = (bf16[2,224,384]{2,1,0:T(8,128)(2,1)S(1)}, bf16[2,224,384]{2,1,0:T(8,128)(2,1)S(1)}, u32[]{:S(2)}, u32[]{:S(2)}) collective-permute-start(bf16[2,224,384]{2,1,0:T(8,128)(2,1)S(1)} %get-tuple-element.105.refs_6_), channel_id=1, source_target_pairs={{0,8},{4,12},{8,0},{12,4},{16,24},{20,28},{24,16},{28,20},{1,9},{5... | collective-permute-start | bytes 1032200 | tf_op jit(solution)/shard_map/ppermute | solution.py:360
  66.3 5.2 %collective-permute-start.18 = (bf16[4,224,384]{2,1,0:T(8,128)(2,1)S(1)}, bf16[4,224,384]{2,1,0:T(8,128)(2,1)S(1)}, u32[]{:S(2)}, u32[]{:S(2)}) collective-permute-start(bf16[4,224,384]{2,1,0:T(8,128)(2,1)S(1)} %get-tuple-element.107), channel_id=1, source_target_pairs={{0,1},{1,0},{2,3},{3,2},{4,5},{5,4},{6,7},{7,6},{8,9},{9,8},{10,11... | collective-permute-start | bytes 2064392 | tf_op jit(solution)/shard_map/ppermute | solution.py:360
  70.2 49.1 %collective-permute-start.27 = (bf16[512,1792]{1,0:T(8,128)(2,1)}, bf16[512,1792]{1,0:T(8,128)(2,1)}, u32[]{:S(2)}, u32[]{:S(2)}) collective-permute-start(bf16[512,1792]{1,0:T(8,128)(2,1)} %input_part.5.refs_3_), channel_id=1, source_target_pairs={{0,2},{2,0},{1,3},{3,1},{4,6},{6,4},{5,7},{7,5},{8,10},{10,8},{9,1... | collective-permute-start | bytes 5505032 | tf_op jit(solution)/shard_map/ppermute | solution.py:360
  72.1 15.9 %collective-permute-start.22 = (bf16[2,224,384]{2,1,0:T(8,128)(2,1)S(1)}, bf16[2,224,384]{2,1,0:T(8,128)(2,1)S(1)}, u32[]{:S(2)}, u32[]{:S(2)}) collective-permute-start(bf16[2,224,384]{2,1,0:T(8,128)(2,1)S(1)} %get-tuple-element.108.refs_3_), channel_id=1, source_target_pairs={{0,8},{4,12},{8,0},{12,4},{16,24},{20,28},{24,16},{28,20},{1,9},{5... | collective-permute-start | bytes 1032200 | tf_op jit(solution)/shard_map/ppermute | solution.py:360
  74.2 13.8 %collective-permute-start.23 = (bf16[1,224,384]{2,1,0:T(8,128)(2,1)S(1)}, bf16[1,224,384]{2,1,0:T(8,128)(2,1)S(1)}, u32[]{:S(2)}, u32[]{:S(2)}) collective-permute-start(bf16[1,224,384]{2,1,0:T(8,128)(2,1)S(1)} %get-tuple-element.109.refs_6_), channel_id=1, source_target_pairs={{0,16},{4,20},{8,24},{12,28},{16,0},{20,4},{24,8},{28,12},{1,17},{... | collective-permute-start | bytes 516104 | tf_op jit(solution)/shard_map/ppermute | solution.py:360
  80.1 2.7 %collective-permute-start.20 = (bf16[4,224,512]{2,1,0:T(8,128)(2,1)S(1)}, bf16[4,224,512]{2,1,0:T(8,128)(2,1)S(1)}, u32[]{:S(2)}, u32[]{:S(2)}) collective-permute-start(bf16[4,224,512]{2,1,0:T(8,128)(2,1)S(1)} %get-tuple-element.111), channel_id=1, source_target_pairs={{0,1},{1,0},{2,3},{3,2},{4,5},{5,4},{6,7},{7,6},{8,9},{9,8},{10,11... | collective-permute-start | bytes 2752520 | tf_op jit(solution)/shard_map/ppermute | solution.py:360
  83.6 17.1 %collective-permute-start.26 = (bf16[2,224,512]{2,1,0:T(8,128)(2,1)S(1)}, bf16[2,224,512]{2,1,0:T(8,128)(2,1)S(1)}, u32[]{:S(2)}, u32[]{:S(2)}) collective-permute-start(bf16[2,224,512]{2,1,0:T(8,128)(2,1)S(1)} %get-tuple-element.112.refs_6_), channel_id=1, source_target_pairs={{0,8},{4,12},{8,0},{12,4},{16,24},{20,28},{24,16},{28,20},{1,9},{5... | collective-permute-start | bytes 1376264 | tf_op jit(solution)/shard_map/ppermute | solution.py:360
  87.8 3.2 %collective-permute-start.21 = (bf16[4,224,512]{2,1,0:T(8,128)(2,1)S(1)}, bf16[4,224,512]{2,1,0:T(8,128)(2,1)S(1)}, u32[]{:S(2)}, u32[]{:S(2)}) collective-permute-start(bf16[4,224,512]{2,1,0:T(8,128)(2,1)S(1)} %get-tuple-element.114), channel_id=1, source_target_pairs={{0,1},{1,0},{2,3},{3,2},{4,5},{5,4},{6,7},{7,6},{8,9},{9,8},{10,11... | collective-permute-start | bytes 2752520 | tf_op jit(solution)/shard_map/ppermute | solution.py:360
  88.6 33.7 %collective-permute-start.28 = (bf16[1,224,384]{2,1,0:T(8,128)(2,1)S(1)}, bf16[1,224,384]{2,1,0:T(8,128)(2,1)S(1)}, u32[]{:S(2)}, u32[]{:S(2)}) collective-permute-start(bf16[1,224,384]{2,1,0:T(8,128)(2,1)S(1)} %get-tuple-element.116.refs_3_), channel_id=1, source_target_pairs={{0,16},{4,20},{8,24},{12,28},{16,0},{20,4},{24,8},{28,12},{1,17},{... | collective-permute-start | bytes 516104 | tf_op jit(solution)/shard_map/ppermute | solution.py:360
  91.7 18.8 %collective-permute-start.25 = (bf16[2,224,256]{2,1,0:T(8,128)(2,1)S(1)}, bf16[2,224,256]{2,1,0:T(8,128)(2,1)S(1)}, u32[]{:S(2)}, u32[]{:S(2)}) collective-permute-start(bf16[2,224,256]{2,1,0:T(8,128)(2,1)S(1)} %get-tuple-element.117.refs_3_), channel_id=1, source_target_pairs={{0,8},{4,12},{8,0},{12,4},{16,24},{20,28},{24,16},{28,20},{1,9},{5... | collective-permute-start | bytes 688136 | tf_op jit(solution)/shard_map/ppermute | solution.py:360
  93.1 22.0 %collective-permute-start.24 = (bf16[2,224,256]{2,1,0:T(8,128)(2,1)S(1)}, bf16[2,224,256]{2,1,0:T(8,128)(2,1)S(1)}, u32[]{:S(2)}, u32[]{:S(2)}) collective-permute-start(bf16[2,224,256]{2,1,0:T(8,128)(2,1)S(1)} %get-tuple-element.119.refs_3_), channel_id=1, source_target_pairs={{0,8},{4,12},{8,0},{12,4},{16,24},{20,28},{24,16},{28,20},{1,9},{5... | collective-permute-start | bytes 688136 | tf_op jit(solution)/shard_map/ppermute | solution.py:360
  101.3 21.0 %collective-permute-start.29 = (bf16[1,224,512]{2,1,0:T(8,128)(2,1)S(1)}, bf16[1,224,512]{2,1,0:T(8,128)(2,1)S(1)}, u32[]{:S(2)}, u32[]{:S(2)}) collective-permute-start(bf16[1,224,512]{2,1,0:T(8,128)(2,1)S(1)} %get-tuple-element.122.refs_3_), channel_id=1, source_target_pairs={{0,16},{4,20},{8,24},{12,28},{16,0},{20,4},{24,8},{28,12},{1,17},{... | collective-permute-start | bytes 688136 | tf_op jit(solution)/shard_map/ppermute | solution.py:360
  110.5 6.1 %slice-start.4 = ((s8[12845056]{0:T(1024)(128)(4,1)}), s8[4194304]{0:T(1024)(128)(4,1)S(1)}, s32[]{:S(2)}) async-start(s8[12845056]{0:T(1024)(128)(4,1)} %bitcast.18), calls=%async_computation.4 | async-start | bytes 8388608
  110.5 6.1 %slice-start.5 = ((s8[12845056]{0:T(1024)(128)(4,1)}), s8[4194304]{0:T(1024)(128)(4,1)S(1)}, s32[]{:S(2)}) async-start(s8[12845056]{0:T(1024)(128)(4,1)} %bitcast.18), calls=%async_computation.5 | async-start | bytes 8388608
  111.1 5.5 %slice-start.6 = ((s8[12845056]{0:T(1024)(128)(4,1)}), s8[4194304]{0:T(1024)(128)(4,1)S(1)}, s32[]{:S(2)}) async-start(s8[12845056]{0:T(1024)(128)(4,1)} %bitcast.18), calls=%async_computation.6 | async-start | bytes 8388608
  111.1 14.9 %collective-permute-start.30 = (bf16[1,224,256]{2,1,0:T(8,128)(2,1)S(1)}, bf16[1,224,256]{2,1,0:T(8,128)(2,1)S(1)}, u32[]{:S(2)}, u32[]{:S(2)}) collective-permute-start(bf16[1,224,256]{2,1,0:T(8,128)(2,1)S(1)} %get-tuple-element.123.refs_3_), channel_id=1, source_target_pairs={{0,16},{4,20},{8,24},{12,28},{16,0},{20,4},{24,8},{28,12},{1,17},{... | collective-permute-start | bytes 344072 | tf_op jit(solution)/shard_map/ppermute | solution.py:360
  115.1 1.4 %slice-start.7 = ((s8[12845056]{0:T(1024)(128)(4,1)}), s8[262144]{0:T(1024)(128)(4,1)S(1)}, s32[]{:S(2)}) async-start(s8[12845056]{0:T(1024)(128)(4,1)} %bitcast.18), calls=%async_computation.7 | async-start | bytes 524288
  115.7 10.3 %collective-permute-start.31 = (bf16[1,224,256]{2,1,0:T(8,128)(2,1)S(1)}, bf16[1,224,256]{2,1,0:T(8,128)(2,1)S(1)}, u32[]{:S(2)}, u32[]{:S(2)}) collective-permute-start(bf16[1,224,256]{2,1,0:T(8,128)(2,1)S(1)} %get-tuple-element.124.refs_4_), channel_id=1, source_target_pairs={{0,16},{4,20},{8,24},{12,28},{16,0},{20,4},{24,8},{28,12},{1,17},{... | collective-permute-start | bytes 344072 | tf_op jit(solution)/shard_map/ppermute | solution.py:360

commit v7 on v6

--- a/solution.py
+++ b/solution.py
@@ -455,9 +455,10 @@
             kept[i, j] = (keep, swap_with(away, "seq", 2 << bit))
 
     others = []
-    middle = rows_here // 2 if rows_here % 256 == 0 else 0
+    shares = (6, 9) if rows_here % (14 * HD) == 0 else (0, 0)
 
     def input_parts(at, dtype, step):
+        middle = rows_here // 14 * shares[at != at_sides]
         common = (value_weight, rows_here, dtype)
         if step == 0 and not middle:
             return pause(line)

time: 128 us -> 128 us (level)
  transfers between devices with their start and end apart: 32 -> 32, of which waited for: 10 -> 10; matrix products, arithmetic and copies ran while one was open for 0% -> 0% of each run, Pallas kernels for 43% -> 42%
where the time goes in v7:
time: 128 us; the launch traced here: 127 us
  Pallas kernels  57.1 us (45%)
  starting transfers between devices  36.5 us (29%)
  waiting for transfers between devices  30.3 us (24%)
  local copies, waits for them, and re-layouts  2.24 us (2%)
    pallas_call x39, Pallas kernels, __call__(): pl.pallas_call(body, in_specs=[SM] * len(smalls) + [VM] * len(arrays) + [...  57.1 us
    ppermute x28, starting transfers between devices, swap_with(): lax.ppermute(x, axis, [(i, i ^ bit) for i in range(lax.axis_size(axis))])  31.1 us
    ppermute x28, waiting for transfers between devices, swap_with(): lax.ppermute(x, axis, [(i, i ^ bit) for i in range(lax.axis_size(axis))])  30.2 us
    ppermute x4, starting transfers between devices, from_later(): lax.ppermute(x, axis, [(i, i - shift) for i in range(shift, lax.axis_size...  5.46 us
  transfers between devices with their start and end apart: 32, of which 10 were waited for; matrix products, arithmetic and copies ran while one was open for 0% of the time, Pallas kernels for 42%

profile of v7, /device:TPU:0, one launch (start us, length us, event | category | flops | bytes accessed | tf_op | source)
XLA Modules:
  0.0 127.2 jit_solution(11537811485443711305)
XLA Ops:
  0.8 1.5 %copy-done.2 = bf16[1,512,1792]{2,1,0:T(8,128)(2,1)S(1)} copy-done((bf16[1,512,1792]{2,1,0:T(8,128)(2,1)S(1)}, bf16[1,512,1792]{2,1,0:T(8,128)(2,1)}, u32[]{:S(2)}) %copy-start.2) | copy-done | bytes 1835032
  2.3 2.1 %transpose_inputs.1 = (bf16[2,2,224,512]{3,2,1,0:T(8,128)(2,1)}, bf16[1,2,224,512]{3,2,1,0:T(8,128)(2,1)S(1)}, bf16[1,2,224,512]{3,2,1,0:T(8,128)(2,1)S(1)}) custom-call(s32[8]{0:T(128)S(1)} %stack.27.refs_0_, bf16[512,1792]{1,0:T(8,128)(2,1)S(1)} %bitcast.24), custom_call_target="tpu_custom_call" | custom-call | flops 20000000000 | tf_op jit(solution)/shard_map/transpose_inputs/pallas_call | solution.py:45
  4.4 2.9 %collective-permute-start.9 = (bf16[2,2,224,512]{3,2,1,0:T(8,128)(2,1)}, bf16[2,2,224,512]{3,2,1,0:T(8,128)(2,1)}, u32[]{:S(2)}, u32[]{:S(2)}) collective-permute-start(bf16[2,2,224,512]{3,2,1,0:T(8,128)(2,1)} %get-tuple-element.67.refs_4_.refs_0_), channel_id=1, source_target_pairs={{0,2},{2,0},{1,3},{3,1},{4,6},{6,4},{5,7},{7,5},{8,10},{10,8},{9,1... | collective-permute-start | bytes 2752520 | tf_op jit(solution)/shard_map/ppermute | solution.py:360
  7.3 2.1 %state_terms.2 = (bf16[432,128]{1,0:T(8,128)(2,1)S(1)}, f32[432,128]{1,0:T(8,128)S(1)}, f32[16,512]{1,0:T(8,128)S(1)}, f32[512,128]{1,0:T(8,128)S(1)}, bf16[512,768]{1,0:T(8,128)(2,1)S(1)}) custom-call(s32[8]{0:T(128)S(1)} %stack.27.refs_0_, f32[14,512]{1,0:T(8,128)S(1)} %bitcast.14, s32[512,1792]{1,0:T(8,128)S(1)} %bitcast.20, ...), custom_call_target="tpu_custom_call" | custom-call | flops 20000000000 | tf_op jit(solution)/shard_map/state_terms/pallas_call | solution.py:45
  9.5 1.6 %collective-permute-start.1 = (bf16[432,128]{1,0:T(8,128)(2,1)S(1)}, bf16[432,128]{1,0:T(8,128)(2,1)S(1)}, u32[]{:S(2)}, u32[]{:S(2)}) collective-permute-start(bf16[432,128]{1,0:T(8,128)(2,1)S(1)} %get-tuple-element.71.refs_4_), channel_id=1, source_target_pairs={{0,4},{4,0},{8,12},{12,8},{16,20},{20,16},{24,28},{28,24},{1,5},{5... | collective-permute-start | bytes 331784 | tf_op jit(solution)/shard_map/ppermute | solution.py:360
  11.0 2.3 %state_terms.3 = (bf16[560,128]{1,0:T(8,128)(2,1)S(1)}, f32[560,128]{1,0:T(8,128)S(1)}, f32[16,512]{1,0:T(8,128)S(1)}, f32[512,128]{1,0:T(8,128)S(1)}, bf16[512,1024]{1,0:T(8,128)(2,1)S(1)}) custom-call(s32[8]{0:T(128)S(1)} %stack.27.refs_0_, f32[14,512]{1,0:T(8,128)S(1)} %bitcast.15, s32[512,1792]{1,0:T(8,128)S(1)} %bitcast.21, ...), custom_call_target="tpu_custom_call" | custom-call | flops 20000000000 | tf_op jit(solution)/shard_map/state_terms/pallas_call | solution.py:45
  13.9 1.5 %collective-permute-start.4 = (bf16[1,2,224,512]{3,2,1,0:T(8,128)(2,1)S(1)}, bf16[1,2,224,512]{3,2,1,0:T(8,128)(2,1)S(1)}, u32[]{:S(2)}, u32[]{:S(2)}) collective-permute-start(bf16[1,2,224,512]{3,2,1,0:T(8,128)(2,1)S(1)} %get-tuple-element.83.refs_4_), channel_id=1, source_target_pairs={{0,4},{4,0},{8,12},{12,8},{16,20},{20,16},{24,28},{28,24},{1,5},{5... | collective-permute-start | bytes 1376264 | tf_op jit(solution)/shard_map/ppermute | solution.py:360
  16.0 1.3 %collective-permute-start.2 = (bf16[432,128]{1,0:T(8,128)(2,1)S(1)}, bf16[432,128]{1,0:T(8,128)(2,1)S(1)}, u32[]{:S(2)}, u32[]{:S(2)}) collective-permute-start(bf16[432,128]{1,0:T(8,128)(2,1)S(1)} %get-tuple-element.76.refs_3_), channel_id=1, source_target_pairs={{8,0},{12,4},{16,8},{20,12},{24,16},{28,20},{9,1},{13,5},{17,9},{2... | collective-permute-start | bytes 331784 | tf_op jit(solution)/shard_map/ppermute | solution.py:364
  17.9 2.2 %collective-permute-done.refs_2_ = bf16[560,128]{1,0:T(8,128)(2,1)S(1)} collective-permute-done((bf16[560,128]{1,0:T(8,128)(2,1)S(1)}, bf16[560,128]{1,0:T(8,128)(2,1)S(1)}, u32[]{:S(2)}, u32[]{:S(2)}) %collective-permute-start) | collective-permute-done | bytes 143392 | tf_op jit(solution)/shard_map/ppermute | solution.py:360
  20.7 1.4 %collective-permute-start.5 = (bf16[560,128]{1,0:T(8,128)(2,1)S(1)}, bf16[560,128]{1,0:T(8,128)(2,1)S(1)}, u32[]{:S(2)}, u32[]{:S(2)}) collective-permute-start(bf16[560,128]{1,0:T(8,128)(2,1)S(1)} %get-tuple-element.78.refs_5_), channel_id=1, source_target_pairs={{8,0},{12,4},{16,8},{20,12},{24,16},{28,20},{9,1},{13,5},{17,9},{2... | collective-permute-start | bytes 430088 | tf_op jit(solution)/shard_map/ppermute | solution.py:364
  22.2 1.9 %local_part.2 = (f32[512,768]{1,0:T(8,128)S(1)}, bf16[512,768]{1,0:T(8,128)(2,1)S(1)}) custom-call(bf16[512,768]{1,0:T(8,128)(2,1)S(1)} %get-tuple-element.68.refs_0_, s32[512,1792]{1,0:T(8,128)S(1)} %bitcast.22, bf16[512,1792]{1,0:T(8,128)(2,1)S(1)} %bitcast.27, f32[16,512]{1,0:T(8,128)S(1)} %get-tuple-element.69.refs_3_, ...), custom_call_target="tpu_custom_call" | custom-call | flops 20000000000 | tf_op jit(solution)/shard_map/local_part/pallas_call | solution.py:45
  24.1 1.3 join_states.6
  25.4 1.3 %collective-permute-start.3 = (bf16[432,128]{1,0:T(8,128)(2,1)S(1)}, bf16[432,128]{1,0:T(8,128)(2,1)S(1)}, u32[]{:S(2)}, u32[]{:S(2)}) collective-permute-start(bf16[432,128]{1,0:T(8,128)(2,1)S(1)} %get-tuple-element.82.refs_5_), channel_id=1, source_target_pairs={{16,0},{20,4},{24,8},{28,12},{17,1},{21,5},{25,9},{29,13},{18,2},{... | collective-permute-start | bytes 331784 | tf_op jit(solution)/shard_map/ppermute | solution.py:364
  26.7 2.5 %local_part.3 = (f32[512,1024]{1,0:T(8,128)S(1)}, bf16[512,1024]{1,0:T(8,128)(2,1)S(1)}) custom-call(bf16[512,1024]{1,0:T(8,128)(2,1)S(1)} %get-tuple-element.85.refs_0_, s32[512,1792]{1,0:T(8,128)S(1)} %bitcast.23, bf16[512,1792]{1,0:T(8,128)(2,1)S(1)} %bitcast.28, f32[16,512]{1,0:T(8,128)S(1)} %get-tuple-element.86.refs_3_, ...), custom_call_target="tpu_custom_call" | custom-call | flops 20000000000 | tf_op jit(solution)/shard_map/local_part/pallas_call | solution.py:45
  29.2 1.3 %join_states.7 = (bf16[560,128]{1,0:T(8,128)(2,1)S(1)}, f32[560,128]{1,0:T(8,128)}) custom-call(s32[8]{0:T(128)S(1)} %stack.27.refs_0_, f32[560,128]{1,0:T(8,128)S(1)} %get-tuple-element.84.refs_1_, bf16[560,128]{1,0:T(8,128)(2,1)S(1)} %collective-permute-done.5.refs_2_.refs_3_, f32[512,1024]{1,0:T(8,128)S(1)} %get-tuple-element.88.refs_3_.refs_2_), custom_call_target="tpu_custom_call" | custom-call | flops 20000000000 | tf_op jit(solution)/shard_map/join_states/pallas_call | solution.py:45
  30.5 1.5 %collective-permute-start.7 = (bf16[560,128]{1,0:T(8,128)(2,1)S(1)}, bf16[560,128]{1,0:T(8,128)(2,1)S(1)}, u32[]{:S(2)}, u32[]{:S(2)}) collective-permute-start(bf16[560,128]{1,0:T(8,128)(2,1)S(1)} %get-tuple-element.89.refs_1_), channel_id=1, source_target_pairs={{16,0},{20,4},{24,8},{28,12},{17,1},{21,5},{25,9},{29,13},{18,2},{... | collective-permute-start | bytes 430088 | tf_op jit(solution)/shard_map/ppermute | solution.py:364
  32.0 0.9 collective-permute-start.11
  34.2 4.9 %collective-permute-done.8.refs_0_ = bf16[1,2,224,512]{3,2,1,0:T(8,128)(2,1)S(1)} collective-permute-done((bf16[1,2,224,512]{3,2,1,0:T(8,128)(2,1)S(1)}, bf16[1,2,224,512]{3,2,1,0:T(8,128)(2,1)S(1)}, u32[]{:S(2)}, u32[]{:S(2)}) %collective-permute-start.8) | collective-permute-done | bytes 458784 | tf_op jit(solution)/shard_map/ppermute | solution.py:360
  39.1 1.2 collective-permute-start.12
  40.3 0.6 carries.3
  40.9 1.4 %collective-permute-start.10 = (bf16[512,128]{1,0:T(8,128)(2,1)S(1)}, bf16[512,128]{1,0:T(8,128)(2,1)S(1)}, u32[]{:S(2)}, u32[]{:S(2)}) collective-permute-start(bf16[512,128]{1,0:T(8,128)(2,1)S(1)} %get-tuple-element.93.refs_6_), channel_id=1, source_target_pairs={{0,4},{4,0},{8,12},{12,8},{16,20},{20,16},{24,28},{28,24},{1,5},{5... | collective-permute-start | bytes 393224 | tf_op jit(solution)/shard_map/ppermute | solution.py:360
  42.4 0.9 value_grad.4.refs_6_.refs_4_.refs_1_
  43.3 0.7 collective-permute-start.13
  44.0 0.9 value_grad.5.refs_6_.refs_2_.refs_4_
  44.9 1.4 %collective-permute-start.17 = (bf16[512,384]{1,0:T(8,128)(2,1)S(1)}, bf16[512,384]{1,0:T(8,128)(2,1)S(1)}, u32[]{:S(2)}, u32[]{:S(2)}) collective-permute-start(bf16[512,384]{1,0:T(8,128)(2,1)S(1)} %value_grad.5.refs_6_.refs_2_.refs_4_), channel_id=1, source_target_pairs={{0,4},{4,0},{8,12},{12,8},{16,20},{20,16},{24,28},{28,24},{1,5},{5... | collective-permute-start | bytes 1179656 | tf_op jit(solution)/shard_map/ppermute | solution.py:360
  46.4 1.0 collective-permute-done.10.refs_5_
  47.4 1.8 %value_grad.6.refs_6_.refs_3_.refs_4_ = bf16[512,512]{1,0:T(8,128)(2,1)} custom-call(s32[8]{0:T(128)S(1)} %stack.27.refs_0_, bf16[512,1024]{1,0:T(8,128)(2,1)S(1)} %get-tuple-element.94.refs_1_, f32[512,1024]{1,0:T(8,128)S(1)} %get-tuple-element.88.refs_3_.refs_2_, f32[512,128]{1,0:T(8,128)S(1)} %get-tuple-element.87.refs_4_.refs_3_, ...), custom_call_target="tpu_custom_call" | custom-call | flops 20000000000 | tf_op jit(solution)/shard_map/value_grad/pallas_call | solution.py:45
  49.2 1.4 %collective-permute-start.14 = (bf16[512,512]{1,0:T(8,128)(2,1)}, bf16[512,512]{1,0:T(8,128)(2,1)}, u32[]{:S(2)}, u32[]{:S(2)}) collective-permute-start(bf16[512,512]{1,0:T(8,128)(2,1)} %value_grad.6.refs_6_.refs_3_.refs_4_), channel_id=1, source_target_pairs={{0,4},{4,0},{8,12},{12,8},{16,20},{20,16},{24,28},{28,24},{1,5},{5... | collective-permute-start | bytes 1572872 | tf_op jit(solution)/shard_map/ppermute | solution.py:360
  50.6 1.8 %value_grad.7.refs_6_.refs_4_ = bf16[512,512]{1,0:T(8,128)(2,1)} custom-call(s32[8]{0:T(128)S(1)} %stack.27.refs_0_, bf16[512,1024]{1,0:T(8,128)(2,1)S(1)} %get-tuple-element.94.refs_1_, f32[512,1024]{1,0:T(8,128)S(1)} %get-tuple-element.88.refs_3_.refs_2_, f32[512,128]{1,0:T(8,128)S(1)} %get-tuple-element.87.refs_4_.refs_3_, ...), custom_call_target="tpu_custom_call" | custom-call | flops 20000000000 | tf_op jit(solution)/shard_map/value_grad/pallas_call | solution.py:45
  53.0 1.8 %merge_inputs.1 = (bf16[2,2,224,512]{3,2,1,0:T(8,128)(2,1)S(1)}, bf16[2,2,224,512]{3,2,1,0:T(8,128)(2,1)S(1)}, bf16[2,2,224,512]{3,2,1,0:T(8,128)(2,1)S(1)}, bf16[2,2,224,512]{3,2,1,0:T(8,128)(2,1)S(1)}) custom-call(bf16[2,2,224,512]{3,2,1,0:T(8,128)(2,1)} %get-tuple-element.67.refs_4_.refs_0_, ...), custom_call_target="tpu_custom_call" | custom-call | flops 20000000000 | tf_op jit(solution)/shard_map/merge_inputs/pallas_call | solution.py:45
  54.9 0.9 collective-permute-done.13.refs_5_
  55.8 2.1 %weight_part.4 = (bf16[4,224,384]{2,1,0:T(8,128)(2,1)S(1)}, f32[4,224,384]{2,1,0:T(8,128)S(1)}) custom-call(bf16[2,2,224,512]{3,2,1,0:T(8,128)(2,1)S(1)} %get-tuple-element.96.refs_0_.refs_6_, bf16[2,2,224,512]{3,2,1,0:T(8,128)(2,1)S(1)} %get-tuple-element.97.refs_1_, bf16[2,2,224,512]{3,2,1,0:T(8,128)(2,1)S(1)} %get-tuple-element.98.refs_2_, ...), custom_call_target="tpu_custom_call" | custom-call | flops 20000000000 | tf_op jit(solution)/shard_map/weight_part/pallas_call | solution.py:45
  58.5 3.8 %input_part.4 = (bf16[512,1152]{1,0:T(8,128)(2,1)S(1)}, bf16[512,1792]{1,0:T(8,128)(2,1)S(1)}) custom-call(s32[8]{0:T(128)S(1)} %stack.27.refs_0_, bf16[512,384]{1,0:T(8,128)(2,1)S(1)} %value_grad.4.refs_6_.refs_4_.refs_1_, bf16[512,384]{1,0:T(8,128)(2,1)S(1)} %value_grad.5.refs_6_.refs_2_.refs_4_, bf16[512,512]{1,0:T(8,128)(2,1)} %value_grad.6.refs_6_.refs_3_.refs_4_, ...), custom_call_target="tpu_custom_call" | custom-call | flops 20000000000 | tf_op jit(solution)/shard_map/input_part/pallas_call | solution.py:45
  62.3 0.7 fold_weight.10
  63.0 1.7 %collective-permute-start.16 = (bf16[2,224,384]{2,1,0:T(8,128)(2,1)S(1)}, bf16[2,224,384]{2,1,0:T(8,128)(2,1)S(1)}, u32[]{:S(2)}, u32[]{:S(2)}) collective-permute-start(bf16[2,224,384]{2,1,0:T(8,128)(2,1)S(1)} %get-tuple-element.105.refs_6_), channel_id=1, source_target_pairs={{0,8},{4,12},{8,0},{12,4},{16,24},{20,28},{24,16},{28,20},{1,9},{5... | collective-permute-start | bytes 1032200 | tf_op jit(solution)/shard_map/ppermute | solution.py:360
  64.7 2.1 %weight_part.5 = (bf16[4,224,384]{2,1,0:T(8,128)(2,1)S(1)}, f32[4,224,384]{2,1,0:T(8,128)S(1)}) custom-call(bf16[2,2,224,512]{3,2,1,0:T(8,128)(2,1)S(1)} %get-tuple-element.96.refs_0_.refs_6_, bf16[2,2,224,512]{3,2,1,0:T(8,128)(2,1)S(1)} %get-tuple-element.97.refs_1_, bf16[2,2,224,512]{3,2,1,0:T(8,128)(2,1)S(1)} %get-tuple-element.98.refs_2_, ...), custom_call_target="tpu_custom_call" | custom-call | flops 20000000000 | tf_op jit(solution)/shard_map/weight_part/pallas_call | solution.py:45
  66.8 3.4 %input_part.5.refs_3_ = bf16[512,1792]{1,0:T(8,128)(2,1)} custom-call(s32[8]{0:T(128)S(1)} %stack.27.refs_0_, bf16[512,1152]{1,0:T(8,128)(2,1)S(1)} %get-tuple-element.103.refs_3_.refs_1_, bf16[512,1792]{1,0:T(8,128)(2,1)S(1)} %get-tuple-element.101.refs_2_.refs_1_, bf16[3584,1792]{1,0:T(8,128)(2,1)S(1)} %bitcast.17, ...), custom_call_target="tpu_custom_call" | custom-call | flops 20000000000 | tf_op jit(solution)/shard_map/input_part/pallas_call | solution.py:45
  70.2 0.9 collective-permute-start.27
  71.2 0.7 fold_weight.11
  71.8 1.3 collective-permute-start.22
  73.1 0.6 fold_weight.12
  73.7 2.7 %collective-permute-start.23 = (bf16[1,224,384]{2,1,0:T(8,128)(2,1)S(1)}, bf16[1,224,384]{2,1,0:T(8,128)(2,1)S(1)}, u32[]{:S(2)}, u32[]{:S(2)}) collective-permute-start(bf16[1,224,384]{2,1,0:T(8,128)(2,1)S(1)} %get-tuple-element.109.refs_6_), channel_id=1, source_target_pairs={{0,16},{4,20},{8,24},{12,28},{16,0},{20,4},{24,8},{28,12},{1,17},{... | collective-permute-start | bytes 516104 | tf_op jit(solution)/shard_map/ppermute | solution.py:360
  76.4 3.3 %weight_part.6 = (bf16[4,224,512]{2,1,0:T(8,128)(2,1)S(1)}, f32[4,224,512]{2,1,0:T(8,128)S(1)}) custom-call(bf16[2,2,224,512]{3,2,1,0:T(8,128)(2,1)S(1)} %get-tuple-element.96.refs_0_.refs_6_, bf16[2,2,224,512]{3,2,1,0:T(8,128)(2,1)S(1)} %get-tuple-element.97.refs_1_, bf16[2,2,224,512]{3,2,1,0:T(8,128)(2,1)S(1)} %get-tuple-element.98.refs_2_, ...), custom_call_target="tpu_custom_call" | custom-call | flops 20000000000 | tf_op jit(solution)/shard_map/weight_part/pallas_call | solution.py:45
  79.7 2.2 %input_part.6.refs_3_.refs_1_ = f32[512,768]{1,0:T(8,128)S(1)} custom-call(s32[8]{0:T(128)S(1)} %stack.27.refs_0_, bf16[512,1792]{1,0:T(8,128)(2,1)S(1)} %get-tuple-element.101.refs_2_.refs_1_, bf16[3584,1792]{1,0:T(8,128)(2,1)S(1)} %bitcast.17, f32[4,224,512]{2,1,0:T(8,128)S(1)} %get-tuple-element.110.refs_3_.refs_1_), custom_call_target="tpu_custom_call" | custom-call | flops 20000000000 | tf_op jit(solution)/shard_map/input_part/pallas_call | solution.py:45
  82.2 0.7 fold_weight.13
  83.0 1.5 %collective-permute-start.26 = (bf16[2,224,512]{2,1,0:T(8,128)(2,1)S(1)}, bf16[2,224,512]{2,1,0:T(8,128)(2,1)S(1)}, u32[]{:S(2)}, u32[]{:S(2)}) collective-permute-start(bf16[2,224,512]{2,1,0:T(8,128)(2,1)S(1)} %get-tuple-element.112.refs_6_), channel_id=1, source_target_pairs={{0,8},{4,12},{8,0},{12,4},{16,24},{20,28},{24,16},{28,20},{1,9},{5... | collective-permute-start | bytes 1376264 | tf_op jit(solution)/shard_map/ppermute | solution.py:360
  84.6 3.5 %weight_part.7 = (bf16[4,224,512]{2,1,0:T(8,128)(2,1)S(1)}, f32[4,224,512]{2,1,0:T(8,128)S(1)}) custom-call(bf16[2,2,224,512]{3,2,1,0:T(8,128)(2,1)S(1)} %get-tuple-element.96.refs_0_.refs_6_, bf16[2,2,224,512]{3,2,1,0:T(8,128)(2,1)S(1)} %get-tuple-element.97.refs_1_, bf16[2,2,224,512]{3,2,1,0:T(8,128)(2,1)S(1)} %get-tuple-element.98.refs_2_, ...), custom_call_target="tpu_custom_call" | custom-call | flops 20000000000 | tf_op jit(solution)/shard_map/weight_part/pallas_call | solution.py:45
  88.4 0.6 fold_weight.14
  89.0 1.9 %collective-permute-start.28 = (bf16[1,224,384]{2,1,0:T(8,128)(2,1)S(1)}, bf16[1,224,384]{2,1,0:T(8,128)(2,1)S(1)}, u32[]{:S(2)}, u32[]{:S(2)}) collective-permute-start(bf16[1,224,384]{2,1,0:T(8,128)(2,1)S(1)} %get-tuple-element.116.refs_3_), channel_id=1, source_target_pairs={{0,16},{4,20},{8,24},{12,28},{16,0},{20,4},{24,8},{28,12},{1,17},{... | collective-permute-start | bytes 516104 | tf_op jit(solution)/shard_map/ppermute | solution.py:360
  90.9 0.7 fold_weight.15
  91.6 0.7 collective-permute-start.25
  92.3 0.7 fold_weight.16
  93.0 1.4 %collective-permute-start.24 = (bf16[2,224,256]{2,1,0:T(8,128)(2,1)S(1)}, bf16[2,224,256]{2,1,0:T(8,128)(2,1)S(1)}, u32[]{:S(2)}, u32[]{:S(2)}) collective-permute-start(bf16[2,224,256]{2,1,0:T(8,128)(2,1)S(1)} %get-tuple-element.119.refs_3_), channel_id=1, source_target_pairs={{0,8},{4,12},{8,0},{12,4},{16,24},{20,28},{24,16},{28,20},{1,9},{5... | collective-permute-start | bytes 688136 | tf_op jit(solution)/shard_map/ppermute | solution.py:360
  94.4 5.6 %collective-permute-done.26.refs_2_ = bf16[2,224,512]{2,1,0:T(8,128)(2,1)S(1)} collective-permute-done((bf16[2,224,512]{2,1,0:T(8,128)(2,1)S(1)}, bf16[2,224,512]{2,1,0:T(8,128)(2,1)S(1)}, u32[]{:S(2)}, u32[]{:S(2)}) %collective-permute-start.26) | collective-permute-done | bytes 458784 | tf_op jit(solution)/shard_map/ppermute | solution.py:360
  100.0 0.6 fold_weight.17
  100.7 1.0 collective-permute-start.29
  101.7 8.2 %collective-permute-done.25.refs_2_ = bf16[2,224,256]{2,1,0:T(8,128)(2,1)S(1)} collective-permute-done((bf16[2,224,256]{2,1,0:T(8,128)(2,1)S(1)}, bf16[2,224,256]{2,1,0:T(8,128)(2,1)S(1)}, u32[]{:S(2)}, u32[]{:S(2)}) %collective-permute-start.25) | collective-permute-done | bytes 229408 | tf_op jit(solution)/shard_map/ppermute | solution.py:360
  110.5 1.0 collective-permute-start.30
  111.5 3.0 %collective-permute-done.24.refs_2_ = bf16[2,224,256]{2,1,0:T(8,128)(2,1)S(1)} collective-permute-done((bf16[2,224,256]{2,1,0:T(8,128)(2,1)S(1)}, bf16[2,224,256]{2,1,0:T(8,128)(2,1)S(1)}, u32[]{:S(2)}, u32[]{:S(2)}) %collective-permute-start.24) | collective-permute-done | bytes 229408 | tf_op jit(solution)/shard_map/ppermute | solution.py:360
  115.1 1.0 collective-permute-start.31
  116.1 2.7 %input_part.7.refs_0_.refs_2_ = f32[512,1792]{1,0:T(8,128)S(1)} custom-call(s32[8]{0:T(128)S(1)} %stack.27.refs_0_, f32[512,768]{1,0:T(8,128)S(1)} %copy-done.5, bf16[512,1792]{1,0:T(8,128)(2,1)S(1)} %get-tuple-element.101.refs_2_.refs_1_, bf16[3584,1792]{1,0:T(8,128)(2,1)S(1)} %bitcast.19, bf16[1,224,256]{2,1,0:T(8,128)(2,1)S(1)} %get-tuple-element.124.refs_4_), custom_call_target="tpu_custom_call" | custom-call | flops 20000000000 | tf_op jit(solution)/shard_map/input_part/pallas_call | solution.py:45
  118.9 3.0 %grad_input.1 = (bf16[512,1792]{1,0:T(8,128)(2,1)}, f32[8,128]{1,0:T(8,128)S(1)}) custom-call(f32[512,1792]{1,0:T(8,128)S(1)} %input_part.7.refs_0_.refs_2_, bf16[512,1792]{1,0:T(8,128)(2,1)} %collective-permute-done.27.refs_1_, f32[512,1792]{1,0:T(8,128)S(1)} %input_part.7.refs_0_.refs_2_), custom_call_target="tpu_custom_call" | custom-call | flops 20000000000 | tf_op jit(solution)/shard_map/grad_input/pallas_call | solution.py:45
  121.9 4.0 %collective-permute-done.31.refs_9_ = bf16[1,224,256]{2,1,0:T(8,128)(2,1)S(1)} collective-permute-done((bf16[1,224,256]{2,1,0:T(8,128)(2,1)S(1)}, bf16[1,224,256]{2,1,0:T(8,128)(2,1)S(1)}, u32[]{:S(2)}, u32[]{:S(2)}) %collective-permute-start.31) | collective-permute-done | bytes 114720 | tf_op jit(solution)/shard_map/ppermute | solution.py:360
  125.9 1.3 %grad_weight.1 = f32[224,1792]{1,0:T(8,128)} custom-call(f32[1,224,384]{2,1,0:T(8,128)S(1)} %get-tuple-element.126.refs_0_, bf16[1,224,384]{2,1,0:T(8,128)(2,1)S(1)} %collective-permute-done.23.refs_1_, f32[1,224,384]{2,1,0:T(8,128)S(1)} %get-tuple-element.127.refs_2_, bf16[1,224,384]{2,1,0:T(8,128)(2,1)S(1)} %collective-permute-done.28.refs_3_, ...), custom_call_target="tpu_custom_call" | custom-call | flops 20000000000 | tf_op jit(solution)/shard_map/grad_weight/pallas_call | solution.py:45
  (73 shorter events, 7.0 us)
Async XLA Ops:
  0.8 1.5 %copy-start.2 = (bf16[1,512,1792]{2,1,0:T(8,128)(2,1)S(1)}, bf16[1,512,1792]{2,1,0:T(8,128)(2,1)}, u32[]{:S(2)}) copy-start(bf16[1,512,1792]{2,1,0:T(8,128)(2,1)} %param.6) | copy-start | bytes 5505028
  2.3 5.1 %copy-start.6 = (f32[1,14,512]{2,0,1:T(1,128)S(1)}, f32[1,14,512]{2,0,1:T(1,128)}, u32[]{:S(2)}) copy-start(f32[1,14,512]{2,0,1:T(1,128)} %param.11) | copy-start | bytes 86020
  2.3 5.1 %copy-start = (s32[1,512,1792]{2,1,0:T(8,128)S(1)}, s32[1,512,1792]{2,1,0:T(8,128)}, u32[]{:S(2)}) copy-start(s32[1,512,1792]{2,1,0:T(8,128)} %param.9) | copy-start | bytes 11010052
  2.3 5.1 %copy-start.3 = (bf16[1,512,1792]{2,1,0:T(8,128)(2,1)S(1)}, bf16[1,512,1792]{2,1,0:T(8,128)(2,1)}, u32[]{:S(2)}) copy-start(bf16[1,512,1792]{2,1,0:T(8,128)(2,1)} %param.8) | copy-start | bytes 5505028
  4.4 38.0 %collective-permute-start.9 = (bf16[2,2,224,512]{3,2,1,0:T(8,128)(2,1)}, bf16[2,2,224,512]{3,2,1,0:T(8,128)(2,1)}, u32[]{:S(2)}, u32[]{:S(2)}) collective-permute-start(bf16[2,2,224,512]{3,2,1,0:T(8,128)(2,1)} %get-tuple-element.67.refs_4_.refs_0_), channel_id=1, source_target_pairs={{0,2},{2,0},{1,3},{3,1},{4,6},{6,4},{5,7},{7,5},{8,10},{10,8},{9,1... | collective-permute-start | bytes 2752520 | tf_op jit(solution)/shard_map/ppermute | solution.py:360
  9.5 6.0 %collective-permute-start.1 = (bf16[432,128]{1,0:T(8,128)(2,1)S(1)}, bf16[432,128]{1,0:T(8,128)(2,1)S(1)}, u32[]{:S(2)}, u32[]{:S(2)}) collective-permute-start(bf16[432,128]{1,0:T(8,128)(2,1)S(1)} %get-tuple-element.71.refs_4_), channel_id=1, source_target_pairs={{0,4},{4,0},{8,12},{12,8},{16,20},{20,16},{24,28},{28,24},{1,5},{5... | collective-permute-start | bytes 331784 | tf_op jit(solution)/shard_map/ppermute | solution.py:360
  13.4 6.8 %collective-permute-start = (bf16[560,128]{1,0:T(8,128)(2,1)S(1)}, bf16[560,128]{1,0:T(8,128)(2,1)S(1)}, u32[]{:S(2)}, u32[]{:S(2)}) collective-permute-start(bf16[560,128]{1,0:T(8,128)(2,1)S(1)} %get-tuple-element.73.refs_3_), channel_id=1, source_target_pairs={{0,4},{4,0},{8,12},{12,8},{16,20},{20,16},{24,28},{28,24},{1,5},{5... | collective-permute-start | bytes 430088 | tf_op jit(solution)/shard_map/ppermute | solution.py:360
  13.9 18.0 %collective-permute-start.4 = (bf16[1,2,224,512]{3,2,1,0:T(8,128)(2,1)S(1)}, bf16[1,2,224,512]{3,2,1,0:T(8,128)(2,1)S(1)}, u32[]{:S(2)}, u32[]{:S(2)}) collective-permute-start(bf16[1,2,224,512]{3,2,1,0:T(8,128)(2,1)S(1)} %get-tuple-element.83.refs_4_), channel_id=1, source_target_pairs={{0,4},{4,0},{8,12},{12,8},{16,20},{20,16},{24,28},{28,24},{1,5},{5... | collective-permute-start | bytes 1376264 | tf_op jit(solution)/shard_map/ppermute | solution.py:360
  16.0 8.1 %collective-permute-start.2 = (bf16[432,128]{1,0:T(8,128)(2,1)S(1)}, bf16[432,128]{1,0:T(8,128)(2,1)S(1)}, u32[]{:S(2)}, u32[]{:S(2)}) collective-permute-start(bf16[432,128]{1,0:T(8,128)(2,1)S(1)} %get-tuple-element.76.refs_3_), channel_id=1, source_target_pairs={{8,0},{12,4},{16,8},{20,12},{24,16},{28,20},{9,1},{13,5},{17,9},{2... | collective-permute-start | bytes 331784 | tf_op jit(solution)/shard_map/ppermute | solution.py:364
  17.3 21.7 %collective-permute-start.8 = (bf16[1,2,224,512]{3,2,1,0:T(8,128)(2,1)S(1)}, bf16[1,2,224,512]{3,2,1,0:T(8,128)(2,1)S(1)}, u32[]{:S(2)}, u32[]{:S(2)}) collective-permute-start(bf16[1,2,224,512]{3,2,1,0:T(8,128)(2,1)S(1)} %get-tuple-element.92.refs_4_), channel_id=1, source_target_pairs={{0,4},{4,0},{8,12},{12,8},{16,20},{20,16},{24,28},{28,24},{1,5},{5... | collective-permute-start | bytes 1376264 | tf_op jit(solution)/shard_map/ppermute | solution.py:360
  20.1 2.0 %copy-start.1 = (s32[1,512,1792]{2,1,0:T(8,128)S(1)}, s32[1,512,1792]{2,1,0:T(8,128)}, u32[]{:S(2)}) copy-start(s32[1,512,1792]{2,1,0:T(8,128)} %param.10) | copy-start | bytes 11010052
  20.7 8.5 %collective-permute-start.5 = (bf16[560,128]{1,0:T(8,128)(2,1)S(1)}, bf16[560,128]{1,0:T(8,128)(2,1)S(1)}, u32[]{:S(2)}, u32[]{:S(2)}) collective-permute-start(bf16[560,128]{1,0:T(8,128)(2,1)S(1)} %get-tuple-element.78.refs_5_), channel_id=1, source_target_pairs={{8,0},{12,4},{16,8},{20,12},{24,16},{28,20},{9,1},{13,5},{17,9},{2... | collective-permute-start | bytes 430088 | tf_op jit(solution)/shard_map/ppermute | solution.py:364
  25.4 7.6 %collective-permute-start.3 = (bf16[432,128]{1,0:T(8,128)(2,1)S(1)}, bf16[432,128]{1,0:T(8,128)(2,1)S(1)}, u32[]{:S(2)}, u32[]{:S(2)}) collective-permute-start(bf16[432,128]{1,0:T(8,128)(2,1)S(1)} %get-tuple-element.82.refs_5_), channel_id=1, source_target_pairs={{16,0},{20,4},{24,8},{28,12},{17,1},{21,5},{25,9},{29,13},{18,2},{... | collective-permute-start | bytes 331784 | tf_op jit(solution)/shard_map/ppermute | solution.py:364
  30.5 9.8 %collective-permute-start.7 = (bf16[560,128]{1,0:T(8,128)(2,1)S(1)}, bf16[560,128]{1,0:T(8,128)(2,1)S(1)}, u32[]{:S(2)}, u32[]{:S(2)}) collective-permute-start(bf16[560,128]{1,0:T(8,128)(2,1)S(1)} %get-tuple-element.89.refs_1_), channel_id=1, source_target_pairs={{16,0},{20,4},{24,8},{28,12},{17,1},{21,5},{25,9},{29,13},{18,2},{... | collective-permute-start | bytes 430088 | tf_op jit(solution)/shard_map/ppermute | solution.py:364
  32.0 15.3 %collective-permute-start.11 = (bf16[1,2,224,512]{3,2,1,0:T(8,128)(2,1)S(1)}, bf16[1,2,224,512]{3,2,1,0:T(8,128)(2,1)S(1)}, u32[]{:S(2)}, u32[]{:S(2)}) collective-permute-start(bf16[1,2,224,512]{3,2,1,0:T(8,128)(2,1)S(1)} %pass_on.2.refs_5_.refs_2_), channel_id=1, source_target_pairs={{0,2},{2,0},{1,3},{3,1},{4,6},{6,4},{5,7},{7,5},{8,10},{10,8},{9,1... | collective-permute-start | bytes 1376264 | tf_op jit(solution)/shard_map/ppermute | solution.py:360
  33.6 8.7 %collective-permute-start.6 = (bf16[384,128]{1,0:T(8,128)(2,1)S(1)}, bf16[384,128]{1,0:T(8,128)(2,1)S(1)}, u32[]{:S(2)}, u32[]{:S(2)}) collective-permute-start(bf16[384,128]{1,0:T(8,128)(2,1)S(1)} %get-tuple-element.91.refs_1_), channel_id=1, source_target_pairs={{0,4},{4,0},{8,12},{12,8},{16,20},{20,16},{24,28},{28,24},{1,5},{5... | collective-permute-start | bytes 294920 | tf_op jit(solution)/shard_map/ppermute | solution.py:360
  39.1 13.9 %collective-permute-start.12 = (bf16[1,2,224,512]{3,2,1,0:T(8,128)(2,1)S(1)}, bf16[1,2,224,512]{3,2,1,0:T(8,128)(2,1)S(1)}, u32[]{:S(2)}, u32[]{:S(2)}) collective-permute-start(bf16[1,2,224,512]{3,2,1,0:T(8,128)(2,1)S(1)} %pass_on.3.refs_5_.refs_3_), channel_id=1, source_target_pairs={{0,2},{2,0},{1,3},{3,1},{4,6},{6,4},{5,7},{7,5},{8,10},{10,8},{9,1... | collective-permute-start | bytes 1376264 | tf_op jit(solution)/shard_map/ppermute | solution.py:360
  40.9 6.4 %collective-permute-start.10 = (bf16[512,128]{1,0:T(8,128)(2,1)S(1)}, bf16[512,128]{1,0:T(8,128)(2,1)S(1)}, u32[]{:S(2)}, u32[]{:S(2)}) collective-permute-start(bf16[512,128]{1,0:T(8,128)(2,1)S(1)} %get-tuple-element.93.refs_6_), channel_id=1, source_target_pairs={{0,4},{4,0},{8,12},{12,8},{16,20},{20,16},{24,28},{28,24},{1,5},{5... | collective-permute-start | bytes 393224 | tf_op jit(solution)/shard_map/ppermute | solution.py:360
  43.3 12.5 %collective-permute-start.13 = (bf16[512,384]{1,0:T(8,128)(2,1)S(1)}, bf16[512,384]{1,0:T(8,128)(2,1)S(1)}, u32[]{:S(2)}, u32[]{:S(2)}) collective-permute-start(bf16[512,384]{1,0:T(8,128)(2,1)S(1)} %value_grad.4.refs_6_.refs_4_.refs_1_), channel_id=1, source_target_pairs={{0,4},{4,0},{8,12},{12,8},{16,20},{20,16},{24,28},{28,24},{1,5},{5... | collective-permute-start | bytes 1179656 | tf_op jit(solution)/shard_map/ppermute | solution.py:360
  44.9 19.7 %collective-permute-start.17 = (bf16[512,384]{1,0:T(8,128)(2,1)S(1)}, bf16[512,384]{1,0:T(8,128)(2,1)S(1)}, u32[]{:S(2)}, u32[]{:S(2)}) collective-permute-start(bf16[512,384]{1,0:T(8,128)(2,1)S(1)} %value_grad.5.refs_6_.refs_2_.refs_4_), channel_id=1, source_target_pairs={{0,4},{4,0},{8,12},{12,8},{16,20},{20,16},{24,28},{28,24},{1,5},{5... | collective-permute-start | bytes 1179656 | tf_op jit(solution)/shard_map/ppermute | solution.py:360
  49.2 27.2 %collective-permute-start.14 = (bf16[512,512]{1,0:T(8,128)(2,1)}, bf16[512,512]{1,0:T(8,128)(2,1)}, u32[]{:S(2)}, u32[]{:S(2)}) collective-permute-start(bf16[512,512]{1,0:T(8,128)(2,1)} %value_grad.6.refs_6_.refs_3_.refs_4_), channel_id=1, source_target_pairs={{0,4},{4,0},{8,12},{12,8},{16,20},{20,16},{24,28},{28,24},{1,5},{5... | collective-permute-start | bytes 1572872 | tf_op jit(solution)/shard_map/ppermute | solution.py:360
  52.4 32.2 %collective-permute-start.19 = (bf16[512,512]{1,0:T(8,128)(2,1)}, bf16[512,512]{1,0:T(8,128)(2,1)}, u32[]{:S(2)}, u32[]{:S(2)}) collective-permute-start(bf16[512,512]{1,0:T(8,128)(2,1)} %value_grad.7.refs_6_.refs_4_), channel_id=1, source_target_pairs={{0,4},{4,0},{8,12},{12,8},{16,20},{20,16},{24,28},{28,24},{1,5},{5... | collective-permute-start | bytes 1572872 | tf_op jit(solution)/shard_map/ppermute | solution.py:360
  53.0 4.9 %slice-start = ((s8[12845056]{0:T(1024)(128)(4,1)}), s8[4194304]{0:T(1024)(128)(4,1)S(1)}, s32[]{:S(2)}) async-start(s8[12845056]{0:T(1024)(128)(4,1)} %bitcast.16), calls=%async_computation | async-start | bytes 8388608
  53.0 4.9 %slice-start.1 = ((s8[12845056]{0:T(1024)(128)(4,1)}), s8[4194304]{0:T(1024)(128)(4,1)S(1)}, s32[]{:S(2)}) async-start(s8[12845056]{0:T(1024)(128)(4,1)} %bitcast.16), calls=%async_computation.1 | async-start | bytes 8388608
  55.8 2.7 %slice-start.2 = ((s8[12845056]{0:T(1024)(128)(4,1)}), s8[4194304]{0:T(1024)(128)(4,1)S(1)}, s32[]{:S(2)}) async-start(s8[12845056]{0:T(1024)(128)(4,1)} %bitcast.16), calls=%async_computation.2 | async-start | bytes 8388608
  55.8 2.7 %slice-start.3 = ((s8[12845056]{0:T(1024)(128)(4,1)}), s8[262144]{0:T(1024)(128)(4,1)S(1)}, s32[]{:S(2)}) async-start(s8[12845056]{0:T(1024)(128)(4,1)} %bitcast.16), calls=%async_computation.3 | async-start | bytes 524288
  57.9 4.4 %collective-permute-start.15 = (bf16[4,224,384]{2,1,0:T(8,128)(2,1)S(1)}, bf16[4,224,384]{2,1,0:T(8,128)(2,1)S(1)}, u32[]{:S(2)}, u32[]{:S(2)}) collective-permute-start(bf16[4,224,384]{2,1,0:T(8,128)(2,1)S(1)} %get-tuple-element.102), channel_id=1, source_target_pairs={{0,1},{1,0},{2,3},{3,2},{4,5},{5,4},{6,7},{7,6},{8,9},{9,8},{10,11... | collective-permute-start | bytes 2064392 | tf_op jit(solution)/shard_map/ppermute | solution.py:360
  63.0 10.1 %collective-permute-start.16 = (bf16[2,224,384]{2,1,0:T(8,128)(2,1)S(1)}, bf16[2,224,384]{2,1,0:T(8,128)(2,1)S(1)}, u32[]{:S(2)}, u32[]{:S(2)}) collective-permute-start(bf16[2,224,384]{2,1,0:T(8,128)(2,1)S(1)} %get-tuple-element.105.refs_6_), channel_id=1, source_target_pairs={{0,8},{4,12},{8,0},{12,4},{16,24},{20,28},{24,16},{28,20},{1,9},{5... | collective-permute-start | bytes 1032200 | tf_op jit(solution)/shard_map/ppermute | solution.py:360
  66.7 4.4 %collective-permute-start.18 = (bf16[4,224,384]{2,1,0:T(8,128)(2,1)S(1)}, bf16[4,224,384]{2,1,0:T(8,128)(2,1)S(1)}, u32[]{:S(2)}, u32[]{:S(2)}) collective-permute-start(bf16[4,224,384]{2,1,0:T(8,128)(2,1)S(1)} %get-tuple-element.107), channel_id=1, source_target_pairs={{0,1},{1,0},{2,3},{3,2},{4,5},{5,4},{6,7},{7,6},{8,9},{9,8},{10,11... | collective-permute-start | bytes 2064392 | tf_op jit(solution)/shard_map/ppermute | solution.py:360
  70.2 48.7 %collective-permute-start.27 = (bf16[512,1792]{1,0:T(8,128)(2,1)}, bf16[512,1792]{1,0:T(8,128)(2,1)}, u32[]{:S(2)}, u32[]{:S(2)}) collective-permute-start(bf16[512,1792]{1,0:T(8,128)(2,1)} %input_part.5.refs_3_), channel_id=1, source_target_pairs={{0,2},{2,0},{1,3},{3,1},{4,6},{6,4},{5,7},{7,5},{8,10},{10,8},{9,1... | collective-permute-start | bytes 5505032 | tf_op jit(solution)/shard_map/ppermute | solution.py:360
  71.8 16.5 %collective-permute-start.22 = (bf16[2,224,384]{2,1,0:T(8,128)(2,1)S(1)}, bf16[2,224,384]{2,1,0:T(8,128)(2,1)S(1)}, u32[]{:S(2)}, u32[]{:S(2)}) collective-permute-start(bf16[2,224,384]{2,1,0:T(8,128)(2,1)S(1)} %get-tuple-element.108.refs_3_), channel_id=1, source_target_pairs={{0,8},{4,12},{8,0},{12,4},{16,24},{20,28},{24,16},{28,20},{1,9},{5... | collective-permute-start | bytes 1032200 | tf_op jit(solution)/shard_map/ppermute | solution.py:360
  73.7 14.6 %collective-permute-start.23 = (bf16[1,224,384]{2,1,0:T(8,128)(2,1)S(1)}, bf16[1,224,384]{2,1,0:T(8,128)(2,1)S(1)}, u32[]{:S(2)}, u32[]{:S(2)}) collective-permute-start(bf16[1,224,384]{2,1,0:T(8,128)(2,1)S(1)} %get-tuple-element.109.refs_6_), channel_id=1, source_target_pairs={{0,16},{4,20},{8,24},{12,28},{16,0},{20,4},{24,8},{28,12},{1,17},{... | collective-permute-start | bytes 516104 | tf_op jit(solution)/shard_map/ppermute | solution.py:360
  79.7 2.5 %collective-permute-start.20 = (bf16[4,224,512]{2,1,0:T(8,128)(2,1)S(1)}, bf16[4,224,512]{2,1,0:T(8,128)(2,1)S(1)}, u32[]{:S(2)}, u32[]{:S(2)}) collective-permute-start(bf16[4,224,512]{2,1,0:T(8,128)(2,1)S(1)} %get-tuple-element.111), channel_id=1, source_target_pairs={{0,1},{1,0},{2,3},{3,2},{4,5},{5,4},{6,7},{7,6},{8,9},{9,8},{10,11... | collective-permute-start | bytes 2752520 | tf_op jit(solution)/shard_map/ppermute | solution.py:360
  81.9 1.1 copy-start.4
  83.0 17.0 %collective-permute-start.26 = (bf16[2,224,512]{2,1,0:T(8,128)(2,1)S(1)}, bf16[2,224,512]{2,1,0:T(8,128)(2,1)S(1)}, u32[]{:S(2)}, u32[]{:S(2)}) collective-permute-start(bf16[2,224,512]{2,1,0:T(8,128)(2,1)S(1)} %get-tuple-element.112.refs_6_), channel_id=1, source_target_pairs={{0,8},{4,12},{8,0},{12,4},{16,24},{20,28},{24,16},{28,20},{1,9},{5... | collective-permute-start | bytes 1376264 | tf_op jit(solution)/shard_map/ppermute | solution.py:360
  88.1 2.8 %collective-permute-start.21 = (bf16[4,224,512]{2,1,0:T(8,128)(2,1)S(1)}, bf16[4,224,512]{2,1,0:T(8,128)(2,1)S(1)}, u32[]{:S(2)}, u32[]{:S(2)}) collective-permute-start(bf16[4,224,512]{2,1,0:T(8,128)(2,1)S(1)} %get-tuple-element.114), channel_id=1, source_target_pairs={{0,1},{1,0},{2,3},{3,2},{4,5},{5,4},{6,7},{7,6},{8,9},{9,8},{10,11... | collective-permute-start | bytes 2752520 | tf_op jit(solution)/shard_map/ppermute | solution.py:360
  89.0 32.9 %collective-permute-start.28 = (bf16[1,224,384]{2,1,0:T(8,128)(2,1)S(1)}, bf16[1,224,384]{2,1,0:T(8,128)(2,1)S(1)}, u32[]{:S(2)}, u32[]{:S(2)}) collective-permute-start(bf16[1,224,384]{2,1,0:T(8,128)(2,1)S(1)} %get-tuple-element.116.refs_3_), channel_id=1, source_target_pairs={{0,16},{4,20},{8,24},{12,28},{16,0},{20,4},{24,8},{28,12},{1,17},{... | collective-permute-start | bytes 516104 | tf_op jit(solution)/shard_map/ppermute | solution.py:360
  91.6 18.3 %collective-permute-start.25 = (bf16[2,224,256]{2,1,0:T(8,128)(2,1)S(1)}, bf16[2,224,256]{2,1,0:T(8,128)(2,1)S(1)}, u32[]{:S(2)}, u32[]{:S(2)}) collective-permute-start(bf16[2,224,256]{2,1,0:T(8,128)(2,1)S(1)} %get-tuple-element.117.refs_3_), channel_id=1, source_target_pairs={{0,8},{4,12},{8,0},{12,4},{16,24},{20,28},{24,16},{28,20},{1,9},{5... | collective-permute-start | bytes 688136 | tf_op jit(solution)/shard_map/ppermute | solution.py:360
  93.0 21.5 %collective-permute-start.24 = (bf16[2,224,256]{2,1,0:T(8,128)(2,1)S(1)}, bf16[2,224,256]{2,1,0:T(8,128)(2,1)S(1)}, u32[]{:S(2)}, u32[]{:S(2)}) collective-permute-start(bf16[2,224,256]{2,1,0:T(8,128)(2,1)S(1)} %get-tuple-element.119.refs_3_), channel_id=1, source_target_pairs={{0,8},{4,12},{8,0},{12,4},{16,24},{20,28},{24,16},{28,20},{1,9},{5... | collective-permute-start | bytes 688136 | tf_op jit(solution)/shard_map/ppermute | solution.py:360
  100.7 21.2 %collective-permute-start.29 = (bf16[1,224,512]{2,1,0:T(8,128)(2,1)S(1)}, bf16[1,224,512]{2,1,0:T(8,128)(2,1)S(1)}, u32[]{:S(2)}, u32[]{:S(2)}) collective-permute-start(bf16[1,224,512]{2,1,0:T(8,128)(2,1)S(1)} %get-tuple-element.122.refs_3_), channel_id=1, source_target_pairs={{0,16},{4,20},{8,24},{12,28},{16,0},{20,4},{24,8},{28,12},{1,17},{... | collective-permute-start | bytes 688136 | tf_op jit(solution)/shard_map/ppermute | solution.py:360
  109.9 6.2 %slice-start.4 = ((s8[12845056]{0:T(1024)(128)(4,1)}), s8[4194304]{0:T(1024)(128)(4,1)S(1)}, s32[]{:S(2)}) async-start(s8[12845056]{0:T(1024)(128)(4,1)} %bitcast.18), calls=%async_computation.4 | async-start | bytes 8388608
  109.9 6.2 %slice-start.5 = ((s8[12845056]{0:T(1024)(128)(4,1)}), s8[4194304]{0:T(1024)(128)(4,1)S(1)}, s32[]{:S(2)}) async-start(s8[12845056]{0:T(1024)(128)(4,1)} %bitcast.18), calls=%async_computation.5 | async-start | bytes 8388608
  110.5 5.6 %slice-start.6 = ((s8[12845056]{0:T(1024)(128)(4,1)}), s8[4194304]{0:T(1024)(128)(4,1)S(1)}, s32[]{:S(2)}) async-start(s8[12845056]{0:T(1024)(128)(4,1)} %bitcast.18), calls=%async_computation.6 | async-start | bytes 8388608
  110.5 15.4 %collective-permute-start.30 = (bf16[1,224,256]{2,1,0:T(8,128)(2,1)S(1)}, bf16[1,224,256]{2,1,0:T(8,128)(2,1)S(1)}, u32[]{:S(2)}, u32[]{:S(2)}) collective-permute-start(bf16[1,224,256]{2,1,0:T(8,128)(2,1)S(1)} %get-tuple-element.123.refs_3_), channel_id=1, source_target_pairs={{0,16},{4,20},{8,24},{12,28},{16,0},{20,4},{24,8},{28,12},{1,17},{... | collective-permute-start | bytes 344072 | tf_op jit(solution)/shard_map/ppermute | solution.py:360
  114.5 1.6 %slice-start.7 = ((s8[12845056]{0:T(1024)(128)(4,1)}), s8[262144]{0:T(1024)(128)(4,1)S(1)}, s32[]{:S(2)}) async-start(s8[12845056]{0:T(1024)(128)(4,1)} %bitcast.18), calls=%async_computation.7 | async-start | bytes 524288
  114.5 1.6 %copy-start.5 = (f32[512,768]{1,0:T(8,128)S(1)}, f32[512,768]{1,0:T(8,128)}, u32[]{:S(2)}) copy-start(f32[512,768]{1,0:T(8,128)} %copy-done.4) | copy-start | bytes 4718596
  115.1 10.8 %collective-permute-start.31 = (bf16[1,224,256]{2,1,0:T(8,128)(2,1)S(1)}, bf16[1,224,256]{2,1,0:T(8,128)(2,1)S(1)}, u32[]{:S(2)}, u32[]{:S(2)}) collective-permute-start(bf16[1,224,256]{2,1,0:T(8,128)(2,1)S(1)} %get-tuple-element.124.refs_4_), channel_id=1, source_target_pairs={{0,16},{4,20},{8,24},{12,28},{16,0},{20,4},{24,8},{28,12},{1,17},{... | collective-permute-start | bytes 344072 | tf_op jit(solution)/shard_map/ppermute | solution.py:360
